TPU v7x, 512 devices: a whole 4x4x16 slice. The times are simulated.
512 devices in a mesh: grp: 32 (over z, y_hi), col: 16 (over x, y_lo, core).
Axes of the slice: x: 4, y: 4 (y_hi: 2, y_lo: 2; y = y_hi * 2 + y_lo), z: 16, core: 2. Of those that a mesh axis runs over, the one named last changes fastest.
Arguments:
- window_rows: bfloat16 [122880, 1024], P('grp', 'col'), may hold values from -0.0234375 to 0.0234375
- secular: bfloat16 [122880, 4096], P('grp', 'col'), may hold values from -6 to 6
- source: int32 [122880], P('grp'), may hold values from 0 to 122879, as said below
- kept_count: int32 [1], replicated, may hold values from 61440 to 122879
Outputs:
- merged: bfloat16 [2, 1024, 4096], P(None, 'grp', 'col')
Inputs may be any that keep to these rules, and one draw needn't show every extreme that they name: source is a permutation of 0 to 122879; for j in block b of 3840 indices, source[j] lies in block b or in block b + 16 (b < 16) or b - 16 (b >= 16).
All inputs are finite; a program needn't handle non-finite values.
Results may differ from a plain program's by a relative error of at most 0.0011.
Values may be sent and summed in bfloat16 or wider, within the bound.
No kernel may reach another device: no remote copies, remote signals or barrier semaphores. Data moves between devices by JAX's collectives and lax.ppermute only.
A program may use at most 64 MiB of HBM per device.

v0:
```python
import jax
import jax.numpy as jnp
from jax import lax
from jax.sharding import PartitionSpec as P


def partner_2(value, axis, bit):
    mask = 2**bit
    pairs = [(source, source ^ mask) for source in range(lax.axis_size(axis))]
    return lax.ppermute(value, axis, pairs)


def per_device(window_rows, secular, source, kept_count):
    blk = secular.shape[0]
    groups = lax.axis_size("grp")
    pairs = groups // 2
    half_bit = groups.bit_length() - 2
    group_index = lax.axis_index("grp")
    own_base = group_index * blk
    partner_base = jnp.bitwise_xor(group_index, pairs) * blk
    half_index = group_index // pairs
    limit = kept_count[0]
    summed = None
    terms = None
    partner = partner_2(secular, "grp", half_bit)
    stacked = jnp.concatenate([secular, partner], axis=0)
    inside = (source >= own_base) & (source < own_base + blk)
    picks = jnp.where(inside, source - own_base, blk + source - partner_base)
    slab_rows = jnp.where((source < limit)[:, None], stacked[picks], jnp.zeros((), stacked.dtype))
    partial_sum = lax.dot_general(
        lax.all_gather(window_rows, "col", axis=1, tiled=True),
        slab_rows,
        (((0,), (0,)), ((), ())),
        preferred_element_type=jnp.float32,
    )
    upper_flag = (half_index == 0).astype(jnp.float32)
    terms = jnp.stack([partial_sum * upper_flag, partial_sum * (1.0 - upper_flag)])
    summed = lax.psum_scatter(terms, "grp", scatter_dimension=1, tiled=True)
    return summed.astype(jnp.bfloat16)


def solution(mesh):
    return jax.shard_map(
        per_device,
        mesh=mesh,
        in_specs=(P("grp", "col"), P("grp", "col"), P("grp"), P()),
        out_specs=P(None, "grp", "col"),
        check_vma=False,
    )
```

profile of v0, /device:TPU:6, one launch (start us, length us, event | category | flops | bytes accessed | tf_op | source)
XLA Modules:
  0.0 402.1 jit_solution(4799918271873668091)
XLA Ops:
  6.5 0.0 all-gather.2.cloned.1.call-start
  6.5 0.7 all-gather.2.cloned.1.call-update
  7.3 15.7 %collective-permute-start = (bf16[3840,256]{1,0:T(8,128)(2,1)}, bf16[3840,256]{1,0:T(8,128)(2,1)S(1)}, u32[]{:S(2)}, u32[]{:S(2)}) collective-permute-start(bf16[3840,256]{1,0:T(8,128)(2,1)} %param.5), channel_id=1, source_target_pairs={{0,256},{16,272},{32,288},{48,304},{64,320},{80,336},{96,352},{112... | collective-permute-start | bytes 5898248 | tf_op jit(solution)/shard_map/ppermute | solution.py:10
  23.7 1.3 dynamic-slice
  25.7 0.7 compare_select_fusion
  26.4 0.7 broadcast_compare_fusion
  27.1 163.5 %collective-permute-done = bf16[3840,256]{1,0:T(8,128)(2,1)S(1)} collective-permute-done((bf16[3840,256]{1,0:T(8,128)(2,1)}, bf16[3840,256]{1,0:T(8,128)(2,1)S(1)}, u32[]{:S(2)}, u32[]{:S(2)}) %collective-permute-start) | collective-permute-done | bytes 1966112 | tf_op jit(solution)/shard_map/ppermute | solution.py:10
  190.7 3.8 pad_maximum_fusion
  194.4 11.0 %gather_fusion = bf16[3840,256]{1,0:T(8,128)(2,1)S(1)} fusion(bf16[7680,256]{1,0:T(8,128)(2,1)} %pad_maximum_fusion, s32[4096]{0:T(1024)S(1)} %pad_clamp_fusion), kind=kCustom, calls=%fused_computation | custom fusion | bytes 3947520 | tf_op jit(solution)/shard_map/gather | solution.py:29
  205.4 0.0 all-gather.2.cloned.1.call-done
  205.4 6.1 %multiply_bitcast_fusion.1 = (f32[1,1024,256]{1,2,0:T(8,128)S(1)}, f32[1,1024,256]{1,2,0:T(8,128)S(1)}) fusion(f32[]{:T(128)S(6)} %convert_element_type.6, f32[]{:T(128)S(6)} %sub.21, bf16[3840,1024]{0,1:T(8,128)(2,1)} %all-gather.2.cloned.1.call-done, bf16[3840,256]{1,0:T(8,128)(2,1)S(1)} %gather_fusion, pred[3840]{0:T(1024)(128)(4,1)S(1)} %broadcast_compare_fusion), kind=kOutput, calls=%fused_computation.7 | convolution fusion | flops 2014773248 | bytes 11931400 | tf_op jit(solution)/shard_map/dot_general | solution.py:30
  211.5 0.2 pad_maximum_fusion.1
  211.8 2.4 copy.6
  214.1 180.5 %all-reduce.2 = bf16[2,1024,256]{2,0,1:T(2,128)(2,1)S(1)} all-reduce(f32[2,1024,256]{2,0,1:T(2,128)} %copy.6), channel_id=2, replica_groups=mesh['grp'=32,'col'=16] {'grp'}, use_global_device_ids=true, to_apply=%region_0.1.clone | all-reduce | flops 524288 | bytes 3145728
  394.6 0.6 copy.7
  (2 shorter events, 0.0 us)
Async XLA Ops:
  6.5 198.9 %all-gather.2.cloned.1.call-start = ((), (), s32[]{:S(2)}) async-start(), calls=%async_computation | async-start | bytes 8355840 | tf_op jit(solution)/shard_map/all_gather | solution.py:31
  7.3 183.4 %collective-permute-start = (bf16[3840,256]{1,0:T(8,128)(2,1)}, bf16[3840,256]{1,0:T(8,128)(2,1)S(1)}, u32[]{:S(2)}, u32[]{:S(2)}) collective-permute-start(bf16[3840,256]{1,0:T(8,128)(2,1)} %param.5), channel_id=1, source_target_pairs={{0,256},{16,272},{32,288},{48,304},{64,320},{80,336},{96,352},{112... | collective-permute-start | bytes 5898248 | tf_op jit(solution)/shard_map/ppermute | solution.py:10
Sparse Core Ops, SparseCore 0:
  9.5 61.6 all-gather.1
where the time goes:
time: 403 us; the launch traced here: 402 us
  blocking collectives  180 us (45%)
  waiting for transfers between devices  164 us (41%)
  starting transfers between devices  15.7 us (4%)
  local copies, waits for them, and re-layouts  15.3 us (4%)
  between operations  14.8 us (4%)
  matrix products  6.09 us (2%)
  other arithmetic  5.49 us (1%)
    unnamed x1, blocking collectives  180 us
    ppermute x1, waiting for transfers between devices, partner_2(): return lax.ppermute(value, axis, pairs)  164 us
    ppermute x1, starting transfers between devices, partner_2(): return lax.ppermute(value, axis, pairs)  15.7 us
    gather x1, local copies, waits for them, and re-layouts, per_device(): stacked[picks]  11 us
  transfers between devices with their start and end apart: 2, of which 1 were waited for; matrix products, arithmetic and copies ran while one was open for 4% of the time, Pallas kernels for 0%

commit v1 on v0

v1 whole, which is shorter than its diff:
```python
import functools

import jax
import jax.numpy as jnp
from jax import lax
from jax.experimental import pallas as pl
from jax.experimental.pallas import tpu as pltpu
from jax.sharding import PartitionSpec as P

LANES = 128
UNROLL = 16
K_TILE = 768


def scatter_kernel(place_ref, w_ref, own_ref, cross_ref, flag_ref, rows, spread):
    width, blk = w_ref.shape
    tiles = blk // LANES
    ones = jnp.ones((LANES - width, LANES), jnp.float32)

    def load(i, carry):
        at = pl.multiple_of(i * LANES, LANES)
        part = w_ref[:, pl.ds(at, LANES)].astype(jnp.float32)
        rows[pl.ds(at, LANES), :] = jnp.concatenate([part, ones], axis=0).T
        spread[pl.ds(at, LANES), :] = jnp.zeros((LANES, LANES), jnp.float32)
        spread[pl.ds(blk + at, LANES), :] = jnp.zeros((LANES, LANES), jnp.float32)
        return carry

    lax.fori_loop(0, tiles, load, 0)

    def move(i, carry):
        for u in range(UNROLL):
            j = i * UNROLL + u
            spread[pl.ds(place_ref[j], 1), :] = rows[pl.ds(j, 1), :]
        return carry

    lax.fori_loop(0, blk // UNROLL, move, 0)

    def store(i, carry):
        at = pl.multiple_of(i * LANES, LANES)
        own = spread[pl.ds(at, LANES), :]
        own_ref[:, pl.ds(at, LANES)] = own.T[:width].astype(jnp.bfloat16)
        cross = spread[pl.ds(blk + at, LANES), :]
        cross_ref[:, pl.ds(at, LANES)] = cross.T[:width].astype(jnp.bfloat16)
        mark = own[:, width:]
        flag_ref[pl.ds(at, LANES), :] = jnp.concatenate([mark, mark], axis=1)
        return carry

    lax.fori_loop(0, tiles, store, 0)


def scatter_rows(place, w_t):
    width, blk = w_t.shape
    return pl.pallas_call(
        scatter_kernel,
        out_shape=[
            jax.ShapeDtypeStruct((width, blk), jnp.bfloat16),
            jax.ShapeDtypeStruct((width, blk), jnp.bfloat16),
            jax.ShapeDtypeStruct((blk, LANES), jnp.float32),
        ],
        in_specs=[pl.BlockSpec(memory_space=pltpu.SMEM), pl.BlockSpec(memory_space=pltpu.VMEM)],
        out_specs=[pl.BlockSpec(memory_space=pltpu.VMEM)] * 3,
        scratch_shapes=[pltpu.VMEM((blk, LANES), jnp.float32), pltpu.VMEM((2 * blk, LANES), jnp.float32)],
        compiler_params=pltpu.CompilerParams(vmem_limit_bytes=32 * 2**20),
    )(place, w_t)


def halves_kernel(info_ref, flag_ref, own_ref, other_ref, out_ref):
    tile, cols = own_ref.shape
    row = lax.broadcasted_iota(jnp.int32, (tile, LANES), 0) + pl.program_id(0) * tile
    mark = flag_ref[...]
    alive = row < info_ref[1]
    mine = alive & (mark > 0.5)
    theirs = alive & (mark < 0.5)
    lower = info_ref[0] > 0
    in_half = (
        jnp.where(lower, theirs.astype(jnp.float32), mine.astype(jnp.float32)),
        jnp.where(lower, mine.astype(jnp.float32), theirs.astype(jnp.float32)),
    )
    for c, ref in enumerate((own_ref, other_ref)):
        for h in range(2):
            for v in range(cols // LANES):
                values = ref[:, v * LANES : (v + 1) * LANES].astype(jnp.float32)
                at = (c * 2 + h) * cols + v * LANES
                out_ref[:, at : at + LANES] = jnp.where(in_half[h] > 0.5, values, 0.0).astype(jnp.bfloat16)


def split_halves(info, flag, own, other):
    blk, cols = own.shape
    return pl.pallas_call(
        halves_kernel,
        grid=(blk // K_TILE,),
        out_shape=jax.ShapeDtypeStruct((blk, 4 * cols), jnp.bfloat16),
        in_specs=[
            pl.BlockSpec(memory_space=pltpu.SMEM),
            pl.BlockSpec((K_TILE, LANES), lambda i: (i, 0)),
            pl.BlockSpec((K_TILE, cols), lambda i: (i, 0)),
            pl.BlockSpec((K_TILE, cols), lambda i: (i, 0)),
        ],
        out_specs=pl.BlockSpec((K_TILE, 4 * cols), lambda i: (i, 0)),
        compiler_params=pltpu.CompilerParams(vmem_limit_bytes=32 * 2**20),
    )(info, flag, own, other)


def product_kernel(slot_ref, *refs):
    pieces, s_ref, out_ref, total = refs[:-3], refs[-3], refs[-2], refs[-1]
    step = pl.program_id(0)
    rows = pieces[0].shape[0]
    lhs = jnp.concatenate([ref[...] for ref in pieces], axis=0)
    term = jnp.dot(lhs, s_ref[...], preferred_element_type=jnp.float32)

    @pl.when(step == 0)
    def _():
        total[...] = term

    @pl.when(step > 0)
    def _():
        total[...] += term

    @pl.when(step == pl.num_programs(0) - 1)
    def _():
        for i in range(len(pieces)):
            out_ref[slot_ref[i]] = total[i * rows : (i + 1) * rows, :]


def product(slots, pieces, s_both):
    rows, blk = pieces[0].shape
    cols = s_both.shape[1]
    count = len(pieces)
    return pl.pallas_call(
        product_kernel,
        grid=(blk // K_TILE,),
        out_shape=jax.ShapeDtypeStruct((count, rows, cols), jnp.float32),
        in_specs=[pl.BlockSpec(memory_space=pltpu.SMEM)]
        + [pl.BlockSpec((rows, K_TILE), lambda i: (0, i))] * count
        + [pl.BlockSpec((K_TILE, cols), lambda i: (i, 0))],
        out_specs=pl.BlockSpec((count, rows, cols), lambda i: (0, 0, 0)),
        scratch_shapes=[pltpu.VMEM((count * rows, cols), jnp.float32)],
        compiler_params=pltpu.CompilerParams(vmem_limit_bytes=48 * 2**20),
    )(slots, *pieces, s_both)


def col_move(value, target):
    pairs = []
    for c in range(16):
        x, y, core = c // 4, c // 2 % 2, c % 2
        tx, ty, tcore = target(x, y, core)
        pairs.append((c, tx % 4 * 4 + ty * 2 + tcore))
    return lax.ppermute(value, "col", pairs)


def slice_move(value, target):
    pairs = []
    for g in range(32):
        for c in range(16):
            to = target(g // 2, g % 2, c)
            if to is not None:
                pairs.append((g * 16 + c, (to[0] % 16 * 2 + to[1]) * 16 + to[2]))
    return lax.ppermute(value, ("grp", "col"), pairs)


def exchange(step, z, y_hi, c):
    even = (c - z) % 2 == 0
    return (z + 1 if even == (step % 2 == 1) else z - 1, y_hi, c)


ORDER_EVEN = (7, 6, 4, 2, 0, 1, 3, 5)
ORDER_ODD = (7, 5, 3, 1, 0, 2, 4, 6)


def per_device(window_rows, secular, source, kept_count):
    blk = secular.shape[0]
    g = lax.axis_index("grp")
    c = lax.axis_index("col")
    z, y_hi = g // 2, g % 2
    x, y_lo, core = c // 4, c // 2 % 2, c % 2
    odd = (core + z) % 2
    own_base = g * blk
    partner_base = jnp.bitwise_xor(g, 16) * blk

    other = col_move(secular, lambda x, y, k: (x, y, 1 - k))
    inside = (source >= own_base) & (source < own_base + blk)
    place = jnp.where(inside, source - own_base, blk + source - partner_base)
    own_part, cross_part, flag = scatter_rows(place, window_rows.T)
    arrived = lax.ppermute(cross_part, "grp", [(i, i ^ 16) for i in range(32)])
    info = jnp.stack([g // 16, kept_count[0] - own_base]).astype(jnp.int32)
    s_both = split_halves(info, flag, secular, other)

    here = own_part + arrived
    pieces = {(0, 0): here}
    for d in (1, 3, 2):
        pieces[d, 0] = col_move(here, lambda x, y, k, d=d: (x - d, y, k))
    pieces[0, 1] = col_move(here, lambda x, y, k: (x, 1 - y, k))
    pieces[2, 1] = col_move(pieces[0, 1], lambda x, y, k: (x - 2, y, k))
    for d in (1, 3):
        pieces[d, 1] = col_move(pieces[d, 0], lambda x, y, k: (x, 1 - y, k))

    places = list(pieces)
    targets = jnp.stack([(x + dx) % 4 * 4 + jnp.bitwise_xor(y_lo, dy) * 2 + core for dx, dy in places])
    above = (targets - z - odd) % 16 // 2
    orders = jnp.where(odd == 1, jnp.array(ORDER_ODD, jnp.int32), jnp.array(ORDER_EVEN, jnp.int32))
    slots = orders[above].astype(jnp.int32)
    terms = product(slots, [pieces[p] for p in places], s_both)

    moving = terms[0]
    for step in range(1, 8):
        moving = terms[step] + slice_move(moving, functools.partial(exchange, step))
    half_cols = moving.shape[1] // 2
    mine, theirs = moving[:, :half_cols], moving[:, half_cols:]
    is_odd = odd == 1

    def last(z, y_hi, c):
        return (z + 1, y_hi, c) if (c - z) % 2 else (z, y_hi, c ^ 1)

    def last_other(z, y_hi, c):
        return (z + 1, y_hi, c ^ 1) if (c - z) % 2 else None

    first_in = slice_move(jnp.where(is_odd, mine, theirs), last)
    second_in = slice_move(theirs, last_other)
    summed = jnp.where(is_odd, second_in, mine) + first_in
    rows = summed.shape[0] // 2
    low, high = summed[:rows], summed[rows:]
    is_high = y_hi == 1
    across = lax.ppermute(jnp.where(is_high, low, high), "grp", [(i, i ^ 1) for i in range(32)])
    final = (jnp.where(is_high, high, low) + across).astype(jnp.bfloat16)
    return final.reshape(rows, 2, half_cols // 2).transpose(1, 0, 2)


def solution(mesh):
    return jax.shard_map(
        per_device,
        mesh=mesh,
        in_specs=(P("grp", "col"), P("grp", "col"), P("grp"), P()),
        out_specs=P(None, "grp", "col"),
        check_vma=False,
    )
```

time: 403 us -> 231 us (0.57)
  blocking collectives: 180 us -> 0 us
  starting transfers between devices: 15.7 us -> 107 us
  waiting for transfers between devices: 164 us -> 87.3 us
  Pallas kernels: 0 us -> 24.8 us
  between operations: 14.8 us -> 1.15 us
  local copies, waits for them, and re-layouts: 15.3 us -> 8.3 us
  matrix products: 6.09 us -> 0 us
  other arithmetic: 5.49 us -> 1.23 us
    unnamed x1 -> x0, blocking collectives: 180 us -> none
    ppermute x1 -> x19, starting transfers between devices: 15.7 us -> 107 us  [the longest x9 53.4 us: slice_move(): return lax.ppermute(value, ('grp', 'col'), pairs)]
    ppermute x1 -> x19, waiting for transfers between devices: 164 us -> 87.3 us  [the longest x9 48.5 us: slice_move(): return lax.ppermute(value, ('grp', 'col'), pairs)]
    pallas_call x0 -> x3, Pallas kernels: none -> 24.8 us  [the longest x1 11.1 us: scatter_rows(): pl.pallas_call(scatter_kernel, out_shape=[jax.ShapeDtypeStruct((width, bl...]
    gather x1, local copies, waits for them, and re-layouts: 11 us -> 0.64 us  [per_device(): slots = orders[above].astype(jnp.int32)]
    dot_general x1 -> x0, matrix products: 6.09 us -> none  [per_device(): lax.dot_general(lax.all_gather(window_rows, 'col', axis=1, tiled=True), s...]
    unnamed x1 -> x14, local copies, waits for them, and re-layouts: 1.34 us -> 6.92 us
  transfers between devices with their start and end apart: 2 -> 19, of which waited for: 1 -> 12; matrix products, arithmetic and copies ran while one was open for 4% -> 1% of each run, Pallas kernels for 0% -> 7%
where the time goes in v1:
time: 231 us; the launch traced here: 230 us
  starting transfers between devices  107 us (46%)
  waiting for transfers between devices  87.3 us (38%)
  Pallas kernels  24.8 us (11%)
  local copies, waits for them, and re-layouts  8.3 us (4%)
    ppermute x9, starting transfers between devices, slice_move(): return lax.ppermute(value, ('grp', 'col'), pairs)  53.4 us
    ppermute x9, waiting for transfers between devices, slice_move(): return lax.ppermute(value, ('grp', 'col'), pairs)  48.5 us
    ppermute x8, starting transfers between devices, col_move(): return lax.ppermute(value, 'col', pairs)  33.6 us
    ppermute x8, waiting for transfers between devices, col_move(): return lax.ppermute(value, 'col', pairs)  19.6 us
    ppermute x1, waiting for transfers between devices, per_device(): arrived = lax.ppermute(cross_part, 'grp', [(i, i ^ 16) for i in range(32)])  16.4 us
    ppermute x1, starting transfers between devices, per_device(): arrived = lax.ppermute(cross_part, 'grp', [(i, i ^ 16) for i in range(32)])  15.7 us
    pallas_call x1, Pallas kernels, scatter_rows(): pl.pallas_call(scatter_kernel, out_shape=[jax.ShapeDtypeStruct((width, bl...  11.1 us
    pallas_call x1, Pallas kernels, product(): pl.pallas_call(product_kernel, grid=(blk // K_TILE,), out_shape=jax.Shape...  8.7 us
  transfers between devices with their start and end apart: 19, of which 12 were waited for; matrix products, arithmetic and copies ran while one was open for 1% of the time, Pallas kernels for 7%

profile of v1, /device:TPU:6, one launch (start us, length us, event | category | flops | bytes accessed | tf_op | source)
XLA Modules:
  0.0 230.3 jit_solution(2478992294861325293)
XLA Ops:
  0.0 2.0 collective-permute-start.8
  3.8 11.1 %shard_map.64 = (bf16[64,3840]{1,0:T(8,128)(2,1)S(1)}, bf16[64,3840]{1,0:T(8,128)(2,1)S(1)}, f32[3840,128]{1,0:T(8,128)S(1)}) custom-call(s32[3840]{0:T(1024)S(1)} %subtract_select_fusion.place_ref, bf16[64,3840]{1,0:T(8,128)(2,1)S(1)} %bitcast.52), custom_call_target="tpu_custom_call" | custom-call | tf_op jit(solution)/shard_map/pallas_call | solution.py:53
  16.2 15.7 %collective-permute-start = (bf16[64,3840]{1,0:T(8,128)(2,1)S(1)}, bf16[64,3840]{1,0:T(8,128)(2,1)S(1)}, u32[]{:S(2)}, u32[]{:S(2)}) collective-permute-start(bf16[64,3840]{1,0:T(8,128)(2,1)S(1)} %get-tuple-element.9), channel_id=1, source_target_pairs={{0,256},{16,272},{32,288},{48,304},{64,320},{80,336},{96,352},{112... | collective-permute-start | bytes 1474568 | tf_op jit(solution)/shard_map/ppermute | solution.py:184
  31.9 16.4 %collective-permute-done = bf16[64,3840]{1,0:T(8,128)(2,1)S(1)} collective-permute-done((bf16[64,3840]{1,0:T(8,128)(2,1)S(1)}, bf16[64,3840]{1,0:T(8,128)(2,1)S(1)}, u32[]{:S(2)}, u32[]{:S(2)}) %collective-permute-start) | collective-permute-done | bytes 491552 | tf_op jit(solution)/shard_map/ppermute | solution.py:184
  48.4 3.5 %collective-permute-start.4 = (bf16[64,3840]{1,0:T(8,128)(2,1)S(1)}, bf16[64,3840]{1,0:T(8,128)(2,1)S(1)}, u32[]{:S(2)}, u32[]{:S(2)}) collective-permute-start(bf16[64,3840]{1,0:T(8,128)(2,1)S(1)} %add.199.refs_0_), channel_id=1, source_target_pairs={{0,2},{1,3},{2,0},{3,1},{4,6},{5,7},{6,4},{7,5},{8,10},{9,11},{10,... | collective-permute-start | bytes 1474568 | tf_op jit(solution)/shard_map/ppermute | solution.py:148
  51.9 2.7 %collective-permute-start.1 = (bf16[64,3840]{1,0:T(8,128)(2,1)S(1)}, bf16[64,3840]{1,0:T(8,128)(2,1)S(1)}, u32[]{:S(2)}, u32[]{:S(2)}) collective-permute-start(bf16[64,3840]{1,0:T(8,128)(2,1)S(1)} %add.199.refs_0_), channel_id=1, source_target_pairs={{0,12},{1,13},{2,14},{3,15},{4,0},{5,1},{6,2},{7,3},{8,4},{9,5},{1... | collective-permute-start | bytes 1474568 | tf_op jit(solution)/shard_map/ppermute | solution.py:148
  54.6 10.5 %collective-permute-start.2 = (bf16[64,3840]{1,0:T(8,128)(2,1)S(1)}, bf16[64,3840]{1,0:T(8,128)(2,1)}, u32[]{:S(2)}, u32[]{:S(2)}) collective-permute-start(bf16[64,3840]{1,0:T(8,128)(2,1)S(1)} %add.199.refs_0_), channel_id=1, source_target_pairs={{0,4},{1,5},{2,6},{3,7},{4,8},{5,9},{6,10},{7,11},{8,12},{9,13},{1... | collective-permute-start | bytes 1474568 | tf_op jit(solution)/shard_map/ppermute | solution.py:148
  65.4 3.4 %collective-permute-start.3 = (bf16[64,3840]{1,0:T(8,128)(2,1)S(1)}, bf16[64,3840]{1,0:T(8,128)(2,1)}, u32[]{:S(2)}, u32[]{:S(2)}) collective-permute-start(bf16[64,3840]{1,0:T(8,128)(2,1)S(1)} %add.199.refs_0_), channel_id=1, source_target_pairs={{0,8},{1,9},{2,10},{3,11},{4,12},{5,13},{6,14},{7,15},{8,0},{9,1},... | collective-permute-start | bytes 1474568 | tf_op jit(solution)/shard_map/ppermute | solution.py:148
  68.7 4.0 %collective-permute-start.5 = (bf16[64,3840]{1,0:T(8,128)(2,1)S(1)}, bf16[64,3840]{1,0:T(8,128)(2,1)}, u32[]{:S(2)}, u32[]{:S(2)}) collective-permute-start(bf16[64,3840]{1,0:T(8,128)(2,1)S(1)} %collective-permute-done.4.refs_4_), channel_id=1, source_target_pairs={{0,8},{1,9},{2,10},{3,11},{4,12},{5,13},{6,14},{7,15},{8,0},{9,1},... | collective-permute-start | bytes 1474568 | tf_op jit(solution)/shard_map/ppermute | solution.py:148
  74.4 3.9 %collective-permute-start.6 = (bf16[64,3840]{1,0:T(8,128)(2,1)S(1)}, bf16[64,3840]{1,0:T(8,128)(2,1)}, u32[]{:S(2)}, u32[]{:S(2)}) collective-permute-start(bf16[64,3840]{1,0:T(8,128)(2,1)S(1)} %collective-permute-done.1.refs_1_), channel_id=1, source_target_pairs={{0,2},{1,3},{2,0},{3,1},{4,6},{5,7},{6,4},{7,5},{8,10},{9,11},{10,... | collective-permute-start | bytes 1474568 | tf_op jit(solution)/shard_map/ppermute | solution.py:148
  78.3 17.9 %collective-permute-done.2.refs_2_ = bf16[64,3840]{1,0:T(8,128)(2,1)} collective-permute-done((bf16[64,3840]{1,0:T(8,128)(2,1)S(1)}, bf16[64,3840]{1,0:T(8,128)(2,1)}, u32[]{:S(2)}, u32[]{:S(2)}) %collective-permute-start.2) | collective-permute-done | bytes 491552 | tf_op jit(solution)/shard_map/ppermute | solution.py:148
  96.2 3.6 %collective-permute-start.7 = (bf16[64,3840]{1,0:T(8,128)(2,1)}, bf16[64,3840]{1,0:T(8,128)(2,1)}, u32[]{:S(2)}, u32[]{:S(2)}) collective-permute-start(bf16[64,3840]{1,0:T(8,128)(2,1)} %collective-permute-done.2.refs_2_), channel_id=1, source_target_pairs={{0,2},{1,3},{2,0},{3,1},{4,6},{5,7},{6,4},{7,5},{8,10},{9,11},{10,... | collective-permute-start | bytes 1474568 | tf_op jit(solution)/shard_map/ppermute | solution.py:148
  102.9 5.1 %shard_map.65.refs_8_ = bf16[3840,1024]{1,0:T(8,128)(2,1)S(1)} custom-call(s32[2]{0:T(128)S(1)} %pad_add_fusion.info_ref, f32[3840,128]{1,0:T(8,128)S(1)} %copy-done.3, bf16[3840,256]{1,0:T(8,128)(2,1)S(1)} %copy-done.1, bf16[3840,256]{1,0:T(8,128)(2,1)} %collective-permute-done.8.other_ref), custom_call_target="tpu_custom_call" | custom-call | tf_op jit(solution)/shard_map/pallas_call | solution.py:89
  107.9 3.1 %copy-done = bf16[3840,1024]{1,0:T(8,128)(2,1)} copy-done((bf16[3840,1024]{1,0:T(8,128)(2,1)}, bf16[3840,1024]{1,0:T(8,128)(2,1)S(1)}, u32[]{:S(2)}) %copy-start) | copy-done | bytes 7864344
  111.0 8.7 %shard_map.66 = f32[8,64,1024]{2,1,0:T(8,128)S(1)} custom-call(s32[8]{0:T(128)S(1)} %gather_fusion, bf16[64,3840]{1,0:T(8,128)(2,1)S(1)} %add.199.refs_0_, bf16[64,3840]{1,0:T(8,128)(2,1)S(1)} %collective-permute-done.1.refs_1_, bf16[64,3840]{1,0:T(8,128)(2,1)} %collective-permute-done.2.refs_2_, bf16[64,3840]{1,0:T(8,128)(2,1)} %collective-permute-done.3.refs_3_, ...), custom_call_target="tpu_custom_call" | custom-call | tf_op jit(solution)/shard_map/pallas_call | solution.py:129
  119.8 24.9 %collective-permute-start.9 = (f32[64,1024]{1,0:T(8,128)S(1)}, f32[64,1024]{1,0:T(8,128)S(1)}, u32[]{:S(2)}, u32[]{:S(2)}) collective-permute-start(f32[64,1024]{1,0:T(8,128)S(1)} %slice_bitcast_fusion), channel_id=1, source_target_pairs={{0,32},{1,481},{2,34},{3,483},{4,36},{5,485},{6,38},{7,487},{8,40}... | collective-permute-start | bytes 786440 | tf_op jit(solution)/shard_map/ppermute | solution.py:158
  144.7 4.3 %collective-permute-done.9 = f32[64,1024]{1,0:T(8,128)S(1)} collective-permute-done((f32[64,1024]{1,0:T(8,128)S(1)}, f32[64,1024]{1,0:T(8,128)S(1)}, u32[]{:S(2)}, u32[]{:S(2)}) %collective-permute-start.9) | collective-permute-done | bytes 262176 | tf_op jit(solution)/shard_map/ppermute | solution.py:158
  149.1 8.8 %collective-permute-start.10 = (f32[64,1024]{1,0:T(8,128)S(1)}, f32[64,1024]{1,0:T(8,128)S(1)}, u32[]{:S(2)}, u32[]{:S(2)}) collective-permute-start(f32[64,1024]{1,0:T(8,128)S(1)} %fusion), channel_id=1, source_target_pairs={{0,480},{1,33},{2,482},{3,35},{4,484},{5,37},{6,486},{7,39},{8,488... | collective-permute-start | bytes 786440 | tf_op jit(solution)/shard_map/ppermute | solution.py:158
  157.9 6.4 %collective-permute-done.10 = f32[64,1024]{1,0:T(8,128)S(1)} collective-permute-done((f32[64,1024]{1,0:T(8,128)S(1)}, f32[64,1024]{1,0:T(8,128)S(1)}, u32[]{:S(2)}, u32[]{:S(2)}) %collective-permute-start.10) | collective-permute-done | bytes 262176 | tf_op jit(solution)/shard_map/ppermute | solution.py:158
  164.3 1.9 collective-permute-start.11
  166.2 8.8 %collective-permute-done.11 = f32[64,1024]{1,0:T(8,128)S(1)} collective-permute-done((f32[64,1024]{1,0:T(8,128)S(1)}, f32[64,1024]{1,0:T(8,128)S(1)}, u32[]{:S(2)}, u32[]{:S(2)}) %collective-permute-start.11) | collective-permute-done | bytes 262176 | tf_op jit(solution)/shard_map/ppermute | solution.py:158
  175.0 5.1 %collective-permute-start.12 = (f32[64,1024]{1,0:T(8,128)S(1)}, f32[64,1024]{1,0:T(8,128)S(1)}, u32[]{:S(2)}, u32[]{:S(2)}) collective-permute-start(f32[64,1024]{1,0:T(8,128)S(1)} %fusion.2), channel_id=1, source_target_pairs={{0,480},{1,33},{2,482},{3,35},{4,484},{5,37},{6,486},{7,39},{8,488... | collective-permute-start | bytes 786440 | tf_op jit(solution)/shard_map/ppermute | solution.py:158
  180.2 6.0 %collective-permute-done.12 = f32[64,1024]{1,0:T(8,128)S(1)} collective-permute-done((f32[64,1024]{1,0:T(8,128)S(1)}, f32[64,1024]{1,0:T(8,128)S(1)}, u32[]{:S(2)}, u32[]{:S(2)}) %collective-permute-start.12) | collective-permute-done | bytes 262176 | tf_op jit(solution)/shard_map/ppermute | solution.py:158
  186.2 1.9 collective-permute-start.13
  188.1 6.3 %collective-permute-done.13 = f32[64,1024]{1,0:T(8,128)S(1)} collective-permute-done((f32[64,1024]{1,0:T(8,128)S(1)}, f32[64,1024]{1,0:T(8,128)S(1)}, u32[]{:S(2)}, u32[]{:S(2)}) %collective-permute-start.13) | collective-permute-done | bytes 262176 | tf_op jit(solution)/shard_map/ppermute | solution.py:158
  194.5 4.8 %collective-permute-start.14 = (f32[64,1024]{1,0:T(8,128)S(1)}, f32[64,1024]{1,0:T(8,128)S(1)}, u32[]{:S(2)}, u32[]{:S(2)}) collective-permute-start(f32[64,1024]{1,0:T(8,128)S(1)} %fusion.4), channel_id=1, source_target_pairs={{0,480},{1,33},{2,482},{3,35},{4,484},{5,37},{6,486},{7,39},{8,488... | collective-permute-start | bytes 786440 | tf_op jit(solution)/shard_map/ppermute | solution.py:158
  199.3 4.7 %collective-permute-done.14 = f32[64,1024]{1,0:T(8,128)S(1)} collective-permute-done((f32[64,1024]{1,0:T(8,128)S(1)}, f32[64,1024]{1,0:T(8,128)S(1)}, u32[]{:S(2)}, u32[]{:S(2)}) %collective-permute-start.14) | collective-permute-done | bytes 262176 | tf_op jit(solution)/shard_map/ppermute | solution.py:158
  205.9 6.3 %collective-permute-done.15 = f32[64,1024]{1,0:T(8,128)S(1)} collective-permute-done((f32[64,1024]{1,0:T(8,128)S(1)}, f32[64,1024]{1,0:T(8,128)S(1)}, u32[]{:S(2)}, u32[]{:S(2)}) %collective-permute-start.15) | collective-permute-done | bytes 262176 | tf_op jit(solution)/shard_map/ppermute | solution.py:158
  213.0 3.3 %collective-permute-start.17 = (f32[64,512]{1,0:T(8,128)S(1)}, f32[64,512]{1,0:T(8,128)S(1)}, u32[]{:S(2)}, u32[]{:S(2)}) collective-permute-start(f32[64,512]{1,0:T(8,128)S(1)} %get-tuple-element.12), channel_id=1, source_target_pairs={{0,1},{1,33},{2,3},{3,35},{4,5},{5,37},{6,7},{7,39},{8,9},{9,41},{... | collective-permute-start | bytes 393224 | tf_op jit(solution)/shard_map/ppermute | solution.py:158
  216.3 5.7 %collective-permute-done.17 = f32[64,512]{1,0:T(8,128)S(1)} collective-permute-done((f32[64,512]{1,0:T(8,128)S(1)}, f32[64,512]{1,0:T(8,128)S(1)}, u32[]{:S(2)}, u32[]{:S(2)}) %collective-permute-start.17) | collective-permute-done | bytes 131104 | tf_op jit(solution)/shard_map/ppermute | solution.py:158
  222.0 4.8 %collective-permute-start.18 = (f32[32,512]{1,0:T(8,128)S(1)}, f32[32,512]{1,0:T(8,128)S(1)}, u32[]{:S(2)}, u32[]{:S(2)}) collective-permute-start(f32[32,512]{1,0:T(8,128)S(1)} %slice_select_fusion.1), channel_id=1, source_target_pairs={{0,16},{16,0},{32,48},{48,32},{64,80},{80,64},{96,112},{112,96},{1... | collective-permute-start | bytes 196616 | tf_op jit(solution)/shard_map/ppermute | solution.py:223
  226.8 2.8 %collective-permute-done.18 = f32[32,512]{1,0:T(8,128)S(1)} collective-permute-done((f32[32,512]{1,0:T(8,128)S(1)}, f32[32,512]{1,0:T(8,128)S(1)}, u32[]{:S(2)}, u32[]{:S(2)}) %collective-permute-start.18) | collective-permute-done | bytes 65568 | tf_op jit(solution)/shard_map/ppermute | solution.py:223
  (44 shorter events, 10.8 us)
Async XLA Ops:
  0.0 100.6 %copy-start.5 = (s32[8]{0:T(128)S(1)}, s32[8]{0:T(128)}, u32[]{:S(2)}) copy-start(s32[8]{0:T(128)} %constant.133.clone) | copy-start | bytes 100
  0.0 101.3 %copy-start.1 = (bf16[3840,256]{1,0:T(8,128)(2,1)S(1)}, bf16[3840,256]{1,0:T(8,128)(2,1)}, u32[]{:S(2)}) copy-start(bf16[3840,256]{1,0:T(8,128)(2,1)} %own_ref.1) | copy-start | bytes 5898244
  0.0 101.3 %collective-permute-start.8 = (bf16[3840,256]{1,0:T(8,128)(2,1)}, bf16[3840,256]{1,0:T(8,128)(2,1)}, u32[]{:S(2)}, u32[]{:S(2)}) collective-permute-start(bf16[3840,256]{1,0:T(8,128)(2,1)} %own_ref.1), channel_id=1, source_target_pairs={{0,1},{1,0},{2,3},{3,2},{4,5},{5,4},{6,7},{7,6},{8,9},{9,8},{10,11... | collective-permute-start | bytes 5898248 | tf_op jit(solution)/shard_map/ppermute | solution.py:148
  2.8 1.0 copy-start.4
  3.8 96.8 %copy-start.6 = (s32[8]{0:T(128)S(1)}, s32[8]{0:T(128)}, u32[]{:S(2)}) copy-start(s32[8]{0:T(128)} %constant.134.clone) | copy-start | bytes 100
  14.9 1.3 copy-start.2
  16.2 32.1 %collective-permute-start = (bf16[64,3840]{1,0:T(8,128)(2,1)S(1)}, bf16[64,3840]{1,0:T(8,128)(2,1)S(1)}, u32[]{:S(2)}, u32[]{:S(2)}) collective-permute-start(bf16[64,3840]{1,0:T(8,128)(2,1)S(1)} %get-tuple-element.9), channel_id=1, source_target_pairs={{0,256},{16,272},{32,288},{48,304},{64,320},{80,336},{96,352},{112... | collective-permute-start | bytes 1474568 | tf_op jit(solution)/shard_map/ppermute | solution.py:184
  48.4 20.3 %collective-permute-start.4 = (bf16[64,3840]{1,0:T(8,128)(2,1)S(1)}, bf16[64,3840]{1,0:T(8,128)(2,1)S(1)}, u32[]{:S(2)}, u32[]{:S(2)}) collective-permute-start(bf16[64,3840]{1,0:T(8,128)(2,1)S(1)} %add.199.refs_0_), channel_id=1, source_target_pairs={{0,2},{1,3},{2,0},{3,1},{4,6},{5,7},{6,4},{7,5},{8,10},{9,11},{10,... | collective-permute-start | bytes 1474568 | tf_op jit(solution)/shard_map/ppermute | solution.py:148
  51.9 22.5 %collective-permute-start.1 = (bf16[64,3840]{1,0:T(8,128)(2,1)S(1)}, bf16[64,3840]{1,0:T(8,128)(2,1)S(1)}, u32[]{:S(2)}, u32[]{:S(2)}) collective-permute-start(bf16[64,3840]{1,0:T(8,128)(2,1)S(1)} %add.199.refs_0_), channel_id=1, source_target_pairs={{0,12},{1,13},{2,14},{3,15},{4,0},{5,1},{6,2},{7,3},{8,4},{9,5},{1... | collective-permute-start | bytes 1474568 | tf_op jit(solution)/shard_map/ppermute | solution.py:148
  54.6 41.6 %collective-permute-start.2 = (bf16[64,3840]{1,0:T(8,128)(2,1)S(1)}, bf16[64,3840]{1,0:T(8,128)(2,1)}, u32[]{:S(2)}, u32[]{:S(2)}) collective-permute-start(bf16[64,3840]{1,0:T(8,128)(2,1)S(1)} %add.199.refs_0_), channel_id=1, source_target_pairs={{0,4},{1,5},{2,6},{3,7},{4,8},{5,9},{6,10},{7,11},{8,12},{9,13},{1... | collective-permute-start | bytes 1474568 | tf_op jit(solution)/shard_map/ppermute | solution.py:148
  65.4 45.6 %collective-permute-start.3 = (bf16[64,3840]{1,0:T(8,128)(2,1)S(1)}, bf16[64,3840]{1,0:T(8,128)(2,1)}, u32[]{:S(2)}, u32[]{:S(2)}) collective-permute-start(bf16[64,3840]{1,0:T(8,128)(2,1)S(1)} %add.199.refs_0_), channel_id=1, source_target_pairs={{0,8},{1,9},{2,10},{3,11},{4,12},{5,13},{6,14},{7,15},{8,0},{9,1},... | collective-permute-start | bytes 1474568 | tf_op jit(solution)/shard_map/ppermute | solution.py:148
  68.7 42.3 %collective-permute-start.5 = (bf16[64,3840]{1,0:T(8,128)(2,1)S(1)}, bf16[64,3840]{1,0:T(8,128)(2,1)}, u32[]{:S(2)}, u32[]{:S(2)}) collective-permute-start(bf16[64,3840]{1,0:T(8,128)(2,1)S(1)} %collective-permute-done.4.refs_4_), channel_id=1, source_target_pairs={{0,8},{1,9},{2,10},{3,11},{4,12},{5,13},{6,14},{7,15},{8,0},{9,1},... | collective-permute-start | bytes 1474568 | tf_op jit(solution)/shard_map/ppermute | solution.py:148
  74.4 36.6 %collective-permute-start.6 = (bf16[64,3840]{1,0:T(8,128)(2,1)S(1)}, bf16[64,3840]{1,0:T(8,128)(2,1)}, u32[]{:S(2)}, u32[]{:S(2)}) collective-permute-start(bf16[64,3840]{1,0:T(8,128)(2,1)S(1)} %collective-permute-done.1.refs_1_), channel_id=1, source_target_pairs={{0,2},{1,3},{2,0},{3,1},{4,6},{5,7},{6,4},{7,5},{8,10},{9,11},{10,... | collective-permute-start | bytes 1474568 | tf_op jit(solution)/shard_map/ppermute | solution.py:148
  96.2 14.8 %collective-permute-start.7 = (bf16[64,3840]{1,0:T(8,128)(2,1)}, bf16[64,3840]{1,0:T(8,128)(2,1)}, u32[]{:S(2)}, u32[]{:S(2)}) collective-permute-start(bf16[64,3840]{1,0:T(8,128)(2,1)} %collective-permute-done.2.refs_2_), channel_id=1, source_target_pairs={{0,2},{1,3},{2,0},{3,1},{4,6},{5,7},{6,4},{7,5},{8,10},{9,11},{10,... | collective-permute-start | bytes 1474568 | tf_op jit(solution)/shard_map/ppermute | solution.py:148
  101.3 1.5 copy-start.3
  107.9 3.1 %copy-start = (bf16[3840,1024]{1,0:T(8,128)(2,1)}, bf16[3840,1024]{1,0:T(8,128)(2,1)S(1)}, u32[]{:S(2)}) copy-start(bf16[3840,1024]{1,0:T(8,128)(2,1)S(1)} %shard_map.65.refs_8_) | copy-start | bytes 23592964
  119.8 29.3 %collective-permute-start.9 = (f32[64,1024]{1,0:T(8,128)S(1)}, f32[64,1024]{1,0:T(8,128)S(1)}, u32[]{:S(2)}, u32[]{:S(2)}) collective-permute-start(f32[64,1024]{1,0:T(8,128)S(1)} %slice_bitcast_fusion), channel_id=1, source_target_pairs={{0,32},{1,481},{2,34},{3,483},{4,36},{5,485},{6,38},{7,487},{8,40}... | collective-permute-start | bytes 786440 | tf_op jit(solution)/shard_map/ppermute | solution.py:158
  149.1 15.2 %collective-permute-start.10 = (f32[64,1024]{1,0:T(8,128)S(1)}, f32[64,1024]{1,0:T(8,128)S(1)}, u32[]{:S(2)}, u32[]{:S(2)}) collective-permute-start(f32[64,1024]{1,0:T(8,128)S(1)} %fusion), channel_id=1, source_target_pairs={{0,480},{1,33},{2,482},{3,35},{4,484},{5,37},{6,486},{7,39},{8,488... | collective-permute-start | bytes 786440 | tf_op jit(solution)/shard_map/ppermute | solution.py:158
  164.3 10.7 %collective-permute-start.11 = (f32[64,1024]{1,0:T(8,128)S(1)}, f32[64,1024]{1,0:T(8,128)S(1)}, u32[]{:S(2)}, u32[]{:S(2)}) collective-permute-start(f32[64,1024]{1,0:T(8,128)S(1)} %fusion.1), channel_id=1, source_target_pairs={{0,32},{1,481},{2,34},{3,483},{4,36},{5,485},{6,38},{7,487},{8,40}... | collective-permute-start | bytes 786440 | tf_op jit(solution)/shard_map/ppermute | solution.py:158
  175.0 11.1 %collective-permute-start.12 = (f32[64,1024]{1,0:T(8,128)S(1)}, f32[64,1024]{1,0:T(8,128)S(1)}, u32[]{:S(2)}, u32[]{:S(2)}) collective-permute-start(f32[64,1024]{1,0:T(8,128)S(1)} %fusion.2), channel_id=1, source_target_pairs={{0,480},{1,33},{2,482},{3,35},{4,484},{5,37},{6,486},{7,39},{8,488... | collective-permute-start | bytes 786440 | tf_op jit(solution)/shard_map/ppermute | solution.py:158
  186.2 8.3 %collective-permute-start.13 = (f32[64,1024]{1,0:T(8,128)S(1)}, f32[64,1024]{1,0:T(8,128)S(1)}, u32[]{:S(2)}, u32[]{:S(2)}) collective-permute-start(f32[64,1024]{1,0:T(8,128)S(1)} %fusion.3), channel_id=1, source_target_pairs={{0,32},{1,481},{2,34},{3,483},{4,36},{5,485},{6,38},{7,487},{8,40}... | collective-permute-start | bytes 786440 | tf_op jit(solution)/shard_map/ppermute | solution.py:158
  194.5 9.5 %collective-permute-start.14 = (f32[64,1024]{1,0:T(8,128)S(1)}, f32[64,1024]{1,0:T(8,128)S(1)}, u32[]{:S(2)}, u32[]{:S(2)}) collective-permute-start(f32[64,1024]{1,0:T(8,128)S(1)} %fusion.4), channel_id=1, source_target_pairs={{0,480},{1,33},{2,482},{3,35},{4,484},{5,37},{6,486},{7,39},{8,488... | collective-permute-start | bytes 786440 | tf_op jit(solution)/shard_map/ppermute | solution.py:158
  204.0 8.3 %collective-permute-start.15 = (f32[64,1024]{1,0:T(8,128)S(1)}, f32[64,1024]{1,0:T(8,128)S(1)}, u32[]{:S(2)}, u32[]{:S(2)}) collective-permute-start(f32[64,1024]{1,0:T(8,128)S(1)} %fusion.5), channel_id=1, source_target_pairs={{0,32},{1,481},{2,34},{3,483},{4,36},{5,485},{6,38},{7,487},{8,40}... | collective-permute-start | bytes 786440 | tf_op jit(solution)/shard_map/ppermute | solution.py:158
  212.3 4.0 %collective-permute-start.16 = (f32[64,512]{1,0:T(8,128)S(1)}, f32[64,512]{1,0:T(8,128)S(1)}, u32[]{:S(2)}, u32[]{:S(2)}) collective-permute-start(f32[64,512]{1,0:T(8,128)S(1)} %get-tuple-element.11), channel_id=1, source_target_pairs={{1,32},{3,34},{5,36},{7,38},{9,40},{11,42},{13,44},{15,46},{17,48}... | collective-permute-start | bytes 393224 | tf_op jit(solution)/shard_map/ppermute | solution.py:158
  213.0 9.0 %collective-permute-start.17 = (f32[64,512]{1,0:T(8,128)S(1)}, f32[64,512]{1,0:T(8,128)S(1)}, u32[]{:S(2)}, u32[]{:S(2)}) collective-permute-start(f32[64,512]{1,0:T(8,128)S(1)} %get-tuple-element.12), channel_id=1, source_target_pairs={{0,1},{1,33},{2,3},{3,35},{4,5},{5,37},{6,7},{7,39},{8,9},{9,41},{... | collective-permute-start | bytes 393224 | tf_op jit(solution)/shard_map/ppermute | solution.py:158
  222.0 7.7 %collective-permute-start.18 = (f32[32,512]{1,0:T(8,128)S(1)}, f32[32,512]{1,0:T(8,128)S(1)}, u32[]{:S(2)}, u32[]{:S(2)}) collective-permute-start(f32[32,512]{1,0:T(8,128)S(1)} %slice_select_fusion.1), channel_id=1, source_target_pairs={{0,16},{16,0},{32,48},{48,32},{64,80},{80,64},{96,112},{112,96},{1... | collective-permute-start | bytes 196616 | tf_op jit(solution)/shard_map/ppermute | solution.py:223

commit v2 on v1

v2 whole, which is shorter than its diff:
```python
import functools

import jax
import jax.numpy as jnp
from jax import lax
from jax.experimental import pallas as pl
from jax.experimental.pallas import tpu as pltpu
from jax.sharding import PartitionSpec as P

LANES = 128
UNROLL = 32
K_TILE = 768
CHUNKS = 2
PLACES = ((0, 0), (1, 0), (3, 0), (2, 0), (0, 1), (2, 1), (1, 1), (3, 1))


def scatter_kernel(place_ref, w_ref, *refs):
    outs, flag_ref, rows, spread = refs[:-3], refs[-3], refs[-2], refs[-1]
    width, blk = w_ref.shape
    part_rows = width // CHUNKS
    ones = jnp.ones((LANES - width, LANES), jnp.float32)
    spread[...] = jnp.zeros_like(spread)
    for at in range(0, blk, LANES):
        part = w_ref[:, at : at + LANES].astype(jnp.float32)
        rows[at : at + LANES, :] = jnp.concatenate([part, ones], axis=0).T

    def move(i, carry):
        for u in range(UNROLL):
            j = i * UNROLL + u
            spread[pl.ds(place_ref[j], 1), :] = rows[pl.ds(j, 1), :]
        return carry

    lax.fori_loop(0, blk // UNROLL, move, 0)
    for side in range(2):
        for at in range(0, blk, LANES):
            block = spread[side * blk + at : side * blk + at + LANES, :]
            turned = block.T[:width].astype(jnp.bfloat16)
            for h in range(CHUNKS):
                outs[side * CHUNKS + h][:, at : at + LANES] = turned[h * part_rows : (h + 1) * part_rows]
            if side == 0:
                mark = block[:, width:]
                flag_ref[at : at + LANES, :] = jnp.concatenate([mark, mark], axis=1).astype(jnp.bfloat16)


def scatter_rows(place, w_t):
    width, blk = w_t.shape
    return pl.pallas_call(
        scatter_kernel,
        out_shape=[jax.ShapeDtypeStruct((width // CHUNKS, blk), jnp.bfloat16)] * (2 * CHUNKS)
        + [jax.ShapeDtypeStruct((blk, LANES), jnp.bfloat16)],
        in_specs=[pl.BlockSpec(memory_space=pltpu.SMEM), pl.BlockSpec(memory_space=pltpu.VMEM)],
        out_specs=[pl.BlockSpec(memory_space=pltpu.VMEM)] * (2 * CHUNKS + 1),
        scratch_shapes=[pltpu.VMEM((blk, LANES), jnp.float32), pltpu.VMEM((2 * blk, LANES), jnp.float32)],
        compiler_params=pltpu.CompilerParams(vmem_limit_bytes=16 * 2**20),
    )(place, w_t)


def halves_kernel(kept_ref, flag_ref, own_ref, other_ref, out_ref, done_ref):
    tile, cols = own_ref.shape
    g = lax.axis_index("grp")
    base = (g * pl.num_programs(0) + pl.program_id(0)) * tile
    row = lax.broadcasted_iota(jnp.int32, (tile, LANES), 0) + base
    done_ref[...] = jnp.zeros_like(done_ref)
    mark = flag_ref[...].astype(jnp.float32)
    alive = row < kept_ref[0]
    mine = alive & (mark > 0.5)
    theirs = alive & (mark < 0.5)
    lower = g >= 16
    in_half = (
        jnp.where(lower, theirs.astype(jnp.float32), mine.astype(jnp.float32)),
        jnp.where(lower, mine.astype(jnp.float32), theirs.astype(jnp.float32)),
    )
    for c, ref in enumerate((own_ref, other_ref)):
        for h in range(2):
            for v in range(cols // LANES):
                values = ref[:, v * LANES : (v + 1) * LANES].astype(jnp.float32)
                at = (c * 2 + h) * cols + v * LANES
                out_ref[:, at : at + LANES] = jnp.where(in_half[h] > 0.5, values, 0.0).astype(jnp.bfloat16)


def split_halves(kept, flag, own, other):
    blk, cols = own.shape
    return pl.pallas_call(
        halves_kernel,
        grid=(blk // K_TILE,),
        out_shape=[
            jax.ShapeDtypeStruct((blk, 4 * cols), jnp.bfloat16),
            jax.ShapeDtypeStruct((8, LANES), jnp.float32),
        ],
        in_specs=[
            pl.BlockSpec(memory_space=pltpu.SMEM),
            pl.BlockSpec((K_TILE, LANES), lambda i: (i, 0)),
            pl.BlockSpec((K_TILE, cols), lambda i: (i, 0)),
            pl.BlockSpec((K_TILE, cols), lambda i: (i, 0)),
        ],
        out_specs=[pl.BlockSpec((K_TILE, 4 * cols), lambda i: (i, 0)), pl.BlockSpec((8, LANES), lambda i: (0, 0))],
        compiler_params=pltpu.CompilerParams(vmem_limit_bytes=12 * 2**20),
    )(kept, flag, own, other)


def slot_of(z, x, y_lo, core, dx, dy):
    odd = (core + z) % 2
    target = (x + dx) % 4 * 4 + (y_lo + dy) % 2 * 2 + core
    above = (target + 16 - z - odd) % 16 // 2
    even_slot = jnp.where(above > 4, 2 * above - 9, jnp.minimum(8 - 2 * above, 7))
    odd_slot = jnp.where(above > 4, 2 * above - 8, jnp.maximum(7 - 2 * above, 0))
    return jnp.where(odd == 1, odd_slot, even_slot)


def product_kernel(*refs):
    pieces, s_ref, out_ref, total = refs[:-3], refs[-3], refs[-2], refs[-1]
    z, c = lax.axis_index("grp") // 2, lax.axis_index("col")
    step = pl.program_id(0)
    rows = pieces[0].shape[0]
    lhs = jnp.concatenate([ref[...] for ref in pieces], axis=0)
    term = jnp.dot(lhs, s_ref[...], preferred_element_type=jnp.float32)

    @pl.when(step == 0)
    def _():
        total[...] = term

    @pl.when(step > 0)
    def _():
        total[...] += term

    @pl.when(step == pl.num_programs(0) - 1)
    def _():
        for i in range(len(pieces)):
            slot = slot_of(z, c // 4, c // 2 % 2, c % 2, *PLACES[i])
            out_ref[slot] = total[i * rows : (i + 1) * rows, :]


def product(pieces, s_both):
    rows, blk = pieces[0].shape
    cols = s_both.shape[1]
    count = len(pieces)
    return pl.pallas_call(
        product_kernel,
        grid=(blk // K_TILE,),
        out_shape=jax.ShapeDtypeStruct((count, rows, cols), jnp.float32),
        in_specs=[pl.BlockSpec((rows, K_TILE), lambda i: (0, i))] * count
        + [pl.BlockSpec((K_TILE, cols), lambda i: (i, 0))],
        out_specs=pl.BlockSpec((count, rows, cols), lambda i: (0, 0, 0)),
        scratch_shapes=[pltpu.VMEM((count * rows, cols), jnp.float32)],
        compiler_params=pltpu.CompilerParams(vmem_limit_bytes=16 * 2**20),
    )(*pieces, s_both)


def col_move(value, target):
    pairs = []
    for c in range(16):
        x, y, core = c // 4, c // 2 % 2, c % 2
        tx, ty, tcore = target(x, y, core)
        pairs.append((c, tx % 4 * 4 + ty * 2 + tcore))
    return lax.ppermute(value, "col", pairs)


def slice_move(value, target):
    pairs = []
    for g in range(32):
        for c in range(16):
            to = target(g // 2, g % 2, c)
            if to is not None:
                pairs.append((g * 16 + c, (to[0] % 16 * 2 + to[1]) * 16 + to[2]))
    return lax.ppermute(value, ("grp", "col"), pairs)


def exchange(step, z, y_hi, c):
    even = (c - z) % 2 == 0
    return (z + 1 if even == (step % 2 == 1) else z - 1, y_hi, c)


def combine_kernel(count, *refs):
    own_ref, arrived_ref = refs[0], refs[1]
    outs = refs[len(refs) - count :]
    outs[0][...] = own_ref[...] + arrived_ref[...]
    if count == 2:
        outs[1][...] = refs[2][...]


def combine(own, arrived, following, after):
    count = 1 if following is None else 2
    arrays = [own, arrived] + ([] if following is None else [following])
    whole = pl.BlockSpec(memory_space=pltpu.VMEM)
    return pl.pallas_call(
        functools.partial(combine_kernel, count),
        out_shape=[jax.ShapeDtypeStruct(own.shape, own.dtype)] * count,
        in_specs=[whole] * len(arrays) + [pl.BlockSpec(memory_space=pl.ANY)],
        out_specs=[whole] * count,
        compiler_params=pltpu.CompilerParams(vmem_limit_bytes=4 * 2**20),
    )(*arrays, after)


def gather_col(here):
    pieces = {(0, 0): here}
    for d in (1, 3, 2):
        pieces[d, 0] = col_move(here, lambda x, y, k, d=d: (x - d, y, k))
    pieces[0, 1] = col_move(here, lambda x, y, k: (x, 1 - y, k))
    pieces[2, 1] = col_move(pieces[0, 1], lambda x, y, k: (x - 2, y, k))
    for d in (1, 3):
        pieces[d, 1] = col_move(pieces[d, 0], lambda x, y, k: (x, 1 - y, k))
    return pieces


def last(z, y_hi, c):
    return (z + 1, y_hi, c) if (c - z) % 2 else (z, y_hi, c ^ 1)


def last_other(z, y_hi, c):
    return (z + 1, y_hi, c ^ 1) if (c - z) % 2 else None


def per_device(window_rows, secular, source, kept_count):
    blk = secular.shape[0]
    g = lax.axis_index("grp")
    c = lax.axis_index("col")
    z, y_hi = g // 2, g % 2
    is_odd = (c + z) % 2 == 1
    is_high = y_hi == 1
    own_base = g * blk
    partner_base = jnp.bitwise_xor(g, 16) * blk

    other = col_move(secular, lambda x, y, k: (x, y, 1 - k))
    inside = (source >= own_base) & (source < own_base + blk)
    place = jnp.where(inside, source - own_base, blk + source - partner_base)
    *parts, flag = scatter_rows(place, window_rows.T)
    own_parts, cross_parts = parts[:CHUNKS], parts[CHUNKS:]
    s_both, masked = split_halves(kept_count, flag, secular, other)

    sums = []
    leaving, after = cross_parts[0], masked
    for h in range(CHUNKS):
        arrived = lax.ppermute(leaving, "grp", [(i, i ^ 16) for i in range(32)])
        here, *next_leaving = combine(own_parts[h], arrived, cross_parts[h + 1] if h + 1 < CHUNKS else None, after)
        if next_leaving:
            leaving = next_leaving[0]
        pieces = gather_col(here)
        terms = product([pieces[p] for p in PLACES], s_both)
        after = pieces[3, 1]
        moving = terms[0]
        for step in range(1, 8):
            moving = terms[step] + slice_move(moving, functools.partial(exchange, step))
        half_cols = moving.shape[1] // 2
        mine, theirs = moving[:, :half_cols], moving[:, half_cols:]
        first_in = slice_move(jnp.where(is_odd, mine, theirs), last)
        second_in = slice_move(theirs, last_other)
        sums.append(jnp.where(is_odd, second_in, mine) + first_in)

    low, high = sums
    across = lax.ppermute(jnp.where(is_high, low, high), "grp", [(i, i ^ 1) for i in range(32)])
    final = (jnp.where(is_high, high, low) + across).astype(jnp.bfloat16)
    return final.reshape(final.shape[0], 2, -1).transpose(1, 0, 2)


def solution(mesh):
    return jax.shard_map(
        per_device,
        mesh=mesh,
        in_specs=(P("grp", "col"), P("grp", "col"), P("grp"), P()),
        out_specs=P(None, "grp", "col"),
        check_vma=False,
    )
```

time: 231 us -> 207 us (0.90); the launches traced: 230 us -> 203 us
  waiting for transfers between devices: 87.3 us -> 24.4 us
  starting transfers between devices: 107 us -> 153 us
  Pallas kernels: 24.8 us -> 17.1 us
    ppermute x9 -> x18, waiting for transfers between devices: 48.5 us -> 17.4 us  [slice_move(): return lax.ppermute(value, ('grp', 'col'), pairs)]
    ppermute x8 -> x15, starting transfers between devices: 33.6 us -> 53.6 us  [col_move(): return lax.ppermute(value, 'col', pairs)]
    ppermute x8 -> x15, waiting for transfers between devices: 19.6 us -> 0.04 us  [col_move(): return lax.ppermute(value, 'col', pairs)]
    ppermute x9 -> x18, starting transfers between devices: 53.4 us -> 69.4 us  [slice_move(): return lax.ppermute(value, ('grp', 'col'), pairs)]
    ppermute x1 -> x2, waiting for transfers between devices: 16.4 us -> 1.22 us  [per_device(): arrived = lax.ppermute(leaving, 'grp', [(i, i ^ 16) for i in range(32)])]
    ppermute x1 -> x2, starting transfers between devices: 15.7 us -> 28.2 us  [per_device(): arrived = lax.ppermute(leaving, 'grp', [(i, i ^ 16) for i in range(32)])]
    pallas_call x2 -> x4, Pallas kernels: 16.1 us -> 9.29 us  [the longest x1 5.76 us: scatter_rows(): pl.pallas_call(scatter_kernel, out_shape=[jax.ShapeDtypeStruct((width //...]
    ppermute x1, waiting for transfers between devices: 2.85 us -> 5.74 us  [per_device(): lax.ppermute(jnp.where(is_high, low, high), 'grp', [(i, i ^ 1) for i in r...]
  transfers between devices with their start and end apart: 19 -> 36, of which waited for: 12 -> 9; matrix products, arithmetic and copies ran while one was open for 1% -> 0% of each run, Pallas kernels for 7% -> 8%
where the time goes in v2:
time: 207 us; the launch traced here: 203 us
  starting transfers between devices  153 us (74%)
  waiting for transfers between devices  24.4 us (12%)
  Pallas kernels  17.1 us (8%)
  local copies, waits for them, and re-layouts  6.44 us (3%)
    ppermute x18, starting transfers between devices, slice_move(): return lax.ppermute(value, ('grp', 'col'), pairs)  69.4 us
    ppermute x15, starting transfers between devices, col_move(): return lax.ppermute(value, 'col', pairs)  53.6 us
    ppermute x2, starting transfers between devices, per_device(): arrived = lax.ppermute(leaving, 'grp', [(i, i ^ 16) for i in range(32)])  28.2 us
    ppermute x18, waiting for transfers between devices, slice_move(): return lax.ppermute(value, ('grp', 'col'), pairs)  17.4 us
    pallas_call x2, Pallas kernels, product(): pl.pallas_call(product_kernel, grid=(blk // K_TILE,), out_shape=jax.Shape...  7.81 us
    unnamed x8, local copies, waits for them, and re-layouts  5.8 us
    pallas_call x1, Pallas kernels, scatter_rows(): pl.pallas_call(scatter_kernel, out_shape=[jax.ShapeDtypeStruct((width //...  5.76 us
    ppermute x1, waiting for transfers between devices, per_device(): lax.ppermute(jnp.where(is_high, low, high), 'grp', [(i, i ^ 1) for i in r...  5.74 us
  transfers between devices with their start and end apart: 36, of which 9 were waited for; matrix products, arithmetic and copies ran while one was open for 0% of the time, Pallas kernels for 8%

profile of v2, /device:TPU:6, one launch (start us, length us, event | category | flops | bytes accessed | tf_op | source)
XLA Modules:
  0.0 203.5 jit_solution(14068437910076059)
XLA Ops:
  3.7 5.8 %shard_map.46 = (bf16[32,3840]{1,0:T(8,128)(2,1)S(1)}, bf16[32,3840]{1,0:T(8,128)(2,1)S(1)}, bf16[32,3840]{1,0:T(8,128)(2,1)S(1)}, bf16[32,3840]{1,0:T(8,128)(2,1)S(1)}, bf16[3840,128]{1,0:T(8,128)(2,1)S(1)}) custom-call(s32[3840]{0:T(1024)S(1)} %subtract_select_fusion.place_ref, bf16[64,3840]{1,0:T(8,128)(2,1)S(1)} %bitcast.68), custom_call_target="tpu_custom_call" | custom-call | tf_op jit(solution)/shard_map/pallas_call | solution.py:47
  9.4 15.7 %collective-permute-start = (bf16[32,3840]{1,0:T(8,128)(2,1)S(1)}, bf16[32,3840]{1,0:T(8,128)(2,1)S(1)}, u32[]{:S(2)}, u32[]{:S(2)}) collective-permute-start(bf16[32,3840]{1,0:T(8,128)(2,1)S(1)} %get-tuple-element.16), channel_id=1, source_target_pairs={{0,256},{16,272},{32,288},{48,304},{64,320},{80,336},{96,352},{112... | collective-permute-start | bytes 737288 | tf_op jit(solution)/shard_map/ppermute | solution.py:233
  27.4 3.5 %shard_map.47 = (bf16[3840,1024]{1,0:T(8,128)(2,1)S(1)}, f32[8,128]{1,0:T(8,128)S(1)}) custom-call(s32[1]{0:T(128)S(6)} %copy.9.kept_ref, bf16[3840,128]{1,0:T(8,128)(2,1)S(1)} %get-tuple-element.18.flag_ref, bf16[3840,256]{1,0:T(8,128)(2,1)S(1)} %copy-done.2, bf16[3840,256]{1,0:T(8,128)(2,1)S(1)} %collective-permute-done.1.other_ref), custom_call_target="tpu_custom_call" | custom-call | tf_op jit(solution)/shard_map/pallas_call | solution.py:83
  32.1 10.5 %collective-permute-start.3 = (bf16[32,3840]{1,0:T(8,128)(2,1)S(1)}, bf16[32,3840]{1,0:T(8,128)(2,1)S(1)}, u32[]{:S(2)}, u32[]{:S(2)}) collective-permute-start(bf16[32,3840]{1,0:T(8,128)(2,1)S(1)} %get-tuple-element.21.refs_0_), channel_id=1, source_target_pairs={{0,4},{1,5},{2,6},{3,7},{4,8},{5,9},{6,10},{7,11},{8,12},{9,13},{1... | collective-permute-start | bytes 737288 | tf_op jit(solution)/shard_map/ppermute | solution.py:155
  46.5 12.4 %collective-permute-start.2 = (bf16[32,3840]{1,0:T(8,128)(2,1)S(1)}, bf16[32,3840]{1,0:T(8,128)(2,1)S(1)}, u32[]{:S(2)}, u32[]{:S(2)}) collective-permute-start(bf16[32,3840]{1,0:T(8,128)(2,1)S(1)} %get-tuple-element.20), channel_id=1, source_target_pairs={{0,256},{16,272},{32,288},{48,304},{64,320},{80,336},{96,352},{112... | collective-permute-start | bytes 737288 | tf_op jit(solution)/shard_map/ppermute | solution.py:233
  59.0 3.9 %collective-permute-start.4 = (bf16[32,3840]{1,0:T(8,128)(2,1)S(1)}, bf16[32,3840]{1,0:T(8,128)(2,1)S(1)}, u32[]{:S(2)}, u32[]{:S(2)}) collective-permute-start(bf16[32,3840]{1,0:T(8,128)(2,1)S(1)} %collective-permute-done.3.refs_2_), channel_id=1, source_target_pairs={{0,2},{1,3},{2,0},{3,1},{4,6},{5,7},{6,4},{7,5},{8,10},{9,11},{10,... | collective-permute-start | bytes 737288 | tf_op jit(solution)/shard_map/ppermute | solution.py:155
  62.9 3.4 %collective-permute-start.22 = (bf16[32,3840]{1,0:T(8,128)(2,1)S(1)}, bf16[32,3840]{1,0:T(8,128)(2,1)S(1)}, u32[]{:S(2)}, u32[]{:S(2)}) collective-permute-start(bf16[32,3840]{1,0:T(8,128)(2,1)S(1)} %get-tuple-element.21.refs_0_), channel_id=1, source_target_pairs={{0,8},{1,9},{2,10},{3,11},{4,12},{5,13},{6,14},{7,15},{8,0},{9,1},... | collective-permute-start | bytes 737288 | tf_op jit(solution)/shard_map/ppermute | solution.py:155
  66.3 4.0 %collective-permute-start.24 = (bf16[32,3840]{1,0:T(8,128)(2,1)S(1)}, bf16[32,3840]{1,0:T(8,128)(2,1)S(1)}, u32[]{:S(2)}, u32[]{:S(2)}) collective-permute-start(bf16[32,3840]{1,0:T(8,128)(2,1)S(1)} %collective-permute-done.23.refs_4_), channel_id=1, source_target_pairs={{0,8},{1,9},{2,10},{3,11},{4,12},{5,13},{6,14},{7,15},{8,0},{9,1},... | collective-permute-start | bytes 737288 | tf_op jit(solution)/shard_map/ppermute | solution.py:155
  72.2 3.9 %collective-permute-start.8 = (bf16[32,3840]{1,0:T(8,128)(2,1)S(1)}, bf16[32,3840]{1,0:T(8,128)(2,1)S(1)}, u32[]{:S(2)}, u32[]{:S(2)}) collective-permute-start(bf16[32,3840]{1,0:T(8,128)(2,1)S(1)} %shard_map.49.refs_0_), channel_id=1, source_target_pairs={{0,2},{1,3},{2,0},{3,1},{4,6},{5,7},{6,4},{7,5},{8,10},{9,11},{10,... | collective-permute-start | bytes 737288 | tf_op jit(solution)/shard_map/ppermute | solution.py:155
  76.2 5.1 %collective-permute-start.6 = (bf16[32,3840]{1,0:T(8,128)(2,1)S(1)}, bf16[32,3840]{1,0:T(8,128)(2,1)S(1)}, u32[]{:S(2)}, u32[]{:S(2)}) collective-permute-start(bf16[32,3840]{1,0:T(8,128)(2,1)S(1)} %shard_map.49.refs_0_), channel_id=1, source_target_pairs={{0,4},{1,5},{2,6},{3,7},{4,8},{5,9},{6,10},{7,11},{8,12},{9,13},{1... | collective-permute-start | bytes 737288 | tf_op jit(solution)/shard_map/ppermute | solution.py:155
  83.3 3.9 %shard_map.51 = f32[8,32,1024]{2,1,0:T(8,128)S(1)} custom-call(bf16[32,3840]{1,0:T(8,128)(2,1)S(1)} %get-tuple-element.21.refs_0_, bf16[32,3840]{1,0:T(8,128)(2,1)S(1)} %collective-permute-done.21.refs_1_, bf16[32,3840]{1,0:T(8,128)(2,1)S(1)} %collective-permute-done.3.refs_2_, bf16[32,3840]{1,0:T(8,128)(2,1)S(1)} %collective-permute-done.22.refs_3_, ...), custom_call_target="tpu_custom_call" | custom-call | tf_op jit(solution)/shard_map/pallas_call | solution.py:137
  87.2 11.7 %collective-permute-start.26 = (f32[32,1024]{1,0:T(8,128)S(1)}, f32[32,1024]{1,0:T(8,128)S(1)}, u32[]{:S(2)}, u32[]{:S(2)}) collective-permute-start(f32[32,1024]{1,0:T(8,128)S(1)} %slice_bitcast_fusion), channel_id=1, source_target_pairs={{0,32},{1,481},{2,34},{3,483},{4,36},{5,485},{6,38},{7,487},{8,40}... | collective-permute-start | bytes 393224 | tf_op jit(solution)/shard_map/ppermute | solution.py:165
  99.0 3.3 %collective-permute-start.7 = (bf16[32,3840]{1,0:T(8,128)(2,1)S(1)}, bf16[32,3840]{1,0:T(8,128)(2,1)S(1)}, u32[]{:S(2)}, u32[]{:S(2)}) collective-permute-start(bf16[32,3840]{1,0:T(8,128)(2,1)S(1)} %shard_map.49.refs_0_), channel_id=1, source_target_pairs={{0,8},{1,9},{2,10},{3,11},{4,12},{5,13},{6,14},{7,15},{8,0},{9,1},... | collective-permute-start | bytes 737288 | tf_op jit(solution)/shard_map/ppermute | solution.py:155
  102.3 4.0 %collective-permute-start.9 = (bf16[32,3840]{1,0:T(8,128)(2,1)S(1)}, bf16[32,3840]{1,0:T(8,128)(2,1)S(1)}, u32[]{:S(2)}, u32[]{:S(2)}) collective-permute-start(bf16[32,3840]{1,0:T(8,128)(2,1)S(1)} %collective-permute-done.8.refs_4_), channel_id=1, source_target_pairs={{0,8},{1,9},{2,10},{3,11},{4,12},{5,13},{6,14},{7,15},{8,0},{9,1},... | collective-permute-start | bytes 737288 | tf_op jit(solution)/shard_map/ppermute | solution.py:155
  106.3 3.5 %collective-permute-start.11 = (bf16[32,3840]{1,0:T(8,128)(2,1)S(1)}, bf16[32,3840]{1,0:T(8,128)(2,1)S(1)}, u32[]{:S(2)}, u32[]{:S(2)}) collective-permute-start(bf16[32,3840]{1,0:T(8,128)(2,1)S(1)} %collective-permute-done.6.refs_2_), channel_id=1, source_target_pairs={{0,2},{1,3},{2,0},{3,1},{4,6},{5,7},{6,4},{7,5},{8,10},{9,11},{10,... | collective-permute-start | bytes 737288 | tf_op jit(solution)/shard_map/ppermute | solution.py:155
  109.9 2.4 %collective-permute-start.10 = (bf16[32,3840]{1,0:T(8,128)(2,1)S(1)}, bf16[32,3840]{1,0:T(8,128)(2,1)S(1)}, u32[]{:S(2)}, u32[]{:S(2)}) collective-permute-start(bf16[32,3840]{1,0:T(8,128)(2,1)S(1)} %collective-permute-done.5.refs_1_), channel_id=1, source_target_pairs={{0,2},{1,3},{2,0},{3,1},{4,6},{5,7},{6,4},{7,5},{8,10},{9,11},{10,... | collective-permute-start | bytes 737288 | tf_op jit(solution)/shard_map/ppermute | solution.py:155
  112.3 9.5 %collective-permute-start.27 = (f32[32,1024]{1,0:T(8,128)S(1)}, f32[32,1024]{1,0:T(8,128)S(1)}, u32[]{:S(2)}, u32[]{:S(2)}) collective-permute-start(f32[32,1024]{1,0:T(8,128)S(1)} %fusion), channel_id=1, source_target_pairs={{0,480},{1,33},{2,482},{3,35},{4,484},{5,37},{6,486},{7,39},{8,488... | collective-permute-start | bytes 393224 | tf_op jit(solution)/shard_map/ppermute | solution.py:165
  121.8 3.2 %copy-done.1 = bf16[3840,1024]{1,0:T(8,128)(2,1)S(1)} copy-done((bf16[3840,1024]{1,0:T(8,128)(2,1)S(1)}, bf16[3840,1024]{1,0:T(8,128)(2,1)}, u32[]{:S(2)}) %copy-start.1) | copy-done | bytes 7864344
  125.0 3.9 %shard_map.50 = f32[8,32,1024]{2,1,0:T(8,128)S(1)} custom-call(bf16[32,3840]{1,0:T(8,128)(2,1)S(1)} %shard_map.49.refs_0_, bf16[32,3840]{1,0:T(8,128)(2,1)S(1)} %collective-permute-done.5.refs_1_, bf16[32,3840]{1,0:T(8,128)(2,1)S(1)} %collective-permute-done.6.refs_2_, bf16[32,3840]{1,0:T(8,128)(2,1)S(1)} %collective-permute-done.7.refs_3_, ...), custom_call_target="tpu_custom_call" | custom-call | tf_op jit(solution)/shard_map/pallas_call | solution.py:137
  130.9 3.9 %collective-permute-start.28 = (f32[32,1024]{1,0:T(8,128)S(1)}, f32[32,1024]{1,0:T(8,128)S(1)}, u32[]{:S(2)}, u32[]{:S(2)}) collective-permute-start(f32[32,1024]{1,0:T(8,128)S(1)} %fusion.1), channel_id=1, source_target_pairs={{0,32},{1,481},{2,34},{3,483},{4,36},{5,485},{6,38},{7,487},{8,40}... | collective-permute-start | bytes 393224 | tf_op jit(solution)/shard_map/ppermute | solution.py:165
  136.1 5.6 %collective-permute-start.13 = (f32[32,1024]{1,0:T(8,128)S(1)}, f32[32,1024]{1,0:T(8,128)S(1)}, u32[]{:S(2)}, u32[]{:S(2)}) collective-permute-start(f32[32,1024]{1,0:T(8,128)S(1)} %fusion.7), channel_id=1, source_target_pairs={{0,480},{1,33},{2,482},{3,35},{4,484},{5,37},{6,486},{7,39},{8,488... | collective-permute-start | bytes 393224 | tf_op jit(solution)/shard_map/ppermute | solution.py:165
  141.8 4.4 %collective-permute-start.29 = (f32[32,1024]{1,0:T(8,128)S(1)}, f32[32,1024]{1,0:T(8,128)S(1)}, u32[]{:S(2)}, u32[]{:S(2)}) collective-permute-start(f32[32,1024]{1,0:T(8,128)S(1)} %fusion.2), channel_id=1, source_target_pairs={{0,480},{1,33},{2,482},{3,35},{4,484},{5,37},{6,486},{7,39},{8,488... | collective-permute-start | bytes 393224 | tf_op jit(solution)/shard_map/ppermute | solution.py:165
  149.9 2.2 %collective-permute-start.30 = (f32[32,1024]{1,0:T(8,128)S(1)}, f32[32,1024]{1,0:T(8,128)S(1)}, u32[]{:S(2)}, u32[]{:S(2)}) collective-permute-start(f32[32,1024]{1,0:T(8,128)S(1)} %fusion.3), channel_id=1, source_target_pairs={{0,32},{1,481},{2,34},{3,483},{4,36},{5,485},{6,38},{7,487},{8,40}... | collective-permute-start | bytes 393224 | tf_op jit(solution)/shard_map/ppermute | solution.py:165
  154.0 2.8 %collective-permute-start.15 = (f32[32,1024]{1,0:T(8,128)S(1)}, f32[32,1024]{1,0:T(8,128)S(1)}, u32[]{:S(2)}, u32[]{:S(2)}) collective-permute-start(f32[32,1024]{1,0:T(8,128)S(1)} %fusion.9), channel_id=1, source_target_pairs={{0,480},{1,33},{2,482},{3,35},{4,484},{5,37},{6,486},{7,39},{8,488... | collective-permute-start | bytes 393224 | tf_op jit(solution)/shard_map/ppermute | solution.py:165
  156.8 6.2 %collective-permute-start.31 = (f32[32,1024]{1,0:T(8,128)S(1)}, f32[32,1024]{1,0:T(8,128)S(1)}, u32[]{:S(2)}, u32[]{:S(2)}) collective-permute-start(f32[32,1024]{1,0:T(8,128)S(1)} %fusion.4), channel_id=1, source_target_pairs={{0,480},{1,33},{2,482},{3,35},{4,484},{5,37},{6,486},{7,39},{8,488... | collective-permute-start | bytes 393224 | tf_op jit(solution)/shard_map/ppermute | solution.py:165
  166.8 2.2 %collective-permute-start.32 = (f32[32,1024]{1,0:T(8,128)S(1)}, f32[32,1024]{1,0:T(8,128)S(1)}, u32[]{:S(2)}, u32[]{:S(2)}) collective-permute-start(f32[32,1024]{1,0:T(8,128)S(1)} %fusion.5), channel_id=1, source_target_pairs={{0,32},{1,481},{2,34},{3,483},{4,36},{5,485},{6,38},{7,487},{8,40}... | collective-permute-start | bytes 393224 | tf_op jit(solution)/shard_map/ppermute | solution.py:165
  170.2 3.4 %collective-permute-start.17 = (f32[32,1024]{1,0:T(8,128)S(1)}, f32[32,1024]{1,0:T(8,128)S(1)}, u32[]{:S(2)}, u32[]{:S(2)}) collective-permute-start(f32[32,1024]{1,0:T(8,128)S(1)} %fusion.11), channel_id=1, source_target_pairs={{0,480},{1,33},{2,482},{3,35},{4,484},{5,37},{6,486},{7,39},{8,488... | collective-permute-start | bytes 393224 | tf_op jit(solution)/shard_map/ppermute | solution.py:165
  173.7 4.6 %collective-permute-done.17 = f32[32,1024]{1,0:T(8,128)S(1)} collective-permute-done((f32[32,1024]{1,0:T(8,128)S(1)}, f32[32,1024]{1,0:T(8,128)S(1)}, u32[]{:S(2)}, u32[]{:S(2)}) %collective-permute-start.17) | collective-permute-done | bytes 131104 | tf_op jit(solution)/shard_map/ppermute | solution.py:165
  180.9 5.3 %collective-permute-start.34 = (f32[32,512]{1,0:T(8,128)S(1)}, f32[32,512]{1,0:T(8,128)S(1)}, u32[]{:S(2)}, u32[]{:S(2)}) collective-permute-start(f32[32,512]{1,0:T(8,128)S(1)} %get-tuple-element.27), channel_id=1, source_target_pairs={{0,1},{1,33},{2,3},{3,35},{4,5},{5,37},{6,7},{7,39},{8,9},{9,41},{... | collective-permute-start | bytes 196616 | tf_op jit(solution)/shard_map/ppermute | solution.py:165
  186.9 3.2 %collective-permute-start.20 = (f32[32,512]{1,0:T(8,128)S(1)}, f32[32,512]{1,0:T(8,128)S(1)}, u32[]{:S(2)}, u32[]{:S(2)}) collective-permute-start(f32[32,512]{1,0:T(8,128)S(1)} %get-tuple-element.29), channel_id=1, source_target_pairs={{0,1},{1,33},{2,3},{3,35},{4,5},{5,37},{6,7},{7,39},{8,9},{9,41},{... | collective-permute-start | bytes 196616 | tf_op jit(solution)/shard_map/ppermute | solution.py:165
  190.1 5.0 %collective-permute-done.20 = f32[32,512]{1,0:T(8,128)S(1)} collective-permute-done((f32[32,512]{1,0:T(8,128)S(1)}, f32[32,512]{1,0:T(8,128)S(1)}, u32[]{:S(2)}, u32[]{:S(2)}) %collective-permute-start.20) | collective-permute-done | bytes 65568 | tf_op jit(solution)/shard_map/ppermute | solution.py:165
  197.1 5.7 %collective-permute-done.35 = f32[32,512]{1,0:T(8,128)S(1)} collective-permute-done((f32[32,512]{1,0:T(8,128)S(1)}, f32[32,512]{1,0:T(8,128)S(1)}, u32[]{:S(2)}, u32[]{:S(2)}) %collective-permute-start.35) | collective-permute-done | bytes 65568 | tf_op jit(solution)/shard_map/ppermute | solution.py:250
  (76 shorter events, 33.9 us)
Async XLA Ops:
  0.0 25.8 %collective-permute-start.1 = (bf16[3840,256]{1,0:T(8,128)(2,1)}, bf16[3840,256]{1,0:T(8,128)(2,1)S(1)}, u32[]{:S(2)}, u32[]{:S(2)}) collective-permute-start(bf16[3840,256]{1,0:T(8,128)(2,1)} %own_ref.1), channel_id=1, source_target_pairs={{0,1},{1,0},{2,3},{3,2},{4,5},{5,4},{6,7},{7,6},{8,9},{9,8},{10,11... | collective-permute-start | bytes 5898248 | tf_op jit(solution)/shard_map/ppermute | solution.py:155
  9.4 22.6 %collective-permute-start = (bf16[32,3840]{1,0:T(8,128)(2,1)S(1)}, bf16[32,3840]{1,0:T(8,128)(2,1)S(1)}, u32[]{:S(2)}, u32[]{:S(2)}) collective-permute-start(bf16[32,3840]{1,0:T(8,128)(2,1)S(1)} %get-tuple-element.16), channel_id=1, source_target_pairs={{0,256},{16,272},{32,288},{48,304},{64,320},{80,336},{96,352},{112... | collective-permute-start | bytes 737288 | tf_op jit(solution)/shard_map/ppermute | solution.py:233
  32.1 26.8 %collective-permute-start.3 = (bf16[32,3840]{1,0:T(8,128)(2,1)S(1)}, bf16[32,3840]{1,0:T(8,128)(2,1)S(1)}, u32[]{:S(2)}, u32[]{:S(2)}) collective-permute-start(bf16[32,3840]{1,0:T(8,128)(2,1)S(1)} %get-tuple-element.21.refs_0_), channel_id=1, source_target_pairs={{0,4},{1,5},{2,6},{3,7},{4,8},{5,9},{6,10},{7,11},{8,12},{9,13},{1... | collective-permute-start | bytes 737288 | tf_op jit(solution)/shard_map/ppermute | solution.py:155
  42.6 23.6 %collective-permute-start.23 = (bf16[32,3840]{1,0:T(8,128)(2,1)S(1)}, bf16[32,3840]{1,0:T(8,128)(2,1)S(1)}, u32[]{:S(2)}, u32[]{:S(2)}) collective-permute-start(bf16[32,3840]{1,0:T(8,128)(2,1)S(1)} %get-tuple-element.21.refs_0_), channel_id=1, source_target_pairs={{0,2},{1,3},{2,0},{3,1},{4,6},{5,7},{6,4},{7,5},{8,10},{9,11},{10,... | collective-permute-start | bytes 737288 | tf_op jit(solution)/shard_map/ppermute | solution.py:155
  44.6 25.7 %collective-permute-start.21 = (bf16[32,3840]{1,0:T(8,128)(2,1)S(1)}, bf16[32,3840]{1,0:T(8,128)(2,1)S(1)}, u32[]{:S(2)}, u32[]{:S(2)}) collective-permute-start(bf16[32,3840]{1,0:T(8,128)(2,1)S(1)} %get-tuple-element.21.refs_0_), channel_id=1, source_target_pairs={{0,12},{1,13},{2,14},{3,15},{4,0},{5,1},{6,2},{7,3},{8,4},{9,5},{1... | collective-permute-start | bytes 737288 | tf_op jit(solution)/shard_map/ppermute | solution.py:155
  46.5 25.7 %collective-permute-start.2 = (bf16[32,3840]{1,0:T(8,128)(2,1)S(1)}, bf16[32,3840]{1,0:T(8,128)(2,1)S(1)}, u32[]{:S(2)}, u32[]{:S(2)}) collective-permute-start(bf16[32,3840]{1,0:T(8,128)(2,1)S(1)} %get-tuple-element.20), channel_id=1, source_target_pairs={{0,256},{16,272},{32,288},{48,304},{64,320},{80,336},{96,352},{112... | collective-permute-start | bytes 737288 | tf_op jit(solution)/shard_map/ppermute | solution.py:233
  59.0 13.3 %collective-permute-start.4 = (bf16[32,3840]{1,0:T(8,128)(2,1)S(1)}, bf16[32,3840]{1,0:T(8,128)(2,1)S(1)}, u32[]{:S(2)}, u32[]{:S(2)}) collective-permute-start(bf16[32,3840]{1,0:T(8,128)(2,1)S(1)} %collective-permute-done.3.refs_2_), channel_id=1, source_target_pairs={{0,2},{1,3},{2,0},{3,1},{4,6},{5,7},{6,4},{7,5},{8,10},{9,11},{10,... | collective-permute-start | bytes 737288 | tf_op jit(solution)/shard_map/ppermute | solution.py:155
  62.9 18.4 %collective-permute-start.22 = (bf16[32,3840]{1,0:T(8,128)(2,1)S(1)}, bf16[32,3840]{1,0:T(8,128)(2,1)S(1)}, u32[]{:S(2)}, u32[]{:S(2)}) collective-permute-start(bf16[32,3840]{1,0:T(8,128)(2,1)S(1)} %get-tuple-element.21.refs_0_), channel_id=1, source_target_pairs={{0,8},{1,9},{2,10},{3,11},{4,12},{5,13},{6,14},{7,15},{8,0},{9,1},... | collective-permute-start | bytes 737288 | tf_op jit(solution)/shard_map/ppermute | solution.py:155
  66.3 17.0 %collective-permute-start.24 = (bf16[32,3840]{1,0:T(8,128)(2,1)S(1)}, bf16[32,3840]{1,0:T(8,128)(2,1)S(1)}, u32[]{:S(2)}, u32[]{:S(2)}) collective-permute-start(bf16[32,3840]{1,0:T(8,128)(2,1)S(1)} %collective-permute-done.23.refs_4_), channel_id=1, source_target_pairs={{0,8},{1,9},{2,10},{3,11},{4,12},{5,13},{6,14},{7,15},{8,0},{9,1},... | collective-permute-start | bytes 737288 | tf_op jit(solution)/shard_map/ppermute | solution.py:155
  70.3 13.0 %collective-permute-start.25 = (bf16[32,3840]{1,0:T(8,128)(2,1)S(1)}, bf16[32,3840]{1,0:T(8,128)(2,1)S(1)}, u32[]{:S(2)}, u32[]{:S(2)}) collective-permute-start(bf16[32,3840]{1,0:T(8,128)(2,1)S(1)} %collective-permute-done.21.refs_1_), channel_id=1, source_target_pairs={{0,2},{1,3},{2,0},{3,1},{4,6},{5,7},{6,4},{7,5},{8,10},{9,11},{10,... | collective-permute-start | bytes 737288 | tf_op jit(solution)/shard_map/ppermute | solution.py:155
  72.2 30.0 %collective-permute-start.8 = (bf16[32,3840]{1,0:T(8,128)(2,1)S(1)}, bf16[32,3840]{1,0:T(8,128)(2,1)S(1)}, u32[]{:S(2)}, u32[]{:S(2)}) collective-permute-start(bf16[32,3840]{1,0:T(8,128)(2,1)S(1)} %shard_map.49.refs_0_), channel_id=1, source_target_pairs={{0,2},{1,3},{2,0},{3,1},{4,6},{5,7},{6,4},{7,5},{8,10},{9,11},{10,... | collective-permute-start | bytes 737288 | tf_op jit(solution)/shard_map/ppermute | solution.py:155
  76.2 30.2 %collective-permute-start.6 = (bf16[32,3840]{1,0:T(8,128)(2,1)S(1)}, bf16[32,3840]{1,0:T(8,128)(2,1)S(1)}, u32[]{:S(2)}, u32[]{:S(2)}) collective-permute-start(bf16[32,3840]{1,0:T(8,128)(2,1)S(1)} %shard_map.49.refs_0_), channel_id=1, source_target_pairs={{0,4},{1,5},{2,6},{3,7},{4,8},{5,9},{6,10},{7,11},{8,12},{9,13},{1... | collective-permute-start | bytes 737288 | tf_op jit(solution)/shard_map/ppermute | solution.py:155
  81.3 28.5 %collective-permute-start.5 = (bf16[32,3840]{1,0:T(8,128)(2,1)S(1)}, bf16[32,3840]{1,0:T(8,128)(2,1)S(1)}, u32[]{:S(2)}, u32[]{:S(2)}) collective-permute-start(bf16[32,3840]{1,0:T(8,128)(2,1)S(1)} %shard_map.49.refs_0_), channel_id=1, source_target_pairs={{0,12},{1,13},{2,14},{3,15},{4,0},{5,1},{6,2},{7,3},{8,4},{9,5},{1... | collective-permute-start | bytes 737288 | tf_op jit(solution)/shard_map/ppermute | solution.py:155
  87.2 25.0 %collective-permute-start.26 = (f32[32,1024]{1,0:T(8,128)S(1)}, f32[32,1024]{1,0:T(8,128)S(1)}, u32[]{:S(2)}, u32[]{:S(2)}) collective-permute-start(f32[32,1024]{1,0:T(8,128)S(1)} %slice_bitcast_fusion), channel_id=1, source_target_pairs={{0,32},{1,481},{2,34},{3,483},{4,36},{5,485},{6,38},{7,487},{8,40}... | collective-permute-start | bytes 393224 | tf_op jit(solution)/shard_map/ppermute | solution.py:165
  99.0 22.8 %collective-permute-start.7 = (bf16[32,3840]{1,0:T(8,128)(2,1)S(1)}, bf16[32,3840]{1,0:T(8,128)(2,1)S(1)}, u32[]{:S(2)}, u32[]{:S(2)}) collective-permute-start(bf16[32,3840]{1,0:T(8,128)(2,1)S(1)} %shard_map.49.refs_0_), channel_id=1, source_target_pairs={{0,8},{1,9},{2,10},{3,11},{4,12},{5,13},{6,14},{7,15},{8,0},{9,1},... | collective-permute-start | bytes 737288 | tf_op jit(solution)/shard_map/ppermute | solution.py:155
  102.3 19.5 %collective-permute-start.9 = (bf16[32,3840]{1,0:T(8,128)(2,1)S(1)}, bf16[32,3840]{1,0:T(8,128)(2,1)S(1)}, u32[]{:S(2)}, u32[]{:S(2)}) collective-permute-start(bf16[32,3840]{1,0:T(8,128)(2,1)S(1)} %collective-permute-done.8.refs_4_), channel_id=1, source_target_pairs={{0,8},{1,9},{2,10},{3,11},{4,12},{5,13},{6,14},{7,15},{8,0},{9,1},... | collective-permute-start | bytes 737288 | tf_op jit(solution)/shard_map/ppermute | solution.py:155
  106.3 15.4 %collective-permute-start.11 = (bf16[32,3840]{1,0:T(8,128)(2,1)S(1)}, bf16[32,3840]{1,0:T(8,128)(2,1)S(1)}, u32[]{:S(2)}, u32[]{:S(2)}) collective-permute-start(bf16[32,3840]{1,0:T(8,128)(2,1)S(1)} %collective-permute-done.6.refs_2_), channel_id=1, source_target_pairs={{0,2},{1,3},{2,0},{3,1},{4,6},{5,7},{6,4},{7,5},{8,10},{9,11},{10,... | collective-permute-start | bytes 737288 | tf_op jit(solution)/shard_map/ppermute | solution.py:155
  109.9 11.9 %collective-permute-start.10 = (bf16[32,3840]{1,0:T(8,128)(2,1)S(1)}, bf16[32,3840]{1,0:T(8,128)(2,1)S(1)}, u32[]{:S(2)}, u32[]{:S(2)}) collective-permute-start(bf16[32,3840]{1,0:T(8,128)(2,1)S(1)} %collective-permute-done.5.refs_1_), channel_id=1, source_target_pairs={{0,2},{1,3},{2,0},{3,1},{4,6},{5,7},{6,4},{7,5},{8,10},{9,11},{10,... | collective-permute-start | bytes 737288 | tf_op jit(solution)/shard_map/ppermute | solution.py:155
  112.3 18.6 %collective-permute-start.27 = (f32[32,1024]{1,0:T(8,128)S(1)}, f32[32,1024]{1,0:T(8,128)S(1)}, u32[]{:S(2)}, u32[]{:S(2)}) collective-permute-start(f32[32,1024]{1,0:T(8,128)S(1)} %fusion), channel_id=1, source_target_pairs={{0,480},{1,33},{2,482},{3,35},{4,484},{5,37},{6,486},{7,39},{8,488... | collective-permute-start | bytes 393224 | tf_op jit(solution)/shard_map/ppermute | solution.py:165
  129.0 7.2 %collective-permute-start.12 = (f32[32,1024]{1,0:T(8,128)S(1)}, f32[32,1024]{1,0:T(8,128)S(1)}, u32[]{:S(2)}, u32[]{:S(2)}) collective-permute-start(f32[32,1024]{1,0:T(8,128)S(1)} %slice_bitcast_fusion.8), channel_id=1, source_target_pairs={{0,32},{1,481},{2,34},{3,483},{4,36},{5,485},{6,38},{7,487},{8,40}... | collective-permute-start | bytes 393224 | tf_op jit(solution)/shard_map/ppermute | solution.py:165
  130.9 10.8 %collective-permute-start.28 = (f32[32,1024]{1,0:T(8,128)S(1)}, f32[32,1024]{1,0:T(8,128)S(1)}, u32[]{:S(2)}, u32[]{:S(2)}) collective-permute-start(f32[32,1024]{1,0:T(8,128)S(1)} %fusion.1), channel_id=1, source_target_pairs={{0,32},{1,481},{2,34},{3,483},{4,36},{5,485},{6,38},{7,487},{8,40}... | collective-permute-start | bytes 393224 | tf_op jit(solution)/shard_map/ppermute | solution.py:165
  136.1 10.1 %collective-permute-start.13 = (f32[32,1024]{1,0:T(8,128)S(1)}, f32[32,1024]{1,0:T(8,128)S(1)}, u32[]{:S(2)}, u32[]{:S(2)}) collective-permute-start(f32[32,1024]{1,0:T(8,128)S(1)} %fusion.7), channel_id=1, source_target_pairs={{0,480},{1,33},{2,482},{3,35},{4,484},{5,37},{6,486},{7,39},{8,488... | collective-permute-start | bytes 393224 | tf_op jit(solution)/shard_map/ppermute | solution.py:165
  141.8 8.1 %collective-permute-start.29 = (f32[32,1024]{1,0:T(8,128)S(1)}, f32[32,1024]{1,0:T(8,128)S(1)}, u32[]{:S(2)}, u32[]{:S(2)}) collective-permute-start(f32[32,1024]{1,0:T(8,128)S(1)} %fusion.2), channel_id=1, source_target_pairs={{0,480},{1,33},{2,482},{3,35},{4,484},{5,37},{6,486},{7,39},{8,488... | collective-permute-start | bytes 393224 | tf_op jit(solution)/shard_map/ppermute | solution.py:165
  146.2 7.8 %collective-permute-start.14 = (f32[32,1024]{1,0:T(8,128)S(1)}, f32[32,1024]{1,0:T(8,128)S(1)}, u32[]{:S(2)}, u32[]{:S(2)}) collective-permute-start(f32[32,1024]{1,0:T(8,128)S(1)} %fusion.8), channel_id=1, source_target_pairs={{0,32},{1,481},{2,34},{3,483},{4,36},{5,485},{6,38},{7,487},{8,40}... | collective-permute-start | bytes 393224 | tf_op jit(solution)/shard_map/ppermute | solution.py:165
  154.0 9.1 %collective-permute-start.15 = (f32[32,1024]{1,0:T(8,128)S(1)}, f32[32,1024]{1,0:T(8,128)S(1)}, u32[]{:S(2)}, u32[]{:S(2)}) collective-permute-start(f32[32,1024]{1,0:T(8,128)S(1)} %fusion.9), channel_id=1, source_target_pairs={{0,480},{1,33},{2,482},{3,35},{4,484},{5,37},{6,486},{7,39},{8,488... | collective-permute-start | bytes 393224 | tf_op jit(solution)/shard_map/ppermute | solution.py:165
  156.8 9.9 %collective-permute-start.31 = (f32[32,1024]{1,0:T(8,128)S(1)}, f32[32,1024]{1,0:T(8,128)S(1)}, u32[]{:S(2)}, u32[]{:S(2)}) collective-permute-start(f32[32,1024]{1,0:T(8,128)S(1)} %fusion.4), channel_id=1, source_target_pairs={{0,480},{1,33},{2,482},{3,35},{4,484},{5,37},{6,486},{7,39},{8,488... | collective-permute-start | bytes 393224 | tf_op jit(solution)/shard_map/ppermute | solution.py:165
  170.2 8.1 %collective-permute-start.17 = (f32[32,1024]{1,0:T(8,128)S(1)}, f32[32,1024]{1,0:T(8,128)S(1)}, u32[]{:S(2)}, u32[]{:S(2)}) collective-permute-start(f32[32,1024]{1,0:T(8,128)S(1)} %fusion.11), channel_id=1, source_target_pairs={{0,480},{1,33},{2,482},{3,35},{4,484},{5,37},{6,486},{7,39},{8,488... | collective-permute-start | bytes 393224 | tf_op jit(solution)/shard_map/ppermute | solution.py:165
  178.3 7.9 %collective-permute-start.18 = (f32[32,1024]{1,0:T(8,128)S(1)}, f32[32,1024]{1,0:T(8,128)S(1)}, u32[]{:S(2)}, u32[]{:S(2)}) collective-permute-start(f32[32,1024]{1,0:T(8,128)S(1)} %fusion.12), channel_id=1, source_target_pairs={{0,32},{1,481},{2,34},{3,483},{4,36},{5,485},{6,38},{7,487},{8,40}... | collective-permute-start | bytes 393224 | tf_op jit(solution)/shard_map/ppermute | solution.py:165
  180.2 9.9 %collective-permute-start.33 = (f32[32,512]{1,0:T(8,128)S(1)}, f32[32,512]{1,0:T(8,128)S(1)}, u32[]{:S(2)}, u32[]{:S(2)}) collective-permute-start(f32[32,512]{1,0:T(8,128)S(1)} %get-tuple-element.26), channel_id=1, source_target_pairs={{1,32},{3,34},{5,36},{7,38},{9,40},{11,42},{13,44},{15,46},{17,48}... | collective-permute-start | bytes 196616 | tf_op jit(solution)/shard_map/ppermute | solution.py:165
  180.9 9.2 %collective-permute-start.34 = (f32[32,512]{1,0:T(8,128)S(1)}, f32[32,512]{1,0:T(8,128)S(1)}, u32[]{:S(2)}, u32[]{:S(2)}) collective-permute-start(f32[32,512]{1,0:T(8,128)S(1)} %get-tuple-element.27), channel_id=1, source_target_pairs={{0,1},{1,33},{2,3},{3,35},{4,5},{5,37},{6,7},{7,39},{8,9},{9,41},{... | collective-permute-start | bytes 196616 | tf_op jit(solution)/shard_map/ppermute | solution.py:165
  186.9 8.2 %collective-permute-start.20 = (f32[32,512]{1,0:T(8,128)S(1)}, f32[32,512]{1,0:T(8,128)S(1)}, u32[]{:S(2)}, u32[]{:S(2)}) collective-permute-start(f32[32,512]{1,0:T(8,128)S(1)} %get-tuple-element.29), channel_id=1, source_target_pairs={{0,1},{1,33},{2,3},{3,35},{4,5},{5,37},{6,7},{7,39},{8,9},{9,41},{... | collective-permute-start | bytes 196616 | tf_op jit(solution)/shard_map/ppermute | solution.py:165
  195.2 7.7 %collective-permute-start.35 = (f32[32,512]{1,0:T(8,128)S(1)}, f32[32,512]{1,0:T(8,128)S(1)}, u32[]{:S(2)}, u32[]{:S(2)}) collective-permute-start(f32[32,512]{1,0:T(8,128)S(1)} %get-tuple-element.23), channel_id=1, source_target_pairs={{0,16},{16,0},{32,48},{48,32},{64,80},{80,64},{96,112},{112,96},{1... | collective-permute-start | bytes 196616 | tf_op jit(solution)/shard_map/ppermute | solution.py:250
  (8 other events, 86.9 us)

commit v3 on v2

--- a/solution.py
+++ b/solution.py
@@ -10,7 +10,7 @@
 LANES = 128
 UNROLL = 32
 K_TILE = 768
-CHUNKS = 2
+CHUNKS = 1
 PLACES = ((0, 0), (1, 0), (3, 0), (2, 0), (0, 1), (2, 1), (1, 1), (3, 1))
 
 
@@ -111,7 +111,7 @@
     pieces, s_ref, out_ref, total = refs[:-3], refs[-3], refs[-2], refs[-1]
     z, c = lax.axis_index("grp") // 2, lax.axis_index("col")
     step = pl.program_id(0)
-    rows = pieces[0].shape[0]
+    rows = out_ref.shape[1]
     lhs = jnp.concatenate([ref[...] for ref in pieces], axis=0)
     term = jnp.dot(lhs, s_ref[...], preferred_element_type=jnp.float32)
 
@@ -125,24 +125,24 @@
 
     @pl.when(step == pl.num_programs(0) - 1)
     def _():
-        for i in range(len(pieces)):
-            slot = slot_of(z, c // 4, c // 2 % 2, c % 2, *PLACES[i])
+        for i, place in enumerate(PLACES):
+            slot = slot_of(z, c // 4, c // 2 % 2, c % 2, *place)
             out_ref[slot] = total[i * rows : (i + 1) * rows, :]
 
 
-def product(pieces, s_both):
+def product(pieces, s_both, half):
     rows, blk = pieces[0].shape
-    cols = s_both.shape[1]
-    count = len(pieces)
+    cols = s_both.shape[1] // 2
+    block_rows = rows * len(pieces) // len(PLACES)
     return pl.pallas_call(
         product_kernel,
         grid=(blk // K_TILE,),
-        out_shape=jax.ShapeDtypeStruct((count, rows, cols), jnp.float32),
-        in_specs=[pl.BlockSpec((rows, K_TILE), lambda i: (0, i))] * count
-        + [pl.BlockSpec((K_TILE, cols), lambda i: (i, 0))],
-        out_specs=pl.BlockSpec((count, rows, cols), lambda i: (0, 0, 0)),
-        scratch_shapes=[pltpu.VMEM((count * rows, cols), jnp.float32)],
-        compiler_params=pltpu.CompilerParams(vmem_limit_bytes=16 * 2**20),
+        out_shape=jax.ShapeDtypeStruct((len(PLACES), block_rows, cols), jnp.float32),
+        in_specs=[pl.BlockSpec((rows, K_TILE), lambda i: (0, i))] * len(pieces)
+        + [pl.BlockSpec((K_TILE, cols), lambda i: (i, half))],
+        out_specs=pl.BlockSpec((len(PLACES), block_rows, cols), lambda i: (0, 0, 0)),
+        scratch_shapes=[pltpu.VMEM((len(PLACES) * block_rows, cols), jnp.float32)],
+        compiler_params=pltpu.CompilerParams(vmem_limit_bytes=12 * 2**20),
     )(*pieces, s_both)
 
 
@@ -202,21 +202,12 @@
     return pieces
 
 
-def last(z, y_hi, c):
-    return (z + 1, y_hi, c) if (c - z) % 2 else (z, y_hi, c ^ 1)
-
-
-def last_other(z, y_hi, c):
-    return (z + 1, y_hi, c ^ 1) if (c - z) % 2 else None
-
-
 def per_device(window_rows, secular, source, kept_count):
     blk = secular.shape[0]
     g = lax.axis_index("grp")
     c = lax.axis_index("col")
     z, y_hi = g // 2, g % 2
     is_odd = (c + z) % 2 == 1
-    is_high = y_hi == 1
     own_base = g * blk
     partner_base = jnp.bitwise_xor(g, 16) * blk
 
@@ -227,29 +218,47 @@
     own_parts, cross_parts = parts[:CHUNKS], parts[CHUNKS:]
     s_both, masked = split_halves(kept_count, flag, secular, other)
 
-    sums = []
+    pieces = []
     leaving, after = cross_parts[0], masked
     for h in range(CHUNKS):
         arrived = lax.ppermute(leaving, "grp", [(i, i ^ 16) for i in range(32)])
         here, *next_leaving = combine(own_parts[h], arrived, cross_parts[h + 1] if h + 1 < CHUNKS else None, after)
         if next_leaving:
             leaving = next_leaving[0]
-        pieces = gather_col(here)
-        terms = product([pieces[p] for p in PLACES], s_both)
-        after = pieces[3, 1]
-        moving = terms[0]
-        for step in range(1, 8):
-            moving = terms[step] + slice_move(moving, functools.partial(exchange, step))
-        half_cols = moving.shape[1] // 2
-        mine, theirs = moving[:, :half_cols], moving[:, half_cols:]
-        first_in = slice_move(jnp.where(is_odd, mine, theirs), last)
-        second_in = slice_move(theirs, last_other)
-        sums.append(jnp.where(is_odd, second_in, mine) + first_in)
-
-    low, high = sums
-    across = lax.ppermute(jnp.where(is_high, low, high), "grp", [(i, i ^ 1) for i in range(32)])
-    final = (jnp.where(is_high, high, low) + across).astype(jnp.bfloat16)
-    return final.reshape(final.shape[0], 2, -1).transpose(1, 0, 2)
+        gathered = gather_col(here)
+        pieces.append(gathered)
+        after = gathered[3, 1]
+    pieces = [gathered[p] for p in PLACES for gathered in pieces]
+
+    s_both = pltpu.with_memory_space_constraint(s_both, pltpu.HBM)
+    terms = [product(pieces, s_both, half) for half in range(2)]
+    moving = [term[0] for term in terms]
+    for step in range(1, 8):
+        for half in range(2):
+            moving[half] = terms[half][step] + slice_move(moving[half], functools.partial(exchange, step))
+
+    mine, theirs = moving
+    rows = mine.shape[0] // 2
+
+    def part(value, y):
+        return jnp.where(y == 1, value[rows:], value[:rows])
+
+    def odd_or_even(when_odd, when_even):
+        def target(z, y_hi, c):
+            is_odd = (c - z) % 2
+            flips = when_odd if is_odd else when_even
+            return None if flips is None else (z + is_odd, y_hi ^ flips[0], c ^ flips[1])
+
+        return target
+
+    mine_here, mine_across = part(mine, y_hi), part(mine, 1 - y_hi)
+    theirs_here, theirs_across = part(theirs, y_hi), part(theirs, 1 - y_hi)
+    total = slice_move(theirs_across, odd_or_even((1, 1), None))
+    total += slice_move(jnp.where(is_odd, mine_here, theirs_here), odd_or_even((0, 0), (0, 1)))
+    total += slice_move(jnp.where(is_odd, mine_across, theirs_across), odd_or_even((1, 0), (1, 1)))
+    total += slice_move(jnp.where(is_odd, theirs_here, mine_across), odd_or_even((0, 1), (1, 0)))
+    final = jnp.where(is_odd, total, total + mine_here).astype(jnp.bfloat16)
+    return final.reshape(rows, 2, -1).transpose(1, 0, 2)
 
 
 def solution(mesh):

time: 207 us -> 218 us (1.053)
  waiting for transfers between devices: 24.4 us -> 53.3 us
  starting transfers between devices: 153 us -> 132 us
  Pallas kernels: 17.1 us -> 21.3 us
    ppermute x15 -> x8, waiting for transfers between devices: 0.04 us -> 29.7 us  [col_move(): return lax.ppermute(value, 'col', pairs)]
    ppermute x15 -> x8, starting transfers between devices: 53.6 us -> 33.5 us  [col_move(): return lax.ppermute(value, 'col', pairs)]
    ppermute x18, starting transfers between devices: 69.4 us -> 82.8 us  [slice_move(): return lax.ppermute(value, ('grp', 'col'), pairs)]
    ppermute x2 -> x1, starting transfers between devices: 28.2 us -> 15.7 us  [per_device(): arrived = lax.ppermute(leaving, 'grp', [(i, i ^ 16) for i in range(32)])]
    ppermute x2 -> x1, waiting for transfers between devices: 1.22 us -> 7.67 us  [per_device(): arrived = lax.ppermute(leaving, 'grp', [(i, i ^ 16) for i in range(32)])]
    ppermute x1 -> x0, waiting for transfers between devices: 5.74 us -> none  [per_device(): lax.ppermute(jnp.where(is_high, low, high), 'grp', [(i, i ^ 1) for i in r...]
    pallas_call x2, Pallas kernels: 7.81 us -> 12 us  [product(): pl.pallas_call(product_kernel, grid=(blk // K_TILE,), out_shape=jax.Shape...]
    unnamed x8 -> x6, local copies, waits for them, and re-layouts: 5.8 us -> 5.62 us
  transfers between devices with their start and end apart: 36 -> 27, of which waited for: 9 -> 15; matrix products, arithmetic and copies ran while one was open for 0% -> 0% of each run, Pallas kernels for 8% -> 7%
where the time goes in v3:
time: 218 us; the launch traced here: 215 us
  starting transfers between devices  132 us (61%)
  waiting for transfers between devices  53.3 us (24%)
  Pallas kernels  21.3 us (10%)
  local copies, waits for them, and re-layouts  6.26 us (3%)
    ppermute x18, starting transfers between devices, slice_move(): return lax.ppermute(value, ('grp', 'col'), pairs)  82.8 us
    ppermute x8, starting transfers between devices, col_move(): return lax.ppermute(value, 'col', pairs)  33.5 us
    ppermute x8, waiting for transfers between devices, col_move(): return lax.ppermute(value, 'col', pairs)  29.7 us
    ppermute x18, waiting for transfers between devices, slice_move(): return lax.ppermute(value, ('grp', 'col'), pairs)  15.9 us
    ppermute x1, starting transfers between devices, per_device(): arrived = lax.ppermute(leaving, 'grp', [(i, i ^ 16) for i in range(32)])  15.7 us
    pallas_call x2, Pallas kernels, product(): pl.pallas_call(product_kernel, grid=(blk // K_TILE,), out_shape=jax.Shape...  12 us
    ppermute x1, waiting for transfers between devices, per_device(): arrived = lax.ppermute(leaving, 'grp', [(i, i ^ 16) for i in range(32)])  7.67 us
    pallas_call x1, Pallas kernels, scatter_rows(): pl.pallas_call(scatter_kernel, out_shape=[jax.ShapeDtypeStruct((width //...  5.76 us
  transfers between devices with their start and end apart: 27, of which 15 were waited for; matrix products, arithmetic and copies ran while one was open for 0% of the time, Pallas kernels for 7%

profile of v3, /device:TPU:6, one launch (start us, length us, event | category | flops | bytes accessed | tf_op | source)
XLA Modules:
  0.0 215.1 jit_solution(7194090753287655345)
XLA Ops:
  3.7 5.8 %shard_map.46 = (bf16[64,3840]{1,0:T(8,128)(2,1)S(1)}, bf16[64,3840]{1,0:T(8,128)(2,1)S(1)}, bf16[3840,128]{1,0:T(8,128)(2,1)S(1)}) custom-call(s32[3840]{0:T(1024)S(1)} %subtract_select_fusion.place_ref, bf16[64,3840]{1,0:T(8,128)(2,1)S(1)} %bitcast.68), custom_call_target="tpu_custom_call" | custom-call | tf_op jit(solution)/shard_map/pallas_call | solution.py:47
  9.4 15.7 %collective-permute-start = (bf16[64,3840]{1,0:T(8,128)(2,1)S(1)}, bf16[64,3840]{1,0:T(8,128)(2,1)S(1)}, u32[]{:S(2)}, u32[]{:S(2)}) collective-permute-start(bf16[64,3840]{1,0:T(8,128)(2,1)S(1)} %get-tuple-element.11), channel_id=1, source_target_pairs={{0,256},{16,272},{32,288},{48,304},{64,320},{80,336},{96,352},{112... | collective-permute-start | bytes 1474568 | tf_op jit(solution)/shard_map/ppermute | solution.py:224
  27.4 3.5 %shard_map.47 = (bf16[3840,1024]{1,0:T(8,128)(2,1)S(1)}, f32[8,128]{1,0:T(8,128)S(1)}) custom-call(s32[1]{0:T(128)S(6)} %copy.9.kept_ref, bf16[3840,128]{1,0:T(8,128)(2,1)S(1)} %get-tuple-element.12.flag_ref, bf16[3840,256]{1,0:T(8,128)(2,1)S(1)} %copy-done.1, bf16[3840,256]{1,0:T(8,128)(2,1)S(1)} %collective-permute-done.1.other_ref), custom_call_target="tpu_custom_call" | custom-call | tf_op jit(solution)/shard_map/pallas_call | solution.py:83
  30.9 3.1 %copy-done = bf16[3840,1024]{1,0:T(8,128)(2,1)} copy-done((bf16[3840,1024]{1,0:T(8,128)(2,1)}, bf16[3840,1024]{1,0:T(8,128)(2,1)S(1)}, u32[]{:S(2)}) %copy-start) | copy-done | bytes 7864344
  33.9 7.7 %collective-permute-done.refs_1_ = bf16[64,3840]{1,0:T(8,128)(2,1)S(1)} collective-permute-done((bf16[64,3840]{1,0:T(8,128)(2,1)S(1)}, bf16[64,3840]{1,0:T(8,128)(2,1)S(1)}, u32[]{:S(2)}, u32[]{:S(2)}) %collective-permute-start) | collective-permute-done | bytes 491552 | tf_op jit(solution)/shard_map/ppermute | solution.py:224
  41.6 3.5 %collective-permute-start.5 = (bf16[64,3840]{1,0:T(8,128)(2,1)S(1)}, bf16[64,3840]{1,0:T(8,128)(2,1)S(1)}, u32[]{:S(2)}, u32[]{:S(2)}) collective-permute-start(bf16[64,3840]{1,0:T(8,128)(2,1)S(1)} %shard_map.48.refs_0_), channel_id=1, source_target_pairs={{0,2},{1,3},{2,0},{3,1},{4,6},{5,7},{6,4},{7,5},{8,10},{9,11},{10,... | collective-permute-start | bytes 1474568 | tf_op jit(solution)/shard_map/ppermute | solution.py:155
  45.1 2.7 %collective-permute-start.2 = (bf16[64,3840]{1,0:T(8,128)(2,1)S(1)}, bf16[64,3840]{1,0:T(8,128)(2,1)S(1)}, u32[]{:S(2)}, u32[]{:S(2)}) collective-permute-start(bf16[64,3840]{1,0:T(8,128)(2,1)S(1)} %shard_map.48.refs_0_), channel_id=1, source_target_pairs={{0,12},{1,13},{2,14},{3,15},{4,0},{5,1},{6,2},{7,3},{8,4},{9,5},{1... | collective-permute-start | bytes 1474568 | tf_op jit(solution)/shard_map/ppermute | solution.py:155
  47.9 10.5 %collective-permute-start.3 = (bf16[64,3840]{1,0:T(8,128)(2,1)S(1)}, bf16[64,3840]{1,0:T(8,128)(2,1)S(1)}, u32[]{:S(2)}, u32[]{:S(2)}) collective-permute-start(bf16[64,3840]{1,0:T(8,128)(2,1)S(1)} %shard_map.48.refs_0_), channel_id=1, source_target_pairs={{0,4},{1,5},{2,6},{3,7},{4,8},{5,9},{6,10},{7,11},{8,12},{9,13},{1... | collective-permute-start | bytes 1474568 | tf_op jit(solution)/shard_map/ppermute | solution.py:155
  58.3 3.4 %collective-permute-start.4 = (bf16[64,3840]{1,0:T(8,128)(2,1)S(1)}, bf16[64,3840]{1,0:T(8,128)(2,1)S(1)}, u32[]{:S(2)}, u32[]{:S(2)}) collective-permute-start(bf16[64,3840]{1,0:T(8,128)(2,1)S(1)} %shard_map.48.refs_0_), channel_id=1, source_target_pairs={{0,8},{1,9},{2,10},{3,11},{4,12},{5,13},{6,14},{7,15},{8,0},{9,1},... | collective-permute-start | bytes 1474568 | tf_op jit(solution)/shard_map/ppermute | solution.py:155
  61.7 4.0 %collective-permute-start.6 = (bf16[64,3840]{1,0:T(8,128)(2,1)S(1)}, bf16[64,3840]{1,0:T(8,128)(2,1)S(1)}, u32[]{:S(2)}, u32[]{:S(2)}) collective-permute-start(bf16[64,3840]{1,0:T(8,128)(2,1)S(1)} %collective-permute-done.5.refs_4_), channel_id=1, source_target_pairs={{0,8},{1,9},{2,10},{3,11},{4,12},{5,13},{6,14},{7,15},{8,0},{9,1},... | collective-permute-start | bytes 1474568 | tf_op jit(solution)/shard_map/ppermute | solution.py:155
  67.6 3.9 %collective-permute-start.7 = (bf16[64,3840]{1,0:T(8,128)(2,1)S(1)}, bf16[64,3840]{1,0:T(8,128)(2,1)S(1)}, u32[]{:S(2)}, u32[]{:S(2)}) collective-permute-start(bf16[64,3840]{1,0:T(8,128)(2,1)S(1)} %collective-permute-done.2.refs_1_), channel_id=1, source_target_pairs={{0,2},{1,3},{2,0},{3,1},{4,6},{5,7},{6,4},{7,5},{8,10},{9,11},{10,... | collective-permute-start | bytes 1474568 | tf_op jit(solution)/shard_map/ppermute | solution.py:155
  71.6 17.9 %collective-permute-done.3.refs_2_ = bf16[64,3840]{1,0:T(8,128)(2,1)S(1)} collective-permute-done((bf16[64,3840]{1,0:T(8,128)(2,1)S(1)}, bf16[64,3840]{1,0:T(8,128)(2,1)S(1)}, u32[]{:S(2)}, u32[]{:S(2)}) %collective-permute-start.3) | collective-permute-done | bytes 491552 | tf_op jit(solution)/shard_map/ppermute | solution.py:155
  89.5 3.6 %collective-permute-start.8 = (bf16[64,3840]{1,0:T(8,128)(2,1)S(1)}, bf16[64,3840]{1,0:T(8,128)(2,1)}, u32[]{:S(2)}, u32[]{:S(2)}) collective-permute-start(bf16[64,3840]{1,0:T(8,128)(2,1)S(1)} %collective-permute-done.3.refs_2_), channel_id=1, source_target_pairs={{0,2},{1,3},{2,0},{3,1},{4,6},{5,7},{6,4},{7,5},{8,10},{9,11},{10,... | collective-permute-start | bytes 1474568 | tf_op jit(solution)/shard_map/ppermute | solution.py:155
  93.2 9.9 %collective-permute-done.8.refs_7_ = bf16[64,3840]{1,0:T(8,128)(2,1)} collective-permute-done((bf16[64,3840]{1,0:T(8,128)(2,1)S(1)}, bf16[64,3840]{1,0:T(8,128)(2,1)}, u32[]{:S(2)}, u32[]{:S(2)}) %collective-permute-start.8) | collective-permute-done | bytes 491552 | tf_op jit(solution)/shard_map/ppermute | solution.py:155
  103.1 6.0 %shard_map.49 = f32[8,64,512]{2,1,0:T(8,128)S(1)} custom-call(bf16[64,3840]{1,0:T(8,128)(2,1)S(1)} %shard_map.48.refs_0_, bf16[64,3840]{1,0:T(8,128)(2,1)S(1)} %collective-permute-done.2.refs_1_, bf16[64,3840]{1,0:T(8,128)(2,1)S(1)} %collective-permute-done.3.refs_2_, bf16[64,3840]{1,0:T(8,128)(2,1)S(1)} %collective-permute-done.4.refs_3_, ...), custom_call_target="tpu_custom_call" | custom-call | tf_op jit(solution)/shard_map/pallas_call | solution.py:137
  109.1 25.2 %collective-permute-start.9 = (f32[64,512]{1,0:T(8,128)S(1)}, f32[64,512]{1,0:T(8,128)S(1)}, u32[]{:S(2)}, u32[]{:S(2)}) collective-permute-start(f32[64,512]{1,0:T(8,128)S(1)} %slice_bitcast_fusion.8), channel_id=1, source_target_pairs={{0,32},{1,481},{2,34},{3,483},{4,36},{5,485},{6,38},{7,487},{8,40}... | collective-permute-start | bytes 393224 | tf_op jit(solution)/shard_map/ppermute | solution.py:165
  134.3 6.0 %shard_map.50 = f32[8,64,512]{2,1,0:T(8,128)S(1)} custom-call(bf16[64,3840]{1,0:T(8,128)(2,1)S(1)} %shard_map.48.refs_0_, bf16[64,3840]{1,0:T(8,128)(2,1)S(1)} %collective-permute-done.2.refs_1_, bf16[64,3840]{1,0:T(8,128)(2,1)S(1)} %collective-permute-done.3.refs_2_, bf16[64,3840]{1,0:T(8,128)(2,1)S(1)} %collective-permute-done.4.refs_3_, ...), custom_call_target="tpu_custom_call" | custom-call | tf_op jit(solution)/shard_map/pallas_call | solution.py:137
  142.3 7.7 %collective-permute-start.10 = (f32[64,512]{1,0:T(8,128)S(1)}, f32[64,512]{1,0:T(8,128)S(1)}, u32[]{:S(2)}, u32[]{:S(2)}) collective-permute-start(f32[64,512]{1,0:T(8,128)S(1)} %fusion.7), channel_id=1, source_target_pairs={{0,480},{1,33},{2,482},{3,35},{4,484},{5,37},{6,486},{7,39},{8,488... | collective-permute-start | bytes 393224 | tf_op jit(solution)/shard_map/ppermute | solution.py:165
  150.0 4.9 %collective-permute-start.18 = (f32[64,512]{1,0:T(8,128)S(1)}, f32[64,512]{1,0:T(8,128)S(1)}, u32[]{:S(2)}, u32[]{:S(2)}) collective-permute-start(f32[64,512]{1,0:T(8,128)S(1)} %fusion), channel_id=1, source_target_pairs={{0,480},{1,33},{2,482},{3,35},{4,484},{5,37},{6,486},{7,39},{8,488... | collective-permute-start | bytes 393224 | tf_op jit(solution)/shard_map/ppermute | solution.py:165
  158.1 2.7 %collective-permute-start.19 = (f32[64,512]{1,0:T(8,128)S(1)}, f32[64,512]{1,0:T(8,128)S(1)}, u32[]{:S(2)}, u32[]{:S(2)}) collective-permute-start(f32[64,512]{1,0:T(8,128)S(1)} %fusion.1), channel_id=1, source_target_pairs={{0,32},{1,481},{2,34},{3,483},{4,36},{5,485},{6,38},{7,487},{8,40}... | collective-permute-start | bytes 393224 | tf_op jit(solution)/shard_map/ppermute | solution.py:165
  160.8 2.3 %collective-permute-done.11 = f32[64,512]{1,0:T(8,128)S(1)} collective-permute-done((f32[64,512]{1,0:T(8,128)S(1)}, f32[64,512]{1,0:T(8,128)S(1)}, u32[]{:S(2)}, u32[]{:S(2)}) %collective-permute-start.11) | collective-permute-done | bytes 131104 | tf_op jit(solution)/shard_map/ppermute | solution.py:165
  163.1 2.7 %collective-permute-start.12 = (f32[64,512]{1,0:T(8,128)S(1)}, f32[64,512]{1,0:T(8,128)S(1)}, u32[]{:S(2)}, u32[]{:S(2)}) collective-permute-start(f32[64,512]{1,0:T(8,128)S(1)} %fusion.9), channel_id=1, source_target_pairs={{0,480},{1,33},{2,482},{3,35},{4,484},{5,37},{6,486},{7,39},{8,488... | collective-permute-start | bytes 393224 | tf_op jit(solution)/shard_map/ppermute | solution.py:165
  165.9 4.4 %collective-permute-start.20 = (f32[64,512]{1,0:T(8,128)S(1)}, f32[64,512]{1,0:T(8,128)S(1)}, u32[]{:S(2)}, u32[]{:S(2)}) collective-permute-start(f32[64,512]{1,0:T(8,128)S(1)} %fusion.2), channel_id=1, source_target_pairs={{0,480},{1,33},{2,482},{3,35},{4,484},{5,37},{6,486},{7,39},{8,488... | collective-permute-start | bytes 393224 | tf_op jit(solution)/shard_map/ppermute | solution.py:165
  174.0 3.7 %collective-permute-start.21 = (f32[64,512]{1,0:T(8,128)S(1)}, f32[64,512]{1,0:T(8,128)S(1)}, u32[]{:S(2)}, u32[]{:S(2)}) collective-permute-start(f32[64,512]{1,0:T(8,128)S(1)} %fusion.3), channel_id=1, source_target_pairs={{0,32},{1,481},{2,34},{3,483},{4,36},{5,485},{6,38},{7,487},{8,40}... | collective-permute-start | bytes 393224 | tf_op jit(solution)/shard_map/ppermute | solution.py:165
  178.7 3.1 %collective-permute-start.14 = (f32[64,512]{1,0:T(8,128)S(1)}, f32[64,512]{1,0:T(8,128)S(1)}, u32[]{:S(2)}, u32[]{:S(2)}) collective-permute-start(f32[64,512]{1,0:T(8,128)S(1)} %fusion.11), channel_id=1, source_target_pairs={{0,480},{1,33},{2,482},{3,35},{4,484},{5,37},{6,486},{7,39},{8,488... | collective-permute-start | bytes 393224 | tf_op jit(solution)/shard_map/ppermute | solution.py:165
  181.8 4.0 %collective-permute-start.22 = (f32[64,512]{1,0:T(8,128)S(1)}, f32[64,512]{1,0:T(8,128)S(1)}, u32[]{:S(2)}, u32[]{:S(2)}) collective-permute-start(f32[64,512]{1,0:T(8,128)S(1)} %fusion.4), channel_id=1, source_target_pairs={{0,480},{1,33},{2,482},{3,35},{4,484},{5,37},{6,486},{7,39},{8,488... | collective-permute-start | bytes 393224 | tf_op jit(solution)/shard_map/ppermute | solution.py:165
  189.9 2.8 %collective-permute-start.23 = (f32[64,512]{1,0:T(8,128)S(1)}, f32[64,512]{1,0:T(8,128)S(1)}, u32[]{:S(2)}, u32[]{:S(2)}) collective-permute-start(f32[64,512]{1,0:T(8,128)S(1)} %fusion.5), channel_id=1, source_target_pairs={{0,32},{1,481},{2,34},{3,483},{4,36},{5,485},{6,38},{7,487},{8,40}... | collective-permute-start | bytes 393224 | tf_op jit(solution)/shard_map/ppermute | solution.py:165
  193.7 3.1 %collective-permute-done.23 = f32[64,512]{1,0:T(8,128)S(1)} collective-permute-done((f32[64,512]{1,0:T(8,128)S(1)}, f32[64,512]{1,0:T(8,128)S(1)}, u32[]{:S(2)}, u32[]{:S(2)}) %collective-permute-start.23) | collective-permute-done | bytes 131104 | tf_op jit(solution)/shard_map/ppermute | solution.py:165
  197.5 6.5 %collective-permute-start.24 = (f32[32,512]{1,0:T(8,128)S(1)}, f32[32,512]{1,0:T(8,128)S(1)}, u32[]{:S(2)}, u32[]{:S(2)}) collective-permute-start(f32[32,512]{1,0:T(8,128)S(1)} %get-tuple-element.17), channel_id=1, source_target_pairs={{0,1},{1,33},{2,3},{3,35},{4,5},{5,37},{6,7},{7,39},{8,9},{9,41},{... | collective-permute-start | bytes 196616 | tf_op jit(solution)/shard_map/ppermute | solution.py:165
  204.0 2.1 collective-permute-start.25
  206.1 4.8 %collective-permute-start.26 = (f32[32,512]{1,0:T(8,128)S(1)}, f32[32,512]{1,0:T(8,128)S(1)}, u32[]{:S(2)}, u32[]{:S(2)}) collective-permute-start(f32[32,512]{1,0:T(8,128)S(1)} %get-tuple-element.18), channel_id=1, source_target_pairs={{0,16},{1,32},{2,18},{3,34},{4,20},{5,36},{6,22},{7,38},{8,24},{9,... | collective-permute-start | bytes 196616 | tf_op jit(solution)/shard_map/ppermute | solution.py:165
  211.0 2.8 %collective-permute-done.25 = f32[32,512]{1,0:T(8,128)S(1)} collective-permute-done((f32[32,512]{1,0:T(8,128)S(1)}, f32[32,512]{1,0:T(8,128)S(1)}, u32[]{:S(2)}, u32[]{:S(2)}) %collective-permute-start.25) | collective-permute-done | bytes 65568 | tf_op jit(solution)/shard_map/ppermute | solution.py:165
  (53 shorter events, 24.2 us)
Async XLA Ops:
  0.0 25.8 %collective-permute-start.1 = (bf16[3840,256]{1,0:T(8,128)(2,1)}, bf16[3840,256]{1,0:T(8,128)(2,1)S(1)}, u32[]{:S(2)}, u32[]{:S(2)}) collective-permute-start(bf16[3840,256]{1,0:T(8,128)(2,1)} %own_ref.1), channel_id=1, source_target_pairs={{0,1},{1,0},{2,3},{3,2},{4,5},{5,4},{6,7},{7,6},{8,9},{9,8},{10,11... | collective-permute-start | bytes 5898248 | tf_op jit(solution)/shard_map/ppermute | solution.py:155
  2.7 1.0 copy-start.2
  9.4 32.1 %collective-permute-start = (bf16[64,3840]{1,0:T(8,128)(2,1)S(1)}, bf16[64,3840]{1,0:T(8,128)(2,1)S(1)}, u32[]{:S(2)}, u32[]{:S(2)}) collective-permute-start(bf16[64,3840]{1,0:T(8,128)(2,1)S(1)} %get-tuple-element.11), channel_id=1, source_target_pairs={{0,256},{16,272},{32,288},{48,304},{64,320},{80,336},{96,352},{112... | collective-permute-start | bytes 1474568 | tf_op jit(solution)/shard_map/ppermute | solution.py:224
  25.8 1.5 copy-start.1
  30.9 3.1 %copy-start = (bf16[3840,1024]{1,0:T(8,128)(2,1)}, bf16[3840,1024]{1,0:T(8,128)(2,1)S(1)}, u32[]{:S(2)}) copy-start(bf16[3840,1024]{1,0:T(8,128)(2,1)S(1)} %get-tuple-element.14.refs_8_) | copy-start | bytes 23592964
  41.6 20.1 %collective-permute-start.5 = (bf16[64,3840]{1,0:T(8,128)(2,1)S(1)}, bf16[64,3840]{1,0:T(8,128)(2,1)S(1)}, u32[]{:S(2)}, u32[]{:S(2)}) collective-permute-start(bf16[64,3840]{1,0:T(8,128)(2,1)S(1)} %shard_map.48.refs_0_), channel_id=1, source_target_pairs={{0,2},{1,3},{2,0},{3,1},{4,6},{5,7},{6,4},{7,5},{8,10},{9,11},{10,... | collective-permute-start | bytes 1474568 | tf_op jit(solution)/shard_map/ppermute | solution.py:155
  45.1 22.5 %collective-permute-start.2 = (bf16[64,3840]{1,0:T(8,128)(2,1)S(1)}, bf16[64,3840]{1,0:T(8,128)(2,1)S(1)}, u32[]{:S(2)}, u32[]{:S(2)}) collective-permute-start(bf16[64,3840]{1,0:T(8,128)(2,1)S(1)} %shard_map.48.refs_0_), channel_id=1, source_target_pairs={{0,12},{1,13},{2,14},{3,15},{4,0},{5,1},{6,2},{7,3},{8,4},{9,5},{1... | collective-permute-start | bytes 1474568 | tf_op jit(solution)/shard_map/ppermute | solution.py:155
  47.9 41.6 %collective-permute-start.3 = (bf16[64,3840]{1,0:T(8,128)(2,1)S(1)}, bf16[64,3840]{1,0:T(8,128)(2,1)S(1)}, u32[]{:S(2)}, u32[]{:S(2)}) collective-permute-start(bf16[64,3840]{1,0:T(8,128)(2,1)S(1)} %shard_map.48.refs_0_), channel_id=1, source_target_pairs={{0,4},{1,5},{2,6},{3,7},{4,8},{5,9},{6,10},{7,11},{8,12},{9,13},{1... | collective-permute-start | bytes 1474568 | tf_op jit(solution)/shard_map/ppermute | solution.py:155
  58.3 34.8 %collective-permute-start.4 = (bf16[64,3840]{1,0:T(8,128)(2,1)S(1)}, bf16[64,3840]{1,0:T(8,128)(2,1)S(1)}, u32[]{:S(2)}, u32[]{:S(2)}) collective-permute-start(bf16[64,3840]{1,0:T(8,128)(2,1)S(1)} %shard_map.48.refs_0_), channel_id=1, source_target_pairs={{0,8},{1,9},{2,10},{3,11},{4,12},{5,13},{6,14},{7,15},{8,0},{9,1},... | collective-permute-start | bytes 1474568 | tf_op jit(solution)/shard_map/ppermute | solution.py:155
  61.7 31.4 %collective-permute-start.6 = (bf16[64,3840]{1,0:T(8,128)(2,1)S(1)}, bf16[64,3840]{1,0:T(8,128)(2,1)S(1)}, u32[]{:S(2)}, u32[]{:S(2)}) collective-permute-start(bf16[64,3840]{1,0:T(8,128)(2,1)S(1)} %collective-permute-done.5.refs_4_), channel_id=1, source_target_pairs={{0,8},{1,9},{2,10},{3,11},{4,12},{5,13},{6,14},{7,15},{8,0},{9,1},... | collective-permute-start | bytes 1474568 | tf_op jit(solution)/shard_map/ppermute | solution.py:155
  67.6 25.5 %collective-permute-start.7 = (bf16[64,3840]{1,0:T(8,128)(2,1)S(1)}, bf16[64,3840]{1,0:T(8,128)(2,1)S(1)}, u32[]{:S(2)}, u32[]{:S(2)}) collective-permute-start(bf16[64,3840]{1,0:T(8,128)(2,1)S(1)} %collective-permute-done.2.refs_1_), channel_id=1, source_target_pairs={{0,2},{1,3},{2,0},{3,1},{4,6},{5,7},{6,4},{7,5},{8,10},{9,11},{10,... | collective-permute-start | bytes 1474568 | tf_op jit(solution)/shard_map/ppermute | solution.py:155
  89.5 13.6 %collective-permute-start.8 = (bf16[64,3840]{1,0:T(8,128)(2,1)S(1)}, bf16[64,3840]{1,0:T(8,128)(2,1)}, u32[]{:S(2)}, u32[]{:S(2)}) collective-permute-start(bf16[64,3840]{1,0:T(8,128)(2,1)S(1)} %collective-permute-done.3.refs_2_), channel_id=1, source_target_pairs={{0,2},{1,3},{2,0},{3,1},{4,6},{5,7},{6,4},{7,5},{8,10},{9,11},{10,... | collective-permute-start | bytes 1474568 | tf_op jit(solution)/shard_map/ppermute | solution.py:155
  109.1 33.1 %collective-permute-start.9 = (f32[64,512]{1,0:T(8,128)S(1)}, f32[64,512]{1,0:T(8,128)S(1)}, u32[]{:S(2)}, u32[]{:S(2)}) collective-permute-start(f32[64,512]{1,0:T(8,128)S(1)} %slice_bitcast_fusion.8), channel_id=1, source_target_pairs={{0,32},{1,481},{2,34},{3,483},{4,36},{5,485},{6,38},{7,487},{8,40}... | collective-permute-start | bytes 393224 | tf_op jit(solution)/shard_map/ppermute | solution.py:165
  140.3 9.7 %collective-permute-start.17 = (f32[64,512]{1,0:T(8,128)S(1)}, f32[64,512]{1,0:T(8,128)S(1)}, u32[]{:S(2)}, u32[]{:S(2)}) collective-permute-start(f32[64,512]{1,0:T(8,128)S(1)} %slice_bitcast_fusion), channel_id=1, source_target_pairs={{0,32},{1,481},{2,34},{3,483},{4,36},{5,485},{6,38},{7,487},{8,40}... | collective-permute-start | bytes 393224 | tf_op jit(solution)/shard_map/ppermute | solution.py:165
  142.3 12.6 %collective-permute-start.10 = (f32[64,512]{1,0:T(8,128)S(1)}, f32[64,512]{1,0:T(8,128)S(1)}, u32[]{:S(2)}, u32[]{:S(2)}) collective-permute-start(f32[64,512]{1,0:T(8,128)S(1)} %fusion.7), channel_id=1, source_target_pairs={{0,480},{1,33},{2,482},{3,35},{4,484},{5,37},{6,486},{7,39},{8,488... | collective-permute-start | bytes 393224 | tf_op jit(solution)/shard_map/ppermute | solution.py:165
  150.0 8.1 %collective-permute-start.18 = (f32[64,512]{1,0:T(8,128)S(1)}, f32[64,512]{1,0:T(8,128)S(1)}, u32[]{:S(2)}, u32[]{:S(2)}) collective-permute-start(f32[64,512]{1,0:T(8,128)S(1)} %fusion), channel_id=1, source_target_pairs={{0,480},{1,33},{2,482},{3,35},{4,484},{5,37},{6,486},{7,39},{8,488... | collective-permute-start | bytes 393224 | tf_op jit(solution)/shard_map/ppermute | solution.py:165
  154.9 8.2 %collective-permute-start.11 = (f32[64,512]{1,0:T(8,128)S(1)}, f32[64,512]{1,0:T(8,128)S(1)}, u32[]{:S(2)}, u32[]{:S(2)}) collective-permute-start(f32[64,512]{1,0:T(8,128)S(1)} %fusion.8), channel_id=1, source_target_pairs={{0,32},{1,481},{2,34},{3,483},{4,36},{5,485},{6,38},{7,487},{8,40}... | collective-permute-start | bytes 393224 | tf_op jit(solution)/shard_map/ppermute | solution.py:165
  158.1 7.7 %collective-permute-start.19 = (f32[64,512]{1,0:T(8,128)S(1)}, f32[64,512]{1,0:T(8,128)S(1)}, u32[]{:S(2)}, u32[]{:S(2)}) collective-permute-start(f32[64,512]{1,0:T(8,128)S(1)} %fusion.1), channel_id=1, source_target_pairs={{0,32},{1,481},{2,34},{3,483},{4,36},{5,485},{6,38},{7,487},{8,40}... | collective-permute-start | bytes 393224 | tf_op jit(solution)/shard_map/ppermute | solution.py:165
  163.1 8.6 %collective-permute-start.12 = (f32[64,512]{1,0:T(8,128)S(1)}, f32[64,512]{1,0:T(8,128)S(1)}, u32[]{:S(2)}, u32[]{:S(2)}) collective-permute-start(f32[64,512]{1,0:T(8,128)S(1)} %fusion.9), channel_id=1, source_target_pairs={{0,480},{1,33},{2,482},{3,35},{4,484},{5,37},{6,486},{7,39},{8,488... | collective-permute-start | bytes 393224 | tf_op jit(solution)/shard_map/ppermute | solution.py:165
  165.9 8.1 %collective-permute-start.20 = (f32[64,512]{1,0:T(8,128)S(1)}, f32[64,512]{1,0:T(8,128)S(1)}, u32[]{:S(2)}, u32[]{:S(2)}) collective-permute-start(f32[64,512]{1,0:T(8,128)S(1)} %fusion.2), channel_id=1, source_target_pairs={{0,480},{1,33},{2,482},{3,35},{4,484},{5,37},{6,486},{7,39},{8,488... | collective-permute-start | bytes 393224 | tf_op jit(solution)/shard_map/ppermute | solution.py:165
  171.8 6.9 %collective-permute-start.13 = (f32[64,512]{1,0:T(8,128)S(1)}, f32[64,512]{1,0:T(8,128)S(1)}, u32[]{:S(2)}, u32[]{:S(2)}) collective-permute-start(f32[64,512]{1,0:T(8,128)S(1)} %fusion.10), channel_id=1, source_target_pairs={{0,32},{1,481},{2,34},{3,483},{4,36},{5,485},{6,38},{7,487},{8,40}... | collective-permute-start | bytes 393224 | tf_op jit(solution)/shard_map/ppermute | solution.py:165
  174.0 7.8 %collective-permute-start.21 = (f32[64,512]{1,0:T(8,128)S(1)}, f32[64,512]{1,0:T(8,128)S(1)}, u32[]{:S(2)}, u32[]{:S(2)}) collective-permute-start(f32[64,512]{1,0:T(8,128)S(1)} %fusion.3), channel_id=1, source_target_pairs={{0,32},{1,481},{2,34},{3,483},{4,36},{5,485},{6,38},{7,487},{8,40}... | collective-permute-start | bytes 393224 | tf_op jit(solution)/shard_map/ppermute | solution.py:165
  178.7 8.1 %collective-permute-start.14 = (f32[64,512]{1,0:T(8,128)S(1)}, f32[64,512]{1,0:T(8,128)S(1)}, u32[]{:S(2)}, u32[]{:S(2)}) collective-permute-start(f32[64,512]{1,0:T(8,128)S(1)} %fusion.11), channel_id=1, source_target_pairs={{0,480},{1,33},{2,482},{3,35},{4,484},{5,37},{6,486},{7,39},{8,488... | collective-permute-start | bytes 393224 | tf_op jit(solution)/shard_map/ppermute | solution.py:165
  181.8 8.1 %collective-permute-start.22 = (f32[64,512]{1,0:T(8,128)S(1)}, f32[64,512]{1,0:T(8,128)S(1)}, u32[]{:S(2)}, u32[]{:S(2)}) collective-permute-start(f32[64,512]{1,0:T(8,128)S(1)} %fusion.4), channel_id=1, source_target_pairs={{0,480},{1,33},{2,482},{3,35},{4,484},{5,37},{6,486},{7,39},{8,488... | collective-permute-start | bytes 393224 | tf_op jit(solution)/shard_map/ppermute | solution.py:165
  186.8 6.9 %collective-permute-start.15 = (f32[64,512]{1,0:T(8,128)S(1)}, f32[64,512]{1,0:T(8,128)S(1)}, u32[]{:S(2)}, u32[]{:S(2)}) collective-permute-start(f32[64,512]{1,0:T(8,128)S(1)} %fusion.12), channel_id=1, source_target_pairs={{0,32},{1,481},{2,34},{3,483},{4,36},{5,485},{6,38},{7,487},{8,40}... | collective-permute-start | bytes 393224 | tf_op jit(solution)/shard_map/ppermute | solution.py:165
  189.9 6.9 %collective-permute-start.23 = (f32[64,512]{1,0:T(8,128)S(1)}, f32[64,512]{1,0:T(8,128)S(1)}, u32[]{:S(2)}, u32[]{:S(2)}) collective-permute-start(f32[64,512]{1,0:T(8,128)S(1)} %fusion.5), channel_id=1, source_target_pairs={{0,32},{1,481},{2,34},{3,483},{4,36},{5,485},{6,38},{7,487},{8,40}... | collective-permute-start | bytes 393224 | tf_op jit(solution)/shard_map/ppermute | solution.py:165
  196.8 14.1 %collective-permute-start.16 = (f32[32,512]{1,0:T(8,128)S(1)}, f32[32,512]{1,0:T(8,128)S(1)}, u32[]{:S(2)}, u32[]{:S(2)}) collective-permute-start(f32[32,512]{1,0:T(8,128)S(1)} %get-tuple-element.16), channel_id=1, source_target_pairs={{1,48},{3,50},{5,52},{7,54},{9,56},{11,58},{13,60},{15,62},{17,32}... | collective-permute-start | bytes 196616 | tf_op jit(solution)/shard_map/ppermute | solution.py:165
  197.5 13.5 %collective-permute-start.24 = (f32[32,512]{1,0:T(8,128)S(1)}, f32[32,512]{1,0:T(8,128)S(1)}, u32[]{:S(2)}, u32[]{:S(2)}) collective-permute-start(f32[32,512]{1,0:T(8,128)S(1)} %get-tuple-element.17), channel_id=1, source_target_pairs={{0,1},{1,33},{2,3},{3,35},{4,5},{5,37},{6,7},{7,39},{8,9},{9,41},{... | collective-permute-start | bytes 196616 | tf_op jit(solution)/shard_map/ppermute | solution.py:165
  204.0 9.8 %collective-permute-start.25 = (f32[32,512]{1,0:T(8,128)S(1)}, f32[32,512]{1,0:T(8,128)S(1)}, u32[]{:S(2)}, u32[]{:S(2)}) collective-permute-start(f32[32,512]{1,0:T(8,128)S(1)} %get-tuple-element.15), channel_id=1, source_target_pairs={{0,17},{1,49},{2,19},{3,51},{4,21},{5,53},{6,23},{7,55},{8,25},{9,... | collective-permute-start | bytes 196616 | tf_op jit(solution)/shard_map/ppermute | solution.py:165
  206.1 8.3 %collective-permute-start.26 = (f32[32,512]{1,0:T(8,128)S(1)}, f32[32,512]{1,0:T(8,128)S(1)}, u32[]{:S(2)}, u32[]{:S(2)}) collective-permute-start(f32[32,512]{1,0:T(8,128)S(1)} %get-tuple-element.18), channel_id=1, source_target_pairs={{0,16},{1,32},{2,18},{3,34},{4,20},{5,36},{6,22},{7,38},{8,24},{9,... | collective-permute-start | bytes 196616 | tf_op jit(solution)/shard_map/ppermute | solution.py:165

commit v4 on v3

--- a/solution.py
+++ b/solution.py
@@ -10,7 +10,7 @@
 LANES = 128
 UNROLL = 32
 K_TILE = 768
-CHUNKS = 1
+CHUNKS = 2
 PLACES = ((0, 0), (1, 0), (3, 0), (2, 0), (0, 1), (2, 1), (1, 1), (3, 1))
 
 
@@ -108,41 +108,48 @@
 
 
 def product_kernel(*refs):
-    pieces, s_ref, out_ref, total = refs[:-3], refs[-3], refs[-2], refs[-1]
+    count = len(refs) - 6
+    pieces, s_hbm, outs = refs[:count], refs[count], refs[count + 1 : count + 3]
+    total, s_ref, sems = refs[count + 3 :]
     z, c = lax.axis_index("grp") // 2, lax.axis_index("col")
-    step = pl.program_id(0)
-    rows = out_ref.shape[1]
-    lhs = jnp.concatenate([ref[...] for ref in pieces], axis=0)
-    term = jnp.dot(lhs, s_ref[...], preferred_element_type=jnp.float32)
-
-    @pl.when(step == 0)
-    def _():
-        total[...] = term
-
-    @pl.when(step > 0)
-    def _():
-        total[...] += term
-
-    @pl.when(step == pl.num_programs(0) - 1)
-    def _():
-        for i, place in enumerate(PLACES):
-            slot = slot_of(z, c // 4, c // 2 % 2, c % 2, *place)
-            out_ref[slot] = total[i * rows : (i + 1) * rows, :]
-
-
-def product(pieces, s_both, half):
+    tiles = s_ref.shape[0] // K_TILE
+    spans = [pl.ds(k * K_TILE, K_TILE) for k in range(tiles)]
+    copies = [pltpu.make_async_copy(s_hbm.at[span], s_ref.at[span], sems.at[k]) for k, span in enumerate(spans)]
+    for copy in copies:
+        copy.start()
+    for k, span in enumerate(spans):
+        copies[k].wait()
+        lhs = jnp.concatenate([ref[:, span] for ref in pieces], axis=0)
+        term = jnp.dot(lhs, s_ref[span, :], preferred_element_type=jnp.float32)
+        if k == 0:
+            total[...] = term
+        elif k < tiles - 1:
+            total[...] += term
+        else:
+            term += total[...]
+    rows, cols = outs[0].shape[1:]
+    for i, place in enumerate(PLACES):
+        slot = slot_of(z, c // 4, c // 2 % 2, c % 2, *place)
+        for half in range(2):
+            outs[half][slot] = term[i * rows : (i + 1) * rows, half * cols : (half + 1) * cols]
+
+
+def product(pieces, s_both):
     rows, blk = pieces[0].shape
-    cols = s_both.shape[1] // 2
+    cols = s_both.shape[1]
     block_rows = rows * len(pieces) // len(PLACES)
+    whole = pl.BlockSpec(memory_space=pltpu.VMEM)
     return pl.pallas_call(
         product_kernel,
-        grid=(blk // K_TILE,),
-        out_shape=jax.ShapeDtypeStruct((len(PLACES), block_rows, cols), jnp.float32),
-        in_specs=[pl.BlockSpec((rows, K_TILE), lambda i: (0, i))] * len(pieces)
-        + [pl.BlockSpec((K_TILE, cols), lambda i: (i, half))],
-        out_specs=pl.BlockSpec((len(PLACES), block_rows, cols), lambda i: (0, 0, 0)),
-        scratch_shapes=[pltpu.VMEM((len(PLACES) * block_rows, cols), jnp.float32)],
-        compiler_params=pltpu.CompilerParams(vmem_limit_bytes=12 * 2**20),
+        out_shape=[jax.ShapeDtypeStruct((len(PLACES), block_rows, cols // 2), jnp.float32)] * 2,
+        in_specs=[whole] * len(pieces) + [pl.BlockSpec(memory_space=pltpu.HBM)],
+        out_specs=[whole] * 2,
+        scratch_shapes=[
+            pltpu.VMEM((len(PLACES) * block_rows, cols), jnp.float32),
+            pltpu.VMEM((blk, cols), jnp.bfloat16),
+            pltpu.SemaphoreType.DMA((blk // K_TILE,)),
+        ],
+        compiler_params=pltpu.CompilerParams(vmem_limit_bytes=20 * 2**20),
     )(*pieces, s_both)
 
 
@@ -227,11 +234,11 @@
             leaving = next_leaving[0]
         gathered = gather_col(here)
         pieces.append(gathered)
-        after = gathered[3, 1]
+        after = gathered[2, 1]
     pieces = [gathered[p] for p in PLACES for gathered in pieces]
 
     s_both = pltpu.with_memory_space_constraint(s_both, pltpu.HBM)
-    terms = [product(pieces, s_both, half) for half in range(2)]
+    terms = product(pieces, s_both)
     moving = [term[0] for term in terms]
     for step in range(1, 8):
         for half in range(2):

time: 218 us -> 202 us (0.927)
  waiting for transfers between devices: 53.3 us -> 22.4 us
  starting transfers between devices: 132 us -> 151 us
  Pallas kernels: 21.3 us -> 16.2 us
    ppermute x8 -> x15, waiting for transfers between devices: 29.7 us -> 4.64 us  [col_move(): return lax.ppermute(value, 'col', pairs)]
    ppermute x8 -> x15, starting transfers between devices: 33.5 us -> 54.1 us  [col_move(): return lax.ppermute(value, 'col', pairs)]
    ppermute x18, starting transfers between devices: 82.8 us -> 71.1 us  [slice_move(): return lax.ppermute(value, ('grp', 'col'), pairs)]
    ppermute x1 -> x2, starting transfers between devices: 15.7 us -> 26.2 us  [per_device(): arrived = lax.ppermute(leaving, 'grp', [(i, i ^ 16) for i in range(32)])]
    ppermute x1 -> x2, waiting for transfers between devices: 7.67 us -> 0.01 us  [per_device(): arrived = lax.ppermute(leaving, 'grp', [(i, i ^ 16) for i in range(32)])]
    pallas_call x2 -> x1, Pallas kernels: 12 us -> 6.95 us  [product(): pl.pallas_call(product_kernel, out_shape=[jax.ShapeDtypeStruct((len(PLACE...]
  transfers between devices with their start and end apart: 27 -> 35, of which waited for: 15 -> 12; matrix products, arithmetic and copies ran while one was open for 0% -> 1% of each run, Pallas kernels for 7% -> 5%
where the time goes in v4:
time: 202 us; the launch traced here: 199 us
  starting transfers between devices  151 us (75%)
  waiting for transfers between devices  22.4 us (11%)
  Pallas kernels  16.2 us (8%)
  local copies, waits for them, and re-layouts  6.27 us (3%)
    ppermute x18, starting transfers between devices, slice_move(): return lax.ppermute(value, ('grp', 'col'), pairs)  71.1 us
    ppermute x15, starting transfers between devices, col_move(): return lax.ppermute(value, 'col', pairs)  54.1 us
    ppermute x2, starting transfers between devices, per_device(): arrived = lax.ppermute(leaving, 'grp', [(i, i ^ 16) for i in range(32)])  26.2 us
    ppermute x18, waiting for transfers between devices, slice_move(): return lax.ppermute(value, ('grp', 'col'), pairs)  17.8 us
    pallas_call x1, Pallas kernels, product(): pl.pallas_call(product_kernel, out_shape=[jax.ShapeDtypeStruct((len(PLACE...  6.95 us
    pallas_call x1, Pallas kernels, scatter_rows(): pl.pallas_call(scatter_kernel, out_shape=[jax.ShapeDtypeStruct((width //...  5.76 us
    unnamed x6, local copies, waits for them, and re-layouts  5.63 us
    ppermute x15, waiting for transfers between devices, col_move(): return lax.ppermute(value, 'col', pairs)  4.64 us
  transfers between devices with their start and end apart: 35, of which 12 were waited for; matrix products, arithmetic and copies ran while one was open for 1% of the time, Pallas kernels for 5%

profile of v4, /device:TPU:6, one launch (start us, length us, event | category | flops | bytes accessed | tf_op | source)
XLA Modules:
  0.0 198.7 jit_solution(6738061892584136229)
XLA Ops:
  3.7 5.8 %shard_map.46 = (bf16[32,3840]{1,0:T(8,128)(2,1)S(1)}, bf16[32,3840]{1,0:T(8,128)(2,1)S(1)}, bf16[32,3840]{1,0:T(8,128)(2,1)S(1)}, bf16[32,3840]{1,0:T(8,128)(2,1)S(1)}, bf16[3840,128]{1,0:T(8,128)(2,1)S(1)}) custom-call(s32[3840]{0:T(1024)S(1)} %subtract_select_fusion.place_ref, bf16[64,3840]{1,0:T(8,128)(2,1)S(1)} %bitcast.40), custom_call_target="tpu_custom_call" | custom-call | tf_op jit(solution)/shard_map/pallas_call | solution.py:47
  9.4 15.7 %collective-permute-start = (bf16[32,3840]{1,0:T(8,128)(2,1)S(1)}, bf16[32,3840]{1,0:T(8,128)(2,1)S(1)}, u32[]{:S(2)}, u32[]{:S(2)}) collective-permute-start(bf16[32,3840]{1,0:T(8,128)(2,1)S(1)} %get-tuple-element.17), channel_id=1, source_target_pairs={{0,256},{16,272},{32,288},{48,304},{64,320},{80,336},{96,352},{112... | collective-permute-start | bytes 737288 | tf_op jit(solution)/shard_map/ppermute | solution.py:231
  27.4 3.5 %shard_map.47 = (bf16[3840,1024]{1,0:T(8,128)(2,1)S(1)}, f32[8,128]{1,0:T(8,128)S(1)}) custom-call(s32[1]{0:T(128)S(6)} %copy.9.kept_ref, bf16[3840,128]{1,0:T(8,128)(2,1)S(1)} %get-tuple-element.19.flag_ref, bf16[3840,256]{1,0:T(8,128)(2,1)S(1)} %copy-done.1, bf16[3840,256]{1,0:T(8,128)(2,1)S(1)} %collective-permute-done.1.other_ref), custom_call_target="tpu_custom_call" | custom-call | tf_op jit(solution)/shard_map/pallas_call | solution.py:83
  30.9 3.1 %copy-done = bf16[3840,1024]{1,0:T(8,128)(2,1)} copy-done((bf16[3840,1024]{1,0:T(8,128)(2,1)}, bf16[3840,1024]{1,0:T(8,128)(2,1)S(1)}, u32[]{:S(2)}) %copy-start) | copy-done | bytes 7864344
  34.0 3.5 %collective-permute-start.3 = (bf16[32,3840]{1,0:T(8,128)(2,1)S(1)}, bf16[32,3840]{1,0:T(8,128)(2,1)S(1)}, u32[]{:S(2)}, u32[]{:S(2)}) collective-permute-start(bf16[32,3840]{1,0:T(8,128)(2,1)S(1)} %get-tuple-element.21.refs_0_), channel_id=1, source_target_pairs={{0,2},{1,3},{2,0},{3,1},{4,6},{5,7},{6,4},{7,5},{8,10},{9,11},{10,... | collective-permute-start | bytes 737288 | tf_op jit(solution)/shard_map/ppermute | solution.py:162
  37.5 2.7 %collective-permute-start.5 = (bf16[32,3840]{1,0:T(8,128)(2,1)S(1)}, bf16[32,3840]{1,0:T(8,128)(2,1)S(1)}, u32[]{:S(2)}, u32[]{:S(2)}) collective-permute-start(bf16[32,3840]{1,0:T(8,128)(2,1)S(1)} %get-tuple-element.21.refs_0_), channel_id=1, source_target_pairs={{0,12},{1,13},{2,14},{3,15},{4,0},{5,1},{6,2},{7,3},{8,4},{9,5},{1... | collective-permute-start | bytes 737288 | tf_op jit(solution)/shard_map/ppermute | solution.py:162
  40.2 10.5 %collective-permute-start.2 = (bf16[32,3840]{1,0:T(8,128)(2,1)S(1)}, bf16[32,3840]{1,0:T(8,128)(2,1)S(1)}, u32[]{:S(2)}, u32[]{:S(2)}) collective-permute-start(bf16[32,3840]{1,0:T(8,128)(2,1)S(1)} %get-tuple-element.23), channel_id=1, source_target_pairs={{0,256},{16,272},{32,288},{48,304},{64,320},{80,336},{96,352},{112... | collective-permute-start | bytes 737288 | tf_op jit(solution)/shard_map/ppermute | solution.py:231
  50.7 9.7 %collective-permute-start.4 = (bf16[32,3840]{1,0:T(8,128)(2,1)S(1)}, bf16[32,3840]{1,0:T(8,128)(2,1)S(1)}, u32[]{:S(2)}, u32[]{:S(2)}) collective-permute-start(bf16[32,3840]{1,0:T(8,128)(2,1)S(1)} %collective-permute-done.3.refs_8_), channel_id=1, source_target_pairs={{0,8},{1,9},{2,10},{3,11},{4,12},{5,13},{6,14},{7,15},{8,0},{9,1},... | collective-permute-start | bytes 737288 | tf_op jit(solution)/shard_map/ppermute | solution.py:162
  62.3 3.4 %collective-permute-start.9 = (bf16[32,3840]{1,0:T(8,128)(2,1)S(1)}, bf16[32,3840]{1,0:T(8,128)(2,1)S(1)}, u32[]{:S(2)}, u32[]{:S(2)}) collective-permute-start(bf16[32,3840]{1,0:T(8,128)(2,1)S(1)} %get-tuple-element.21.refs_0_), channel_id=1, source_target_pairs={{0,8},{1,9},{2,10},{3,11},{4,12},{5,13},{6,14},{7,15},{8,0},{9,1},... | collective-permute-start | bytes 737288 | tf_op jit(solution)/shard_map/ppermute | solution.py:162
  65.7 3.9 %collective-permute-start.13 = (bf16[32,3840]{1,0:T(8,128)(2,1)S(1)}, bf16[32,3840]{1,0:T(8,128)(2,1)S(1)}, u32[]{:S(2)}, u32[]{:S(2)}) collective-permute-start(bf16[32,3840]{1,0:T(8,128)(2,1)S(1)} %collective-permute-done.5.refs_2_), channel_id=1, source_target_pairs={{0,2},{1,3},{2,0},{3,1},{4,6},{5,7},{6,4},{7,5},{8,10},{9,11},{10,... | collective-permute-start | bytes 737288 | tf_op jit(solution)/shard_map/ppermute | solution.py:162
  71.6 2.5 %collective-permute-start.6 = (bf16[32,3840]{1,0:T(8,128)(2,1)S(1)}, bf16[32,3840]{1,0:T(8,128)(2,1)S(1)}, u32[]{:S(2)}, u32[]{:S(2)}) collective-permute-start(bf16[32,3840]{1,0:T(8,128)(2,1)S(1)} %shard_map.49.refs_1_), channel_id=1, source_target_pairs={{0,12},{1,13},{2,14},{3,15},{4,0},{5,1},{6,2},{7,3},{8,4},{9,5},{1... | collective-permute-start | bytes 737288 | tf_op jit(solution)/shard_map/ppermute | solution.py:162
  74.1 4.6 %collective-permute-start.8 = (bf16[32,3840]{1,0:T(8,128)(2,1)S(1)}, bf16[32,3840]{1,0:T(8,128)(2,1)S(1)}, u32[]{:S(2)}, u32[]{:S(2)}) collective-permute-start(bf16[32,3840]{1,0:T(8,128)(2,1)S(1)} %shard_map.49.refs_1_), channel_id=1, source_target_pairs={{0,4},{1,5},{2,6},{3,7},{4,8},{5,9},{6,10},{7,11},{8,12},{9,13},{1... | collective-permute-start | bytes 737288 | tf_op jit(solution)/shard_map/ppermute | solution.py:162
  78.7 3.9 %collective-permute-start.15 = (bf16[32,3840]{1,0:T(8,128)(2,1)S(1)}, bf16[32,3840]{1,0:T(8,128)(2,1)S(1)}, u32[]{:S(2)}, u32[]{:S(2)}) collective-permute-start(bf16[32,3840]{1,0:T(8,128)(2,1)S(1)} %collective-permute-done.7.refs_4_), channel_id=1, source_target_pairs={{0,2},{1,3},{2,0},{3,1},{4,6},{5,7},{6,4},{7,5},{8,10},{9,11},{10,... | collective-permute-start | bytes 737288 | tf_op jit(solution)/shard_map/ppermute | solution.py:162
  82.7 3.4 %collective-permute-start.10 = (bf16[32,3840]{1,0:T(8,128)(2,1)S(1)}, bf16[32,3840]{1,0:T(8,128)(2,1)S(1)}, u32[]{:S(2)}, u32[]{:S(2)}) collective-permute-start(bf16[32,3840]{1,0:T(8,128)(2,1)S(1)} %shard_map.49.refs_1_), channel_id=1, source_target_pairs={{0,8},{1,9},{2,10},{3,11},{4,12},{5,13},{6,14},{7,15},{8,0},{9,1},... | collective-permute-start | bytes 737288 | tf_op jit(solution)/shard_map/ppermute | solution.py:162
  86.1 4.0 %collective-permute-start.12 = (bf16[32,3840]{1,0:T(8,128)(2,1)S(1)}, bf16[32,3840]{1,0:T(8,128)(2,1)S(1)}, u32[]{:S(2)}, u32[]{:S(2)}) collective-permute-start(bf16[32,3840]{1,0:T(8,128)(2,1)S(1)} %collective-permute-done.11.refs_9_), channel_id=1, source_target_pairs={{0,8},{1,9},{2,10},{3,11},{4,12},{5,13},{6,14},{7,15},{8,0},{9,1},... | collective-permute-start | bytes 737288 | tf_op jit(solution)/shard_map/ppermute | solution.py:162
  92.0 4.9 %collective-permute-start.16 = (bf16[32,3840]{1,0:T(8,128)(2,1)S(1)}, bf16[32,3840]{1,0:T(8,128)(2,1)}, u32[]{:S(2)}, u32[]{:S(2)}) collective-permute-start(bf16[32,3840]{1,0:T(8,128)(2,1)S(1)} %collective-permute-done.8.refs_5_), channel_id=1, source_target_pairs={{0,2},{1,3},{2,0},{3,1},{4,6},{5,7},{6,4},{7,5},{8,10},{9,11},{10,... | collective-permute-start | bytes 737288 | tf_op jit(solution)/shard_map/ppermute | solution.py:162
  99.0 2.6 %collective-permute-done.16.refs_15_ = bf16[32,3840]{1,0:T(8,128)(2,1)} collective-permute-done((bf16[32,3840]{1,0:T(8,128)(2,1)S(1)}, bf16[32,3840]{1,0:T(8,128)(2,1)}, u32[]{:S(2)}, u32[]{:S(2)}) %collective-permute-start.16) | collective-permute-done | bytes 245792 | tf_op jit(solution)/shard_map/ppermute | solution.py:162
  101.6 7.0 %shard_map.50 = (f32[8,64,512]{2,1,0:T(8,128)S(1)}, f32[8,64,512]{2,1,0:T(8,128)S(1)}) custom-call(bf16[32,3840]{1,0:T(8,128)(2,1)S(1)} %get-tuple-element.21.refs_0_, bf16[32,3840]{1,0:T(8,128)(2,1)S(1)} %shard_map.49.refs_1_, bf16[32,3840]{1,0:T(8,128)(2,1)S(1)} %collective-permute-done.5.refs_2_, bf16[32,3840]{1,0:T(8,128)(2,1)S(1)} %collective-permute-done.6.refs_3_, ...), custom_call_target="tpu_custom_call" | custom-call | tf_op jit(solution)/shard_map/pallas_call | solution.py:142
  108.6 16.0 %collective-permute-start.17 = (f32[64,512]{1,0:T(8,128)S(1)}, f32[64,512]{1,0:T(8,128)S(1)}, u32[]{:S(2)}, u32[]{:S(2)}) collective-permute-start(f32[64,512]{1,0:T(8,128)S(1)} %slice_bitcast_fusion.1), channel_id=1, source_target_pairs={{0,32},{1,481},{2,34},{3,483},{4,36},{5,485},{6,38},{7,487},{8,40}... | collective-permute-start | bytes 393224 | tf_op jit(solution)/shard_map/ppermute | solution.py:172
  127.5 6.6 %collective-permute-start.18 = (f32[64,512]{1,0:T(8,128)S(1)}, f32[64,512]{1,0:T(8,128)S(1)}, u32[]{:S(2)}, u32[]{:S(2)}) collective-permute-start(f32[64,512]{1,0:T(8,128)S(1)} %bitcast_add_fusion.7), channel_id=1, source_target_pairs={{0,480},{1,33},{2,482},{3,35},{4,484},{5,37},{6,486},{7,39},{8,488... | collective-permute-start | bytes 393224 | tf_op jit(solution)/shard_map/ppermute | solution.py:172
  134.1 4.6 %collective-permute-start.26 = (f32[64,512]{1,0:T(8,128)S(1)}, f32[64,512]{1,0:T(8,128)S(1)}, u32[]{:S(2)}, u32[]{:S(2)}) collective-permute-start(f32[64,512]{1,0:T(8,128)S(1)} %bitcast_add_fusion), channel_id=1, source_target_pairs={{0,480},{1,33},{2,482},{3,35},{4,484},{5,37},{6,486},{7,39},{8,488... | collective-permute-start | bytes 393224 | tf_op jit(solution)/shard_map/ppermute | solution.py:172
  142.2 2.5 %collective-permute-start.27 = (f32[64,512]{1,0:T(8,128)S(1)}, f32[64,512]{1,0:T(8,128)S(1)}, u32[]{:S(2)}, u32[]{:S(2)}) collective-permute-start(f32[64,512]{1,0:T(8,128)S(1)} %bitcast_add_fusion.1), channel_id=1, source_target_pairs={{0,32},{1,481},{2,34},{3,483},{4,36},{5,485},{6,38},{7,487},{8,40}... | collective-permute-start | bytes 393224 | tf_op jit(solution)/shard_map/ppermute | solution.py:172
  146.6 2.8 %collective-permute-start.20 = (f32[64,512]{1,0:T(8,128)S(1)}, f32[64,512]{1,0:T(8,128)S(1)}, u32[]{:S(2)}, u32[]{:S(2)}) collective-permute-start(f32[64,512]{1,0:T(8,128)S(1)} %bitcast_add_fusion.9), channel_id=1, source_target_pairs={{0,480},{1,33},{2,482},{3,35},{4,484},{5,37},{6,486},{7,39},{8,488... | collective-permute-start | bytes 393224 | tf_op jit(solution)/shard_map/ppermute | solution.py:172
  149.4 6.2 %collective-permute-start.28 = (f32[64,512]{1,0:T(8,128)S(1)}, f32[64,512]{1,0:T(8,128)S(1)}, u32[]{:S(2)}, u32[]{:S(2)}) collective-permute-start(f32[64,512]{1,0:T(8,128)S(1)} %bitcast_add_fusion.2), channel_id=1, source_target_pairs={{0,480},{1,33},{2,482},{3,35},{4,484},{5,37},{6,486},{7,39},{8,488... | collective-permute-start | bytes 393224 | tf_op jit(solution)/shard_map/ppermute | solution.py:172
  162.7 3.4 %collective-permute-start.22 = (f32[64,512]{1,0:T(8,128)S(1)}, f32[64,512]{1,0:T(8,128)S(1)}, u32[]{:S(2)}, u32[]{:S(2)}) collective-permute-start(f32[64,512]{1,0:T(8,128)S(1)} %bitcast_add_fusion.11), channel_id=1, source_target_pairs={{0,480},{1,33},{2,482},{3,35},{4,484},{5,37},{6,486},{7,39},{8,488... | collective-permute-start | bytes 393224 | tf_op jit(solution)/shard_map/ppermute | solution.py:172
  166.1 4.9 %collective-permute-start.30 = (f32[64,512]{1,0:T(8,128)S(1)}, f32[64,512]{1,0:T(8,128)S(1)}, u32[]{:S(2)}, u32[]{:S(2)}) collective-permute-start(f32[64,512]{1,0:T(8,128)S(1)} %bitcast_add_fusion.4), channel_id=1, source_target_pairs={{0,480},{1,33},{2,482},{3,35},{4,484},{5,37},{6,486},{7,39},{8,488... | collective-permute-start | bytes 393224 | tf_op jit(solution)/shard_map/ppermute | solution.py:172
  174.2 2.7 %collective-permute-start.31 = (f32[64,512]{1,0:T(8,128)S(1)}, f32[64,512]{1,0:T(8,128)S(1)}, u32[]{:S(2)}, u32[]{:S(2)}) collective-permute-start(f32[64,512]{1,0:T(8,128)S(1)} %bitcast_add_fusion.5), channel_id=1, source_target_pairs={{0,32},{1,481},{2,34},{3,483},{4,36},{5,485},{6,38},{7,487},{8,40}... | collective-permute-start | bytes 393224 | tf_op jit(solution)/shard_map/ppermute | solution.py:172
  177.9 3.2 %collective-permute-done.31 = f32[64,512]{1,0:T(8,128)S(1)} collective-permute-done((f32[64,512]{1,0:T(8,128)S(1)}, f32[64,512]{1,0:T(8,128)S(1)}, u32[]{:S(2)}, u32[]{:S(2)}) %collective-permute-start.31) | collective-permute-done | bytes 131104 | tf_op jit(solution)/shard_map/ppermute | solution.py:172
  181.8 4.0 %collective-permute-start.32 = (f32[32,512]{1,0:T(8,128)S(1)}, f32[32,512]{1,0:T(8,128)S(1)}, u32[]{:S(2)}, u32[]{:S(2)}) collective-permute-start(f32[32,512]{1,0:T(8,128)S(1)} %get-tuple-element.29), channel_id=1, source_target_pairs={{0,1},{1,33},{2,3},{3,35},{4,5},{5,37},{6,7},{7,39},{8,9},{9,41},{... | collective-permute-start | bytes 196616 | tf_op jit(solution)/shard_map/ppermute | solution.py:172
  185.8 4.6 %collective-permute-start.33 = (f32[32,512]{1,0:T(8,128)S(1)}, f32[32,512]{1,0:T(8,128)S(1)}, u32[]{:S(2)}, u32[]{:S(2)}) collective-permute-start(f32[32,512]{1,0:T(8,128)S(1)} %get-tuple-element.27), channel_id=1, source_target_pairs={{0,17},{1,49},{2,19},{3,51},{4,21},{5,53},{6,23},{7,55},{8,25},{9,... | collective-permute-start | bytes 196616 | tf_op jit(solution)/shard_map/ppermute | solution.py:172
  192.8 2.8 %collective-permute-done.33 = f32[32,512]{1,0:T(8,128)S(1)} collective-permute-done((f32[32,512]{1,0:T(8,128)S(1)}, f32[32,512]{1,0:T(8,128)S(1)}, u32[]{:S(2)}, u32[]{:S(2)}) %collective-permute-start.33) | collective-permute-done | bytes 65568 | tf_op jit(solution)/shard_map/ppermute | solution.py:172
  195.6 2.5 %collective-permute-done.34 = f32[32,512]{1,0:T(8,128)S(1)} collective-permute-done((f32[32,512]{1,0:T(8,128)S(1)}, f32[32,512]{1,0:T(8,128)S(1)}, u32[]{:S(2)}, u32[]{:S(2)}) %collective-permute-start.34) | collective-permute-done | bytes 65568 | tf_op jit(solution)/shard_map/ppermute | solution.py:172
  (69 shorter events, 36.4 us)
Async XLA Ops:
  0.0 25.8 %collective-permute-start.1 = (bf16[3840,256]{1,0:T(8,128)(2,1)}, bf16[3840,256]{1,0:T(8,128)(2,1)S(1)}, u32[]{:S(2)}, u32[]{:S(2)}) collective-permute-start(bf16[3840,256]{1,0:T(8,128)(2,1)} %own_ref.1), channel_id=1, source_target_pairs={{0,1},{1,0},{2,3},{3,2},{4,5},{5,4},{6,7},{7,6},{8,9},{9,8},{10,11... | collective-permute-start | bytes 5898248 | tf_op jit(solution)/shard_map/ppermute | solution.py:162
  9.4 24.5 %collective-permute-start = (bf16[32,3840]{1,0:T(8,128)(2,1)S(1)}, bf16[32,3840]{1,0:T(8,128)(2,1)S(1)}, u32[]{:S(2)}, u32[]{:S(2)}) collective-permute-start(bf16[32,3840]{1,0:T(8,128)(2,1)S(1)} %get-tuple-element.17), channel_id=1, source_target_pairs={{0,256},{16,272},{32,288},{48,304},{64,320},{80,336},{96,352},{112... | collective-permute-start | bytes 737288 | tf_op jit(solution)/shard_map/ppermute | solution.py:231
  34.0 16.7 %collective-permute-start.3 = (bf16[32,3840]{1,0:T(8,128)(2,1)S(1)}, bf16[32,3840]{1,0:T(8,128)(2,1)S(1)}, u32[]{:S(2)}, u32[]{:S(2)}) collective-permute-start(bf16[32,3840]{1,0:T(8,128)(2,1)S(1)} %get-tuple-element.21.refs_0_), channel_id=1, source_target_pairs={{0,2},{1,3},{2,0},{3,1},{4,6},{5,7},{6,4},{7,5},{8,10},{9,11},{10,... | collective-permute-start | bytes 737288 | tf_op jit(solution)/shard_map/ppermute | solution.py:162
  37.5 28.2 %collective-permute-start.5 = (bf16[32,3840]{1,0:T(8,128)(2,1)S(1)}, bf16[32,3840]{1,0:T(8,128)(2,1)S(1)}, u32[]{:S(2)}, u32[]{:S(2)}) collective-permute-start(bf16[32,3840]{1,0:T(8,128)(2,1)S(1)} %get-tuple-element.21.refs_0_), channel_id=1, source_target_pairs={{0,12},{1,13},{2,14},{3,15},{4,0},{5,1},{6,2},{7,3},{8,4},{9,5},{1... | collective-permute-start | bytes 737288 | tf_op jit(solution)/shard_map/ppermute | solution.py:162
  40.2 29.5 %collective-permute-start.2 = (bf16[32,3840]{1,0:T(8,128)(2,1)S(1)}, bf16[32,3840]{1,0:T(8,128)(2,1)S(1)}, u32[]{:S(2)}, u32[]{:S(2)}) collective-permute-start(bf16[32,3840]{1,0:T(8,128)(2,1)S(1)} %get-tuple-element.23), channel_id=1, source_target_pairs={{0,256},{16,272},{32,288},{48,304},{64,320},{80,336},{96,352},{112... | collective-permute-start | bytes 737288 | tf_op jit(solution)/shard_map/ppermute | solution.py:231
  50.7 19.0 %collective-permute-start.4 = (bf16[32,3840]{1,0:T(8,128)(2,1)S(1)}, bf16[32,3840]{1,0:T(8,128)(2,1)S(1)}, u32[]{:S(2)}, u32[]{:S(2)}) collective-permute-start(bf16[32,3840]{1,0:T(8,128)(2,1)S(1)} %collective-permute-done.3.refs_8_), channel_id=1, source_target_pairs={{0,8},{1,9},{2,10},{3,11},{4,12},{5,13},{6,14},{7,15},{8,0},{9,1},... | collective-permute-start | bytes 737288 | tf_op jit(solution)/shard_map/ppermute | solution.py:162
  60.4 13.7 %collective-permute-start.7 = (bf16[32,3840]{1,0:T(8,128)(2,1)S(1)}, bf16[32,3840]{1,0:T(8,128)(2,1)S(1)}, u32[]{:S(2)}, u32[]{:S(2)}) collective-permute-start(bf16[32,3840]{1,0:T(8,128)(2,1)S(1)} %get-tuple-element.21.refs_0_), channel_id=1, source_target_pairs={{0,4},{1,5},{2,6},{3,7},{4,8},{5,9},{6,10},{7,11},{8,12},{9,13},{1... | collective-permute-start | bytes 737288 | tf_op jit(solution)/shard_map/ppermute | solution.py:162
  62.3 16.4 %collective-permute-start.9 = (bf16[32,3840]{1,0:T(8,128)(2,1)S(1)}, bf16[32,3840]{1,0:T(8,128)(2,1)S(1)}, u32[]{:S(2)}, u32[]{:S(2)}) collective-permute-start(bf16[32,3840]{1,0:T(8,128)(2,1)S(1)} %get-tuple-element.21.refs_0_), channel_id=1, source_target_pairs={{0,8},{1,9},{2,10},{3,11},{4,12},{5,13},{6,14},{7,15},{8,0},{9,1},... | collective-permute-start | bytes 737288 | tf_op jit(solution)/shard_map/ppermute | solution.py:162
  65.7 17.0 %collective-permute-start.13 = (bf16[32,3840]{1,0:T(8,128)(2,1)S(1)}, bf16[32,3840]{1,0:T(8,128)(2,1)S(1)}, u32[]{:S(2)}, u32[]{:S(2)}) collective-permute-start(bf16[32,3840]{1,0:T(8,128)(2,1)S(1)} %collective-permute-done.5.refs_2_), channel_id=1, source_target_pairs={{0,2},{1,3},{2,0},{3,1},{4,6},{5,7},{6,4},{7,5},{8,10},{9,11},{10,... | collective-permute-start | bytes 737288 | tf_op jit(solution)/shard_map/ppermute | solution.py:162
  69.7 16.3 %collective-permute-start.11 = (bf16[32,3840]{1,0:T(8,128)(2,1)S(1)}, bf16[32,3840]{1,0:T(8,128)(2,1)S(1)}, u32[]{:S(2)}, u32[]{:S(2)}) collective-permute-start(bf16[32,3840]{1,0:T(8,128)(2,1)S(1)} %shard_map.49.refs_1_), channel_id=1, source_target_pairs={{0,2},{1,3},{2,0},{3,1},{4,6},{5,7},{6,4},{7,5},{8,10},{9,11},{10,... | collective-permute-start | bytes 737288 | tf_op jit(solution)/shard_map/ppermute | solution.py:162
  71.6 18.4 %collective-permute-start.6 = (bf16[32,3840]{1,0:T(8,128)(2,1)S(1)}, bf16[32,3840]{1,0:T(8,128)(2,1)S(1)}, u32[]{:S(2)}, u32[]{:S(2)}) collective-permute-start(bf16[32,3840]{1,0:T(8,128)(2,1)S(1)} %shard_map.49.refs_1_), channel_id=1, source_target_pairs={{0,12},{1,13},{2,14},{3,15},{4,0},{5,1},{6,2},{7,3},{8,4},{9,5},{1... | collective-permute-start | bytes 737288 | tf_op jit(solution)/shard_map/ppermute | solution.py:162
  74.1 17.9 %collective-permute-start.8 = (bf16[32,3840]{1,0:T(8,128)(2,1)S(1)}, bf16[32,3840]{1,0:T(8,128)(2,1)S(1)}, u32[]{:S(2)}, u32[]{:S(2)}) collective-permute-start(bf16[32,3840]{1,0:T(8,128)(2,1)S(1)} %shard_map.49.refs_1_), channel_id=1, source_target_pairs={{0,4},{1,5},{2,6},{3,7},{4,8},{5,9},{6,10},{7,11},{8,12},{9,13},{1... | collective-permute-start | bytes 737288 | tf_op jit(solution)/shard_map/ppermute | solution.py:162
  78.7 18.2 %collective-permute-start.15 = (bf16[32,3840]{1,0:T(8,128)(2,1)S(1)}, bf16[32,3840]{1,0:T(8,128)(2,1)S(1)}, u32[]{:S(2)}, u32[]{:S(2)}) collective-permute-start(bf16[32,3840]{1,0:T(8,128)(2,1)S(1)} %collective-permute-done.7.refs_4_), channel_id=1, source_target_pairs={{0,2},{1,3},{2,0},{3,1},{4,6},{5,7},{6,4},{7,5},{8,10},{9,11},{10,... | collective-permute-start | bytes 737288 | tf_op jit(solution)/shard_map/ppermute | solution.py:162
  82.7 14.3 %collective-permute-start.10 = (bf16[32,3840]{1,0:T(8,128)(2,1)S(1)}, bf16[32,3840]{1,0:T(8,128)(2,1)S(1)}, u32[]{:S(2)}, u32[]{:S(2)}) collective-permute-start(bf16[32,3840]{1,0:T(8,128)(2,1)S(1)} %shard_map.49.refs_1_), channel_id=1, source_target_pairs={{0,8},{1,9},{2,10},{3,11},{4,12},{5,13},{6,14},{7,15},{8,0},{9,1},... | collective-permute-start | bytes 737288 | tf_op jit(solution)/shard_map/ppermute | solution.py:162
  86.1 10.9 %collective-permute-start.12 = (bf16[32,3840]{1,0:T(8,128)(2,1)S(1)}, bf16[32,3840]{1,0:T(8,128)(2,1)S(1)}, u32[]{:S(2)}, u32[]{:S(2)}) collective-permute-start(bf16[32,3840]{1,0:T(8,128)(2,1)S(1)} %collective-permute-done.11.refs_9_), channel_id=1, source_target_pairs={{0,8},{1,9},{2,10},{3,11},{4,12},{5,13},{6,14},{7,15},{8,0},{9,1},... | collective-permute-start | bytes 737288 | tf_op jit(solution)/shard_map/ppermute | solution.py:162
  90.1 8.9 %collective-permute-start.14 = (bf16[32,3840]{1,0:T(8,128)(2,1)S(1)}, bf16[32,3840]{1,0:T(8,128)(2,1)}, u32[]{:S(2)}, u32[]{:S(2)}) collective-permute-start(bf16[32,3840]{1,0:T(8,128)(2,1)S(1)} %collective-permute-done.6.refs_3_), channel_id=1, source_target_pairs={{0,2},{1,3},{2,0},{3,1},{4,6},{5,7},{6,4},{7,5},{8,10},{9,11},{10,... | collective-permute-start | bytes 737288 | tf_op jit(solution)/shard_map/ppermute | solution.py:162
  92.0 9.6 %collective-permute-start.16 = (bf16[32,3840]{1,0:T(8,128)(2,1)S(1)}, bf16[32,3840]{1,0:T(8,128)(2,1)}, u32[]{:S(2)}, u32[]{:S(2)}) collective-permute-start(bf16[32,3840]{1,0:T(8,128)(2,1)S(1)} %collective-permute-done.8.refs_5_), channel_id=1, source_target_pairs={{0,2},{1,3},{2,0},{3,1},{4,6},{5,7},{6,4},{7,5},{8,10},{9,11},{10,... | collective-permute-start | bytes 737288 | tf_op jit(solution)/shard_map/ppermute | solution.py:162
  108.6 18.9 %collective-permute-start.17 = (f32[64,512]{1,0:T(8,128)S(1)}, f32[64,512]{1,0:T(8,128)S(1)}, u32[]{:S(2)}, u32[]{:S(2)}) collective-permute-start(f32[64,512]{1,0:T(8,128)S(1)} %slice_bitcast_fusion.1), channel_id=1, source_target_pairs={{0,32},{1,481},{2,34},{3,483},{4,36},{5,485},{6,38},{7,487},{8,40}... | collective-permute-start | bytes 393224 | tf_op jit(solution)/shard_map/ppermute | solution.py:172
  124.6 9.5 %collective-permute-start.25 = (f32[64,512]{1,0:T(8,128)S(1)}, f32[64,512]{1,0:T(8,128)S(1)}, u32[]{:S(2)}, u32[]{:S(2)}) collective-permute-start(f32[64,512]{1,0:T(8,128)S(1)} %slice_bitcast_fusion), channel_id=1, source_target_pairs={{0,32},{1,481},{2,34},{3,483},{4,36},{5,485},{6,38},{7,487},{8,40}... | collective-permute-start | bytes 393224 | tf_op jit(solution)/shard_map/ppermute | solution.py:172
  127.5 11.2 %collective-permute-start.18 = (f32[64,512]{1,0:T(8,128)S(1)}, f32[64,512]{1,0:T(8,128)S(1)}, u32[]{:S(2)}, u32[]{:S(2)}) collective-permute-start(f32[64,512]{1,0:T(8,128)S(1)} %bitcast_add_fusion.7), channel_id=1, source_target_pairs={{0,480},{1,33},{2,482},{3,35},{4,484},{5,37},{6,486},{7,39},{8,488... | collective-permute-start | bytes 393224 | tf_op jit(solution)/shard_map/ppermute | solution.py:172
  134.1 8.1 %collective-permute-start.26 = (f32[64,512]{1,0:T(8,128)S(1)}, f32[64,512]{1,0:T(8,128)S(1)}, u32[]{:S(2)}, u32[]{:S(2)}) collective-permute-start(f32[64,512]{1,0:T(8,128)S(1)} %bitcast_add_fusion), channel_id=1, source_target_pairs={{0,480},{1,33},{2,482},{3,35},{4,484},{5,37},{6,486},{7,39},{8,488... | collective-permute-start | bytes 393224 | tf_op jit(solution)/shard_map/ppermute | solution.py:172
  138.8 7.8 %collective-permute-start.19 = (f32[64,512]{1,0:T(8,128)S(1)}, f32[64,512]{1,0:T(8,128)S(1)}, u32[]{:S(2)}, u32[]{:S(2)}) collective-permute-start(f32[64,512]{1,0:T(8,128)S(1)} %bitcast_add_fusion.8), channel_id=1, source_target_pairs={{0,32},{1,481},{2,34},{3,483},{4,36},{5,485},{6,38},{7,487},{8,40}... | collective-permute-start | bytes 393224 | tf_op jit(solution)/shard_map/ppermute | solution.py:172
  142.2 7.2 %collective-permute-start.27 = (f32[64,512]{1,0:T(8,128)S(1)}, f32[64,512]{1,0:T(8,128)S(1)}, u32[]{:S(2)}, u32[]{:S(2)}) collective-permute-start(f32[64,512]{1,0:T(8,128)S(1)} %bitcast_add_fusion.1), channel_id=1, source_target_pairs={{0,32},{1,481},{2,34},{3,483},{4,36},{5,485},{6,38},{7,487},{8,40}... | collective-permute-start | bytes 393224 | tf_op jit(solution)/shard_map/ppermute | solution.py:172
  146.6 9.0 %collective-permute-start.20 = (f32[64,512]{1,0:T(8,128)S(1)}, f32[64,512]{1,0:T(8,128)S(1)}, u32[]{:S(2)}, u32[]{:S(2)}) collective-permute-start(f32[64,512]{1,0:T(8,128)S(1)} %bitcast_add_fusion.9), channel_id=1, source_target_pairs={{0,480},{1,33},{2,482},{3,35},{4,484},{5,37},{6,486},{7,39},{8,488... | collective-permute-start | bytes 393224 | tf_op jit(solution)/shard_map/ppermute | solution.py:172
  149.4 9.8 %collective-permute-start.28 = (f32[64,512]{1,0:T(8,128)S(1)}, f32[64,512]{1,0:T(8,128)S(1)}, u32[]{:S(2)}, u32[]{:S(2)}) collective-permute-start(f32[64,512]{1,0:T(8,128)S(1)} %bitcast_add_fusion.2), channel_id=1, source_target_pairs={{0,480},{1,33},{2,482},{3,35},{4,484},{5,37},{6,486},{7,39},{8,488... | collective-permute-start | bytes 393224 | tf_op jit(solution)/shard_map/ppermute | solution.py:172
  155.6 7.0 %collective-permute-start.21 = (f32[64,512]{1,0:T(8,128)S(1)}, f32[64,512]{1,0:T(8,128)S(1)}, u32[]{:S(2)}, u32[]{:S(2)}) collective-permute-start(f32[64,512]{1,0:T(8,128)S(1)} %bitcast_add_fusion.10), channel_id=1, source_target_pairs={{0,32},{1,481},{2,34},{3,483},{4,36},{5,485},{6,38},{7,487},{8,40}... | collective-permute-start | bytes 393224 | tf_op jit(solution)/shard_map/ppermute | solution.py:172
  162.7 8.3 %collective-permute-start.22 = (f32[64,512]{1,0:T(8,128)S(1)}, f32[64,512]{1,0:T(8,128)S(1)}, u32[]{:S(2)}, u32[]{:S(2)}) collective-permute-start(f32[64,512]{1,0:T(8,128)S(1)} %bitcast_add_fusion.11), channel_id=1, source_target_pairs={{0,480},{1,33},{2,482},{3,35},{4,484},{5,37},{6,486},{7,39},{8,488... | collective-permute-start | bytes 393224 | tf_op jit(solution)/shard_map/ppermute | solution.py:172
  166.1 8.1 %collective-permute-start.30 = (f32[64,512]{1,0:T(8,128)S(1)}, f32[64,512]{1,0:T(8,128)S(1)}, u32[]{:S(2)}, u32[]{:S(2)}) collective-permute-start(f32[64,512]{1,0:T(8,128)S(1)} %bitcast_add_fusion.4), channel_id=1, source_target_pairs={{0,480},{1,33},{2,482},{3,35},{4,484},{5,37},{6,486},{7,39},{8,488... | collective-permute-start | bytes 393224 | tf_op jit(solution)/shard_map/ppermute | solution.py:172
  181.2 11.6 %collective-permute-start.24 = (f32[32,512]{1,0:T(8,128)S(1)}, f32[32,512]{1,0:T(8,128)S(1)}, u32[]{:S(2)}, u32[]{:S(2)}) collective-permute-start(f32[32,512]{1,0:T(8,128)S(1)} %get-tuple-element.28), channel_id=1, source_target_pairs={{1,48},{3,50},{5,52},{7,54},{9,56},{11,58},{13,60},{15,62},{17,32}... | collective-permute-start | bytes 196616 | tf_op jit(solution)/shard_map/ppermute | solution.py:172
  181.8 11.0 %collective-permute-start.32 = (f32[32,512]{1,0:T(8,128)S(1)}, f32[32,512]{1,0:T(8,128)S(1)}, u32[]{:S(2)}, u32[]{:S(2)}) collective-permute-start(f32[32,512]{1,0:T(8,128)S(1)} %get-tuple-element.29), channel_id=1, source_target_pairs={{0,1},{1,33},{2,3},{3,35},{4,5},{5,37},{6,7},{7,39},{8,9},{9,41},{... | collective-permute-start | bytes 196616 | tf_op jit(solution)/shard_map/ppermute | solution.py:172
  185.8 9.8 %collective-permute-start.33 = (f32[32,512]{1,0:T(8,128)S(1)}, f32[32,512]{1,0:T(8,128)S(1)}, u32[]{:S(2)}, u32[]{:S(2)}) collective-permute-start(f32[32,512]{1,0:T(8,128)S(1)} %get-tuple-element.27), channel_id=1, source_target_pairs={{0,17},{1,49},{2,19},{3,51},{4,21},{5,53},{6,23},{7,55},{8,25},{9,... | collective-permute-start | bytes 196616 | tf_op jit(solution)/shard_map/ppermute | solution.py:172
  190.4 7.7 %collective-permute-start.34 = (f32[32,512]{1,0:T(8,128)S(1)}, f32[32,512]{1,0:T(8,128)S(1)}, u32[]{:S(2)}, u32[]{:S(2)}) collective-permute-start(f32[32,512]{1,0:T(8,128)S(1)} %get-tuple-element.30), channel_id=1, source_target_pairs={{0,16},{1,32},{2,18},{3,34},{4,20},{5,36},{6,22},{7,38},{8,24},{9,... | collective-permute-start | bytes 196616 | tf_op jit(solution)/shard_map/ppermute | solution.py:172
  (6 other events, 26.2 us)

commit v5 on v4

--- a/solution.py
+++ b/solution.py
@@ -185,27 +185,31 @@
         outs[1][...] = refs[2][...]
 
 
-def combine(own, arrived, following, after):
+def combine(own, arrived, following, *after):
     count = 1 if following is None else 2
     arrays = [own, arrived] + ([] if following is None else [following])
     whole = pl.BlockSpec(memory_space=pltpu.VMEM)
     return pl.pallas_call(
         functools.partial(combine_kernel, count),
         out_shape=[jax.ShapeDtypeStruct(own.shape, own.dtype)] * count,
-        in_specs=[whole] * len(arrays) + [pl.BlockSpec(memory_space=pl.ANY)],
+        in_specs=[whole] * len(arrays) + [pl.BlockSpec(memory_space=pl.ANY)] * len(after),
         out_specs=[whole] * count,
         compiler_params=pltpu.CompilerParams(vmem_limit_bytes=4 * 2**20),
-    )(*arrays, after)
-
-
-def gather_col(here):
+    )(*arrays, *after)
+
+
+def gather_col(here, direct):
     pieces = {(0, 0): here}
     for d in (1, 3, 2):
         pieces[d, 0] = col_move(here, lambda x, y, k, d=d: (x - d, y, k))
     pieces[0, 1] = col_move(here, lambda x, y, k: (x, 1 - y, k))
-    pieces[2, 1] = col_move(pieces[0, 1], lambda x, y, k: (x - 2, y, k))
-    for d in (1, 3):
-        pieces[d, 1] = col_move(pieces[d, 0], lambda x, y, k: (x, 1 - y, k))
+    if direct:
+        for d in (1, 3, 2):
+            pieces[d, 1] = col_move(here, lambda x, y, k, d=d: (x - d, 1 - y, k))
+    else:
+        pieces[2, 1] = col_move(pieces[0, 1], lambda x, y, k: (x - 2, y, k))
+        for d in (1, 3):
+            pieces[d, 1] = col_move(pieces[d, 0], lambda x, y, k: (x, 1 - y, k))
     return pieces
 
 
@@ -226,15 +230,15 @@
     s_both, masked = split_halves(kept_count, flag, secular, other)
 
     pieces = []
-    leaving, after = cross_parts[0], masked
+    leaving, after = cross_parts[0], [masked]
     for h in range(CHUNKS):
         arrived = lax.ppermute(leaving, "grp", [(i, i ^ 16) for i in range(32)])
-        here, *next_leaving = combine(own_parts[h], arrived, cross_parts[h + 1] if h + 1 < CHUNKS else None, after)
+        here, *next_leaving = combine(own_parts[h], arrived, cross_parts[h + 1] if h + 1 < CHUNKS else None, *after)
         if next_leaving:
             leaving = next_leaving[0]
-        gathered = gather_col(here)
+        gathered = gather_col(here, h + 1 < CHUNKS)
         pieces.append(gathered)
-        after = gathered[2, 1]
+        after = [gathered[2, 0], gathered[2, 1]]
     pieces = [gathered[p] for p in PLACES for gathered in pieces]
 
     s_both = pltpu.with_memory_space_constraint(s_both, pltpu.HBM)

time: 202 us -> 203 us (level)
  waiting for transfers between devices: 22.4 us -> 27.1 us
    ppermute x18, starting transfers between devices: 71.1 us -> 63.5 us  [slice_move(): return lax.ppermute(value, ('grp', 'col'), pairs)]
    ppermute x15, starting transfers between devices: 54.1 us -> 59.5 us  [col_move(): return lax.ppermute(value, 'col', pairs)]
    ppermute x18, waiting for transfers between devices: 17.8 us -> 20.9 us  [slice_move(): return lax.ppermute(value, ('grp', 'col'), pairs)]
  transfers between devices with their start and end apart: 35 -> 35, of which waited for: 12 -> 13; matrix products, arithmetic and copies ran while one was open for 1% -> 1% of each run, Pallas kernels for 5% -> 5%
where the time goes in v5:
time: 203 us; the launch traced here: 201 us
  starting transfers between devices  149 us (73%)
  waiting for transfers between devices  27.1 us (13%)
  Pallas kernels  16.2 us (8%)
  local copies, waits for them, and re-layouts  6.27 us (3%)
    ppermute x18, starting transfers between devices, slice_move(): return lax.ppermute(value, ('grp', 'col'), pairs)  63.5 us
    ppermute x15, starting transfers between devices, col_move(): return lax.ppermute(value, 'col', pairs)  59.5 us
    ppermute x2, starting transfers between devices, per_device(): arrived = lax.ppermute(leaving, 'grp', [(i, i ^ 16) for i in range(32)])  26.2 us
    ppermute x18, waiting for transfers between devices, slice_move(): return lax.ppermute(value, ('grp', 'col'), pairs)  20.9 us
    pallas_call x1, Pallas kernels, product(): pl.pallas_call(product_kernel, out_shape=[jax.ShapeDtypeStruct((len(PLACE...  6.95 us
    ppermute x15, waiting for transfers between devices, col_move(): return lax.ppermute(value, 'col', pairs)  6.23 us
    pallas_call x1, Pallas kernels, scatter_rows(): pl.pallas_call(scatter_kernel, out_shape=[jax.ShapeDtypeStruct((width //...  5.76 us
    unnamed x6, local copies, waits for them, and re-layouts  5.63 us
  transfers between devices with their start and end apart: 35, of which 13 were waited for; matrix products, arithmetic and copies ran while one was open for 1% of the time, Pallas kernels for 5%

profile of v5, /device:TPU:6, one launch (start us, length us, event | category | flops | bytes accessed | tf_op | source)
XLA Modules:
  0.0 201.3 jit_solution(14571786054779962412)
XLA Ops:
  3.7 5.8 %shard_map.46 = (bf16[32,3840]{1,0:T(8,128)(2,1)S(1)}, bf16[32,3840]{1,0:T(8,128)(2,1)S(1)}, bf16[32,3840]{1,0:T(8,128)(2,1)S(1)}, bf16[32,3840]{1,0:T(8,128)(2,1)S(1)}, bf16[3840,128]{1,0:T(8,128)(2,1)S(1)}) custom-call(s32[3840]{0:T(1024)S(1)} %subtract_select_fusion.place_ref, bf16[64,3840]{1,0:T(8,128)(2,1)S(1)} %bitcast.40), custom_call_target="tpu_custom_call" | custom-call | tf_op jit(solution)/shard_map/pallas_call | solution.py:47
  9.4 15.7 %collective-permute-start = (bf16[32,3840]{1,0:T(8,128)(2,1)S(1)}, bf16[32,3840]{1,0:T(8,128)(2,1)S(1)}, u32[]{:S(2)}, u32[]{:S(2)}) collective-permute-start(bf16[32,3840]{1,0:T(8,128)(2,1)S(1)} %get-tuple-element.17), channel_id=1, source_target_pairs={{0,256},{16,272},{32,288},{48,304},{64,320},{80,336},{96,352},{112... | collective-permute-start | bytes 737288 | tf_op jit(solution)/shard_map/ppermute | solution.py:235
  27.4 3.5 %shard_map.47 = (bf16[3840,1024]{1,0:T(8,128)(2,1)S(1)}, f32[8,128]{1,0:T(8,128)S(1)}) custom-call(s32[1]{0:T(128)S(6)} %copy.9.kept_ref, bf16[3840,128]{1,0:T(8,128)(2,1)S(1)} %get-tuple-element.19.flag_ref, bf16[3840,256]{1,0:T(8,128)(2,1)S(1)} %copy-done.1, bf16[3840,256]{1,0:T(8,128)(2,1)S(1)} %collective-permute-done.1.other_ref), custom_call_target="tpu_custom_call" | custom-call | tf_op jit(solution)/shard_map/pallas_call | solution.py:83
  30.9 3.1 %copy-done = bf16[3840,1024]{1,0:T(8,128)(2,1)} copy-done((bf16[3840,1024]{1,0:T(8,128)(2,1)}, bf16[3840,1024]{1,0:T(8,128)(2,1)S(1)}, u32[]{:S(2)}) %copy-start) | copy-done | bytes 7864344
  34.0 3.3 %collective-permute-start.3 = (bf16[32,3840]{1,0:T(8,128)(2,1)S(1)}, bf16[32,3840]{1,0:T(8,128)(2,1)S(1)}, u32[]{:S(2)}, u32[]{:S(2)}) collective-permute-start(bf16[32,3840]{1,0:T(8,128)(2,1)S(1)} %get-tuple-element.21.refs_0_), channel_id=1, source_target_pairs={{0,8},{1,9},{2,10},{3,11},{4,12},{5,13},{6,14},{7,15},{8,0},{9,1},... | collective-permute-start | bytes 737288 | tf_op jit(solution)/shard_map/ppermute | solution.py:162
  37.3 5.0 %collective-permute-start.4 = (bf16[32,3840]{1,0:T(8,128)(2,1)S(1)}, bf16[32,3840]{1,0:T(8,128)(2,1)S(1)}, u32[]{:S(2)}, u32[]{:S(2)}) collective-permute-start(bf16[32,3840]{1,0:T(8,128)(2,1)S(1)} %get-tuple-element.21.refs_0_), channel_id=1, source_target_pairs={{0,10},{1,11},{2,8},{3,9},{4,14},{5,15},{6,12},{7,13},{8,2},{9,3},... | collective-permute-start | bytes 737288 | tf_op jit(solution)/shard_map/ppermute | solution.py:162
  42.3 10.5 %collective-permute-start.2 = (bf16[32,3840]{1,0:T(8,128)(2,1)S(1)}, bf16[32,3840]{1,0:T(8,128)(2,1)S(1)}, u32[]{:S(2)}, u32[]{:S(2)}) collective-permute-start(bf16[32,3840]{1,0:T(8,128)(2,1)S(1)} %get-tuple-element.23), channel_id=1, source_target_pairs={{0,256},{16,272},{32,288},{48,304},{64,320},{80,336},{96,352},{112... | collective-permute-start | bytes 737288 | tf_op jit(solution)/shard_map/ppermute | solution.py:235
  52.9 2.4 %collective-permute-start.10 = (bf16[32,3840]{1,0:T(8,128)(2,1)S(1)}, bf16[32,3840]{1,0:T(8,128)(2,1)S(1)}, u32[]{:S(2)}, u32[]{:S(2)}) collective-permute-start(bf16[32,3840]{1,0:T(8,128)(2,1)S(1)} %get-tuple-element.21.refs_0_), channel_id=1, source_target_pairs={{0,2},{1,3},{2,0},{3,1},{4,6},{5,7},{6,4},{7,5},{8,10},{9,11},{10,... | collective-permute-start | bytes 737288 | tf_op jit(solution)/shard_map/ppermute | solution.py:162
  55.2 7.9 %collective-permute-start.13 = (bf16[32,3840]{1,0:T(8,128)(2,1)S(1)}, bf16[32,3840]{1,0:T(8,128)(2,1)S(1)}, u32[]{:S(2)}, u32[]{:S(2)}) collective-permute-start(bf16[32,3840]{1,0:T(8,128)(2,1)S(1)} %get-tuple-element.21.refs_0_), channel_id=1, source_target_pairs={{0,14},{1,15},{2,12},{3,13},{4,2},{5,3},{6,0},{7,1},{8,6},{9,7},{1... | collective-permute-start | bytes 737288 | tf_op jit(solution)/shard_map/ppermute | solution.py:162
  63.2 4.0 %collective-permute-start.15 = (bf16[32,3840]{1,0:T(8,128)(2,1)S(1)}, bf16[32,3840]{1,0:T(8,128)(2,1)S(1)}, u32[]{:S(2)}, u32[]{:S(2)}) collective-permute-start(bf16[32,3840]{1,0:T(8,128)(2,1)S(1)} %get-tuple-element.21.refs_0_), channel_id=1, source_target_pairs={{0,6},{1,7},{2,4},{3,5},{4,10},{5,11},{6,8},{7,9},{8,14},{9,15},{1... | collective-permute-start | bytes 737288 | tf_op jit(solution)/shard_map/ppermute | solution.py:162
  67.2 2.7 %collective-permute-start.5 = (bf16[32,3840]{1,0:T(8,128)(2,1)S(1)}, bf16[32,3840]{1,0:T(8,128)(2,1)S(1)}, u32[]{:S(2)}, u32[]{:S(2)}) collective-permute-start(bf16[32,3840]{1,0:T(8,128)(2,1)S(1)} %get-tuple-element.21.refs_0_), channel_id=1, source_target_pairs={{0,12},{1,13},{2,14},{3,15},{4,0},{5,1},{6,2},{7,3},{8,4},{9,5},{1... | collective-permute-start | bytes 737288 | tf_op jit(solution)/shard_map/ppermute | solution.py:162
  70.0 3.1 %collective-permute-start.11 = (bf16[32,3840]{1,0:T(8,128)(2,1)S(1)}, bf16[32,3840]{1,0:T(8,128)(2,1)S(1)}, u32[]{:S(2)}, u32[]{:S(2)}) collective-permute-start(bf16[32,3840]{1,0:T(8,128)(2,1)S(1)} %shard_map.49.refs_1_), channel_id=1, source_target_pairs={{0,2},{1,3},{2,0},{3,1},{4,6},{5,7},{6,4},{7,5},{8,10},{9,11},{10,... | collective-permute-start | bytes 737288 | tf_op jit(solution)/shard_map/ppermute | solution.py:162
  73.1 7.2 %collective-permute-start.6 = (bf16[32,3840]{1,0:T(8,128)(2,1)S(1)}, bf16[32,3840]{1,0:T(8,128)(2,1)S(1)}, u32[]{:S(2)}, u32[]{:S(2)}) collective-permute-start(bf16[32,3840]{1,0:T(8,128)(2,1)S(1)} %shard_map.49.refs_1_), channel_id=1, source_target_pairs={{0,12},{1,13},{2,14},{3,15},{4,0},{5,1},{6,2},{7,3},{8,4},{9,5},{1... | collective-permute-start | bytes 737288 | tf_op jit(solution)/shard_map/ppermute | solution.py:162
  80.4 4.3 %collective-permute-start.8 = (bf16[32,3840]{1,0:T(8,128)(2,1)S(1)}, bf16[32,3840]{1,0:T(8,128)(2,1)S(1)}, u32[]{:S(2)}, u32[]{:S(2)}) collective-permute-start(bf16[32,3840]{1,0:T(8,128)(2,1)S(1)} %shard_map.49.refs_1_), channel_id=1, source_target_pairs={{0,4},{1,5},{2,6},{3,7},{4,8},{5,9},{6,10},{7,11},{8,12},{9,13},{1... | collective-permute-start | bytes 737288 | tf_op jit(solution)/shard_map/ppermute | solution.py:162
  84.7 3.9 %collective-permute-start.7 = (bf16[32,3840]{1,0:T(8,128)(2,1)S(1)}, bf16[32,3840]{1,0:T(8,128)(2,1)S(1)}, u32[]{:S(2)}, u32[]{:S(2)}) collective-permute-start(bf16[32,3840]{1,0:T(8,128)(2,1)S(1)} %get-tuple-element.21.refs_0_), channel_id=1, source_target_pairs={{0,4},{1,5},{2,6},{3,7},{4,8},{5,9},{6,10},{7,11},{8,12},{9,13},{1... | collective-permute-start | bytes 737288 | tf_op jit(solution)/shard_map/ppermute | solution.py:162
  90.6 5.4 %collective-permute-start.12 = (bf16[32,3840]{1,0:T(8,128)(2,1)S(1)}, bf16[32,3840]{1,0:T(8,128)(2,1)S(1)}, u32[]{:S(2)}, u32[]{:S(2)}) collective-permute-start(bf16[32,3840]{1,0:T(8,128)(2,1)S(1)} %collective-permute-done.11.refs_9_), channel_id=1, source_target_pairs={{0,8},{1,9},{2,10},{3,11},{4,12},{5,13},{6,14},{7,15},{8,0},{9,1},... | collective-permute-start | bytes 737288 | tf_op jit(solution)/shard_map/ppermute | solution.py:162
  96.0 4.4 %collective-permute-start.14 = (bf16[32,3840]{1,0:T(8,128)(2,1)S(1)}, bf16[32,3840]{1,0:T(8,128)(2,1)}, u32[]{:S(2)}, u32[]{:S(2)}) collective-permute-start(bf16[32,3840]{1,0:T(8,128)(2,1)S(1)} %collective-permute-done.6.refs_3_), channel_id=1, source_target_pairs={{0,2},{1,3},{2,0},{3,1},{4,6},{5,7},{6,4},{7,5},{8,10},{9,11},{10,... | collective-permute-start | bytes 737288 | tf_op jit(solution)/shard_map/ppermute | solution.py:162
  102.4 2.3 %collective-permute-done.14.refs_13_ = bf16[32,3840]{1,0:T(8,128)(2,1)} collective-permute-done((bf16[32,3840]{1,0:T(8,128)(2,1)S(1)}, bf16[32,3840]{1,0:T(8,128)(2,1)}, u32[]{:S(2)}, u32[]{:S(2)}) %collective-permute-start.14) | collective-permute-done | bytes 245792 | tf_op jit(solution)/shard_map/ppermute | solution.py:162
  104.7 3.9 %collective-permute-done.16.refs_15_ = bf16[32,3840]{1,0:T(8,128)(2,1)} collective-permute-done((bf16[32,3840]{1,0:T(8,128)(2,1)S(1)}, bf16[32,3840]{1,0:T(8,128)(2,1)}, u32[]{:S(2)}, u32[]{:S(2)}) %collective-permute-start.16) | collective-permute-done | bytes 245792 | tf_op jit(solution)/shard_map/ppermute | solution.py:162
  108.6 7.0 %shard_map.50 = (f32[8,64,512]{2,1,0:T(8,128)S(1)}, f32[8,64,512]{2,1,0:T(8,128)S(1)}) custom-call(bf16[32,3840]{1,0:T(8,128)(2,1)S(1)} %get-tuple-element.21.refs_0_, bf16[32,3840]{1,0:T(8,128)(2,1)S(1)} %shard_map.49.refs_1_, bf16[32,3840]{1,0:T(8,128)(2,1)S(1)} %collective-permute-done.5.refs_2_, bf16[32,3840]{1,0:T(8,128)(2,1)S(1)} %collective-permute-done.6.refs_3_, ...), custom_call_target="tpu_custom_call" | custom-call | tf_op jit(solution)/shard_map/pallas_call | solution.py:142
  115.6 10.4 %collective-permute-start.17 = (f32[64,512]{1,0:T(8,128)S(1)}, f32[64,512]{1,0:T(8,128)S(1)}, u32[]{:S(2)}, u32[]{:S(2)}) collective-permute-start(f32[64,512]{1,0:T(8,128)S(1)} %slice_bitcast_fusion.1), channel_id=1, source_target_pairs={{0,32},{1,481},{2,34},{3,483},{4,36},{5,485},{6,38},{7,487},{8,40}... | collective-permute-start | bytes 393224 | tf_op jit(solution)/shard_map/ppermute | solution.py:172
  129.1 8.2 %collective-permute-start.18 = (f32[64,512]{1,0:T(8,128)S(1)}, f32[64,512]{1,0:T(8,128)S(1)}, u32[]{:S(2)}, u32[]{:S(2)}) collective-permute-start(f32[64,512]{1,0:T(8,128)S(1)} %bitcast_add_fusion.7), channel_id=1, source_target_pairs={{0,480},{1,33},{2,482},{3,35},{4,484},{5,37},{6,486},{7,39},{8,488... | collective-permute-start | bytes 393224 | tf_op jit(solution)/shard_map/ppermute | solution.py:172
  137.4 3.9 %collective-permute-start.26 = (f32[64,512]{1,0:T(8,128)S(1)}, f32[64,512]{1,0:T(8,128)S(1)}, u32[]{:S(2)}, u32[]{:S(2)}) collective-permute-start(f32[64,512]{1,0:T(8,128)S(1)} %bitcast_add_fusion), channel_id=1, source_target_pairs={{0,480},{1,33},{2,482},{3,35},{4,484},{5,37},{6,486},{7,39},{8,488... | collective-permute-start | bytes 393224 | tf_op jit(solution)/shard_map/ppermute | solution.py:172
  143.3 2.2 %collective-permute-done.26 = f32[64,512]{1,0:T(8,128)S(1)} collective-permute-done((f32[64,512]{1,0:T(8,128)S(1)}, f32[64,512]{1,0:T(8,128)S(1)}, u32[]{:S(2)}, u32[]{:S(2)}) %collective-permute-start.26) | collective-permute-done | bytes 131104 | tf_op jit(solution)/shard_map/ppermute | solution.py:172
  149.2 3.5 %collective-permute-start.20 = (f32[64,512]{1,0:T(8,128)S(1)}, f32[64,512]{1,0:T(8,128)S(1)}, u32[]{:S(2)}, u32[]{:S(2)}) collective-permute-start(f32[64,512]{1,0:T(8,128)S(1)} %bitcast_add_fusion.9), channel_id=1, source_target_pairs={{0,480},{1,33},{2,482},{3,35},{4,484},{5,37},{6,486},{7,39},{8,488... | collective-permute-start | bytes 393224 | tf_op jit(solution)/shard_map/ppermute | solution.py:172
  153.2 4.9 %collective-permute-start.28 = (f32[64,512]{1,0:T(8,128)S(1)}, f32[64,512]{1,0:T(8,128)S(1)}, u32[]{:S(2)}, u32[]{:S(2)}) collective-permute-start(f32[64,512]{1,0:T(8,128)S(1)} %bitcast_add_fusion.2), channel_id=1, source_target_pairs={{0,480},{1,33},{2,482},{3,35},{4,484},{5,37},{6,486},{7,39},{8,488... | collective-permute-start | bytes 393224 | tf_op jit(solution)/shard_map/ppermute | solution.py:172
  165.2 4.2 %collective-permute-start.22 = (f32[64,512]{1,0:T(8,128)S(1)}, f32[64,512]{1,0:T(8,128)S(1)}, u32[]{:S(2)}, u32[]{:S(2)}) collective-permute-start(f32[64,512]{1,0:T(8,128)S(1)} %bitcast_add_fusion.11), channel_id=1, source_target_pairs={{0,480},{1,33},{2,482},{3,35},{4,484},{5,37},{6,486},{7,39},{8,488... | collective-permute-start | bytes 393224 | tf_op jit(solution)/shard_map/ppermute | solution.py:172
  169.5 4.1 %collective-permute-start.30 = (f32[64,512]{1,0:T(8,128)S(1)}, f32[64,512]{1,0:T(8,128)S(1)}, u32[]{:S(2)}, u32[]{:S(2)}) collective-permute-start(f32[64,512]{1,0:T(8,128)S(1)} %bitcast_add_fusion.4), channel_id=1, source_target_pairs={{0,480},{1,33},{2,482},{3,35},{4,484},{5,37},{6,486},{7,39},{8,488... | collective-permute-start | bytes 393224 | tf_op jit(solution)/shard_map/ppermute | solution.py:172
  180.5 3.9 %collective-permute-done.31 = f32[64,512]{1,0:T(8,128)S(1)} collective-permute-done((f32[64,512]{1,0:T(8,128)S(1)}, f32[64,512]{1,0:T(8,128)S(1)}, u32[]{:S(2)}, u32[]{:S(2)}) %collective-permute-start.31) | collective-permute-done | bytes 131104 | tf_op jit(solution)/shard_map/ppermute | solution.py:172
  187.2 5.8 %collective-permute-start.33 = (f32[32,512]{1,0:T(8,128)S(1)}, f32[32,512]{1,0:T(8,128)S(1)}, u32[]{:S(2)}, u32[]{:S(2)}) collective-permute-start(f32[32,512]{1,0:T(8,128)S(1)} %get-tuple-element.27), channel_id=1, source_target_pairs={{0,17},{1,49},{2,19},{3,51},{4,21},{5,53},{6,23},{7,55},{8,25},{9,... | collective-permute-start | bytes 196616 | tf_op jit(solution)/shard_map/ppermute | solution.py:172
  193.0 2.3 %collective-permute-start.34 = (f32[32,512]{1,0:T(8,128)S(1)}, f32[32,512]{1,0:T(8,128)S(1)}, u32[]{:S(2)}, u32[]{:S(2)}) collective-permute-start(f32[32,512]{1,0:T(8,128)S(1)} %get-tuple-element.30), channel_id=1, source_target_pairs={{0,16},{1,32},{2,18},{3,34},{4,20},{5,36},{6,22},{7,38},{8,24},{9,... | collective-permute-start | bytes 196616 | tf_op jit(solution)/shard_map/ppermute | solution.py:172
  197.0 3.7 %collective-permute-done.34 = f32[32,512]{1,0:T(8,128)S(1)} collective-permute-done((f32[32,512]{1,0:T(8,128)S(1)}, f32[32,512]{1,0:T(8,128)S(1)}, u32[]{:S(2)}, u32[]{:S(2)}) %collective-permute-start.34) | collective-permute-done | bytes 65568 | tf_op jit(solution)/shard_map/ppermute | solution.py:172
  (69 shorter events, 37.5 us)
Async XLA Ops:
  0.0 25.8 %collective-permute-start.1 = (bf16[3840,256]{1,0:T(8,128)(2,1)}, bf16[3840,256]{1,0:T(8,128)(2,1)S(1)}, u32[]{:S(2)}, u32[]{:S(2)}) collective-permute-start(bf16[3840,256]{1,0:T(8,128)(2,1)} %own_ref.1), channel_id=1, source_target_pairs={{0,1},{1,0},{2,3},{3,2},{4,5},{5,4},{6,7},{7,6},{8,9},{9,8},{10,11... | collective-permute-start | bytes 5898248 | tf_op jit(solution)/shard_map/ppermute | solution.py:162
  9.4 24.5 %collective-permute-start = (bf16[32,3840]{1,0:T(8,128)(2,1)S(1)}, bf16[32,3840]{1,0:T(8,128)(2,1)S(1)}, u32[]{:S(2)}, u32[]{:S(2)}) collective-permute-start(bf16[32,3840]{1,0:T(8,128)(2,1)S(1)} %get-tuple-element.17), channel_id=1, source_target_pairs={{0,256},{16,272},{32,288},{48,304},{64,320},{80,336},{96,352},{112... | collective-permute-start | bytes 737288 | tf_op jit(solution)/shard_map/ppermute | solution.py:235
  34.0 29.2 %collective-permute-start.3 = (bf16[32,3840]{1,0:T(8,128)(2,1)S(1)}, bf16[32,3840]{1,0:T(8,128)(2,1)S(1)}, u32[]{:S(2)}, u32[]{:S(2)}) collective-permute-start(bf16[32,3840]{1,0:T(8,128)(2,1)S(1)} %get-tuple-element.21.refs_0_), channel_id=1, source_target_pairs={{0,8},{1,9},{2,10},{3,11},{4,12},{5,13},{6,14},{7,15},{8,0},{9,1},... | collective-permute-start | bytes 737288 | tf_op jit(solution)/shard_map/ppermute | solution.py:162
  37.3 29.9 %collective-permute-start.4 = (bf16[32,3840]{1,0:T(8,128)(2,1)S(1)}, bf16[32,3840]{1,0:T(8,128)(2,1)S(1)}, u32[]{:S(2)}, u32[]{:S(2)}) collective-permute-start(bf16[32,3840]{1,0:T(8,128)(2,1)S(1)} %get-tuple-element.21.refs_0_), channel_id=1, source_target_pairs={{0,10},{1,11},{2,8},{3,9},{4,14},{5,15},{6,12},{7,13},{8,2},{9,3},... | collective-permute-start | bytes 737288 | tf_op jit(solution)/shard_map/ppermute | solution.py:162
  42.3 27.6 %collective-permute-start.2 = (bf16[32,3840]{1,0:T(8,128)(2,1)S(1)}, bf16[32,3840]{1,0:T(8,128)(2,1)S(1)}, u32[]{:S(2)}, u32[]{:S(2)}) collective-permute-start(bf16[32,3840]{1,0:T(8,128)(2,1)S(1)} %get-tuple-element.23), channel_id=1, source_target_pairs={{0,256},{16,272},{32,288},{48,304},{64,320},{80,336},{96,352},{112... | collective-permute-start | bytes 737288 | tf_op jit(solution)/shard_map/ppermute | solution.py:235
  52.9 20.3 %collective-permute-start.10 = (bf16[32,3840]{1,0:T(8,128)(2,1)S(1)}, bf16[32,3840]{1,0:T(8,128)(2,1)S(1)}, u32[]{:S(2)}, u32[]{:S(2)}) collective-permute-start(bf16[32,3840]{1,0:T(8,128)(2,1)S(1)} %get-tuple-element.21.refs_0_), channel_id=1, source_target_pairs={{0,2},{1,3},{2,0},{3,1},{4,6},{5,7},{6,4},{7,5},{8,10},{9,11},{10,... | collective-permute-start | bytes 737288 | tf_op jit(solution)/shard_map/ppermute | solution.py:162
  55.2 25.2 %collective-permute-start.13 = (bf16[32,3840]{1,0:T(8,128)(2,1)S(1)}, bf16[32,3840]{1,0:T(8,128)(2,1)S(1)}, u32[]{:S(2)}, u32[]{:S(2)}) collective-permute-start(bf16[32,3840]{1,0:T(8,128)(2,1)S(1)} %get-tuple-element.21.refs_0_), channel_id=1, source_target_pairs={{0,14},{1,15},{2,12},{3,13},{4,2},{5,3},{6,0},{7,1},{8,6},{9,7},{1... | collective-permute-start | bytes 737288 | tf_op jit(solution)/shard_map/ppermute | solution.py:162
  63.2 21.5 %collective-permute-start.15 = (bf16[32,3840]{1,0:T(8,128)(2,1)S(1)}, bf16[32,3840]{1,0:T(8,128)(2,1)S(1)}, u32[]{:S(2)}, u32[]{:S(2)}) collective-permute-start(bf16[32,3840]{1,0:T(8,128)(2,1)S(1)} %get-tuple-element.21.refs_0_), channel_id=1, source_target_pairs={{0,6},{1,7},{2,4},{3,5},{4,10},{5,11},{6,8},{7,9},{8,14},{9,15},{1... | collective-permute-start | bytes 737288 | tf_op jit(solution)/shard_map/ppermute | solution.py:162
  67.2 21.4 %collective-permute-start.5 = (bf16[32,3840]{1,0:T(8,128)(2,1)S(1)}, bf16[32,3840]{1,0:T(8,128)(2,1)S(1)}, u32[]{:S(2)}, u32[]{:S(2)}) collective-permute-start(bf16[32,3840]{1,0:T(8,128)(2,1)S(1)} %get-tuple-element.21.refs_0_), channel_id=1, source_target_pairs={{0,12},{1,13},{2,14},{3,15},{4,0},{5,1},{6,2},{7,3},{8,4},{9,5},{1... | collective-permute-start | bytes 737288 | tf_op jit(solution)/shard_map/ppermute | solution.py:162
  70.0 20.6 %collective-permute-start.11 = (bf16[32,3840]{1,0:T(8,128)(2,1)S(1)}, bf16[32,3840]{1,0:T(8,128)(2,1)S(1)}, u32[]{:S(2)}, u32[]{:S(2)}) collective-permute-start(bf16[32,3840]{1,0:T(8,128)(2,1)S(1)} %shard_map.49.refs_1_), channel_id=1, source_target_pairs={{0,2},{1,3},{2,0},{3,1},{4,6},{5,7},{6,4},{7,5},{8,10},{9,11},{10,... | collective-permute-start | bytes 737288 | tf_op jit(solution)/shard_map/ppermute | solution.py:162
  73.1 22.9 %collective-permute-start.6 = (bf16[32,3840]{1,0:T(8,128)(2,1)S(1)}, bf16[32,3840]{1,0:T(8,128)(2,1)S(1)}, u32[]{:S(2)}, u32[]{:S(2)}) collective-permute-start(bf16[32,3840]{1,0:T(8,128)(2,1)S(1)} %shard_map.49.refs_1_), channel_id=1, source_target_pairs={{0,12},{1,13},{2,14},{3,15},{4,0},{5,1},{6,2},{7,3},{8,4},{9,5},{1... | collective-permute-start | bytes 737288 | tf_op jit(solution)/shard_map/ppermute | solution.py:162
  80.4 20.0 %collective-permute-start.8 = (bf16[32,3840]{1,0:T(8,128)(2,1)S(1)}, bf16[32,3840]{1,0:T(8,128)(2,1)S(1)}, u32[]{:S(2)}, u32[]{:S(2)}) collective-permute-start(bf16[32,3840]{1,0:T(8,128)(2,1)S(1)} %shard_map.49.refs_1_), channel_id=1, source_target_pairs={{0,4},{1,5},{2,6},{3,7},{4,8},{5,9},{6,10},{7,11},{8,12},{9,13},{1... | collective-permute-start | bytes 737288 | tf_op jit(solution)/shard_map/ppermute | solution.py:162
  84.7 17.7 %collective-permute-start.7 = (bf16[32,3840]{1,0:T(8,128)(2,1)S(1)}, bf16[32,3840]{1,0:T(8,128)(2,1)S(1)}, u32[]{:S(2)}, u32[]{:S(2)}) collective-permute-start(bf16[32,3840]{1,0:T(8,128)(2,1)S(1)} %get-tuple-element.21.refs_0_), channel_id=1, source_target_pairs={{0,4},{1,5},{2,6},{3,7},{4,8},{5,9},{6,10},{7,11},{8,12},{9,13},{1... | collective-permute-start | bytes 737288 | tf_op jit(solution)/shard_map/ppermute | solution.py:162
  88.6 13.8 %collective-permute-start.9 = (bf16[32,3840]{1,0:T(8,128)(2,1)S(1)}, bf16[32,3840]{1,0:T(8,128)(2,1)S(1)}, u32[]{:S(2)}, u32[]{:S(2)}) collective-permute-start(bf16[32,3840]{1,0:T(8,128)(2,1)S(1)} %shard_map.49.refs_1_), channel_id=1, source_target_pairs={{0,8},{1,9},{2,10},{3,11},{4,12},{5,13},{6,14},{7,15},{8,0},{9,1},... | collective-permute-start | bytes 737288 | tf_op jit(solution)/shard_map/ppermute | solution.py:162
  90.6 11.9 %collective-permute-start.12 = (bf16[32,3840]{1,0:T(8,128)(2,1)S(1)}, bf16[32,3840]{1,0:T(8,128)(2,1)S(1)}, u32[]{:S(2)}, u32[]{:S(2)}) collective-permute-start(bf16[32,3840]{1,0:T(8,128)(2,1)S(1)} %collective-permute-done.11.refs_9_), channel_id=1, source_target_pairs={{0,8},{1,9},{2,10},{3,11},{4,12},{5,13},{6,14},{7,15},{8,0},{9,1},... | collective-permute-start | bytes 737288 | tf_op jit(solution)/shard_map/ppermute | solution.py:162
  96.0 8.7 %collective-permute-start.14 = (bf16[32,3840]{1,0:T(8,128)(2,1)S(1)}, bf16[32,3840]{1,0:T(8,128)(2,1)}, u32[]{:S(2)}, u32[]{:S(2)}) collective-permute-start(bf16[32,3840]{1,0:T(8,128)(2,1)S(1)} %collective-permute-done.6.refs_3_), channel_id=1, source_target_pairs={{0,2},{1,3},{2,0},{3,1},{4,6},{5,7},{6,4},{7,5},{8,10},{9,11},{10,... | collective-permute-start | bytes 737288 | tf_op jit(solution)/shard_map/ppermute | solution.py:162
  100.4 8.2 %collective-permute-start.16 = (bf16[32,3840]{1,0:T(8,128)(2,1)S(1)}, bf16[32,3840]{1,0:T(8,128)(2,1)}, u32[]{:S(2)}, u32[]{:S(2)}) collective-permute-start(bf16[32,3840]{1,0:T(8,128)(2,1)S(1)} %collective-permute-done.8.refs_5_), channel_id=1, source_target_pairs={{0,2},{1,3},{2,0},{3,1},{4,6},{5,7},{6,4},{7,5},{8,10},{9,11},{10,... | collective-permute-start | bytes 737288 | tf_op jit(solution)/shard_map/ppermute | solution.py:162
  115.6 13.5 %collective-permute-start.17 = (f32[64,512]{1,0:T(8,128)S(1)}, f32[64,512]{1,0:T(8,128)S(1)}, u32[]{:S(2)}, u32[]{:S(2)}) collective-permute-start(f32[64,512]{1,0:T(8,128)S(1)} %slice_bitcast_fusion.1), channel_id=1, source_target_pairs={{0,32},{1,481},{2,34},{3,483},{4,36},{5,485},{6,38},{7,487},{8,40}... | collective-permute-start | bytes 393224 | tf_op jit(solution)/shard_map/ppermute | solution.py:172
  126.0 11.3 %collective-permute-start.25 = (f32[64,512]{1,0:T(8,128)S(1)}, f32[64,512]{1,0:T(8,128)S(1)}, u32[]{:S(2)}, u32[]{:S(2)}) collective-permute-start(f32[64,512]{1,0:T(8,128)S(1)} %slice_bitcast_fusion), channel_id=1, source_target_pairs={{0,32},{1,481},{2,34},{3,483},{4,36},{5,485},{6,38},{7,487},{8,40}... | collective-permute-start | bytes 393224 | tf_op jit(solution)/shard_map/ppermute | solution.py:172
  129.1 12.2 %collective-permute-start.18 = (f32[64,512]{1,0:T(8,128)S(1)}, f32[64,512]{1,0:T(8,128)S(1)}, u32[]{:S(2)}, u32[]{:S(2)}) collective-permute-start(f32[64,512]{1,0:T(8,128)S(1)} %bitcast_add_fusion.7), channel_id=1, source_target_pairs={{0,480},{1,33},{2,482},{3,35},{4,484},{5,37},{6,486},{7,39},{8,488... | collective-permute-start | bytes 393224 | tf_op jit(solution)/shard_map/ppermute | solution.py:172
  137.4 8.1 %collective-permute-start.26 = (f32[64,512]{1,0:T(8,128)S(1)}, f32[64,512]{1,0:T(8,128)S(1)}, u32[]{:S(2)}, u32[]{:S(2)}) collective-permute-start(f32[64,512]{1,0:T(8,128)S(1)} %bitcast_add_fusion), channel_id=1, source_target_pairs={{0,480},{1,33},{2,482},{3,35},{4,484},{5,37},{6,486},{7,39},{8,488... | collective-permute-start | bytes 393224 | tf_op jit(solution)/shard_map/ppermute | solution.py:172
  141.4 7.8 %collective-permute-start.19 = (f32[64,512]{1,0:T(8,128)S(1)}, f32[64,512]{1,0:T(8,128)S(1)}, u32[]{:S(2)}, u32[]{:S(2)}) collective-permute-start(f32[64,512]{1,0:T(8,128)S(1)} %bitcast_add_fusion.8), channel_id=1, source_target_pairs={{0,32},{1,481},{2,34},{3,483},{4,36},{5,485},{6,38},{7,487},{8,40}... | collective-permute-start | bytes 393224 | tf_op jit(solution)/shard_map/ppermute | solution.py:172
  145.5 7.7 %collective-permute-start.27 = (f32[64,512]{1,0:T(8,128)S(1)}, f32[64,512]{1,0:T(8,128)S(1)}, u32[]{:S(2)}, u32[]{:S(2)}) collective-permute-start(f32[64,512]{1,0:T(8,128)S(1)} %bitcast_add_fusion.1), channel_id=1, source_target_pairs={{0,32},{1,481},{2,34},{3,483},{4,36},{5,485},{6,38},{7,487},{8,40}... | collective-permute-start | bytes 393224 | tf_op jit(solution)/shard_map/ppermute | solution.py:172
  149.2 9.0 %collective-permute-start.20 = (f32[64,512]{1,0:T(8,128)S(1)}, f32[64,512]{1,0:T(8,128)S(1)}, u32[]{:S(2)}, u32[]{:S(2)}) collective-permute-start(f32[64,512]{1,0:T(8,128)S(1)} %bitcast_add_fusion.9), channel_id=1, source_target_pairs={{0,480},{1,33},{2,482},{3,35},{4,484},{5,37},{6,486},{7,39},{8,488... | collective-permute-start | bytes 393224 | tf_op jit(solution)/shard_map/ppermute | solution.py:172
  153.2 8.9 %collective-permute-start.28 = (f32[64,512]{1,0:T(8,128)S(1)}, f32[64,512]{1,0:T(8,128)S(1)}, u32[]{:S(2)}, u32[]{:S(2)}) collective-permute-start(f32[64,512]{1,0:T(8,128)S(1)} %bitcast_add_fusion.2), channel_id=1, source_target_pairs={{0,480},{1,33},{2,482},{3,35},{4,484},{5,37},{6,486},{7,39},{8,488... | collective-permute-start | bytes 393224 | tf_op jit(solution)/shard_map/ppermute | solution.py:172
  162.1 7.3 %collective-permute-start.29 = (f32[64,512]{1,0:T(8,128)S(1)}, f32[64,512]{1,0:T(8,128)S(1)}, u32[]{:S(2)}, u32[]{:S(2)}) collective-permute-start(f32[64,512]{1,0:T(8,128)S(1)} %bitcast_add_fusion.3), channel_id=1, source_target_pairs={{0,32},{1,481},{2,34},{3,483},{4,36},{5,485},{6,38},{7,487},{8,40}... | collective-permute-start | bytes 393224 | tf_op jit(solution)/shard_map/ppermute | solution.py:172
  165.2 8.3 %collective-permute-start.22 = (f32[64,512]{1,0:T(8,128)S(1)}, f32[64,512]{1,0:T(8,128)S(1)}, u32[]{:S(2)}, u32[]{:S(2)}) collective-permute-start(f32[64,512]{1,0:T(8,128)S(1)} %bitcast_add_fusion.11), channel_id=1, source_target_pairs={{0,480},{1,33},{2,482},{3,35},{4,484},{5,37},{6,486},{7,39},{8,488... | collective-permute-start | bytes 393224 | tf_op jit(solution)/shard_map/ppermute | solution.py:172
  169.5 8.1 %collective-permute-start.30 = (f32[64,512]{1,0:T(8,128)S(1)}, f32[64,512]{1,0:T(8,128)S(1)}, u32[]{:S(2)}, u32[]{:S(2)}) collective-permute-start(f32[64,512]{1,0:T(8,128)S(1)} %bitcast_add_fusion.4), channel_id=1, source_target_pairs={{0,480},{1,33},{2,482},{3,35},{4,484},{5,37},{6,486},{7,39},{8,488... | collective-permute-start | bytes 393224 | tf_op jit(solution)/shard_map/ppermute | solution.py:172
  184.5 10.8 %collective-permute-start.24 = (f32[32,512]{1,0:T(8,128)S(1)}, f32[32,512]{1,0:T(8,128)S(1)}, u32[]{:S(2)}, u32[]{:S(2)}) collective-permute-start(f32[32,512]{1,0:T(8,128)S(1)} %get-tuple-element.28), channel_id=1, source_target_pairs={{1,48},{3,50},{5,52},{7,54},{9,56},{11,58},{13,60},{15,62},{17,32}... | collective-permute-start | bytes 196616 | tf_op jit(solution)/shard_map/ppermute | solution.py:172
  185.2 10.1 %collective-permute-start.32 = (f32[32,512]{1,0:T(8,128)S(1)}, f32[32,512]{1,0:T(8,128)S(1)}, u32[]{:S(2)}, u32[]{:S(2)}) collective-permute-start(f32[32,512]{1,0:T(8,128)S(1)} %get-tuple-element.29), channel_id=1, source_target_pairs={{0,1},{1,33},{2,3},{3,35},{4,5},{5,37},{6,7},{7,39},{8,9},{9,41},{... | collective-permute-start | bytes 196616 | tf_op jit(solution)/shard_map/ppermute | solution.py:172
  187.2 9.8 %collective-permute-start.33 = (f32[32,512]{1,0:T(8,128)S(1)}, f32[32,512]{1,0:T(8,128)S(1)}, u32[]{:S(2)}, u32[]{:S(2)}) collective-permute-start(f32[32,512]{1,0:T(8,128)S(1)} %get-tuple-element.27), channel_id=1, source_target_pairs={{0,17},{1,49},{2,19},{3,51},{4,21},{5,53},{6,23},{7,55},{8,25},{9,... | collective-permute-start | bytes 196616 | tf_op jit(solution)/shard_map/ppermute | solution.py:172
  193.0 7.7 %collective-permute-start.34 = (f32[32,512]{1,0:T(8,128)S(1)}, f32[32,512]{1,0:T(8,128)S(1)}, u32[]{:S(2)}, u32[]{:S(2)}) collective-permute-start(f32[32,512]{1,0:T(8,128)S(1)} %get-tuple-element.30), channel_id=1, source_target_pairs={{0,16},{1,32},{2,18},{3,34},{4,20},{5,36},{6,22},{7,38},{8,24},{9,... | collective-permute-start | bytes 196616 | tf_op jit(solution)/shard_map/ppermute | solution.py:172
  (6 other events, 26.3 us)

commit v6 on v4

--- a/solution.py
+++ b/solution.py
@@ -108,9 +108,9 @@
 
 
 def product_kernel(*refs):
-    count = len(refs) - 6
-    pieces, s_hbm, outs = refs[:count], refs[count], refs[count + 1 : count + 3]
-    total, s_ref, sems = refs[count + 3 :]
+    count = len(refs) - 5
+    pieces = refs[:count]
+    s_hbm, out_ref, total, s_ref, sems = refs[count:]
     z, c = lax.axis_index("grp") // 2, lax.axis_index("col")
     tiles = s_ref.shape[0] // K_TILE
     spans = [pl.ds(k * K_TILE, K_TILE) for k in range(tiles)]
@@ -127,11 +127,10 @@
             total[...] += term
         else:
             term += total[...]
-    rows, cols = outs[0].shape[1:]
+    rows = out_ref.shape[1]
     for i, place in enumerate(PLACES):
         slot = slot_of(z, c // 4, c // 2 % 2, c % 2, *place)
-        for half in range(2):
-            outs[half][slot] = term[i * rows : (i + 1) * rows, half * cols : (half + 1) * cols]
+        out_ref[slot] = term[i * rows : (i + 1) * rows, :]
 
 
 def product(pieces, s_both):
@@ -141,9 +140,9 @@
     whole = pl.BlockSpec(memory_space=pltpu.VMEM)
     return pl.pallas_call(
         product_kernel,
-        out_shape=[jax.ShapeDtypeStruct((len(PLACES), block_rows, cols // 2), jnp.float32)] * 2,
+        out_shape=jax.ShapeDtypeStruct((len(PLACES), block_rows, cols), jnp.float32),
         in_specs=[whole] * len(pieces) + [pl.BlockSpec(memory_space=pltpu.HBM)],
-        out_specs=[whole] * 2,
+        out_specs=whole,
         scratch_shapes=[
             pltpu.VMEM((len(PLACES) * block_rows, cols), jnp.float32),
             pltpu.VMEM((blk, cols), jnp.bfloat16),
@@ -196,6 +195,21 @@
         out_specs=[whole] * count,
         compiler_params=pltpu.CompilerParams(vmem_limit_bytes=4 * 2**20),
     )(*arrays, after)
+
+
+def add_term_kernel(slot, terms_ref, arrived_ref, after_ref, out_ref):
+    out_ref[...] = terms_ref[slot] + arrived_ref[...]
+
+
+def add_term(terms, slot, arrived, after):
+    whole = pl.BlockSpec(memory_space=pltpu.VMEM)
+    return pl.pallas_call(
+        functools.partial(add_term_kernel, slot),
+        out_shape=jax.ShapeDtypeStruct(arrived.shape, arrived.dtype),
+        in_specs=[whole, whole, pl.BlockSpec(memory_space=pl.ANY)],
+        out_specs=whole,
+        compiler_params=pltpu.CompilerParams(vmem_limit_bytes=4 * 2**20),
+    )(terms, arrived, after)
 
 
 def gather_col(here):
@@ -239,12 +253,15 @@
 
     s_both = pltpu.with_memory_space_constraint(s_both, pltpu.HBM)
     terms = product(pieces, s_both)
-    moving = [term[0] for term in terms]
-    for step in range(1, 8):
-        for half in range(2):
-            moving[half] = terms[half][step] + slice_move(moving[half], functools.partial(exchange, step))
-
-    mine, theirs = moving
+    outer, inner = terms[0], terms[4]
+    for step in range(1, 4):
+        outer = terms[step] + slice_move(outer, functools.partial(exchange, step))
+        inner = slice_move(inner, functools.partial(exchange, step))
+        inner = add_term(terms, 4 + step, inner, outer) if step < 3 else terms[7] + inner
+    inner += slice_move(outer, lambda z, y_hi, c: (z + 4 if (c - z) % 2 else z - 4, y_hi, c))
+
+    half_cols = inner.shape[1] // 2
+    mine, theirs = inner[:, :half_cols], inner[:, half_cols:]
     rows = mine.shape[0] // 2
 
     def part(value, y):

time: 202 us -> 186 us (0.921); the launches traced: 199 us -> 185 us
  starting transfers between devices: 151 us -> 133 us
  waiting for transfers between devices: 22.4 us -> 28.4 us
    ppermute x18 -> x11, starting transfers between devices: 71.1 us -> 52.5 us  [slice_move(): return lax.ppermute(value, ('grp', 'col'), pairs)]
    ppermute x18 -> x11, waiting for transfers between devices: 17.8 us -> 23.9 us  [slice_move(): return lax.ppermute(value, ('grp', 'col'), pairs)]
    pallas_call x1 -> x3, Pallas kernels: 6.95 us -> 5.97 us  [the longest x1 5.89 us: product(): pl.pallas_call(product_kernel, out_shape=jax.ShapeDtypeStruct((len(PLACES...]
  transfers between devices with their start and end apart: 35 -> 28, of which waited for: 12 -> 8; matrix products, arithmetic and copies ran while one was open for 1% -> 0% of each run, Pallas kernels for 5% -> 5%
where the time goes in v6:
time: 186 us; the launch traced here: 185 us
  starting transfers between devices  133 us (72%)
  waiting for transfers between devices  28.4 us (15%)
  Pallas kernels  15.3 us (8%)
  local copies, waits for them, and re-layouts  6.29 us (3%)
    ppermute x15, starting transfers between devices, col_move(): return lax.ppermute(value, 'col', pairs)  54.1 us
    ppermute x11, starting transfers between devices, slice_move(): return lax.ppermute(value, ('grp', 'col'), pairs)  52.5 us
    ppermute x2, starting transfers between devices, per_device(): arrived = lax.ppermute(leaving, 'grp', [(i, i ^ 16) for i in range(32)])  26.2 us
    ppermute x11, waiting for transfers between devices, slice_move(): return lax.ppermute(value, ('grp', 'col'), pairs)  23.9 us
    pallas_call x1, Pallas kernels, product(): pl.pallas_call(product_kernel, out_shape=jax.ShapeDtypeStruct((len(PLACES...  5.89 us
    pallas_call x1, Pallas kernels, scatter_rows(): pl.pallas_call(scatter_kernel, out_shape=[jax.ShapeDtypeStruct((width //...  5.76 us
    unnamed x6, local copies, waits for them, and re-layouts  5.63 us
    ppermute x15, waiting for transfers between devices, col_move(): return lax.ppermute(value, 'col', pairs)  4.58 us
  transfers between devices with their start and end apart: 28, of which 8 were waited for; matrix products, arithmetic and copies ran while one was open for 0% of the time, Pallas kernels for 5%

profile of v6, /device:TPU:6, one launch (start us, length us, event | category | flops | bytes accessed | tf_op | source)
XLA Modules:
  0.0 184.9 jit_solution(5172645253002748589)
XLA Ops:
  3.7 5.8 %shard_map.46 = (bf16[32,3840]{1,0:T(8,128)(2,1)S(1)}, bf16[32,3840]{1,0:T(8,128)(2,1)S(1)}, bf16[32,3840]{1,0:T(8,128)(2,1)S(1)}, bf16[32,3840]{1,0:T(8,128)(2,1)S(1)}, bf16[3840,128]{1,0:T(8,128)(2,1)S(1)}) custom-call(s32[3840]{0:T(1024)S(1)} %subtract_select_fusion.place_ref, bf16[64,3840]{1,0:T(8,128)(2,1)S(1)} %bitcast.30), custom_call_target="tpu_custom_call" | custom-call | tf_op jit(solution)/shard_map/pallas_call | solution.py:47
  9.4 15.7 %collective-permute-start = (bf16[32,3840]{1,0:T(8,128)(2,1)S(1)}, bf16[32,3840]{1,0:T(8,128)(2,1)S(1)}, u32[]{:S(2)}, u32[]{:S(2)}) collective-permute-start(bf16[32,3840]{1,0:T(8,128)(2,1)S(1)} %get-tuple-element.15), channel_id=1, source_target_pairs={{0,256},{16,272},{32,288},{48,304},{64,320},{80,336},{96,352},{112... | collective-permute-start | bytes 737288 | tf_op jit(solution)/shard_map/ppermute | solution.py:245
  27.4 3.5 %shard_map.47 = (bf16[3840,1024]{1,0:T(8,128)(2,1)S(1)}, f32[8,128]{1,0:T(8,128)S(1)}) custom-call(s32[1]{0:T(128)S(6)} %copy.9.kept_ref, bf16[3840,128]{1,0:T(8,128)(2,1)S(1)} %get-tuple-element.17.flag_ref, bf16[3840,256]{1,0:T(8,128)(2,1)S(1)} %copy-done.1, bf16[3840,256]{1,0:T(8,128)(2,1)S(1)} %collective-permute-done.1.other_ref), custom_call_target="tpu_custom_call" | custom-call | tf_op jit(solution)/shard_map/pallas_call | solution.py:83
  30.9 3.1 %copy-done = bf16[3840,1024]{1,0:T(8,128)(2,1)} copy-done((bf16[3840,1024]{1,0:T(8,128)(2,1)}, bf16[3840,1024]{1,0:T(8,128)(2,1)S(1)}, u32[]{:S(2)}) %copy-start) | copy-done | bytes 7864344
  34.0 3.5 %collective-permute-start.3 = (bf16[32,3840]{1,0:T(8,128)(2,1)S(1)}, bf16[32,3840]{1,0:T(8,128)(2,1)S(1)}, u32[]{:S(2)}, u32[]{:S(2)}) collective-permute-start(bf16[32,3840]{1,0:T(8,128)(2,1)S(1)} %get-tuple-element.19.refs_0_), channel_id=1, source_target_pairs={{0,2},{1,3},{2,0},{3,1},{4,6},{5,7},{6,4},{7,5},{8,10},{9,11},{10,... | collective-permute-start | bytes 737288 | tf_op jit(solution)/shard_map/ppermute | solution.py:161
  37.5 2.7 %collective-permute-start.5 = (bf16[32,3840]{1,0:T(8,128)(2,1)S(1)}, bf16[32,3840]{1,0:T(8,128)(2,1)S(1)}, u32[]{:S(2)}, u32[]{:S(2)}) collective-permute-start(bf16[32,3840]{1,0:T(8,128)(2,1)S(1)} %get-tuple-element.19.refs_0_), channel_id=1, source_target_pairs={{0,12},{1,13},{2,14},{3,15},{4,0},{5,1},{6,2},{7,3},{8,4},{9,5},{1... | collective-permute-start | bytes 737288 | tf_op jit(solution)/shard_map/ppermute | solution.py:161
  40.2 10.5 %collective-permute-start.2 = (bf16[32,3840]{1,0:T(8,128)(2,1)S(1)}, bf16[32,3840]{1,0:T(8,128)(2,1)S(1)}, u32[]{:S(2)}, u32[]{:S(2)}) collective-permute-start(bf16[32,3840]{1,0:T(8,128)(2,1)S(1)} %get-tuple-element.21), channel_id=1, source_target_pairs={{0,256},{16,272},{32,288},{48,304},{64,320},{80,336},{96,352},{112... | collective-permute-start | bytes 737288 | tf_op jit(solution)/shard_map/ppermute | solution.py:245
  50.7 9.7 %collective-permute-start.4 = (bf16[32,3840]{1,0:T(8,128)(2,1)S(1)}, bf16[32,3840]{1,0:T(8,128)(2,1)S(1)}, u32[]{:S(2)}, u32[]{:S(2)}) collective-permute-start(bf16[32,3840]{1,0:T(8,128)(2,1)S(1)} %collective-permute-done.3.refs_8_), channel_id=1, source_target_pairs={{0,8},{1,9},{2,10},{3,11},{4,12},{5,13},{6,14},{7,15},{8,0},{9,1},... | collective-permute-start | bytes 737288 | tf_op jit(solution)/shard_map/ppermute | solution.py:161
  60.4 1.9 %collective-permute-start.7 = (bf16[32,3840]{1,0:T(8,128)(2,1)S(1)}, bf16[32,3840]{1,0:T(8,128)(2,1)S(1)}, u32[]{:S(2)}, u32[]{:S(2)}) collective-permute-start(bf16[32,3840]{1,0:T(8,128)(2,1)S(1)} %get-tuple-element.19.refs_0_), channel_id=1, source_target_pairs={{0,4},{1,5},{2,6},{3,7},{4,8},{5,9},{6,10},{7,11},{8,12},{9,13},{1... | collective-permute-start | bytes 737288 | tf_op jit(solution)/shard_map/ppermute | solution.py:161
  62.3 3.4 %collective-permute-start.9 = (bf16[32,3840]{1,0:T(8,128)(2,1)S(1)}, bf16[32,3840]{1,0:T(8,128)(2,1)S(1)}, u32[]{:S(2)}, u32[]{:S(2)}) collective-permute-start(bf16[32,3840]{1,0:T(8,128)(2,1)S(1)} %get-tuple-element.19.refs_0_), channel_id=1, source_target_pairs={{0,8},{1,9},{2,10},{3,11},{4,12},{5,13},{6,14},{7,15},{8,0},{9,1},... | collective-permute-start | bytes 737288 | tf_op jit(solution)/shard_map/ppermute | solution.py:161
  65.7 3.9 %collective-permute-start.13 = (bf16[32,3840]{1,0:T(8,128)(2,1)S(1)}, bf16[32,3840]{1,0:T(8,128)(2,1)S(1)}, u32[]{:S(2)}, u32[]{:S(2)}) collective-permute-start(bf16[32,3840]{1,0:T(8,128)(2,1)S(1)} %collective-permute-done.5.refs_2_), channel_id=1, source_target_pairs={{0,2},{1,3},{2,0},{3,1},{4,6},{5,7},{6,4},{7,5},{8,10},{9,11},{10,... | collective-permute-start | bytes 737288 | tf_op jit(solution)/shard_map/ppermute | solution.py:161
  69.7 1.9 %collective-permute-start.11 = (bf16[32,3840]{1,0:T(8,128)(2,1)S(1)}, bf16[32,3840]{1,0:T(8,128)(2,1)S(1)}, u32[]{:S(2)}, u32[]{:S(2)}) collective-permute-start(bf16[32,3840]{1,0:T(8,128)(2,1)S(1)} %shard_map.49.refs_1_), channel_id=1, source_target_pairs={{0,2},{1,3},{2,0},{3,1},{4,6},{5,7},{6,4},{7,5},{8,10},{9,11},{10,... | collective-permute-start | bytes 737288 | tf_op jit(solution)/shard_map/ppermute | solution.py:161
  71.6 2.5 %collective-permute-start.6 = (bf16[32,3840]{1,0:T(8,128)(2,1)S(1)}, bf16[32,3840]{1,0:T(8,128)(2,1)S(1)}, u32[]{:S(2)}, u32[]{:S(2)}) collective-permute-start(bf16[32,3840]{1,0:T(8,128)(2,1)S(1)} %shard_map.49.refs_1_), channel_id=1, source_target_pairs={{0,12},{1,13},{2,14},{3,15},{4,0},{5,1},{6,2},{7,3},{8,4},{9,5},{1... | collective-permute-start | bytes 737288 | tf_op jit(solution)/shard_map/ppermute | solution.py:161
  74.1 4.6 %collective-permute-start.8 = (bf16[32,3840]{1,0:T(8,128)(2,1)S(1)}, bf16[32,3840]{1,0:T(8,128)(2,1)S(1)}, u32[]{:S(2)}, u32[]{:S(2)}) collective-permute-start(bf16[32,3840]{1,0:T(8,128)(2,1)S(1)} %shard_map.49.refs_1_), channel_id=1, source_target_pairs={{0,4},{1,5},{2,6},{3,7},{4,8},{5,9},{6,10},{7,11},{8,12},{9,13},{1... | collective-permute-start | bytes 737288 | tf_op jit(solution)/shard_map/ppermute | solution.py:161
  78.7 3.9 %collective-permute-start.15 = (bf16[32,3840]{1,0:T(8,128)(2,1)S(1)}, bf16[32,3840]{1,0:T(8,128)(2,1)S(1)}, u32[]{:S(2)}, u32[]{:S(2)}) collective-permute-start(bf16[32,3840]{1,0:T(8,128)(2,1)S(1)} %collective-permute-done.7.refs_4_), channel_id=1, source_target_pairs={{0,2},{1,3},{2,0},{3,1},{4,6},{5,7},{6,4},{7,5},{8,10},{9,11},{10,... | collective-permute-start | bytes 737288 | tf_op jit(solution)/shard_map/ppermute | solution.py:161
  82.7 3.4 %collective-permute-start.10 = (bf16[32,3840]{1,0:T(8,128)(2,1)S(1)}, bf16[32,3840]{1,0:T(8,128)(2,1)S(1)}, u32[]{:S(2)}, u32[]{:S(2)}) collective-permute-start(bf16[32,3840]{1,0:T(8,128)(2,1)S(1)} %shard_map.49.refs_1_), channel_id=1, source_target_pairs={{0,8},{1,9},{2,10},{3,11},{4,12},{5,13},{6,14},{7,15},{8,0},{9,1},... | collective-permute-start | bytes 737288 | tf_op jit(solution)/shard_map/ppermute | solution.py:161
  86.1 4.0 %collective-permute-start.12 = (bf16[32,3840]{1,0:T(8,128)(2,1)S(1)}, bf16[32,3840]{1,0:T(8,128)(2,1)S(1)}, u32[]{:S(2)}, u32[]{:S(2)}) collective-permute-start(bf16[32,3840]{1,0:T(8,128)(2,1)S(1)} %collective-permute-done.11.refs_9_), channel_id=1, source_target_pairs={{0,8},{1,9},{2,10},{3,11},{4,12},{5,13},{6,14},{7,15},{8,0},{9,1},... | collective-permute-start | bytes 737288 | tf_op jit(solution)/shard_map/ppermute | solution.py:161
  90.1 1.9 %collective-permute-start.14 = (bf16[32,3840]{1,0:T(8,128)(2,1)S(1)}, bf16[32,3840]{1,0:T(8,128)(2,1)S(1)}, u32[]{:S(2)}, u32[]{:S(2)}) collective-permute-start(bf16[32,3840]{1,0:T(8,128)(2,1)S(1)} %collective-permute-done.6.refs_3_), channel_id=1, source_target_pairs={{0,2},{1,3},{2,0},{3,1},{4,6},{5,7},{6,4},{7,5},{8,10},{9,11},{10,... | collective-permute-start | bytes 737288 | tf_op jit(solution)/shard_map/ppermute | solution.py:161
  92.0 4.9 %collective-permute-start.16 = (bf16[32,3840]{1,0:T(8,128)(2,1)S(1)}, bf16[32,3840]{1,0:T(8,128)(2,1)S(1)}, u32[]{:S(2)}, u32[]{:S(2)}) collective-permute-start(bf16[32,3840]{1,0:T(8,128)(2,1)S(1)} %collective-permute-done.8.refs_5_), channel_id=1, source_target_pairs={{0,2},{1,3},{2,0},{3,1},{4,6},{5,7},{6,4},{7,5},{8,10},{9,11},{10,... | collective-permute-start | bytes 737288 | tf_op jit(solution)/shard_map/ppermute | solution.py:161
  98.9 2.6 %collective-permute-done.16.refs_15_ = bf16[32,3840]{1,0:T(8,128)(2,1)S(1)} collective-permute-done((bf16[32,3840]{1,0:T(8,128)(2,1)S(1)}, bf16[32,3840]{1,0:T(8,128)(2,1)S(1)}, u32[]{:S(2)}, u32[]{:S(2)}) %collective-permute-start.16) | collective-permute-done | bytes 245792 | tf_op jit(solution)/shard_map/ppermute | solution.py:161
  101.5 5.9 %shard_map.50.terms_ref = f32[8,64,1024]{2,1,0:T(8,128)S(1)} custom-call(bf16[32,3840]{1,0:T(8,128)(2,1)S(1)} %get-tuple-element.19.refs_0_, bf16[32,3840]{1,0:T(8,128)(2,1)S(1)} %shard_map.49.refs_1_, bf16[32,3840]{1,0:T(8,128)(2,1)S(1)} %collective-permute-done.5.refs_2_, bf16[32,3840]{1,0:T(8,128)(2,1)S(1)} %collective-permute-done.6.refs_3_, ...), custom_call_target="tpu_custom_call" | custom-call | tf_op jit(solution)/shard_map/pallas_call | solution.py:141
  107.4 16.0 %collective-permute-start.18 = (f32[64,1024]{1,0:T(8,128)S(1)}, f32[64,1024]{1,0:T(8,128)S(1)}, u32[]{:S(2)}, u32[]{:S(2)}) collective-permute-start(f32[64,1024]{1,0:T(8,128)S(1)} %get-tuple-element.26), channel_id=1, source_target_pairs={{0,32},{1,481},{2,34},{3,483},{4,36},{5,485},{6,38},{7,487},{8,40}... | collective-permute-start | bytes 786440 | tf_op jit(solution)/shard_map/ppermute | solution.py:171
  123.4 1.9 %collective-permute-start.17 = (f32[64,1024]{1,0:T(8,128)S(1)}, f32[64,1024]{1,0:T(8,128)S(1)}, u32[]{:S(2)}, u32[]{:S(2)}) collective-permute-start(f32[64,1024]{1,0:T(8,128)S(1)} %get-tuple-element.25), channel_id=1, source_target_pairs={{0,32},{1,481},{2,34},{3,483},{4,36},{5,485},{6,38},{7,487},{8,40}... | collective-permute-start | bytes 786440 | tf_op jit(solution)/shard_map/ppermute | solution.py:171
  125.4 2.4 %collective-permute-done.18 = f32[64,1024]{1,0:T(8,128)S(1)} collective-permute-done((f32[64,1024]{1,0:T(8,128)S(1)}, f32[64,1024]{1,0:T(8,128)S(1)}, u32[]{:S(2)}, u32[]{:S(2)}) %collective-permute-start.18) | collective-permute-done | bytes 262176 | tf_op jit(solution)/shard_map/ppermute | solution.py:171
  127.8 6.6 %collective-permute-start.20 = (f32[64,1024]{1,0:T(8,128)S(1)}, f32[64,1024]{1,0:T(8,128)S(1)}, u32[]{:S(2)}, u32[]{:S(2)}) collective-permute-start(f32[64,1024]{1,0:T(8,128)S(1)} %fusion.2.after_ref), channel_id=1, source_target_pairs={{0,480},{1,33},{2,482},{3,35},{4,484},{5,37},{6,486},{7,39},{8,488... | collective-permute-start | bytes 786440 | tf_op jit(solution)/shard_map/ppermute | solution.py:171
  134.5 5.5 %collective-permute-start.19 = (f32[64,1024]{1,0:T(8,128)S(1)}, f32[64,1024]{1,0:T(8,128)S(1)}, u32[]{:S(2)}, u32[]{:S(2)}) collective-permute-start(f32[64,1024]{1,0:T(8,128)S(1)} %shard_map.51), channel_id=1, source_target_pairs={{0,480},{1,33},{2,482},{3,35},{4,484},{5,37},{6,486},{7,39},{8,488... | collective-permute-start | bytes 786440 | tf_op jit(solution)/shard_map/ppermute | solution.py:171
  142.0 4.7 %collective-permute-done.19.arrived_ref = f32[64,1024]{1,0:T(8,128)S(1)} collective-permute-done((f32[64,1024]{1,0:T(8,128)S(1)}, f32[64,1024]{1,0:T(8,128)S(1)}, u32[]{:S(2)}, u32[]{:S(2)}) %collective-permute-start.19) | collective-permute-done | bytes 262176 | tf_op jit(solution)/shard_map/ppermute | solution.py:171
  148.8 3.9 %collective-permute-start.23 = (f32[64,1024]{1,0:T(8,128)S(1)}, f32[64,1024]{1,0:T(8,128)S(1)}, u32[]{:S(2)}, u32[]{:S(2)}) collective-permute-start(f32[64,1024]{1,0:T(8,128)S(1)} %fusion), channel_id=1, source_target_pairs={{0,384},{1,129},{2,386},{3,131},{4,388},{5,133},{6,390},{7,135},{8... | collective-permute-start | bytes 786440 | tf_op jit(solution)/shard_map/ppermute | solution.py:171
  152.8 13.3 %collective-permute-done.21 = f32[64,1024]{1,0:T(8,128)S(1)} collective-permute-done((f32[64,1024]{1,0:T(8,128)S(1)}, f32[64,1024]{1,0:T(8,128)S(1)}, u32[]{:S(2)}, u32[]{:S(2)}) %collective-permute-start.21) | collective-permute-done | bytes 262176 | tf_op jit(solution)/shard_map/ppermute | solution.py:171
  166.8 7.1 %collective-permute-start.25 = (f32[32,512]{1,0:T(8,128)S(1)}, f32[32,512]{1,0:T(8,128)S(1)}, u32[]{:S(2)}, u32[]{:S(2)}) collective-permute-start(f32[32,512]{1,0:T(8,128)S(1)} %get-tuple-element.27), channel_id=1, source_target_pairs={{0,1},{1,33},{2,3},{3,35},{4,5},{5,37},{6,7},{7,39},{8,9},{9,41},{... | collective-permute-start | bytes 196616 | tf_op jit(solution)/shard_map/ppermute | solution.py:171
  175.8 5.0 %collective-permute-start.27 = (f32[32,512]{1,0:T(8,128)S(1)}, f32[32,512]{1,0:T(8,128)S(1)}, u32[]{:S(2)}, u32[]{:S(2)}) collective-permute-start(f32[32,512]{1,0:T(8,128)S(1)} %get-tuple-element.28), channel_id=1, source_target_pairs={{0,16},{1,32},{2,18},{3,34},{4,20},{5,36},{6,22},{7,38},{8,24},{9,... | collective-permute-start | bytes 196616 | tf_op jit(solution)/shard_map/ppermute | solution.py:171
  180.9 2.9 %collective-permute-done.26 = f32[32,512]{1,0:T(8,128)S(1)} collective-permute-done((f32[32,512]{1,0:T(8,128)S(1)}, f32[32,512]{1,0:T(8,128)S(1)}, u32[]{:S(2)}, u32[]{:S(2)}) %collective-permute-start.26) | collective-permute-done | bytes 65568 | tf_op jit(solution)/shard_map/ppermute | solution.py:171
  (46 shorter events, 15.2 us)
Async XLA Ops:
  0.0 25.8 %collective-permute-start.1 = (bf16[3840,256]{1,0:T(8,128)(2,1)}, bf16[3840,256]{1,0:T(8,128)(2,1)S(1)}, u32[]{:S(2)}, u32[]{:S(2)}) collective-permute-start(bf16[3840,256]{1,0:T(8,128)(2,1)} %own_ref.1), channel_id=1, source_target_pairs={{0,1},{1,0},{2,3},{3,2},{4,5},{5,4},{6,7},{7,6},{8,9},{9,8},{10,11... | collective-permute-start | bytes 5898248 | tf_op jit(solution)/shard_map/ppermute | solution.py:161
  2.7 1.0 copy-start.2
  9.4 24.5 %collective-permute-start = (bf16[32,3840]{1,0:T(8,128)(2,1)S(1)}, bf16[32,3840]{1,0:T(8,128)(2,1)S(1)}, u32[]{:S(2)}, u32[]{:S(2)}) collective-permute-start(bf16[32,3840]{1,0:T(8,128)(2,1)S(1)} %get-tuple-element.15), channel_id=1, source_target_pairs={{0,256},{16,272},{32,288},{48,304},{64,320},{80,336},{96,352},{112... | collective-permute-start | bytes 737288 | tf_op jit(solution)/shard_map/ppermute | solution.py:245
  25.8 1.5 copy-start.1
  30.9 3.1 %copy-start = (bf16[3840,1024]{1,0:T(8,128)(2,1)}, bf16[3840,1024]{1,0:T(8,128)(2,1)S(1)}, u32[]{:S(2)}) copy-start(bf16[3840,1024]{1,0:T(8,128)(2,1)S(1)} %get-tuple-element.22.refs_16_) | copy-start | bytes 23592964
  34.0 16.7 %collective-permute-start.3 = (bf16[32,3840]{1,0:T(8,128)(2,1)S(1)}, bf16[32,3840]{1,0:T(8,128)(2,1)S(1)}, u32[]{:S(2)}, u32[]{:S(2)}) collective-permute-start(bf16[32,3840]{1,0:T(8,128)(2,1)S(1)} %get-tuple-element.19.refs_0_), channel_id=1, source_target_pairs={{0,2},{1,3},{2,0},{3,1},{4,6},{5,7},{6,4},{7,5},{8,10},{9,11},{10,... | collective-permute-start | bytes 737288 | tf_op jit(solution)/shard_map/ppermute | solution.py:161
  37.5 28.2 %collective-permute-start.5 = (bf16[32,3840]{1,0:T(8,128)(2,1)S(1)}, bf16[32,3840]{1,0:T(8,128)(2,1)S(1)}, u32[]{:S(2)}, u32[]{:S(2)}) collective-permute-start(bf16[32,3840]{1,0:T(8,128)(2,1)S(1)} %get-tuple-element.19.refs_0_), channel_id=1, source_target_pairs={{0,12},{1,13},{2,14},{3,15},{4,0},{5,1},{6,2},{7,3},{8,4},{9,5},{1... | collective-permute-start | bytes 737288 | tf_op jit(solution)/shard_map/ppermute | solution.py:161
  40.2 29.5 %collective-permute-start.2 = (bf16[32,3840]{1,0:T(8,128)(2,1)S(1)}, bf16[32,3840]{1,0:T(8,128)(2,1)S(1)}, u32[]{:S(2)}, u32[]{:S(2)}) collective-permute-start(bf16[32,3840]{1,0:T(8,128)(2,1)S(1)} %get-tuple-element.21), channel_id=1, source_target_pairs={{0,256},{16,272},{32,288},{48,304},{64,320},{80,336},{96,352},{112... | collective-permute-start | bytes 737288 | tf_op jit(solution)/shard_map/ppermute | solution.py:245
  50.7 19.0 %collective-permute-start.4 = (bf16[32,3840]{1,0:T(8,128)(2,1)S(1)}, bf16[32,3840]{1,0:T(8,128)(2,1)S(1)}, u32[]{:S(2)}, u32[]{:S(2)}) collective-permute-start(bf16[32,3840]{1,0:T(8,128)(2,1)S(1)} %collective-permute-done.3.refs_8_), channel_id=1, source_target_pairs={{0,8},{1,9},{2,10},{3,11},{4,12},{5,13},{6,14},{7,15},{8,0},{9,1},... | collective-permute-start | bytes 737288 | tf_op jit(solution)/shard_map/ppermute | solution.py:161
  60.4 13.7 %collective-permute-start.7 = (bf16[32,3840]{1,0:T(8,128)(2,1)S(1)}, bf16[32,3840]{1,0:T(8,128)(2,1)S(1)}, u32[]{:S(2)}, u32[]{:S(2)}) collective-permute-start(bf16[32,3840]{1,0:T(8,128)(2,1)S(1)} %get-tuple-element.19.refs_0_), channel_id=1, source_target_pairs={{0,4},{1,5},{2,6},{3,7},{4,8},{5,9},{6,10},{7,11},{8,12},{9,13},{1... | collective-permute-start | bytes 737288 | tf_op jit(solution)/shard_map/ppermute | solution.py:161
  62.3 16.4 %collective-permute-start.9 = (bf16[32,3840]{1,0:T(8,128)(2,1)S(1)}, bf16[32,3840]{1,0:T(8,128)(2,1)S(1)}, u32[]{:S(2)}, u32[]{:S(2)}) collective-permute-start(bf16[32,3840]{1,0:T(8,128)(2,1)S(1)} %get-tuple-element.19.refs_0_), channel_id=1, source_target_pairs={{0,8},{1,9},{2,10},{3,11},{4,12},{5,13},{6,14},{7,15},{8,0},{9,1},... | collective-permute-start | bytes 737288 | tf_op jit(solution)/shard_map/ppermute | solution.py:161
  65.7 17.0 %collective-permute-start.13 = (bf16[32,3840]{1,0:T(8,128)(2,1)S(1)}, bf16[32,3840]{1,0:T(8,128)(2,1)S(1)}, u32[]{:S(2)}, u32[]{:S(2)}) collective-permute-start(bf16[32,3840]{1,0:T(8,128)(2,1)S(1)} %collective-permute-done.5.refs_2_), channel_id=1, source_target_pairs={{0,2},{1,3},{2,0},{3,1},{4,6},{5,7},{6,4},{7,5},{8,10},{9,11},{10,... | collective-permute-start | bytes 737288 | tf_op jit(solution)/shard_map/ppermute | solution.py:161
  69.7 16.3 %collective-permute-start.11 = (bf16[32,3840]{1,0:T(8,128)(2,1)S(1)}, bf16[32,3840]{1,0:T(8,128)(2,1)S(1)}, u32[]{:S(2)}, u32[]{:S(2)}) collective-permute-start(bf16[32,3840]{1,0:T(8,128)(2,1)S(1)} %shard_map.49.refs_1_), channel_id=1, source_target_pairs={{0,2},{1,3},{2,0},{3,1},{4,6},{5,7},{6,4},{7,5},{8,10},{9,11},{10,... | collective-permute-start | bytes 737288 | tf_op jit(solution)/shard_map/ppermute | solution.py:161
  71.6 18.4 %collective-permute-start.6 = (bf16[32,3840]{1,0:T(8,128)(2,1)S(1)}, bf16[32,3840]{1,0:T(8,128)(2,1)S(1)}, u32[]{:S(2)}, u32[]{:S(2)}) collective-permute-start(bf16[32,3840]{1,0:T(8,128)(2,1)S(1)} %shard_map.49.refs_1_), channel_id=1, source_target_pairs={{0,12},{1,13},{2,14},{3,15},{4,0},{5,1},{6,2},{7,3},{8,4},{9,5},{1... | collective-permute-start | bytes 737288 | tf_op jit(solution)/shard_map/ppermute | solution.py:161
  74.1 17.9 %collective-permute-start.8 = (bf16[32,3840]{1,0:T(8,128)(2,1)S(1)}, bf16[32,3840]{1,0:T(8,128)(2,1)S(1)}, u32[]{:S(2)}, u32[]{:S(2)}) collective-permute-start(bf16[32,3840]{1,0:T(8,128)(2,1)S(1)} %shard_map.49.refs_1_), channel_id=1, source_target_pairs={{0,4},{1,5},{2,6},{3,7},{4,8},{5,9},{6,10},{7,11},{8,12},{9,13},{1... | collective-permute-start | bytes 737288 | tf_op jit(solution)/shard_map/ppermute | solution.py:161
  78.7 18.2 %collective-permute-start.15 = (bf16[32,3840]{1,0:T(8,128)(2,1)S(1)}, bf16[32,3840]{1,0:T(8,128)(2,1)S(1)}, u32[]{:S(2)}, u32[]{:S(2)}) collective-permute-start(bf16[32,3840]{1,0:T(8,128)(2,1)S(1)} %collective-permute-done.7.refs_4_), channel_id=1, source_target_pairs={{0,2},{1,3},{2,0},{3,1},{4,6},{5,7},{6,4},{7,5},{8,10},{9,11},{10,... | collective-permute-start | bytes 737288 | tf_op jit(solution)/shard_map/ppermute | solution.py:161
  82.7 14.2 %collective-permute-start.10 = (bf16[32,3840]{1,0:T(8,128)(2,1)S(1)}, bf16[32,3840]{1,0:T(8,128)(2,1)S(1)}, u32[]{:S(2)}, u32[]{:S(2)}) collective-permute-start(bf16[32,3840]{1,0:T(8,128)(2,1)S(1)} %shard_map.49.refs_1_), channel_id=1, source_target_pairs={{0,8},{1,9},{2,10},{3,11},{4,12},{5,13},{6,14},{7,15},{8,0},{9,1},... | collective-permute-start | bytes 737288 | tf_op jit(solution)/shard_map/ppermute | solution.py:161
  86.1 10.9 %collective-permute-start.12 = (bf16[32,3840]{1,0:T(8,128)(2,1)S(1)}, bf16[32,3840]{1,0:T(8,128)(2,1)S(1)}, u32[]{:S(2)}, u32[]{:S(2)}) collective-permute-start(bf16[32,3840]{1,0:T(8,128)(2,1)S(1)} %collective-permute-done.11.refs_9_), channel_id=1, source_target_pairs={{0,8},{1,9},{2,10},{3,11},{4,12},{5,13},{6,14},{7,15},{8,0},{9,1},... | collective-permute-start | bytes 737288 | tf_op jit(solution)/shard_map/ppermute | solution.py:161
  90.1 8.8 %collective-permute-start.14 = (bf16[32,3840]{1,0:T(8,128)(2,1)S(1)}, bf16[32,3840]{1,0:T(8,128)(2,1)S(1)}, u32[]{:S(2)}, u32[]{:S(2)}) collective-permute-start(bf16[32,3840]{1,0:T(8,128)(2,1)S(1)} %collective-permute-done.6.refs_3_), channel_id=1, source_target_pairs={{0,2},{1,3},{2,0},{3,1},{4,6},{5,7},{6,4},{7,5},{8,10},{9,11},{10,... | collective-permute-start | bytes 737288 | tf_op jit(solution)/shard_map/ppermute | solution.py:161
  92.0 9.5 %collective-permute-start.16 = (bf16[32,3840]{1,0:T(8,128)(2,1)S(1)}, bf16[32,3840]{1,0:T(8,128)(2,1)S(1)}, u32[]{:S(2)}, u32[]{:S(2)}) collective-permute-start(bf16[32,3840]{1,0:T(8,128)(2,1)S(1)} %collective-permute-done.8.refs_5_), channel_id=1, source_target_pairs={{0,2},{1,3},{2,0},{3,1},{4,6},{5,7},{6,4},{7,5},{8,10},{9,11},{10,... | collective-permute-start | bytes 737288 | tf_op jit(solution)/shard_map/ppermute | solution.py:161
  107.4 20.3 %collective-permute-start.18 = (f32[64,1024]{1,0:T(8,128)S(1)}, f32[64,1024]{1,0:T(8,128)S(1)}, u32[]{:S(2)}, u32[]{:S(2)}) collective-permute-start(f32[64,1024]{1,0:T(8,128)S(1)} %get-tuple-element.26), channel_id=1, source_target_pairs={{0,32},{1,481},{2,34},{3,483},{4,36},{5,485},{6,38},{7,487},{8,40}... | collective-permute-start | bytes 786440 | tf_op jit(solution)/shard_map/ppermute | solution.py:171
  123.4 11.1 %collective-permute-start.17 = (f32[64,1024]{1,0:T(8,128)S(1)}, f32[64,1024]{1,0:T(8,128)S(1)}, u32[]{:S(2)}, u32[]{:S(2)}) collective-permute-start(f32[64,1024]{1,0:T(8,128)S(1)} %get-tuple-element.25), channel_id=1, source_target_pairs={{0,32},{1,481},{2,34},{3,483},{4,36},{5,485},{6,38},{7,487},{8,40}... | collective-permute-start | bytes 786440 | tf_op jit(solution)/shard_map/ppermute | solution.py:171
  127.8 12.2 %collective-permute-start.20 = (f32[64,1024]{1,0:T(8,128)S(1)}, f32[64,1024]{1,0:T(8,128)S(1)}, u32[]{:S(2)}, u32[]{:S(2)}) collective-permute-start(f32[64,1024]{1,0:T(8,128)S(1)} %fusion.2.after_ref), channel_id=1, source_target_pairs={{0,480},{1,33},{2,482},{3,35},{4,484},{5,37},{6,486},{7,39},{8,488... | collective-permute-start | bytes 786440 | tf_op jit(solution)/shard_map/ppermute | solution.py:171
  134.5 12.2 %collective-permute-start.19 = (f32[64,1024]{1,0:T(8,128)S(1)}, f32[64,1024]{1,0:T(8,128)S(1)}, u32[]{:S(2)}, u32[]{:S(2)}) collective-permute-start(f32[64,1024]{1,0:T(8,128)S(1)} %shard_map.51), channel_id=1, source_target_pairs={{0,480},{1,33},{2,482},{3,35},{4,484},{5,37},{6,486},{7,39},{8,488... | collective-permute-start | bytes 786440 | tf_op jit(solution)/shard_map/ppermute | solution.py:171
  140.1 8.6 %collective-permute-start.22 = (f32[64,1024]{1,0:T(8,128)S(1)}, f32[64,1024]{1,0:T(8,128)S(1)}, u32[]{:S(2)}, u32[]{:S(2)}) collective-permute-start(f32[64,1024]{1,0:T(8,128)S(1)} %fusion.1.after_ref), channel_id=1, source_target_pairs={{0,32},{1,481},{2,34},{3,483},{4,36},{5,485},{6,38},{7,487},{8,40}... | collective-permute-start | bytes 786440 | tf_op jit(solution)/shard_map/ppermute | solution.py:171
  146.8 19.3 %collective-permute-start.21 = (f32[64,1024]{1,0:T(8,128)S(1)}, f32[64,1024]{1,0:T(8,128)S(1)}, u32[]{:S(2)}, u32[]{:S(2)}) collective-permute-start(f32[64,1024]{1,0:T(8,128)S(1)} %shard_map.52), channel_id=1, source_target_pairs={{0,32},{1,481},{2,34},{3,483},{4,36},{5,485},{6,38},{7,487},{8,40}... | collective-permute-start | bytes 786440 | tf_op jit(solution)/shard_map/ppermute | solution.py:171
  148.8 17.3 %collective-permute-start.23 = (f32[64,1024]{1,0:T(8,128)S(1)}, f32[64,1024]{1,0:T(8,128)S(1)}, u32[]{:S(2)}, u32[]{:S(2)}) collective-permute-start(f32[64,1024]{1,0:T(8,128)S(1)} %fusion), channel_id=1, source_target_pairs={{0,384},{1,129},{2,386},{3,131},{4,388},{5,133},{6,390},{7,135},{8... | collective-permute-start | bytes 786440 | tf_op jit(solution)/shard_map/ppermute | solution.py:171
  166.1 14.8 %collective-permute-start.24 = (f32[32,512]{1,0:T(8,128)S(1)}, f32[32,512]{1,0:T(8,128)S(1)}, u32[]{:S(2)}, u32[]{:S(2)}) collective-permute-start(f32[32,512]{1,0:T(8,128)S(1)} %get-tuple-element.24), channel_id=1, source_target_pairs={{1,48},{3,50},{5,52},{7,54},{9,56},{11,58},{13,60},{15,62},{17,32}... | collective-permute-start | bytes 196616 | tf_op jit(solution)/shard_map/ppermute | solution.py:171
  166.8 14.1 %collective-permute-start.25 = (f32[32,512]{1,0:T(8,128)S(1)}, f32[32,512]{1,0:T(8,128)S(1)}, u32[]{:S(2)}, u32[]{:S(2)}) collective-permute-start(f32[32,512]{1,0:T(8,128)S(1)} %get-tuple-element.27), channel_id=1, source_target_pairs={{0,1},{1,33},{2,3},{3,35},{4,5},{5,37},{6,7},{7,39},{8,9},{9,41},{... | collective-permute-start | bytes 196616 | tf_op jit(solution)/shard_map/ppermute | solution.py:171
  173.9 9.9 %collective-permute-start.26 = (f32[32,512]{1,0:T(8,128)S(1)}, f32[32,512]{1,0:T(8,128)S(1)}, u32[]{:S(2)}, u32[]{:S(2)}) collective-permute-start(f32[32,512]{1,0:T(8,128)S(1)} %get-tuple-element.23), channel_id=1, source_target_pairs={{0,17},{1,49},{2,19},{3,51},{4,21},{5,53},{6,23},{7,55},{8,25},{9,... | collective-permute-start | bytes 196616 | tf_op jit(solution)/shard_map/ppermute | solution.py:171
  175.8 8.4 %collective-permute-start.27 = (f32[32,512]{1,0:T(8,128)S(1)}, f32[32,512]{1,0:T(8,128)S(1)}, u32[]{:S(2)}, u32[]{:S(2)}) collective-permute-start(f32[32,512]{1,0:T(8,128)S(1)} %get-tuple-element.28), channel_id=1, source_target_pairs={{0,16},{1,32},{2,18},{3,34},{4,20},{5,36},{6,22},{7,38},{8,24},{9,... | collective-permute-start | bytes 196616 | tf_op jit(solution)/shard_map/ppermute | solution.py:171

commit v7 on v6

--- a/solution.py
+++ b/solution.py
@@ -10,14 +10,14 @@
 LANES = 128
 UNROLL = 32
 K_TILE = 768
-CHUNKS = 2
+CHUNKS = (64,)
 PLACES = ((0, 0), (1, 0), (3, 0), (2, 0), (0, 1), (2, 1), (1, 1), (3, 1))
 
 
 def scatter_kernel(place_ref, w_ref, *refs):
     outs, flag_ref, rows, spread = refs[:-3], refs[-3], refs[-2], refs[-1]
     width, blk = w_ref.shape
-    part_rows = width // CHUNKS
+    starts = [sum(CHUNKS[:h]) for h in range(len(CHUNKS))]
     ones = jnp.ones((LANES - width, LANES), jnp.float32)
     spread[...] = jnp.zeros_like(spread)
     for at in range(0, blk, LANES):
@@ -35,8 +35,8 @@
         for at in range(0, blk, LANES):
             block = spread[side * blk + at : side * blk + at + LANES, :]
             turned = block.T[:width].astype(jnp.bfloat16)
-            for h in range(CHUNKS):
-                outs[side * CHUNKS + h][:, at : at + LANES] = turned[h * part_rows : (h + 1) * part_rows]
+            for h, start in enumerate(starts):
+                outs[side * len(CHUNKS) + h][:, at : at + LANES] = turned[start : start + CHUNKS[h]]
             if side == 0:
                 mark = block[:, width:]
                 flag_ref[at : at + LANES, :] = jnp.concatenate([mark, mark], axis=1).astype(jnp.bfloat16)
@@ -46,10 +46,10 @@
     width, blk = w_t.shape
     return pl.pallas_call(
         scatter_kernel,
-        out_shape=[jax.ShapeDtypeStruct((width // CHUNKS, blk), jnp.bfloat16)] * (2 * CHUNKS)
+        out_shape=[jax.ShapeDtypeStruct((rows, blk), jnp.bfloat16) for rows in CHUNKS] * 2
         + [jax.ShapeDtypeStruct((blk, LANES), jnp.bfloat16)],
         in_specs=[pl.BlockSpec(memory_space=pltpu.SMEM), pl.BlockSpec(memory_space=pltpu.VMEM)],
-        out_specs=[pl.BlockSpec(memory_space=pltpu.VMEM)] * (2 * CHUNKS + 1),
+        out_specs=[pl.BlockSpec(memory_space=pltpu.VMEM)] * (2 * len(CHUNKS) + 1),
         scratch_shapes=[pltpu.VMEM((blk, LANES), jnp.float32), pltpu.VMEM((2 * blk, LANES), jnp.float32)],
         compiler_params=pltpu.CompilerParams(vmem_limit_bytes=16 * 2**20),
     )(place, w_t)
@@ -134,9 +134,8 @@
 
 
 def product(pieces, s_both):
-    rows, blk = pieces[0].shape
-    cols = s_both.shape[1]
-    block_rows = rows * len(pieces) // len(PLACES)
+    blk, cols = s_both.shape
+    block_rows = sum(CHUNKS)
     whole = pl.BlockSpec(memory_space=pltpu.VMEM)
     return pl.pallas_call(
         product_kernel,
@@ -190,7 +189,7 @@
     whole = pl.BlockSpec(memory_space=pltpu.VMEM)
     return pl.pallas_call(
         functools.partial(combine_kernel, count),
-        out_shape=[jax.ShapeDtypeStruct(own.shape, own.dtype)] * count,
+        out_shape=[jax.ShapeDtypeStruct(a.shape, a.dtype) for a in arrays[: 2 * count : 2]],
         in_specs=[whole] * len(arrays) + [pl.BlockSpec(memory_space=pl.ANY)],
         out_specs=[whole] * count,
         compiler_params=pltpu.CompilerParams(vmem_limit_bytes=4 * 2**20),
@@ -212,14 +211,30 @@
     )(terms, arrived, after)
 
 
+def hold_kernel(value_ref, *refs):
+    refs[-1][...] = value_ref[...]
+
+
+def hold(value, after):
+    whole = pl.BlockSpec(memory_space=pltpu.VMEM)
+    return pl.pallas_call(
+        hold_kernel,
+        out_shape=jax.ShapeDtypeStruct(value.shape, value.dtype),
+        in_specs=[whole] + [pl.BlockSpec(memory_space=pl.ANY)] * len(after),
+        out_specs=whole,
+        compiler_params=pltpu.CompilerParams(vmem_limit_bytes=4 * 2**20),
+    )(value, *after)
+
+
 def gather_col(here):
     pieces = {(0, 0): here}
-    for d in (1, 3, 2):
+    pieces[0, 1] = col_move(here, lambda x, y, k: (x, 1 - y, k))
+    for d in (1, 3):
         pieces[d, 0] = col_move(here, lambda x, y, k, d=d: (x - d, y, k))
-    pieces[0, 1] = col_move(here, lambda x, y, k: (x, 1 - y, k))
+        pieces[d, 1] = col_move(pieces[d, 0], lambda x, y, k: (x, 1 - y, k))
+    held = hold(here, [pieces[1, 0], pieces[3, 0]])
+    pieces[2, 0] = col_move(held, lambda x, y, k: (x - 2, y, k))
     pieces[2, 1] = col_move(pieces[0, 1], lambda x, y, k: (x - 2, y, k))
-    for d in (1, 3):
-        pieces[d, 1] = col_move(pieces[d, 0], lambda x, y, k: (x, 1 - y, k))
     return pieces
 
 
@@ -236,19 +251,18 @@
     inside = (source >= own_base) & (source < own_base + blk)
     place = jnp.where(inside, source - own_base, blk + source - partner_base)
     *parts, flag = scatter_rows(place, window_rows.T)
-    own_parts, cross_parts = parts[:CHUNKS], parts[CHUNKS:]
+    own_parts, cross_parts = parts[: len(CHUNKS)], parts[len(CHUNKS) :]
     s_both, masked = split_halves(kept_count, flag, secular, other)
 
     pieces = []
-    leaving, after = cross_parts[0], masked
-    for h in range(CHUNKS):
+    leaving = cross_parts[0]
+    for h in range(len(CHUNKS)):
         arrived = lax.ppermute(leaving, "grp", [(i, i ^ 16) for i in range(32)])
-        here, *next_leaving = combine(own_parts[h], arrived, cross_parts[h + 1] if h + 1 < CHUNKS else None, after)
+        here, *next_leaving = combine(own_parts[h], arrived, cross_parts[h + 1] if h + 1 < len(CHUNKS) else None, masked)
         if next_leaving:
             leaving = next_leaving[0]
         gathered = gather_col(here)
         pieces.append(gathered)
-        after = gathered[2, 1]
     pieces = [gathered[p] for p in PLACES for gathered in pieces]
 
     s_both = pltpu.with_memory_space_constraint(s_both, pltpu.HBM)

time: 186 us -> 190 us (1.022)
  waiting for transfers between devices: 28.4 us -> 55.4 us
  starting transfers between devices: 133 us -> 108 us
    ppermute x15 -> x8, starting transfers between devices: 54.1 us -> 31.9 us  [col_move(): return lax.ppermute(value, 'col', pairs)]
    ppermute x15 -> x8, waiting for transfers between devices: 4.58 us -> 23.8 us  [col_move(): return lax.ppermute(value, 'col', pairs)]
    ppermute x2 -> x1, starting transfers between devices: 26.2 us -> 15.7 us  [per_device(): arrived = lax.ppermute(leaving, 'grp', [(i, i ^ 16) for i in range(32)])]
    ppermute x11, starting transfers between devices: 52.5 us -> 60.8 us  [slice_move(): return lax.ppermute(value, ('grp', 'col'), pairs)]
    ppermute x2 -> x1, waiting for transfers between devices: 0.01 us -> 7.67 us  [per_device(): arrived = lax.ppermute(leaving, 'grp', [(i, i ^ 16) for i in range(32)])]
    pallas_call x1 -> x2, Pallas kernels: 5.76 us -> 5.79 us  [the longest x1 5.76 us: scatter_rows(): pl.pallas_call(scatter_kernel, out_shape=[jax.ShapeDtypeStruct((rows, blk...]
  transfers between devices with their start and end apart: 28 -> 20, of which waited for: 8 -> 11; matrix products, arithmetic and copies ran while one was open for 0% -> 0% of each run, Pallas kernels for 5% -> 5%
where the time goes in v7:
time: 190 us; the launch traced here: 187 us
  starting transfers between devices  108 us (57%)
  waiting for transfers between devices  55.4 us (29%)
  Pallas kernels  15.3 us (8%)
  local copies, waits for them, and re-layouts  6.28 us (3%)
    ppermute x11, starting transfers between devices, slice_move(): return lax.ppermute(value, ('grp', 'col'), pairs)  60.8 us
    ppermute x8, starting transfers between devices, col_move(): return lax.ppermute(value, 'col', pairs)  31.9 us
    ppermute x11, waiting for transfers between devices, slice_move(): return lax.ppermute(value, ('grp', 'col'), pairs)  23.9 us
    ppermute x8, waiting for transfers between devices, col_move(): return lax.ppermute(value, 'col', pairs)  23.8 us
    ppermute x1, starting transfers between devices, per_device(): arrived = lax.ppermute(leaving, 'grp', [(i, i ^ 16) for i in range(32)])  15.7 us
    ppermute x1, waiting for transfers between devices, per_device(): arrived = lax.ppermute(leaving, 'grp', [(i, i ^ 16) for i in range(32)])  7.67 us
    pallas_call x1, Pallas kernels, product(): pl.pallas_call(product_kernel, out_shape=jax.ShapeDtypeStruct((len(PLACES...  5.89 us
    pallas_call x1, Pallas kernels, scatter_rows(): pl.pallas_call(scatter_kernel, out_shape=[jax.ShapeDtypeStruct((rows, blk...  5.76 us
  transfers between devices with their start and end apart: 20, of which 11 were waited for; matrix products, arithmetic and copies ran while one was open for 0% of the time, Pallas kernels for 5%

profile of v7, /device:TPU:6, one launch (start us, length us, event | category | flops | bytes accessed | tf_op | source)
XLA Modules:
  0.0 187.3 jit_solution(2195109825521432706)
XLA Ops:
  0.0 1.9 %collective-permute-start.1 = (bf16[3840,256]{1,0:T(8,128)(2,1)}, bf16[3840,256]{1,0:T(8,128)(2,1)S(1)}, u32[]{:S(2)}, u32[]{:S(2)}) collective-permute-start(bf16[3840,256]{1,0:T(8,128)(2,1)} %own_ref.1), channel_id=1, source_target_pairs={{0,1},{1,0},{2,3},{3,2},{4,5},{5,4},{6,7},{7,6},{8,9},{9,8},{10,11... | collective-permute-start | bytes 5898248 | tf_op jit(solution)/shard_map/ppermute | solution.py:160
  3.7 5.8 %shard_map.46 = (bf16[64,3840]{1,0:T(8,128)(2,1)S(1)}, bf16[64,3840]{1,0:T(8,128)(2,1)S(1)}, bf16[3840,128]{1,0:T(8,128)(2,1)S(1)}) custom-call(s32[3840]{0:T(1024)S(1)} %subtract_select_fusion.place_ref, bf16[64,3840]{1,0:T(8,128)(2,1)S(1)} %bitcast.30), custom_call_target="tpu_custom_call" | custom-call | tf_op jit(solution)/shard_map/pallas_call | solution.py:47
  9.4 15.7 %collective-permute-start = (bf16[64,3840]{1,0:T(8,128)(2,1)S(1)}, bf16[64,3840]{1,0:T(8,128)(2,1)S(1)}, u32[]{:S(2)}, u32[]{:S(2)}) collective-permute-start(bf16[64,3840]{1,0:T(8,128)(2,1)S(1)} %get-tuple-element.11), channel_id=1, source_target_pairs={{0,256},{16,272},{32,288},{48,304},{64,320},{80,336},{96,352},{112... | collective-permute-start | bytes 1474568 | tf_op jit(solution)/shard_map/ppermute | solution.py:260
  27.4 3.5 %shard_map.47 = (bf16[3840,1024]{1,0:T(8,128)(2,1)S(1)}, f32[8,128]{1,0:T(8,128)S(1)}) custom-call(s32[1]{0:T(128)S(6)} %copy.9.kept_ref, bf16[3840,128]{1,0:T(8,128)(2,1)S(1)} %get-tuple-element.12.flag_ref, bf16[3840,256]{1,0:T(8,128)(2,1)S(1)} %copy-done.1, bf16[3840,256]{1,0:T(8,128)(2,1)S(1)} %collective-permute-done.1.other_ref), custom_call_target="tpu_custom_call" | custom-call | tf_op jit(solution)/shard_map/pallas_call | solution.py:83
  30.9 3.0 %copy-done = bf16[3840,1024]{1,0:T(8,128)(2,1)} copy-done((bf16[3840,1024]{1,0:T(8,128)(2,1)}, bf16[3840,1024]{1,0:T(8,128)(2,1)S(1)}, u32[]{:S(2)}) %copy-start) | copy-done | bytes 7864344
  33.9 7.7 %collective-permute-done.refs_1_ = bf16[64,3840]{1,0:T(8,128)(2,1)S(1)} collective-permute-done((bf16[64,3840]{1,0:T(8,128)(2,1)S(1)}, bf16[64,3840]{1,0:T(8,128)(2,1)S(1)}, u32[]{:S(2)}, u32[]{:S(2)}) %collective-permute-start) | collective-permute-done | bytes 491552 | tf_op jit(solution)/shard_map/ppermute | solution.py:260
  41.6 2.7 %collective-permute-start.2 = (bf16[64,3840]{1,0:T(8,128)(2,1)S(1)}, bf16[64,3840]{1,0:T(8,128)(2,1)S(1)}, u32[]{:S(2)}, u32[]{:S(2)}) collective-permute-start(bf16[64,3840]{1,0:T(8,128)(2,1)S(1)} %shard_map.48.value_ref.refs_0_), channel_id=1, source_target_pairs={{0,12},{1,13},{2,14},{3,15},{4,0},{5,1},{6,2},{7,3},{8,4},{9,5},{1... | collective-permute-start | bytes 1474568 | tf_op jit(solution)/shard_map/ppermute | solution.py:160
  44.4 12.0 %collective-permute-start.3 = (bf16[64,3840]{1,0:T(8,128)(2,1)S(1)}, bf16[64,3840]{1,0:T(8,128)(2,1)S(1)}, u32[]{:S(2)}, u32[]{:S(2)}) collective-permute-start(bf16[64,3840]{1,0:T(8,128)(2,1)S(1)} %shard_map.48.value_ref.refs_0_), channel_id=1, source_target_pairs={{0,4},{1,5},{2,6},{3,7},{4,8},{5,9},{6,10},{7,11},{8,12},{9,13},{1... | collective-permute-start | bytes 1474568 | tf_op jit(solution)/shard_map/ppermute | solution.py:160
  56.4 1.9 %collective-permute-start.5 = (bf16[64,3840]{1,0:T(8,128)(2,1)S(1)}, bf16[64,3840]{1,0:T(8,128)(2,1)S(1)}, u32[]{:S(2)}, u32[]{:S(2)}) collective-permute-start(bf16[64,3840]{1,0:T(8,128)(2,1)S(1)} %shard_map.48.value_ref.refs_0_), channel_id=1, source_target_pairs={{0,2},{1,3},{2,0},{3,1},{4,6},{5,7},{6,4},{7,5},{8,10},{9,11},{10,... | collective-permute-start | bytes 1474568 | tf_op jit(solution)/shard_map/ppermute | solution.py:160
  58.3 6.9 %collective-permute-done.2.refs_0_.refs_1_ = bf16[64,3840]{1,0:T(8,128)(2,1)S(1)} collective-permute-done((bf16[64,3840]{1,0:T(8,128)(2,1)S(1)}, bf16[64,3840]{1,0:T(8,128)(2,1)S(1)}, u32[]{:S(2)}, u32[]{:S(2)}) %collective-permute-start.2) | collective-permute-done | bytes 491552 | tf_op jit(solution)/shard_map/ppermute | solution.py:160
  66.5 5.6 %collective-permute-start.4 = (bf16[64,3840]{1,0:T(8,128)(2,1)S(1)}, bf16[64,3840]{1,0:T(8,128)(2,1)S(1)}, u32[]{:S(2)}, u32[]{:S(2)}) collective-permute-start(bf16[64,3840]{1,0:T(8,128)(2,1)S(1)} %shard_map.49), channel_id=1, source_target_pairs={{0,8},{1,9},{2,10},{3,11},{4,12},{5,13},{6,14},{7,15},{8,0},{9,1},... | collective-permute-start | bytes 1474568 | tf_op jit(solution)/shard_map/ppermute | solution.py:160
  72.1 1.9 %collective-permute-start.7 = (bf16[64,3840]{1,0:T(8,128)(2,1)S(1)}, bf16[64,3840]{1,0:T(8,128)(2,1)S(1)}, u32[]{:S(2)}, u32[]{:S(2)}) collective-permute-start(bf16[64,3840]{1,0:T(8,128)(2,1)S(1)} %collective-permute-done.2.refs_0_.refs_1_), channel_id=1, source_target_pairs={{0,2},{1,3},{2,0},{3,1},{4,6},{5,7},{6,4},{7,5},{8,10},{9,11},{10,... | collective-permute-start | bytes 1474568 | tf_op jit(solution)/shard_map/ppermute | solution.py:160
  74.0 3.9 %collective-permute-start.8 = (bf16[64,3840]{1,0:T(8,128)(2,1)S(1)}, bf16[64,3840]{1,0:T(8,128)(2,1)S(1)}, u32[]{:S(2)}, u32[]{:S(2)}) collective-permute-start(bf16[64,3840]{1,0:T(8,128)(2,1)S(1)} %collective-permute-done.3.refs_1_.refs_2_), channel_id=1, source_target_pairs={{0,2},{1,3},{2,0},{3,1},{4,6},{5,7},{6,4},{7,5},{8,10},{9,11},{10,... | collective-permute-start | bytes 1474568 | tf_op jit(solution)/shard_map/ppermute | solution.py:160
  77.9 1.9 %collective-permute-start.6 = (bf16[64,3840]{1,0:T(8,128)(2,1)S(1)}, bf16[64,3840]{1,0:T(8,128)(2,1)S(1)}, u32[]{:S(2)}, u32[]{:S(2)}) collective-permute-start(bf16[64,3840]{1,0:T(8,128)(2,1)S(1)} %collective-permute-done.5.refs_4_), channel_id=1, source_target_pairs={{0,8},{1,9},{2,10},{3,11},{4,12},{5,13},{6,14},{7,15},{8,0},{9,1},... | collective-permute-start | bytes 1474568 | tf_op jit(solution)/shard_map/ppermute | solution.py:160
  79.9 3.9 %collective-permute-done.4.refs_3_ = bf16[64,3840]{1,0:T(8,128)(2,1)S(1)} collective-permute-done((bf16[64,3840]{1,0:T(8,128)(2,1)S(1)}, bf16[64,3840]{1,0:T(8,128)(2,1)S(1)}, u32[]{:S(2)}, u32[]{:S(2)}) %collective-permute-start.4) | collective-permute-done | bytes 491552 | tf_op jit(solution)/shard_map/ppermute | solution.py:160
  83.7 4.4 %collective-permute-done.7.refs_6_ = bf16[64,3840]{1,0:T(8,128)(2,1)S(1)} collective-permute-done((bf16[64,3840]{1,0:T(8,128)(2,1)S(1)}, bf16[64,3840]{1,0:T(8,128)(2,1)S(1)}, u32[]{:S(2)}, u32[]{:S(2)}) %collective-permute-start.7) | collective-permute-done | bytes 491552 | tf_op jit(solution)/shard_map/ppermute | solution.py:160
  88.1 7.4 %collective-permute-done.8.refs_7_ = bf16[64,3840]{1,0:T(8,128)(2,1)S(1)} collective-permute-done((bf16[64,3840]{1,0:T(8,128)(2,1)S(1)}, bf16[64,3840]{1,0:T(8,128)(2,1)S(1)}, u32[]{:S(2)}, u32[]{:S(2)}) %collective-permute-start.8) | collective-permute-done | bytes 491552 | tf_op jit(solution)/shard_map/ppermute | solution.py:160
  95.5 5.9 %shard_map.50.terms_ref = f32[8,64,1024]{2,1,0:T(8,128)S(1)} custom-call(bf16[64,3840]{1,0:T(8,128)(2,1)S(1)} %shard_map.48.value_ref.refs_0_, bf16[64,3840]{1,0:T(8,128)(2,1)S(1)} %collective-permute-done.2.refs_0_.refs_1_, bf16[64,3840]{1,0:T(8,128)(2,1)S(1)} %collective-permute-done.3.refs_1_.refs_2_, ...), custom_call_target="tpu_custom_call" | custom-call | tf_op jit(solution)/shard_map/pallas_call | solution.py:140
  101.5 21.7 %collective-permute-start.10 = (f32[64,1024]{1,0:T(8,128)S(1)}, f32[64,1024]{1,0:T(8,128)S(1)}, u32[]{:S(2)}, u32[]{:S(2)}) collective-permute-start(f32[64,1024]{1,0:T(8,128)S(1)} %get-tuple-element.18), channel_id=1, source_target_pairs={{0,32},{1,481},{2,34},{3,483},{4,36},{5,485},{6,38},{7,487},{8,40}... | collective-permute-start | bytes 786440 | tf_op jit(solution)/shard_map/ppermute | solution.py:170
  123.2 1.9 %collective-permute-start.9 = (f32[64,1024]{1,0:T(8,128)S(1)}, f32[64,1024]{1,0:T(8,128)S(1)}, u32[]{:S(2)}, u32[]{:S(2)}) collective-permute-start(f32[64,1024]{1,0:T(8,128)S(1)} %get-tuple-element.17), channel_id=1, source_target_pairs={{0,32},{1,481},{2,34},{3,483},{4,36},{5,485},{6,38},{7,487},{8,40}... | collective-permute-start | bytes 786440 | tf_op jit(solution)/shard_map/ppermute | solution.py:170
  125.2 2.4 %collective-permute-done.10 = f32[64,1024]{1,0:T(8,128)S(1)} collective-permute-done((f32[64,1024]{1,0:T(8,128)S(1)}, f32[64,1024]{1,0:T(8,128)S(1)}, u32[]{:S(2)}, u32[]{:S(2)}) %collective-permute-start.10) | collective-permute-done | bytes 262176 | tf_op jit(solution)/shard_map/ppermute | solution.py:170
  127.6 7.7 %collective-permute-start.12 = (f32[64,1024]{1,0:T(8,128)S(1)}, f32[64,1024]{1,0:T(8,128)S(1)}, u32[]{:S(2)}, u32[]{:S(2)}) collective-permute-start(f32[64,1024]{1,0:T(8,128)S(1)} %fusion.2.after_ref), channel_id=1, source_target_pairs={{0,480},{1,33},{2,482},{3,35},{4,484},{5,37},{6,486},{7,39},{8,488... | collective-permute-start | bytes 786440 | tf_op jit(solution)/shard_map/ppermute | solution.py:170
  135.3 6.6 %collective-permute-start.11 = (f32[64,1024]{1,0:T(8,128)S(1)}, f32[64,1024]{1,0:T(8,128)S(1)}, u32[]{:S(2)}, u32[]{:S(2)}) collective-permute-start(f32[64,1024]{1,0:T(8,128)S(1)} %shard_map.51), channel_id=1, source_target_pairs={{0,480},{1,33},{2,482},{3,35},{4,484},{5,37},{6,486},{7,39},{8,488... | collective-permute-start | bytes 786440 | tf_op jit(solution)/shard_map/ppermute | solution.py:170
  142.0 1.9 %collective-permute-start.14 = (f32[64,1024]{1,0:T(8,128)S(1)}, f32[64,1024]{1,0:T(8,128)S(1)}, u32[]{:S(2)}, u32[]{:S(2)}) collective-permute-start(f32[64,1024]{1,0:T(8,128)S(1)} %fusion.1.after_ref), channel_id=1, source_target_pairs={{0,32},{1,481},{2,34},{3,483},{4,36},{5,485},{6,38},{7,487},{8,40}... | collective-permute-start | bytes 786440 | tf_op jit(solution)/shard_map/ppermute | solution.py:170
  143.9 5.1 %collective-permute-done.11.arrived_ref = f32[64,1024]{1,0:T(8,128)S(1)} collective-permute-done((f32[64,1024]{1,0:T(8,128)S(1)}, f32[64,1024]{1,0:T(8,128)S(1)}, u32[]{:S(2)}, u32[]{:S(2)}) %collective-permute-start.11) | collective-permute-done | bytes 262176 | tf_op jit(solution)/shard_map/ppermute | solution.py:170
  149.0 1.9 %collective-permute-start.13 = (f32[64,1024]{1,0:T(8,128)S(1)}, f32[64,1024]{1,0:T(8,128)S(1)}, u32[]{:S(2)}, u32[]{:S(2)}) collective-permute-start(f32[64,1024]{1,0:T(8,128)S(1)} %shard_map.52), channel_id=1, source_target_pairs={{0,32},{1,481},{2,34},{3,483},{4,36},{5,485},{6,38},{7,487},{8,40}... | collective-permute-start | bytes 786440 | tf_op jit(solution)/shard_map/ppermute | solution.py:170
  151.0 3.9 %collective-permute-start.15 = (f32[64,1024]{1,0:T(8,128)S(1)}, f32[64,1024]{1,0:T(8,128)S(1)}, u32[]{:S(2)}, u32[]{:S(2)}) collective-permute-start(f32[64,1024]{1,0:T(8,128)S(1)} %fusion), channel_id=1, source_target_pairs={{0,384},{1,129},{2,386},{3,131},{4,388},{5,133},{6,390},{7,135},{8... | collective-permute-start | bytes 786440 | tf_op jit(solution)/shard_map/ppermute | solution.py:170
  155.0 13.1 %collective-permute-done.13 = f32[64,1024]{1,0:T(8,128)S(1)} collective-permute-done((f32[64,1024]{1,0:T(8,128)S(1)}, f32[64,1024]{1,0:T(8,128)S(1)}, u32[]{:S(2)}, u32[]{:S(2)}) %collective-permute-start.13) | collective-permute-done | bytes 262176 | tf_op jit(solution)/shard_map/ppermute | solution.py:170
  168.8 7.5 %collective-permute-start.17 = (f32[32,512]{1,0:T(8,128)S(1)}, f32[32,512]{1,0:T(8,128)S(1)}, u32[]{:S(2)}, u32[]{:S(2)}) collective-permute-start(f32[32,512]{1,0:T(8,128)S(1)} %get-tuple-element.19), channel_id=1, source_target_pairs={{0,1},{1,33},{2,3},{3,35},{4,5},{5,37},{6,7},{7,39},{8,9},{9,41},{... | collective-permute-start | bytes 196616 | tf_op jit(solution)/shard_map/ppermute | solution.py:170
  176.4 1.9 %collective-permute-start.18 = (f32[32,512]{1,0:T(8,128)S(1)}, f32[32,512]{1,0:T(8,128)S(1)}, u32[]{:S(2)}, u32[]{:S(2)}) collective-permute-start(f32[32,512]{1,0:T(8,128)S(1)} %get-tuple-element.15), channel_id=1, source_target_pairs={{0,17},{1,49},{2,19},{3,51},{4,21},{5,53},{6,23},{7,55},{8,25},{9,... | collective-permute-start | bytes 196616 | tf_op jit(solution)/shard_map/ppermute | solution.py:170
  178.3 5.0 %collective-permute-start.19 = (f32[32,512]{1,0:T(8,128)S(1)}, f32[32,512]{1,0:T(8,128)S(1)}, u32[]{:S(2)}, u32[]{:S(2)}) collective-permute-start(f32[32,512]{1,0:T(8,128)S(1)} %get-tuple-element.20), channel_id=1, source_target_pairs={{0,16},{1,32},{2,18},{3,34},{4,20},{5,36},{6,22},{7,38},{8,24},{9,... | collective-permute-start | bytes 196616 | tf_op jit(solution)/shard_map/ppermute | solution.py:170
  183.4 2.9 %collective-permute-done.18 = f32[32,512]{1,0:T(8,128)S(1)} collective-permute-done((f32[32,512]{1,0:T(8,128)S(1)}, f32[32,512]{1,0:T(8,128)S(1)}, u32[]{:S(2)}, u32[]{:S(2)}) %collective-permute-start.18) | collective-permute-done | bytes 65568 | tf_op jit(solution)/shard_map/ppermute | solution.py:170
  (30 shorter events, 6.6 us)
Async XLA Ops:
  0.0 25.8 %collective-permute-start.1 = (bf16[3840,256]{1,0:T(8,128)(2,1)}, bf16[3840,256]{1,0:T(8,128)(2,1)S(1)}, u32[]{:S(2)}, u32[]{:S(2)}) collective-permute-start(bf16[3840,256]{1,0:T(8,128)(2,1)} %own_ref.1), channel_id=1, source_target_pairs={{0,1},{1,0},{2,3},{3,2},{4,5},{5,4},{6,7},{7,6},{8,9},{9,8},{10,11... | collective-permute-start | bytes 5898248 | tf_op jit(solution)/shard_map/ppermute | solution.py:160
  2.7 1.0 copy-start.2
  9.4 32.1 %collective-permute-start = (bf16[64,3840]{1,0:T(8,128)(2,1)S(1)}, bf16[64,3840]{1,0:T(8,128)(2,1)S(1)}, u32[]{:S(2)}, u32[]{:S(2)}) collective-permute-start(bf16[64,3840]{1,0:T(8,128)(2,1)S(1)} %get-tuple-element.11), channel_id=1, source_target_pairs={{0,256},{16,272},{32,288},{48,304},{64,320},{80,336},{96,352},{112... | collective-permute-start | bytes 1474568 | tf_op jit(solution)/shard_map/ppermute | solution.py:260
  25.8 1.5 copy-start.1
  30.9 3.1 %copy-start = (bf16[3840,1024]{1,0:T(8,128)(2,1)}, bf16[3840,1024]{1,0:T(8,128)(2,1)S(1)}, u32[]{:S(2)}) copy-start(bf16[3840,1024]{1,0:T(8,128)(2,1)S(1)} %get-tuple-element.14.refs_8_) | copy-start | bytes 23592964
  41.6 23.6 %collective-permute-start.2 = (bf16[64,3840]{1,0:T(8,128)(2,1)S(1)}, bf16[64,3840]{1,0:T(8,128)(2,1)S(1)}, u32[]{:S(2)}, u32[]{:S(2)}) collective-permute-start(bf16[64,3840]{1,0:T(8,128)(2,1)S(1)} %shard_map.48.value_ref.refs_0_), channel_id=1, source_target_pairs={{0,12},{1,13},{2,14},{3,15},{4,0},{5,1},{6,2},{7,3},{8,4},{9,5},{1... | collective-permute-start | bytes 1474568 | tf_op jit(solution)/shard_map/ppermute | solution.py:160
  44.4 22.1 %collective-permute-start.3 = (bf16[64,3840]{1,0:T(8,128)(2,1)S(1)}, bf16[64,3840]{1,0:T(8,128)(2,1)S(1)}, u32[]{:S(2)}, u32[]{:S(2)}) collective-permute-start(bf16[64,3840]{1,0:T(8,128)(2,1)S(1)} %shard_map.48.value_ref.refs_0_), channel_id=1, source_target_pairs={{0,4},{1,5},{2,6},{3,7},{4,8},{5,9},{6,10},{7,11},{8,12},{9,13},{1... | collective-permute-start | bytes 1474568 | tf_op jit(solution)/shard_map/ppermute | solution.py:160
  56.4 21.5 %collective-permute-start.5 = (bf16[64,3840]{1,0:T(8,128)(2,1)S(1)}, bf16[64,3840]{1,0:T(8,128)(2,1)S(1)}, u32[]{:S(2)}, u32[]{:S(2)}) collective-permute-start(bf16[64,3840]{1,0:T(8,128)(2,1)S(1)} %shard_map.48.value_ref.refs_0_), channel_id=1, source_target_pairs={{0,2},{1,3},{2,0},{3,1},{4,6},{5,7},{6,4},{7,5},{8,10},{9,11},{10,... | collective-permute-start | bytes 1474568 | tf_op jit(solution)/shard_map/ppermute | solution.py:160
  66.5 17.2 %collective-permute-start.4 = (bf16[64,3840]{1,0:T(8,128)(2,1)S(1)}, bf16[64,3840]{1,0:T(8,128)(2,1)S(1)}, u32[]{:S(2)}, u32[]{:S(2)}) collective-permute-start(bf16[64,3840]{1,0:T(8,128)(2,1)S(1)} %shard_map.49), channel_id=1, source_target_pairs={{0,8},{1,9},{2,10},{3,11},{4,12},{5,13},{6,14},{7,15},{8,0},{9,1},... | collective-permute-start | bytes 1474568 | tf_op jit(solution)/shard_map/ppermute | solution.py:160
  72.1 16.1 %collective-permute-start.7 = (bf16[64,3840]{1,0:T(8,128)(2,1)S(1)}, bf16[64,3840]{1,0:T(8,128)(2,1)S(1)}, u32[]{:S(2)}, u32[]{:S(2)}) collective-permute-start(bf16[64,3840]{1,0:T(8,128)(2,1)S(1)} %collective-permute-done.2.refs_0_.refs_1_), channel_id=1, source_target_pairs={{0,2},{1,3},{2,0},{3,1},{4,6},{5,7},{6,4},{7,5},{8,10},{9,11},{10,... | collective-permute-start | bytes 1474568 | tf_op jit(solution)/shard_map/ppermute | solution.py:160
  74.0 21.6 %collective-permute-start.8 = (bf16[64,3840]{1,0:T(8,128)(2,1)S(1)}, bf16[64,3840]{1,0:T(8,128)(2,1)S(1)}, u32[]{:S(2)}, u32[]{:S(2)}) collective-permute-start(bf16[64,3840]{1,0:T(8,128)(2,1)S(1)} %collective-permute-done.3.refs_1_.refs_2_), channel_id=1, source_target_pairs={{0,2},{1,3},{2,0},{3,1},{4,6},{5,7},{6,4},{7,5},{8,10},{9,11},{10,... | collective-permute-start | bytes 1474568 | tf_op jit(solution)/shard_map/ppermute | solution.py:160
  77.9 17.6 %collective-permute-start.6 = (bf16[64,3840]{1,0:T(8,128)(2,1)S(1)}, bf16[64,3840]{1,0:T(8,128)(2,1)S(1)}, u32[]{:S(2)}, u32[]{:S(2)}) collective-permute-start(bf16[64,3840]{1,0:T(8,128)(2,1)S(1)} %collective-permute-done.5.refs_4_), channel_id=1, source_target_pairs={{0,8},{1,9},{2,10},{3,11},{4,12},{5,13},{6,14},{7,15},{8,0},{9,1},... | collective-permute-start | bytes 1474568 | tf_op jit(solution)/shard_map/ppermute | solution.py:160
  101.5 26.1 %collective-permute-start.10 = (f32[64,1024]{1,0:T(8,128)S(1)}, f32[64,1024]{1,0:T(8,128)S(1)}, u32[]{:S(2)}, u32[]{:S(2)}) collective-permute-start(f32[64,1024]{1,0:T(8,128)S(1)} %get-tuple-element.18), channel_id=1, source_target_pairs={{0,32},{1,481},{2,34},{3,483},{4,36},{5,485},{6,38},{7,487},{8,40}... | collective-permute-start | bytes 786440 | tf_op jit(solution)/shard_map/ppermute | solution.py:170
  123.2 12.1 %collective-permute-start.9 = (f32[64,1024]{1,0:T(8,128)S(1)}, f32[64,1024]{1,0:T(8,128)S(1)}, u32[]{:S(2)}, u32[]{:S(2)}) collective-permute-start(f32[64,1024]{1,0:T(8,128)S(1)} %get-tuple-element.17), channel_id=1, source_target_pairs={{0,32},{1,481},{2,34},{3,483},{4,36},{5,485},{6,38},{7,487},{8,40}... | collective-permute-start | bytes 786440 | tf_op jit(solution)/shard_map/ppermute | solution.py:170
  127.6 14.3 %collective-permute-start.12 = (f32[64,1024]{1,0:T(8,128)S(1)}, f32[64,1024]{1,0:T(8,128)S(1)}, u32[]{:S(2)}, u32[]{:S(2)}) collective-permute-start(f32[64,1024]{1,0:T(8,128)S(1)} %fusion.2.after_ref), channel_id=1, source_target_pairs={{0,480},{1,33},{2,482},{3,35},{4,484},{5,37},{6,486},{7,39},{8,488... | collective-permute-start | bytes 786440 | tf_op jit(solution)/shard_map/ppermute | solution.py:170
  135.3 13.6 %collective-permute-start.11 = (f32[64,1024]{1,0:T(8,128)S(1)}, f32[64,1024]{1,0:T(8,128)S(1)}, u32[]{:S(2)}, u32[]{:S(2)}) collective-permute-start(f32[64,1024]{1,0:T(8,128)S(1)} %shard_map.51), channel_id=1, source_target_pairs={{0,480},{1,33},{2,482},{3,35},{4,484},{5,37},{6,486},{7,39},{8,488... | collective-permute-start | bytes 786440 | tf_op jit(solution)/shard_map/ppermute | solution.py:170
  142.0 9.0 %collective-permute-start.14 = (f32[64,1024]{1,0:T(8,128)S(1)}, f32[64,1024]{1,0:T(8,128)S(1)}, u32[]{:S(2)}, u32[]{:S(2)}) collective-permute-start(f32[64,1024]{1,0:T(8,128)S(1)} %fusion.1.after_ref), channel_id=1, source_target_pairs={{0,32},{1,481},{2,34},{3,483},{4,36},{5,485},{6,38},{7,487},{8,40}... | collective-permute-start | bytes 786440 | tf_op jit(solution)/shard_map/ppermute | solution.py:170
  149.0 19.0 %collective-permute-start.13 = (f32[64,1024]{1,0:T(8,128)S(1)}, f32[64,1024]{1,0:T(8,128)S(1)}, u32[]{:S(2)}, u32[]{:S(2)}) collective-permute-start(f32[64,1024]{1,0:T(8,128)S(1)} %shard_map.52), channel_id=1, source_target_pairs={{0,32},{1,481},{2,34},{3,483},{4,36},{5,485},{6,38},{7,487},{8,40}... | collective-permute-start | bytes 786440 | tf_op jit(solution)/shard_map/ppermute | solution.py:170
  151.0 17.1 %collective-permute-start.15 = (f32[64,1024]{1,0:T(8,128)S(1)}, f32[64,1024]{1,0:T(8,128)S(1)}, u32[]{:S(2)}, u32[]{:S(2)}) collective-permute-start(f32[64,1024]{1,0:T(8,128)S(1)} %fusion), channel_id=1, source_target_pairs={{0,384},{1,129},{2,386},{3,131},{4,388},{5,133},{6,390},{7,135},{8... | collective-permute-start | bytes 786440 | tf_op jit(solution)/shard_map/ppermute | solution.py:170
  168.2 15.2 %collective-permute-start.16 = (f32[32,512]{1,0:T(8,128)S(1)}, f32[32,512]{1,0:T(8,128)S(1)}, u32[]{:S(2)}, u32[]{:S(2)}) collective-permute-start(f32[32,512]{1,0:T(8,128)S(1)} %get-tuple-element.16), channel_id=1, source_target_pairs={{1,48},{3,50},{5,52},{7,54},{9,56},{11,58},{13,60},{15,62},{17,32}... | collective-permute-start | bytes 196616 | tf_op jit(solution)/shard_map/ppermute | solution.py:170
  168.8 14.5 %collective-permute-start.17 = (f32[32,512]{1,0:T(8,128)S(1)}, f32[32,512]{1,0:T(8,128)S(1)}, u32[]{:S(2)}, u32[]{:S(2)}) collective-permute-start(f32[32,512]{1,0:T(8,128)S(1)} %get-tuple-element.19), channel_id=1, source_target_pairs={{0,1},{1,33},{2,3},{3,35},{4,5},{5,37},{6,7},{7,39},{8,9},{9,41},{... | collective-permute-start | bytes 196616 | tf_op jit(solution)/shard_map/ppermute | solution.py:170
  176.4 9.9 %collective-permute-start.18 = (f32[32,512]{1,0:T(8,128)S(1)}, f32[32,512]{1,0:T(8,128)S(1)}, u32[]{:S(2)}, u32[]{:S(2)}) collective-permute-start(f32[32,512]{1,0:T(8,128)S(1)} %get-tuple-element.15), channel_id=1, source_target_pairs={{0,17},{1,49},{2,19},{3,51},{4,21},{5,53},{6,23},{7,55},{8,25},{9,... | collective-permute-start | bytes 196616 | tf_op jit(solution)/shard_map/ppermute | solution.py:170
  178.3 8.4 %collective-permute-start.19 = (f32[32,512]{1,0:T(8,128)S(1)}, f32[32,512]{1,0:T(8,128)S(1)}, u32[]{:S(2)}, u32[]{:S(2)}) collective-permute-start(f32[32,512]{1,0:T(8,128)S(1)} %get-tuple-element.20), channel_id=1, source_target_pairs={{0,16},{1,32},{2,18},{3,34},{4,20},{5,36},{6,22},{7,38},{8,24},{9,... | collective-permute-start | bytes 196616 | tf_op jit(solution)/shard_map/ppermute | solution.py:170

commit v8 on v7

--- a/solution.py
+++ b/solution.py
@@ -10,14 +10,14 @@
 LANES = 128
 UNROLL = 32
 K_TILE = 768
-CHUNKS = (64,)
-PLACES = ((0, 0), (1, 0), (3, 0), (2, 0), (0, 1), (2, 1), (1, 1), (3, 1))
+CHUNKS = (32, 32)
+STARTS = tuple(sum(CHUNKS[:h]) for h in range(len(CHUNKS)))
+PEERS = 8
 
 
 def scatter_kernel(place_ref, w_ref, *refs):
     outs, flag_ref, rows, spread = refs[:-3], refs[-3], refs[-2], refs[-1]
     width, blk = w_ref.shape
-    starts = [sum(CHUNKS[:h]) for h in range(len(CHUNKS))]
     ones = jnp.ones((LANES - width, LANES), jnp.float32)
     spread[...] = jnp.zeros_like(spread)
     for at in range(0, blk, LANES):
@@ -35,7 +35,7 @@
         for at in range(0, blk, LANES):
             block = spread[side * blk + at : side * blk + at + LANES, :]
             turned = block.T[:width].astype(jnp.bfloat16)
-            for h, start in enumerate(starts):
+            for h, start in enumerate(STARTS):
                 outs[side * len(CHUNKS) + h][:, at : at + LANES] = turned[start : start + CHUNKS[h]]
             if side == 0:
                 mark = block[:, width:]
@@ -98,9 +98,9 @@
     )(kept, flag, own, other)
 
 
-def slot_of(z, x, y_lo, core, dx, dy):
+def slot_of(z, core, peer):
     odd = (core + z) % 2
-    target = (x + dx) % 4 * 4 + (y_lo + dy) % 2 * 2 + core
+    target = peer * 2 + core
     above = (target + 16 - z - odd) % 16 // 2
     even_slot = jnp.where(above > 4, 2 * above - 9, jnp.minimum(8 - 2 * above, 7))
     odd_slot = jnp.where(above > 4, 2 * above - 8, jnp.maximum(7 - 2 * above, 0))
@@ -127,10 +127,12 @@
             total[...] += term
         else:
             term += total[...]
-    rows = out_ref.shape[1]
-    for i, place in enumerate(PLACES):
-        slot = slot_of(z, c // 4, c // 2 % 2, c % 2, *place)
-        out_ref[slot] = term[i * rows : (i + 1) * rows, :]
+    base = 0
+    for rows, start in zip(CHUNKS, STARTS):
+        for peer in range(PEERS):
+            slot = slot_of(z, c % 2, peer)
+            out_ref[slot, start : start + rows, :] = term[base : base + rows, :]
+            base += rows
 
 
 def product(pieces, s_both):
@@ -139,11 +141,11 @@
     whole = pl.BlockSpec(memory_space=pltpu.VMEM)
     return pl.pallas_call(
         product_kernel,
-        out_shape=jax.ShapeDtypeStruct((len(PLACES), block_rows, cols), jnp.float32),
+        out_shape=jax.ShapeDtypeStruct((PEERS, block_rows, cols), jnp.float32),
         in_specs=[whole] * len(pieces) + [pl.BlockSpec(memory_space=pltpu.HBM)],
         out_specs=whole,
         scratch_shapes=[
-            pltpu.VMEM((len(PLACES) * block_rows, cols), jnp.float32),
+            pltpu.VMEM((PEERS * block_rows, cols), jnp.float32),
             pltpu.VMEM((blk, cols), jnp.bfloat16),
             pltpu.SemaphoreType.DMA((blk // K_TILE,)),
         ],
@@ -178,7 +180,10 @@
 def combine_kernel(count, *refs):
     own_ref, arrived_ref = refs[0], refs[1]
     outs = refs[len(refs) - count :]
-    outs[0][...] = own_ref[...] + arrived_ref[...]
+    here = own_ref[...] + arrived_ref[...]
+    rows = here.shape[0]
+    for peer in range(PEERS):
+        outs[0][peer * rows : (peer + 1) * rows, :] = here
     if count == 2:
         outs[1][...] = refs[2][...]
 
@@ -189,10 +194,11 @@
     whole = pl.BlockSpec(memory_space=pltpu.VMEM)
     return pl.pallas_call(
         functools.partial(combine_kernel, count),
-        out_shape=[jax.ShapeDtypeStruct(a.shape, a.dtype) for a in arrays[: 2 * count : 2]],
+        out_shape=[jax.ShapeDtypeStruct((PEERS * own.shape[0], own.shape[1]), own.dtype)]
+        + [jax.ShapeDtypeStruct(a.shape, a.dtype) for a in arrays[2:]],
         in_specs=[whole] * len(arrays) + [pl.BlockSpec(memory_space=pl.ANY)],
         out_specs=[whole] * count,
-        compiler_params=pltpu.CompilerParams(vmem_limit_bytes=4 * 2**20),
+        compiler_params=pltpu.CompilerParams(vmem_limit_bytes=8 * 2**20),
     )(*arrays, after)
 
 
@@ -211,31 +217,9 @@
     )(terms, arrived, after)
 
 
-def hold_kernel(value_ref, *refs):
-    refs[-1][...] = value_ref[...]
-
-
-def hold(value, after):
-    whole = pl.BlockSpec(memory_space=pltpu.VMEM)
-    return pl.pallas_call(
-        hold_kernel,
-        out_shape=jax.ShapeDtypeStruct(value.shape, value.dtype),
-        in_specs=[whole] + [pl.BlockSpec(memory_space=pl.ANY)] * len(after),
-        out_specs=whole,
-        compiler_params=pltpu.CompilerParams(vmem_limit_bytes=4 * 2**20),
-    )(value, *after)
-
-
-def gather_col(here):
-    pieces = {(0, 0): here}
-    pieces[0, 1] = col_move(here, lambda x, y, k: (x, 1 - y, k))
-    for d in (1, 3):
-        pieces[d, 0] = col_move(here, lambda x, y, k, d=d: (x - d, y, k))
-        pieces[d, 1] = col_move(pieces[d, 0], lambda x, y, k: (x, 1 - y, k))
-    held = hold(here, [pieces[1, 0], pieces[3, 0]])
-    pieces[2, 0] = col_move(held, lambda x, y, k: (x - 2, y, k))
-    pieces[2, 1] = col_move(pieces[0, 1], lambda x, y, k: (x - 2, y, k))
-    return pieces
+def gather_col(copies):
+    groups = [[peer * 2 + core for peer in range(PEERS)] for core in range(2)]
+    return lax.all_to_all(copies, "col", 0, 0, axis_index_groups=groups, tiled=True)
 
 
 def per_device(window_rows, secular, source, kept_count):
@@ -261,9 +245,7 @@
         here, *next_leaving = combine(own_parts[h], arrived, cross_parts[h + 1] if h + 1 < len(CHUNKS) else None, masked)
         if next_leaving:
             leaving = next_leaving[0]
-        gathered = gather_col(here)
-        pieces.append(gathered)
-    pieces = [gathered[p] for p in PLACES for gathered in pieces]
+        pieces.append(gather_col(here))
 
     s_both = pltpu.with_memory_space_constraint(s_both, pltpu.HBM)
     terms = product(pieces, s_both)

time: 190 us -> 189 us (level)
  blocking collectives: 0 us -> 29.6 us
  waiting for transfers between devices: 55.4 us -> 35 us
  starting transfers between devices: 108 us -> 93.3 us
  local copies, waits for them, and re-layouts: 6.28 us -> 10.5 us
    ppermute x8 -> x1, starting transfers between devices: 31.9 us -> 1.91 us  [col_move(): return lax.ppermute(value, 'col', pairs)]
    all_to_all x0 -> x1, blocking collectives: none -> 29.6 us  [gather_col(): lax.all_to_all(copies, 'col', 0, 0, axis_index_groups=groups, tiled=True)]
    ppermute x8 -> x1, waiting for transfers between devices: 23.8 us -> 0.01 us  [col_move(): return lax.ppermute(value, 'col', pairs)]
    ppermute x1 -> x2, starting transfers between devices: 15.7 us -> 28.2 us  [per_device(): arrived = lax.ppermute(leaving, 'grp', [(i, i ^ 16) for i in range(32)])]
    all_to_all x0 -> x1, starting transfers between devices: none -> 10.3 us  [gather_col(): lax.all_to_all(copies, 'col', 0, 0, axis_index_groups=groups, tiled=True)]
    ppermute x11, starting transfers between devices: 60.8 us -> 52.9 us  [slice_move(): return lax.ppermute(value, ('grp', 'col'), pairs)]
    all_to_all x0 -> x1, waiting for transfers between devices: none -> 5.82 us  [gather_col(): lax.all_to_all(copies, 'col', 0, 0, axis_index_groups=groups, tiled=True)]
    unnamed x6 -> x14, local copies, waits for them, and re-layouts: 5.62 us -> 9.81 us
  transfers between devices with their start and end apart: 20 -> 15, of which waited for: 11 -> 7; matrix products, arithmetic and copies ran while one was open for 0% -> 0% of each run, Pallas kernels for 5% -> 5%
where the time goes in v8:
time: 189 us; the launch traced here: 186 us
  starting transfers between devices  93.3 us (49%)
  waiting for transfers between devices  35 us (19%)
  blocking collectives  29.6 us (16%)
  Pallas kernels  15.5 us (8%)
  local copies, waits for them, and re-layouts  10.5 us (6%)
    ppermute x11, starting transfers between devices, slice_move(): return lax.ppermute(value, ('grp', 'col'), pairs)  52.9 us
    all_to_all x1, blocking collectives, gather_col(): lax.all_to_all(copies, 'col', 0, 0, axis_index_groups=groups, tiled=True)  29.6 us
    ppermute x2, starting transfers between devices, per_device(): arrived = lax.ppermute(leaving, 'grp', [(i, i ^ 16) for i in range(32)])  28.2 us
    ppermute x11, waiting for transfers between devices, slice_move(): return lax.ppermute(value, ('grp', 'col'), pairs)  23.4 us
    all_to_all x1, starting transfers between devices, gather_col(): lax.all_to_all(copies, 'col', 0, 0, axis_index_groups=groups, tiled=True)  10.3 us
    unnamed x14, local copies, waits for them, and re-layouts  9.81 us
    pallas_call x1, Pallas kernels, product(): pl.pallas_call(product_kernel, out_shape=jax.ShapeDtypeStruct((PEERS, blo...  5.89 us
    all_to_all x1, waiting for transfers between devices, gather_col(): lax.all_to_all(copies, 'col', 0, 0, axis_index_groups=groups, tiled=True)  5.82 us
  transfers between devices with their start and end apart: 15, of which 7 were waited for; matrix products, arithmetic and copies ran while one was open for 0% of the time, Pallas kernels for 5%

profile of v8, /device:TPU:6, one launch (start us, length us, event | category | flops | bytes accessed | tf_op | source)
XLA Modules:
  0.0 185.7 jit_solution(13967540479888812838)
XLA Ops:
  0.0 1.9 %collective-permute-start.1 = (bf16[3840,256]{1,0:T(8,128)(2,1)}, bf16[3840,256]{1,0:T(8,128)(2,1)S(1)}, u32[]{:S(2)}, u32[]{:S(2)}) collective-permute-start(bf16[3840,256]{1,0:T(8,128)(2,1)} %own_ref.1), channel_id=1, source_target_pairs={{0,1},{1,0},{2,3},{3,2},{4,5},{5,4},{6,7},{7,6},{8,9},{9,8},{10,11... | collective-permute-start | bytes 5898248 | tf_op jit(solution)/shard_map/ppermute | solution.py:162
  1.9 0.7 subtract_select_fusion.place_ref
  2.7 1.0 copy-done.6
  3.7 5.8 %shard_map.46 = (bf16[32,3840]{1,0:T(8,128)(2,1)S(1)}, bf16[32,3840]{1,0:T(8,128)(2,1)S(1)}, bf16[32,3840]{1,0:T(8,128)(2,1)S(1)}, bf16[32,3840]{1,0:T(8,128)(2,1)S(1)}, bf16[3840,128]{1,0:T(8,128)(2,1)S(1)}) custom-call(s32[3840]{0:T(1024)S(1)} %subtract_select_fusion.place_ref, bf16[64,3840]{1,0:T(8,128)(2,1)S(1)} %bitcast.38), custom_call_target="tpu_custom_call" | custom-call | tf_op jit(solution)/shard_map/pallas_call | solution.py:47
  9.4 15.7 %collective-permute-start = (bf16[32,3840]{1,0:T(8,128)(2,1)S(1)}, bf16[32,3840]{1,0:T(8,128)(2,1)S(1)}, u32[]{:S(2)}, u32[]{:S(2)}) collective-permute-start(bf16[32,3840]{1,0:T(8,128)(2,1)S(1)} %get-tuple-element.15), channel_id=1, source_target_pairs={{0,256},{16,272},{32,288},{48,304},{64,320},{80,336},{96,352},{112... | collective-permute-start | bytes 737288 | tf_op jit(solution)/shard_map/ppermute | solution.py:244
  25.8 1.5 copy-done.4
  27.4 3.5 %shard_map.47 = (bf16[3840,1024]{1,0:T(8,128)(2,1)S(1)}, f32[8,128]{1,0:T(8,128)S(1)}) custom-call(s32[1]{0:T(128)S(6)} %copy.9.kept_ref, bf16[3840,128]{1,0:T(8,128)(2,1)S(1)} %get-tuple-element.17.flag_ref, bf16[3840,256]{1,0:T(8,128)(2,1)S(1)} %copy-done.4, bf16[3840,256]{1,0:T(8,128)(2,1)S(1)} %collective-permute-done.1.other_ref), custom_call_target="tpu_custom_call" | custom-call | tf_op jit(solution)/shard_map/pallas_call | solution.py:83
  30.9 3.1 %copy-done = bf16[3840,1024]{1,0:T(8,128)(2,1)} copy-done((bf16[3840,1024]{1,0:T(8,128)(2,1)}, bf16[3840,1024]{1,0:T(8,128)(2,1)S(1)}, u32[]{:S(2)}) %copy-start) | copy-done | bytes 7864344
  34.1 1.3 copy-done.5
  35.4 10.3 %all-to-all-start = ((bf16[8,32,3840]{2,1,0:T(8,128)(2,1)}), bf16[8,32,3840]{2,1,0:T(8,128)(2,1)S(1)}, u32[]{:S(2)}, u32[]{:S(2)}) async-start(bf16[8,32,3840]{2,1,0:T(8,128)(2,1)} %bitcast.37), calls=%async_computation | async-start | bytes 3932160 | tf_op jit(solution)/shard_map/all_to_all | solution.py:222
  45.6 12.4 %collective-permute-start.2 = (bf16[32,3840]{1,0:T(8,128)(2,1)S(1)}, bf16[32,3840]{1,0:T(8,128)(2,1)S(1)}, u32[]{:S(2)}, u32[]{:S(2)}) collective-permute-start(bf16[32,3840]{1,0:T(8,128)(2,1)S(1)} %get-tuple-element.21), channel_id=1, source_target_pairs={{0,256},{16,272},{32,288},{48,304},{64,320},{80,336},{96,352},{112... | collective-permute-start | bytes 737288 | tf_op jit(solution)/shard_map/ppermute | solution.py:244
  58.1 5.8 %collective-permute-done.2.refs_1_ = bf16[32,3840]{1,0:T(8,128)(2,1)S(1)} collective-permute-done((bf16[32,3840]{1,0:T(8,128)(2,1)S(1)}, bf16[32,3840]{1,0:T(8,128)(2,1)S(1)}, u32[]{:S(2)}, u32[]{:S(2)}) %collective-permute-start.2) | collective-permute-done | bytes 245792 | tf_op jit(solution)/shard_map/ppermute | solution.py:244
  64.0 1.4 copy-done.3
  65.4 5.8 %all-to-all-done = bf16[8,32,3840]{2,1,0:T(8,128)(2,1)S(1)} async-done(((bf16[8,32,3840]{2,1,0:T(8,128)(2,1)}), bf16[8,32,3840]{2,1,0:T(8,128)(2,1)S(1)}, u32[]{:S(2)}, u32[]{:S(2)}) %all-to-all-start) | async-done | bytes 1966112 | tf_op jit(solution)/shard_map/all_to_all | solution.py:222
  71.2 29.6 %all_to_all.22 = bf16[8,32,3840]{2,1,0:T(8,128)(2,1)S(1)} all-to-all(bf16[8,32,3840]{2,1,0:T(8,128)(2,1)} %bitcast.35), channel_id=1, replica_groups={{0,2,4,6,8,10,12,14},{1,3,5,7,9,11,13,15},{16,18,20,22,24,26,28,30},{17..., dimensions={0} | all-to-all | bytes 3932160 | tf_op jit(solution)/shard_map/all_to_all | solution.py:222
  100.8 1.5 copy-done.2
  102.3 5.9 %shard_map.50.terms_ref = f32[8,64,1024]{2,1,0:T(8,128)S(1)} custom-call(bf16[256,3840]{1,0:T(8,128)(2,1)S(1)} %bitcast.34, bf16[256,3840]{1,0:T(8,128)(2,1)S(1)} %bitcast.36, bf16[3840,1024]{1,0:T(8,128)(2,1)} %copy-done), custom_call_target="tpu_custom_call" | custom-call | tf_op jit(solution)/shard_map/pallas_call | solution.py:142
  108.3 14.8 %collective-permute-start.4 = (f32[64,1024]{1,0:T(8,128)S(1)}, f32[64,1024]{1,0:T(8,128)S(1)}, u32[]{:S(2)}, u32[]{:S(2)}) collective-permute-start(f32[64,1024]{1,0:T(8,128)S(1)} %get-tuple-element.26), channel_id=1, source_target_pairs={{0,32},{1,481},{2,34},{3,483},{4,36},{5,485},{6,38},{7,487},{8,40}... | collective-permute-start | bytes 786440 | tf_op jit(solution)/shard_map/ppermute | solution.py:172
  123.0 1.9 %collective-permute-start.3 = (f32[64,1024]{1,0:T(8,128)S(1)}, f32[64,1024]{1,0:T(8,128)S(1)}, u32[]{:S(2)}, u32[]{:S(2)}) collective-permute-start(f32[64,1024]{1,0:T(8,128)S(1)} %get-tuple-element.25), channel_id=1, source_target_pairs={{0,32},{1,481},{2,34},{3,483},{4,36},{5,485},{6,38},{7,487},{8,40}... | collective-permute-start | bytes 786440 | tf_op jit(solution)/shard_map/ppermute | solution.py:172
  125.0 2.4 %collective-permute-done.4 = f32[64,1024]{1,0:T(8,128)S(1)} collective-permute-done((f32[64,1024]{1,0:T(8,128)S(1)}, f32[64,1024]{1,0:T(8,128)S(1)}, u32[]{:S(2)}, u32[]{:S(2)}) %collective-permute-start.4) | collective-permute-done | bytes 262176 | tf_op jit(solution)/shard_map/ppermute | solution.py:172
  127.4 9.3 %collective-permute-start.6 = (f32[64,1024]{1,0:T(8,128)S(1)}, f32[64,1024]{1,0:T(8,128)S(1)}, u32[]{:S(2)}, u32[]{:S(2)}) collective-permute-start(f32[64,1024]{1,0:T(8,128)S(1)} %fusion.2.after_ref), channel_id=1, source_target_pairs={{0,480},{1,33},{2,482},{3,35},{4,484},{5,37},{6,486},{7,39},{8,488... | collective-permute-start | bytes 786440 | tf_op jit(solution)/shard_map/ppermute | solution.py:172
  136.8 5.4 %collective-permute-start.5 = (f32[64,1024]{1,0:T(8,128)S(1)}, f32[64,1024]{1,0:T(8,128)S(1)}, u32[]{:S(2)}, u32[]{:S(2)}) collective-permute-start(f32[64,1024]{1,0:T(8,128)S(1)} %shard_map.51), channel_id=1, source_target_pairs={{0,480},{1,33},{2,482},{3,35},{4,484},{5,37},{6,486},{7,39},{8,488... | collective-permute-start | bytes 786440 | tf_op jit(solution)/shard_map/ppermute | solution.py:172
  142.3 1.9 %collective-permute-start.8 = (f32[64,1024]{1,0:T(8,128)S(1)}, f32[64,1024]{1,0:T(8,128)S(1)}, u32[]{:S(2)}, u32[]{:S(2)}) collective-permute-start(f32[64,1024]{1,0:T(8,128)S(1)} %fusion.1.after_ref), channel_id=1, source_target_pairs={{0,32},{1,481},{2,34},{3,483},{4,36},{5,485},{6,38},{7,487},{8,40}... | collective-permute-start | bytes 786440 | tf_op jit(solution)/shard_map/ppermute | solution.py:172
  144.2 4.5 %collective-permute-done.5.arrived_ref = f32[64,1024]{1,0:T(8,128)S(1)} collective-permute-done((f32[64,1024]{1,0:T(8,128)S(1)}, f32[64,1024]{1,0:T(8,128)S(1)}, u32[]{:S(2)}, u32[]{:S(2)}) %collective-permute-start.5) | collective-permute-done | bytes 262176 | tf_op jit(solution)/shard_map/ppermute | solution.py:172
  148.7 1.9 %collective-permute-start.7 = (f32[64,1024]{1,0:T(8,128)S(1)}, f32[64,1024]{1,0:T(8,128)S(1)}, u32[]{:S(2)}, u32[]{:S(2)}) collective-permute-start(f32[64,1024]{1,0:T(8,128)S(1)} %shard_map.52), channel_id=1, source_target_pairs={{0,32},{1,481},{2,34},{3,483},{4,36},{5,485},{6,38},{7,487},{8,40}... | collective-permute-start | bytes 786440 | tf_op jit(solution)/shard_map/ppermute | solution.py:172
  150.7 4.4 %collective-permute-start.9 = (f32[64,1024]{1,0:T(8,128)S(1)}, f32[64,1024]{1,0:T(8,128)S(1)}, u32[]{:S(2)}, u32[]{:S(2)}) collective-permute-start(f32[64,1024]{1,0:T(8,128)S(1)} %fusion), channel_id=1, source_target_pairs={{0,384},{1,129},{2,386},{3,131},{4,388},{5,133},{6,390},{7,135},{8... | collective-permute-start | bytes 786440 | tf_op jit(solution)/shard_map/ppermute | solution.py:172
  155.2 12.3 %collective-permute-done.7 = f32[64,1024]{1,0:T(8,128)S(1)} collective-permute-done((f32[64,1024]{1,0:T(8,128)S(1)}, f32[64,1024]{1,0:T(8,128)S(1)}, u32[]{:S(2)}, u32[]{:S(2)}) %collective-permute-start.7) | collective-permute-done | bytes 262176 | tf_op jit(solution)/shard_map/ppermute | solution.py:172
  168.3 5.6 %collective-permute-start.11 = (f32[32,512]{1,0:T(8,128)S(1)}, f32[32,512]{1,0:T(8,128)S(1)}, u32[]{:S(2)}, u32[]{:S(2)}) collective-permute-start(f32[32,512]{1,0:T(8,128)S(1)} %get-tuple-element.27), channel_id=1, source_target_pairs={{0,1},{1,33},{2,3},{3,35},{4,5},{5,37},{6,7},{7,39},{8,9},{9,41},{... | collective-permute-start | bytes 196616 | tf_op jit(solution)/shard_map/ppermute | solution.py:172
  173.9 3.5 %collective-permute-start.12 = (f32[32,512]{1,0:T(8,128)S(1)}, f32[32,512]{1,0:T(8,128)S(1)}, u32[]{:S(2)}, u32[]{:S(2)}) collective-permute-start(f32[32,512]{1,0:T(8,128)S(1)} %get-tuple-element.23), channel_id=1, source_target_pairs={{0,17},{1,49},{2,19},{3,51},{4,21},{5,53},{6,23},{7,55},{8,25},{9,... | collective-permute-start | bytes 196616 | tf_op jit(solution)/shard_map/ppermute | solution.py:172
  177.4 3.5 %collective-permute-start.13 = (f32[32,512]{1,0:T(8,128)S(1)}, f32[32,512]{1,0:T(8,128)S(1)}, u32[]{:S(2)}, u32[]{:S(2)}) collective-permute-start(f32[32,512]{1,0:T(8,128)S(1)} %get-tuple-element.28), channel_id=1, source_target_pairs={{0,16},{1,32},{2,18},{3,34},{4,20},{5,36},{6,22},{7,38},{8,24},{9,... | collective-permute-start | bytes 196616 | tf_op jit(solution)/shard_map/ppermute | solution.py:172
  180.9 2.8 %collective-permute-done.12 = f32[32,512]{1,0:T(8,128)S(1)} collective-permute-done((f32[32,512]{1,0:T(8,128)S(1)}, f32[32,512]{1,0:T(8,128)S(1)}, u32[]{:S(2)}, u32[]{:S(2)}) %collective-permute-start.12) | collective-permute-done | bytes 65568 | tf_op jit(solution)/shard_map/ppermute | solution.py:172
  183.6 1.4 collective-permute-done.13
  (29 shorter events, 1.9 us)
Async XLA Ops:
  0.0 25.8 %collective-permute-start.1 = (bf16[3840,256]{1,0:T(8,128)(2,1)}, bf16[3840,256]{1,0:T(8,128)(2,1)S(1)}, u32[]{:S(2)}, u32[]{:S(2)}) collective-permute-start(bf16[3840,256]{1,0:T(8,128)(2,1)} %own_ref.1), channel_id=1, source_target_pairs={{0,1},{1,0},{2,3},{3,2},{4,5},{5,4},{6,7},{7,6},{8,9},{9,8},{10,11... | collective-permute-start | bytes 5898248 | tf_op jit(solution)/shard_map/ppermute | solution.py:162
  2.7 1.0 copy-start.6
  9.4 24.5 %collective-permute-start = (bf16[32,3840]{1,0:T(8,128)(2,1)S(1)}, bf16[32,3840]{1,0:T(8,128)(2,1)S(1)}, u32[]{:S(2)}, u32[]{:S(2)}) collective-permute-start(bf16[32,3840]{1,0:T(8,128)(2,1)S(1)} %get-tuple-element.15), channel_id=1, source_target_pairs={{0,256},{16,272},{32,288},{48,304},{64,320},{80,336},{96,352},{112... | collective-permute-start | bytes 737288 | tf_op jit(solution)/shard_map/ppermute | solution.py:244
  25.8 1.5 copy-start.4
  30.8 3.1 %copy-start = (bf16[3840,1024]{1,0:T(8,128)(2,1)}, bf16[3840,1024]{1,0:T(8,128)(2,1)S(1)}, u32[]{:S(2)}) copy-start(bf16[3840,1024]{1,0:T(8,128)(2,1)S(1)} %get-tuple-element.22.refs_2_) | copy-start | bytes 23592964
  34.1 1.3 copy-start.5
  35.4 35.8 %all-to-all-start = ((bf16[8,32,3840]{2,1,0:T(8,128)(2,1)}), bf16[8,32,3840]{2,1,0:T(8,128)(2,1)S(1)}, u32[]{:S(2)}, u32[]{:S(2)}) async-start(bf16[8,32,3840]{2,1,0:T(8,128)(2,1)} %bitcast.37), calls=%async_computation | async-start | bytes 3932160 | tf_op jit(solution)/shard_map/all_to_all | solution.py:222
  45.6 18.2 %collective-permute-start.2 = (bf16[32,3840]{1,0:T(8,128)(2,1)S(1)}, bf16[32,3840]{1,0:T(8,128)(2,1)S(1)}, u32[]{:S(2)}, u32[]{:S(2)}) collective-permute-start(bf16[32,3840]{1,0:T(8,128)(2,1)S(1)} %get-tuple-element.21), channel_id=1, source_target_pairs={{0,256},{16,272},{32,288},{48,304},{64,320},{80,336},{96,352},{112... | collective-permute-start | bytes 737288 | tf_op jit(solution)/shard_map/ppermute | solution.py:244
  64.0 1.4 copy-start.3
  71.2 29.6 %copy-start.1 = (bf16[8,32,3840]{2,1,0:T(8,128)(2,1)}, bf16[8,32,3840]{2,1,0:T(8,128)(2,1)S(1)}, u32[]{:S(2)}) copy-start(bf16[8,32,3840]{2,1,0:T(8,128)(2,1)S(1)} %all-to-all-done) | copy-start | bytes 5898244
  100.8 1.5 copy-start.2
  108.3 19.1 %collective-permute-start.4 = (f32[64,1024]{1,0:T(8,128)S(1)}, f32[64,1024]{1,0:T(8,128)S(1)}, u32[]{:S(2)}, u32[]{:S(2)}) collective-permute-start(f32[64,1024]{1,0:T(8,128)S(1)} %get-tuple-element.26), channel_id=1, source_target_pairs={{0,32},{1,481},{2,34},{3,483},{4,36},{5,485},{6,38},{7,487},{8,40}... | collective-permute-start | bytes 786440 | tf_op jit(solution)/shard_map/ppermute | solution.py:172
  123.0 13.7 %collective-permute-start.3 = (f32[64,1024]{1,0:T(8,128)S(1)}, f32[64,1024]{1,0:T(8,128)S(1)}, u32[]{:S(2)}, u32[]{:S(2)}) collective-permute-start(f32[64,1024]{1,0:T(8,128)S(1)} %get-tuple-element.25), channel_id=1, source_target_pairs={{0,32},{1,481},{2,34},{3,483},{4,36},{5,485},{6,38},{7,487},{8,40}... | collective-permute-start | bytes 786440 | tf_op jit(solution)/shard_map/ppermute | solution.py:172
  127.4 14.8 %collective-permute-start.6 = (f32[64,1024]{1,0:T(8,128)S(1)}, f32[64,1024]{1,0:T(8,128)S(1)}, u32[]{:S(2)}, u32[]{:S(2)}) collective-permute-start(f32[64,1024]{1,0:T(8,128)S(1)} %fusion.2.after_ref), channel_id=1, source_target_pairs={{0,480},{1,33},{2,482},{3,35},{4,484},{5,37},{6,486},{7,39},{8,488... | collective-permute-start | bytes 786440 | tf_op jit(solution)/shard_map/ppermute | solution.py:172
  136.8 11.8 %collective-permute-start.5 = (f32[64,1024]{1,0:T(8,128)S(1)}, f32[64,1024]{1,0:T(8,128)S(1)}, u32[]{:S(2)}, u32[]{:S(2)}) collective-permute-start(f32[64,1024]{1,0:T(8,128)S(1)} %shard_map.51), channel_id=1, source_target_pairs={{0,480},{1,33},{2,482},{3,35},{4,484},{5,37},{6,486},{7,39},{8,488... | collective-permute-start | bytes 786440 | tf_op jit(solution)/shard_map/ppermute | solution.py:172
  142.3 8.4 %collective-permute-start.8 = (f32[64,1024]{1,0:T(8,128)S(1)}, f32[64,1024]{1,0:T(8,128)S(1)}, u32[]{:S(2)}, u32[]{:S(2)}) collective-permute-start(f32[64,1024]{1,0:T(8,128)S(1)} %fusion.1.after_ref), channel_id=1, source_target_pairs={{0,32},{1,481},{2,34},{3,483},{4,36},{5,485},{6,38},{7,487},{8,40}... | collective-permute-start | bytes 786440 | tf_op jit(solution)/shard_map/ppermute | solution.py:172
  148.7 18.8 %collective-permute-start.7 = (f32[64,1024]{1,0:T(8,128)S(1)}, f32[64,1024]{1,0:T(8,128)S(1)}, u32[]{:S(2)}, u32[]{:S(2)}) collective-permute-start(f32[64,1024]{1,0:T(8,128)S(1)} %shard_map.52), channel_id=1, source_target_pairs={{0,32},{1,481},{2,34},{3,483},{4,36},{5,485},{6,38},{7,487},{8,40}... | collective-permute-start | bytes 786440 | tf_op jit(solution)/shard_map/ppermute | solution.py:172
  150.7 16.8 %collective-permute-start.9 = (f32[64,1024]{1,0:T(8,128)S(1)}, f32[64,1024]{1,0:T(8,128)S(1)}, u32[]{:S(2)}, u32[]{:S(2)}) collective-permute-start(f32[64,1024]{1,0:T(8,128)S(1)} %fusion), channel_id=1, source_target_pairs={{0,384},{1,129},{2,386},{3,131},{4,388},{5,133},{6,390},{7,135},{8... | collective-permute-start | bytes 786440 | tf_op jit(solution)/shard_map/ppermute | solution.py:172
  167.6 13.3 %collective-permute-start.10 = (f32[32,512]{1,0:T(8,128)S(1)}, f32[32,512]{1,0:T(8,128)S(1)}, u32[]{:S(2)}, u32[]{:S(2)}) collective-permute-start(f32[32,512]{1,0:T(8,128)S(1)} %get-tuple-element.24), channel_id=1, source_target_pairs={{1,48},{3,50},{5,52},{7,54},{9,56},{11,58},{13,60},{15,62},{17,32}... | collective-permute-start | bytes 196616 | tf_op jit(solution)/shard_map/ppermute | solution.py:172
  168.3 12.6 %collective-permute-start.11 = (f32[32,512]{1,0:T(8,128)S(1)}, f32[32,512]{1,0:T(8,128)S(1)}, u32[]{:S(2)}, u32[]{:S(2)}) collective-permute-start(f32[32,512]{1,0:T(8,128)S(1)} %get-tuple-element.27), channel_id=1, source_target_pairs={{0,1},{1,33},{2,3},{3,35},{4,5},{5,37},{6,7},{7,39},{8,9},{9,41},{... | collective-permute-start | bytes 196616 | tf_op jit(solution)/shard_map/ppermute | solution.py:172
  173.9 9.8 %collective-permute-start.12 = (f32[32,512]{1,0:T(8,128)S(1)}, f32[32,512]{1,0:T(8,128)S(1)}, u32[]{:S(2)}, u32[]{:S(2)}) collective-permute-start(f32[32,512]{1,0:T(8,128)S(1)} %get-tuple-element.23), channel_id=1, source_target_pairs={{0,17},{1,49},{2,19},{3,51},{4,21},{5,53},{6,23},{7,55},{8,25},{9,... | collective-permute-start | bytes 196616 | tf_op jit(solution)/shard_map/ppermute | solution.py:172
  177.4 7.7 %collective-permute-start.13 = (f32[32,512]{1,0:T(8,128)S(1)}, f32[32,512]{1,0:T(8,128)S(1)}, u32[]{:S(2)}, u32[]{:S(2)}) collective-permute-start(f32[32,512]{1,0:T(8,128)S(1)} %get-tuple-element.28), channel_id=1, source_target_pairs={{0,16},{1,32},{2,18},{3,34},{4,20},{5,36},{6,22},{7,38},{8,24},{9,... | collective-permute-start | bytes 196616 | tf_op jit(solution)/shard_map/ppermute | solution.py:172

commit v9 on v8

--- a/solution.py
+++ b/solution.py
@@ -10,6 +10,7 @@
 LANES = 128
 UNROLL = 32
 K_TILE = 768
+OUTER = 3
 CHUNKS = (32, 32)
 STARTS = tuple(sum(CHUNKS[:h]) for h in range(len(CHUNKS)))
 PEERS = 8
@@ -108,18 +109,26 @@
 
 
 def product_kernel(*refs):
-    count = len(refs) - 5
+    count = len(CHUNKS)
     pieces = refs[:count]
-    s_hbm, out_ref, total, s_ref, sems = refs[count:]
+    s_hbm, out_ref, total, lhs_ref, s_ref, sems = refs[count:]
     z, c = lax.axis_index("grp") // 2, lax.axis_index("col")
     tiles = s_ref.shape[0] // K_TILE
     spans = [pl.ds(k * K_TILE, K_TILE) for k in range(tiles)]
-    copies = [pltpu.make_async_copy(s_hbm.at[span], s_ref.at[span], sems.at[k]) for k, span in enumerate(spans)]
-    for copy in copies:
-        copy.start()
+    copies = []
     for k, span in enumerate(spans):
-        copies[k].wait()
-        lhs = jnp.concatenate([ref[:, span] for ref in pieces], axis=0)
+        tile = [pltpu.make_async_copy(s_hbm.at[span], s_ref.at[span], sems.at[k, count])]
+        for h, (rows, start) in enumerate(zip(CHUNKS, STARTS)):
+            there = lhs_ref.at[pl.ds(start * PEERS, rows * PEERS), span]
+            tile.append(pltpu.make_async_copy(pieces[h].at[:, span], there, sems.at[k, h]))
+        copies.append(tile)
+    for tile in copies:
+        for copy in tile:
+            copy.start()
+    for k, span in enumerate(spans):
+        for copy in copies[k]:
+            copy.wait()
+        lhs = lhs_ref[:, span]
         term = jnp.dot(lhs, s_ref[span, :], preferred_element_type=jnp.float32)
         if k == 0:
             total[...] = term
@@ -138,18 +147,19 @@
 def product(pieces, s_both):
     blk, cols = s_both.shape
     block_rows = sum(CHUNKS)
-    whole = pl.BlockSpec(memory_space=pltpu.VMEM)
+    hbm = pl.BlockSpec(memory_space=pltpu.HBM)
     return pl.pallas_call(
         product_kernel,
         out_shape=jax.ShapeDtypeStruct((PEERS, block_rows, cols), jnp.float32),
-        in_specs=[whole] * len(pieces) + [pl.BlockSpec(memory_space=pltpu.HBM)],
-        out_specs=whole,
+        in_specs=[hbm] * (len(pieces) + 1),
+        out_specs=pl.BlockSpec(memory_space=pltpu.VMEM),
         scratch_shapes=[
             pltpu.VMEM((PEERS * block_rows, cols), jnp.float32),
+            pltpu.VMEM((PEERS * block_rows, blk), jnp.bfloat16),
             pltpu.VMEM((blk, cols), jnp.bfloat16),
-            pltpu.SemaphoreType.DMA((blk // K_TILE,)),
+            pltpu.SemaphoreType.DMA((blk // K_TILE, len(CHUNKS) + 1)),
         ],
-        compiler_params=pltpu.CompilerParams(vmem_limit_bytes=20 * 2**20),
+        compiler_params=pltpu.CompilerParams(vmem_limit_bytes=24 * 2**20),
     )(*pieces, s_both)
 
 
@@ -177,28 +187,35 @@
     return (z + 1 if even == (step % 2 == 1) else z - 1, y_hi, c)
 
 
-def combine_kernel(count, *refs):
+def combine_kernel(*refs):
     own_ref, arrived_ref = refs[0], refs[1]
-    outs = refs[len(refs) - count :]
-    here = own_ref[...] + arrived_ref[...]
+    here, sems = refs[-2:]
+    handed_on = len(refs) == 8
+    copies_hbm = refs[4 if handed_on else 3]
+    here[...] = own_ref[...] + arrived_ref[...]
     rows = here.shape[0]
-    for peer in range(PEERS):
-        outs[0][peer * rows : (peer + 1) * rows, :] = here
-    if count == 2:
-        outs[1][...] = refs[2][...]
+    copies = [
+        pltpu.make_async_copy(here, copies_hbm.at[pl.ds(peer * rows, rows)], sems.at[peer]) for peer in range(PEERS)
+    ]
+    for copy in copies:
+        copy.start()
+    if handed_on:
+        refs[5][...] = refs[2][...]
+    for copy in copies:
+        copy.wait()
 
 
 def combine(own, arrived, following, after):
-    count = 1 if following is None else 2
     arrays = [own, arrived] + ([] if following is None else [following])
     whole = pl.BlockSpec(memory_space=pltpu.VMEM)
     return pl.pallas_call(
-        functools.partial(combine_kernel, count),
+        combine_kernel,
         out_shape=[jax.ShapeDtypeStruct((PEERS * own.shape[0], own.shape[1]), own.dtype)]
         + [jax.ShapeDtypeStruct(a.shape, a.dtype) for a in arrays[2:]],
         in_specs=[whole] * len(arrays) + [pl.BlockSpec(memory_space=pl.ANY)],
-        out_specs=[whole] * count,
-        compiler_params=pltpu.CompilerParams(vmem_limit_bytes=8 * 2**20),
+        out_specs=[pl.BlockSpec(memory_space=pltpu.HBM)] + [whole] * (len(arrays) - 2),
+        scratch_shapes=[pltpu.VMEM(own.shape, own.dtype), pltpu.SemaphoreType.DMA((PEERS,))],
+        compiler_params=pltpu.CompilerParams(vmem_limit_bytes=4 * 2**20),
     )(*arrays, after)
 
 
@@ -248,13 +265,17 @@
         pieces.append(gather_col(here))
 
     s_both = pltpu.with_memory_space_constraint(s_both, pltpu.HBM)
+    pieces = [pltpu.with_memory_space_constraint(piece, pltpu.HBM) for piece in pieces]
     terms = product(pieces, s_both)
-    outer, inner = terms[0], terms[4]
-    for step in range(1, 4):
+    outer, inner = terms[0], terms[OUTER]
+    for step in range(1, OUTER):
         outer = terms[step] + slice_move(outer, functools.partial(exchange, step))
-        inner = slice_move(inner, functools.partial(exchange, step))
-        inner = add_term(terms, 4 + step, inner, outer) if step < 3 else terms[7] + inner
-    inner += slice_move(outer, lambda z, y_hi, c: (z + 4 if (c - z) % 2 else z - 4, y_hi, c))
+        inner = slice_move(inner, functools.partial(exchange, step + OUTER))
+        inner = add_term(terms, OUTER + step, inner, outer)
+    skipped = slice_move(outer, lambda z, y_hi, c: (z - 5 if (c - z) % 2 else z + 5, y_hi, c))
+    for step in range(OUTER, 8 - OUTER):
+        inner = terms[OUTER + step] + slice_move(inner, functools.partial(exchange, step + OUTER))
+    inner += skipped
 
     half_cols = inner.shape[1] // 2
     mine, theirs = inner[:, :half_cols], inner[:, half_cols:]

time: 189 us -> 197 us (1.042)
  the two profiles are of different devices: /device:TPU:6 before, /device:TPU:8 now
where the time goes in v9:
time: 197 us
  starting transfers between devices  93.7 us (48%)
  waiting for transfers between devices  46.3 us (24%)
  blocking collectives  28.9 us (15%)
  Pallas kernels  19.5 us (10%)
  local copies, waits for them, and re-layouts  6.27 us (3%)
    ppermute x11, starting transfers between devices, slice_move(): return lax.ppermute(value, ('grp', 'col'), pairs)  52.6 us
    ppermute x11, waiting for transfers between devices, slice_move(): return lax.ppermute(value, ('grp', 'col'), pairs)  34.2 us
    all_to_all x1, blocking collectives, gather_col(): lax.all_to_all(copies, 'col', 0, 0, axis_index_groups=groups, tiled=True)  28.9 us
    ppermute x2, starting transfers between devices, per_device(): arrived = lax.ppermute(leaving, 'grp', [(i, i ^ 16) for i in range(32)])  28.2 us
    all_to_all x1, starting transfers between devices, gather_col(): lax.all_to_all(copies, 'col', 0, 0, axis_index_groups=groups, tiled=True)  11 us
    all_to_all x1, waiting for transfers between devices, gather_col(): lax.all_to_all(copies, 'col', 0, 0, axis_index_groups=groups, tiled=True)  6.31 us
    pallas_call x1, Pallas kernels, product(): pl.pallas_call(product_kernel, out_shape=jax.ShapeDtypeStruct((PEERS, blo...  6.17 us
    ppermute x2, waiting for transfers between devices, per_device(): arrived = lax.ppermute(leaving, 'grp', [(i, i ^ 16) for i in range(32)])  5.8 us
  transfers between devices with their start and end apart: 15, of which 9 were waited for; matrix products, arithmetic and copies ran while one was open for 0% of the time, Pallas kernels for 6%

profile of v9, /device:TPU:8, one launch (start us, length us, event | category | flops | bytes accessed | tf_op | source)
XLA Modules:
  0.0 196.5 jit_solution(15161442935655973123)
XLA Ops:
  0.0 1.9 collective-permute-start.1
  1.9 0.7 subtract_select_fusion.place_ref
  2.7 1.0 copy-done.2
  3.7 5.8 %shard_map.46 = (bf16[32,3840]{1,0:T(8,128)(2,1)S(1)}, bf16[32,3840]{1,0:T(8,128)(2,1)S(1)}, bf16[32,3840]{1,0:T(8,128)(2,1)S(1)}, bf16[32,3840]{1,0:T(8,128)(2,1)S(1)}, bf16[3840,128]{1,0:T(8,128)(2,1)S(1)}) custom-call(s32[3840]{0:T(1024)S(1)} %subtract_select_fusion.place_ref, bf16[64,3840]{1,0:T(8,128)(2,1)S(1)} %bitcast.35), custom_call_target="tpu_custom_call" | custom-call | tf_op jit(solution)/shard_map/pallas_call | solution.py:48
  9.4 15.7 %collective-permute-start = (bf16[32,3840]{1,0:T(8,128)(2,1)S(1)}, bf16[32,3840]{1,0:T(8,128)(2,1)S(1)}, u32[]{:S(2)}, u32[]{:S(2)}) collective-permute-start(bf16[32,3840]{1,0:T(8,128)(2,1)S(1)} %get-tuple-element.15), channel_id=1, source_target_pairs={{0,256},{16,272},{32,288},{48,304},{64,320},{80,336},{96,352},{112... | collective-permute-start | bytes 737288 | tf_op jit(solution)/shard_map/ppermute | solution.py:261
  25.8 1.5 copy-done.1
  27.4 3.5 %shard_map.47 = (bf16[3840,1024]{1,0:T(8,128)(2,1)S(1)}, f32[8,128]{1,0:T(8,128)S(1)}) custom-call(s32[1]{0:T(128)S(6)} %copy.9.kept_ref, bf16[3840,128]{1,0:T(8,128)(2,1)S(1)} %get-tuple-element.17.flag_ref, bf16[3840,256]{1,0:T(8,128)(2,1)S(1)} %copy-done.1, bf16[3840,256]{1,0:T(8,128)(2,1)S(1)} %collective-permute-done.1.other_ref), custom_call_target="tpu_custom_call" | custom-call | tf_op jit(solution)/shard_map/pallas_call | solution.py:84
  30.9 3.0 %copy-done = bf16[3840,1024]{1,0:T(8,128)(2,1)} copy-done((bf16[3840,1024]{1,0:T(8,128)(2,1)}, bf16[3840,1024]{1,0:T(8,128)(2,1)S(1)}, u32[]{:S(2)}) %copy-start) | copy-done | bytes 7864344
  33.9 1.4 shard_map.48
  35.3 11.0 %all-to-all-start = ((bf16[8,32,3840]{2,1,0:T(8,128)(2,1)}), bf16[8,32,3840]{2,1,0:T(8,128)(2,1)}, u32[]{:S(2)}, u32[]{:S(2)}) async-start(bf16[8,32,3840]{2,1,0:T(8,128)(2,1)} %bitcast.1), calls=%async_computation | async-start | bytes 3932160 | tf_op jit(solution)/shard_map/all_to_all | solution.py:239
  46.3 12.4 %collective-permute-start.2 = (bf16[32,3840]{1,0:T(8,128)(2,1)S(1)}, bf16[32,3840]{1,0:T(8,128)(2,1)S(1)}, u32[]{:S(2)}, u32[]{:S(2)}) collective-permute-start(bf16[32,3840]{1,0:T(8,128)(2,1)S(1)} %get-tuple-element.21), channel_id=1, source_target_pairs={{0,256},{16,272},{32,288},{48,304},{64,320},{80,336},{96,352},{112... | collective-permute-start | bytes 737288 | tf_op jit(solution)/shard_map/ppermute | solution.py:261
  58.7 5.8 %collective-permute-done.2.refs_1_ = bf16[32,3840]{1,0:T(8,128)(2,1)S(1)} collective-permute-done((bf16[32,3840]{1,0:T(8,128)(2,1)S(1)}, bf16[32,3840]{1,0:T(8,128)(2,1)S(1)}, u32[]{:S(2)}, u32[]{:S(2)}) %collective-permute-start.2) | collective-permute-done | bytes 245792 | tf_op jit(solution)/shard_map/ppermute | solution.py:261
  64.5 2.6 %shard_map.49 = bf16[256,3840]{1,0:T(8,128)(2,1)S(1)} custom-call(bf16[32,3840]{1,0:T(8,128)(2,1)S(1)} %get-tuple-element.20.refs_0_, bf16[32,3840]{1,0:T(8,128)(2,1)S(1)} %collective-permute-done.2.refs_1_, f32[8,128]{1,0:T(8,128)S(1)} %get-tuple-element.18.refs_3_.refs_2_), custom_call_target="tpu_custom_call" | custom-call | tf_op jit(solution)/shard_map/pallas_call | solution.py:211
  67.2 6.3 %all-to-all-done = bf16[8,32,3840]{2,1,0:T(8,128)(2,1)} async-done(((bf16[8,32,3840]{2,1,0:T(8,128)(2,1)}), bf16[8,32,3840]{2,1,0:T(8,128)(2,1)}, u32[]{:S(2)}, u32[]{:S(2)}) %all-to-all-start) | async-done | bytes 1966112 | tf_op jit(solution)/shard_map/all_to_all | solution.py:239
  73.5 28.9 %all_to_all.22 = bf16[8,32,3840]{2,1,0:T(8,128)(2,1)} all-to-all(bf16[8,32,3840]{2,1,0:T(8,128)(2,1)S(1)} %bitcast.34), channel_id=1, replica_groups={{0,2,4,6,8,10,12,14},{1,3,5,7,9,11,13,15},{16,18,20,22,24,26,28,30},{17..., dimensions={0} | all-to-all | bytes 3932160 | tf_op jit(solution)/shard_map/all_to_all | solution.py:239
  102.3 6.2 %shard_map.50.terms_ref = f32[8,64,1024]{2,1,0:T(8,128)S(1)} custom-call(bf16[256,3840]{1,0:T(8,128)(2,1)} %bitcast.2.refs_0_, bf16[256,3840]{1,0:T(8,128)(2,1)} %bitcast.36, bf16[3840,1024]{1,0:T(8,128)(2,1)} %copy-done), custom_call_target="tpu_custom_call" | custom-call | tf_op jit(solution)/shard_map/pallas_call | solution.py:151
  108.6 15.3 %collective-permute-start.4 = (f32[64,1024]{1,0:T(8,128)S(1)}, f32[64,1024]{1,0:T(8,128)S(1)}, u32[]{:S(2)}, u32[]{:S(2)}) collective-permute-start(f32[64,1024]{1,0:T(8,128)S(1)} %get-tuple-element.26), channel_id=1, source_target_pairs={{0,32},{1,481},{2,34},{3,483},{4,36},{5,485},{6,38},{7,487},{8,40}... | collective-permute-start | bytes 786440 | tf_op jit(solution)/shard_map/ppermute | solution.py:182
  123.9 10.0 %collective-permute-start.3 = (f32[64,1024]{1,0:T(8,128)S(1)}, f32[64,1024]{1,0:T(8,128)S(1)}, u32[]{:S(2)}, u32[]{:S(2)}) collective-permute-start(f32[64,1024]{1,0:T(8,128)S(1)} %get-tuple-element.25), channel_id=1, source_target_pairs={{0,480},{1,33},{2,482},{3,35},{4,484},{5,37},{6,486},{7,39},{8,488... | collective-permute-start | bytes 786440 | tf_op jit(solution)/shard_map/ppermute | solution.py:182
  134.0 7.0 %collective-permute-start.6 = (f32[64,1024]{1,0:T(8,128)S(1)}, f32[64,1024]{1,0:T(8,128)S(1)}, u32[]{:S(2)}, u32[]{:S(2)}) collective-permute-start(f32[64,1024]{1,0:T(8,128)S(1)} %fusion.1.after_ref), channel_id=1, source_target_pairs={{0,480},{1,33},{2,482},{3,35},{4,484},{5,37},{6,486},{7,39},{8,488... | collective-permute-start | bytes 786440 | tf_op jit(solution)/shard_map/ppermute | solution.py:182
  141.1 1.9 collective-permute-start.5
  143.0 4.7 %collective-permute-done.6 = f32[64,1024]{1,0:T(8,128)S(1)} collective-permute-done((f32[64,1024]{1,0:T(8,128)S(1)}, f32[64,1024]{1,0:T(8,128)S(1)}, u32[]{:S(2)}, u32[]{:S(2)}) %collective-permute-start.6) | collective-permute-done | bytes 262176 | tf_op jit(solution)/shard_map/ppermute | solution.py:182
  147.7 1.6 collective-permute-done.5.arrived_ref
  149.4 3.2 %collective-permute-start.7 = (f32[64,1024]{1,0:T(8,128)S(1)}, f32[64,1024]{1,0:T(8,128)S(1)}, u32[]{:S(2)}, u32[]{:S(2)}) collective-permute-start(f32[64,1024]{1,0:T(8,128)S(1)} %shard_map.52), channel_id=1, source_target_pairs={{0,480},{1,33},{2,482},{3,35},{4,484},{5,37},{6,486},{7,39},{8,488... | collective-permute-start | bytes 786440 | tf_op jit(solution)/shard_map/ppermute | solution.py:182
  152.6 2.5 %collective-permute-start.9 = (f32[64,1024]{1,0:T(8,128)S(1)}, f32[64,1024]{1,0:T(8,128)S(1)}, u32[]{:S(2)}, u32[]{:S(2)}) collective-permute-start(f32[64,1024]{1,0:T(8,128)S(1)} %fusion.after_ref), channel_id=1, source_target_pairs={{0,160},{1,353},{2,162},{3,355},{4,164},{5,357},{6,166},{7,359},{8... | collective-permute-start | bytes 786440 | tf_op jit(solution)/shard_map/ppermute | solution.py:182
  155.1 16.2 %collective-permute-done.7 = f32[64,1024]{1,0:T(8,128)S(1)} collective-permute-done((f32[64,1024]{1,0:T(8,128)S(1)}, f32[64,1024]{1,0:T(8,128)S(1)}, u32[]{:S(2)}, u32[]{:S(2)}) %collective-permute-start.7) | collective-permute-done | bytes 262176 | tf_op jit(solution)/shard_map/ppermute | solution.py:182
  171.4 1.9 collective-permute-start.8
  173.9 5.8 %collective-permute-done.8 = f32[64,1024]{1,0:T(8,128)S(1)} collective-permute-done((f32[64,1024]{1,0:T(8,128)S(1)}, f32[64,1024]{1,0:T(8,128)S(1)}, u32[]{:S(2)}, u32[]{:S(2)}) %collective-permute-start.8) | collective-permute-done | bytes 262176 | tf_op jit(solution)/shard_map/ppermute | solution.py:182
  180.4 1.9 collective-permute-start.11
  182.3 5.9 %collective-permute-start.12 = (f32[32,512]{1,0:T(8,128)S(1)}, f32[32,512]{1,0:T(8,128)S(1)}, u32[]{:S(2)}, u32[]{:S(2)}) collective-permute-start(f32[32,512]{1,0:T(8,128)S(1)} %get-tuple-element.23), channel_id=1, source_target_pairs={{0,17},{1,49},{2,19},{3,51},{4,21},{5,53},{6,23},{7,55},{8,25},{9,... | collective-permute-start | bytes 196616 | tf_op jit(solution)/shard_map/ppermute | solution.py:182
  188.2 2.3 %collective-permute-start.13 = (f32[32,512]{1,0:T(8,128)S(1)}, f32[32,512]{1,0:T(8,128)S(1)}, u32[]{:S(2)}, u32[]{:S(2)}) collective-permute-start(f32[32,512]{1,0:T(8,128)S(1)} %get-tuple-element.28), channel_id=1, source_target_pairs={{0,16},{1,32},{2,18},{3,34},{4,20},{5,36},{6,22},{7,38},{8,24},{9,... | collective-permute-start | bytes 196616 | tf_op jit(solution)/shard_map/ppermute | solution.py:182
  190.5 1.6 collective-permute-done.12
  192.1 3.7 %collective-permute-done.13 = f32[32,512]{1,0:T(8,128)S(1)} collective-permute-done((f32[32,512]{1,0:T(8,128)S(1)}, f32[32,512]{1,0:T(8,128)S(1)}, u32[]{:S(2)}, u32[]{:S(2)}) %collective-permute-start.13) | collective-permute-done | bytes 65568 | tf_op jit(solution)/shard_map/ppermute | solution.py:182
  (21 shorter events, 2.2 us)
Async XLA Ops:
  0.0 25.8 %collective-permute-start.1 = (bf16[3840,256]{1,0:T(8,128)(2,1)}, bf16[3840,256]{1,0:T(8,128)(2,1)S(1)}, u32[]{:S(2)}, u32[]{:S(2)}) collective-permute-start(bf16[3840,256]{1,0:T(8,128)(2,1)} %own_ref.1), channel_id=1, source_target_pairs={{0,1},{1,0},{2,3},{3,2},{4,5},{5,4},{6,7},{7,6},{8,9},{9,8},{10,11... | collective-permute-start | bytes 5898248 | tf_op jit(solution)/shard_map/ppermute | solution.py:172
  2.7 1.0 copy-start.2
  9.4 24.5 %collective-permute-start = (bf16[32,3840]{1,0:T(8,128)(2,1)S(1)}, bf16[32,3840]{1,0:T(8,128)(2,1)S(1)}, u32[]{:S(2)}, u32[]{:S(2)}) collective-permute-start(bf16[32,3840]{1,0:T(8,128)(2,1)S(1)} %get-tuple-element.15), channel_id=1, source_target_pairs={{0,256},{16,272},{32,288},{48,304},{64,320},{80,336},{96,352},{112... | collective-permute-start | bytes 737288 | tf_op jit(solution)/shard_map/ppermute | solution.py:261
  25.8 1.5 copy-start.1
  30.9 3.1 %copy-start = (bf16[3840,1024]{1,0:T(8,128)(2,1)}, bf16[3840,1024]{1,0:T(8,128)(2,1)S(1)}, u32[]{:S(2)}) copy-start(bf16[3840,1024]{1,0:T(8,128)(2,1)S(1)} %get-tuple-element.22.refs_2_) | copy-start | bytes 23592964
  35.3 38.2 %all-to-all-start = ((bf16[8,32,3840]{2,1,0:T(8,128)(2,1)}), bf16[8,32,3840]{2,1,0:T(8,128)(2,1)}, u32[]{:S(2)}, u32[]{:S(2)}) async-start(bf16[8,32,3840]{2,1,0:T(8,128)(2,1)} %bitcast.1), calls=%async_computation | async-start | bytes 3932160 | tf_op jit(solution)/shard_map/all_to_all | solution.py:239
  46.3 18.2 %collective-permute-start.2 = (bf16[32,3840]{1,0:T(8,128)(2,1)S(1)}, bf16[32,3840]{1,0:T(8,128)(2,1)S(1)}, u32[]{:S(2)}, u32[]{:S(2)}) collective-permute-start(bf16[32,3840]{1,0:T(8,128)(2,1)S(1)} %get-tuple-element.21), channel_id=1, source_target_pairs={{0,256},{16,272},{32,288},{48,304},{64,320},{80,336},{96,352},{112... | collective-permute-start | bytes 737288 | tf_op jit(solution)/shard_map/ppermute | solution.py:261
  108.6 25.3 %collective-permute-start.4 = (f32[64,1024]{1,0:T(8,128)S(1)}, f32[64,1024]{1,0:T(8,128)S(1)}, u32[]{:S(2)}, u32[]{:S(2)}) collective-permute-start(f32[64,1024]{1,0:T(8,128)S(1)} %get-tuple-element.26), channel_id=1, source_target_pairs={{0,32},{1,481},{2,34},{3,483},{4,36},{5,485},{6,38},{7,487},{8,40}... | collective-permute-start | bytes 786440 | tf_op jit(solution)/shard_map/ppermute | solution.py:182
  123.9 17.1 %collective-permute-start.3 = (f32[64,1024]{1,0:T(8,128)S(1)}, f32[64,1024]{1,0:T(8,128)S(1)}, u32[]{:S(2)}, u32[]{:S(2)}) collective-permute-start(f32[64,1024]{1,0:T(8,128)S(1)} %get-tuple-element.25), channel_id=1, source_target_pairs={{0,480},{1,33},{2,482},{3,35},{4,484},{5,37},{6,486},{7,39},{8,488... | collective-permute-start | bytes 786440 | tf_op jit(solution)/shard_map/ppermute | solution.py:182
  134.0 13.7 %collective-permute-start.6 = (f32[64,1024]{1,0:T(8,128)S(1)}, f32[64,1024]{1,0:T(8,128)S(1)}, u32[]{:S(2)}, u32[]{:S(2)}) collective-permute-start(f32[64,1024]{1,0:T(8,128)S(1)} %fusion.1.after_ref), channel_id=1, source_target_pairs={{0,480},{1,33},{2,482},{3,35},{4,484},{5,37},{6,486},{7,39},{8,488... | collective-permute-start | bytes 786440 | tf_op jit(solution)/shard_map/ppermute | solution.py:182
  141.1 8.3 %collective-permute-start.5 = (f32[64,1024]{1,0:T(8,128)S(1)}, f32[64,1024]{1,0:T(8,128)S(1)}, u32[]{:S(2)}, u32[]{:S(2)}) collective-permute-start(f32[64,1024]{1,0:T(8,128)S(1)} %shard_map.51), channel_id=1, source_target_pairs={{0,32},{1,481},{2,34},{3,483},{4,36},{5,485},{6,38},{7,487},{8,40}... | collective-permute-start | bytes 786440 | tf_op jit(solution)/shard_map/ppermute | solution.py:182
  149.4 22.0 %collective-permute-start.7 = (f32[64,1024]{1,0:T(8,128)S(1)}, f32[64,1024]{1,0:T(8,128)S(1)}, u32[]{:S(2)}, u32[]{:S(2)}) collective-permute-start(f32[64,1024]{1,0:T(8,128)S(1)} %shard_map.52), channel_id=1, source_target_pairs={{0,480},{1,33},{2,482},{3,35},{4,484},{5,37},{6,486},{7,39},{8,488... | collective-permute-start | bytes 786440 | tf_op jit(solution)/shard_map/ppermute | solution.py:182
  152.6 21.2 %collective-permute-start.9 = (f32[64,1024]{1,0:T(8,128)S(1)}, f32[64,1024]{1,0:T(8,128)S(1)}, u32[]{:S(2)}, u32[]{:S(2)}) collective-permute-start(f32[64,1024]{1,0:T(8,128)S(1)} %fusion.after_ref), channel_id=1, source_target_pairs={{0,160},{1,353},{2,162},{3,355},{4,164},{5,357},{6,166},{7,359},{8... | collective-permute-start | bytes 786440 | tf_op jit(solution)/shard_map/ppermute | solution.py:182
  171.4 8.3 %collective-permute-start.8 = (f32[64,1024]{1,0:T(8,128)S(1)}, f32[64,1024]{1,0:T(8,128)S(1)}, u32[]{:S(2)}, u32[]{:S(2)}) collective-permute-start(f32[64,1024]{1,0:T(8,128)S(1)} %fusion.2), channel_id=1, source_target_pairs={{0,32},{1,481},{2,34},{3,483},{4,36},{5,485},{6,38},{7,487},{8,40}... | collective-permute-start | bytes 786440 | tf_op jit(solution)/shard_map/ppermute | solution.py:182
  179.7 10.8 %collective-permute-start.10 = (f32[32,512]{1,0:T(8,128)S(1)}, f32[32,512]{1,0:T(8,128)S(1)}, u32[]{:S(2)}, u32[]{:S(2)}) collective-permute-start(f32[32,512]{1,0:T(8,128)S(1)} %get-tuple-element.24), channel_id=1, source_target_pairs={{1,48},{3,50},{5,52},{7,54},{9,56},{11,58},{13,60},{15,62},{17,32}... | collective-permute-start | bytes 196616 | tf_op jit(solution)/shard_map/ppermute | solution.py:182
  180.4 10.1 %collective-permute-start.11 = (f32[32,512]{1,0:T(8,128)S(1)}, f32[32,512]{1,0:T(8,128)S(1)}, u32[]{:S(2)}, u32[]{:S(2)}) collective-permute-start(f32[32,512]{1,0:T(8,128)S(1)} %get-tuple-element.27), channel_id=1, source_target_pairs={{0,1},{1,33},{2,3},{3,35},{4,5},{5,37},{6,7},{7,39},{8,9},{9,41},{... | collective-permute-start | bytes 196616 | tf_op jit(solution)/shard_map/ppermute | solution.py:182
  182.3 9.8 %collective-permute-start.12 = (f32[32,512]{1,0:T(8,128)S(1)}, f32[32,512]{1,0:T(8,128)S(1)}, u32[]{:S(2)}, u32[]{:S(2)}) collective-permute-start(f32[32,512]{1,0:T(8,128)S(1)} %get-tuple-element.23), channel_id=1, source_target_pairs={{0,17},{1,49},{2,19},{3,51},{4,21},{5,53},{6,23},{7,55},{8,25},{9,... | collective-permute-start | bytes 196616 | tf_op jit(solution)/shard_map/ppermute | solution.py:182
  188.2 7.7 %collective-permute-start.13 = (f32[32,512]{1,0:T(8,128)S(1)}, f32[32,512]{1,0:T(8,128)S(1)}, u32[]{:S(2)}, u32[]{:S(2)}) collective-permute-start(f32[32,512]{1,0:T(8,128)S(1)} %get-tuple-element.28), channel_id=1, source_target_pairs={{0,16},{1,32},{2,18},{3,34},{4,20},{5,36},{6,22},{7,38},{8,24},{9,... | collective-permute-start | bytes 196616 | tf_op jit(solution)/shard_map/ppermute | solution.py:182

commit v10 on v9

--- a/solution.py
+++ b/solution.py
@@ -10,7 +10,6 @@
 LANES = 128
 UNROLL = 32
 K_TILE = 768
-OUTER = 3
 CHUNKS = (32, 32)
 STARTS = tuple(sum(CHUNKS[:h]) for h in range(len(CHUNKS)))
 PEERS = 8
@@ -108,59 +107,51 @@
     return jnp.where(odd == 1, odd_slot, even_slot)
 
 
-def product_kernel(*refs):
-    count = len(CHUNKS)
-    pieces = refs[:count]
-    s_hbm, out_ref, total, lhs_ref, s_ref, sems = refs[count:]
+def product_kernel(piece_hbm, s_hbm, out_ref, total, lhs_ref, s_ref, sems):
     z, c = lax.axis_index("grp") // 2, lax.axis_index("col")
     tiles = s_ref.shape[0] // K_TILE
     spans = [pl.ds(k * K_TILE, K_TILE) for k in range(tiles)]
-    copies = []
-    for k, span in enumerate(spans):
-        tile = [pltpu.make_async_copy(s_hbm.at[span], s_ref.at[span], sems.at[k, count])]
-        for h, (rows, start) in enumerate(zip(CHUNKS, STARTS)):
-            there = lhs_ref.at[pl.ds(start * PEERS, rows * PEERS), span]
-            tile.append(pltpu.make_async_copy(pieces[h].at[:, span], there, sems.at[k, h]))
-        copies.append(tile)
+    copies = [
+        (
+            pltpu.make_async_copy(s_hbm.at[span], s_ref.at[span], sems.at[k, 0]),
+            pltpu.make_async_copy(piece_hbm.at[:, span], lhs_ref.at[:, span], sems.at[k, 1]),
+        )
+        for k, span in enumerate(spans)
+    ]
     for tile in copies:
         for copy in tile:
             copy.start()
     for k, span in enumerate(spans):
         for copy in copies[k]:
             copy.wait()
-        lhs = lhs_ref[:, span]
-        term = jnp.dot(lhs, s_ref[span, :], preferred_element_type=jnp.float32)
+        term = jnp.dot(lhs_ref[:, span], s_ref[span, :], preferred_element_type=jnp.float32)
         if k == 0:
             total[...] = term
         elif k < tiles - 1:
             total[...] += term
         else:
             term += total[...]
-    base = 0
-    for rows, start in zip(CHUNKS, STARTS):
-        for peer in range(PEERS):
-            slot = slot_of(z, c % 2, peer)
-            out_ref[slot, start : start + rows, :] = term[base : base + rows, :]
-            base += rows
-
-
-def product(pieces, s_both):
+    rows = out_ref.shape[1]
+    for peer in range(PEERS):
+        out_ref[slot_of(z, c % 2, peer)] = term[peer * rows : (peer + 1) * rows, :]
+
+
+def product(piece, s_both):
     blk, cols = s_both.shape
-    block_rows = sum(CHUNKS)
-    hbm = pl.BlockSpec(memory_space=pltpu.HBM)
+    rows = piece.shape[0]
     return pl.pallas_call(
         product_kernel,
-        out_shape=jax.ShapeDtypeStruct((PEERS, block_rows, cols), jnp.float32),
-        in_specs=[hbm] * (len(pieces) + 1),
+        out_shape=jax.ShapeDtypeStruct((PEERS, rows // PEERS, cols), jnp.float32),
+        in_specs=[pl.BlockSpec(memory_space=pl.ANY)] * 2,
         out_specs=pl.BlockSpec(memory_space=pltpu.VMEM),
         scratch_shapes=[
-            pltpu.VMEM((PEERS * block_rows, cols), jnp.float32),
-            pltpu.VMEM((PEERS * block_rows, blk), jnp.bfloat16),
+            pltpu.VMEM((rows, cols), jnp.float32),
+            pltpu.VMEM((rows, blk), jnp.bfloat16),
             pltpu.VMEM((blk, cols), jnp.bfloat16),
-            pltpu.SemaphoreType.DMA((blk // K_TILE, len(CHUNKS) + 1)),
+            pltpu.SemaphoreType.DMA((blk // K_TILE, 2)),
         ],
-        compiler_params=pltpu.CompilerParams(vmem_limit_bytes=24 * 2**20),
-    )(*pieces, s_both)
+        compiler_params=pltpu.CompilerParams(vmem_limit_bytes=20 * 2**20),
+    )(piece, s_both)
 
 
 def col_move(value, target):
@@ -219,19 +210,25 @@
     )(*arrays, after)
 
 
-def add_term_kernel(slot, terms_ref, arrived_ref, after_ref, out_ref):
-    out_ref[...] = terms_ref[slot] + arrived_ref[...]
-
-
-def add_term(terms, slot, arrived, after):
+def add_term_kernel(slot, *refs):
+    terms, out_ref = refs[: len(CHUNKS)], refs[-1]
+    arrived_ref = refs[len(CHUNKS)] if len(refs) > len(CHUNKS) + 1 else None
+    for ref, rows, start in zip(terms, CHUNKS, STARTS):
+        value = ref[slot]
+        if arrived_ref is not None:
+            value += arrived_ref[start : start + rows, :]
+        out_ref[start : start + rows, :] = value
+
+
+def add_term(terms, slot, *arrived):
     whole = pl.BlockSpec(memory_space=pltpu.VMEM)
     return pl.pallas_call(
         functools.partial(add_term_kernel, slot),
-        out_shape=jax.ShapeDtypeStruct(arrived.shape, arrived.dtype),
-        in_specs=[whole, whole, pl.BlockSpec(memory_space=pl.ANY)],
+        out_shape=jax.ShapeDtypeStruct((sum(CHUNKS), terms[0].shape[2]), jnp.float32),
+        in_specs=[whole] * (len(terms) + len(arrived[:1])) + [pl.BlockSpec(memory_space=pl.ANY)] * len(arrived[1:]),
         out_specs=whole,
-        compiler_params=pltpu.CompilerParams(vmem_limit_bytes=4 * 2**20),
-    )(terms, arrived, after)
+        compiler_params=pltpu.CompilerParams(vmem_limit_bytes=8 * 2**20),
+    )(*terms, *arrived)
 
 
 def gather_col(copies):
@@ -265,17 +262,14 @@
         pieces.append(gather_col(here))
 
     s_both = pltpu.with_memory_space_constraint(s_both, pltpu.HBM)
-    pieces = [pltpu.with_memory_space_constraint(piece, pltpu.HBM) for piece in pieces]
-    terms = product(pieces, s_both)
-    outer, inner = terms[0], terms[OUTER]
-    for step in range(1, OUTER):
-        outer = terms[step] + slice_move(outer, functools.partial(exchange, step))
-        inner = slice_move(inner, functools.partial(exchange, step + OUTER))
-        inner = add_term(terms, OUTER + step, inner, outer)
-    skipped = slice_move(outer, lambda z, y_hi, c: (z - 5 if (c - z) % 2 else z + 5, y_hi, c))
-    for step in range(OUTER, 8 - OUTER):
-        inner = terms[OUTER + step] + slice_move(inner, functools.partial(exchange, step + OUTER))
-    inner += skipped
+    terms = [product(piece, s_both) for piece in pieces]
+
+    outer, inner = add_term(terms, 0), add_term(terms, 4)
+    for step in range(1, 4):
+        outer = add_term(terms, step, slice_move(outer, functools.partial(exchange, step)))
+        inner = slice_move(inner, functools.partial(exchange, step))
+        inner = add_term(terms, 4 + step, inner, *([outer] if step < 3 else []))
+    inner += slice_move(outer, lambda z, y_hi, c: (z + 4 if (c - z) % 2 else z - 4, y_hi, c))
 
     half_cols = inner.shape[1] // 2
     mine, theirs = inner[:, :half_cols], inner[:, half_cols:]

time: 197 us -> 193 us (0.980)
  the two profiles are of different devices: /device:TPU:8 before, /device:TPU:6 now
where the time goes in v10:
time: 193 us; the launch traced here: 189 us
  starting transfers between devices  106 us (55%)
  waiting for transfers between devices  49.2 us (25%)
  Pallas kernels  23.1 us (12%)
  local copies, waits for them, and re-layouts  8.84 us (5%)
    ppermute x11, starting transfers between devices, slice_move(): return lax.ppermute(value, ('grp', 'col'), pairs)  57.9 us
    ppermute x2, starting transfers between devices, per_device(): arrived = lax.ppermute(leaving, 'grp', [(i, i ^ 16) for i in range(32)])  28.2 us
    all_to_all x2, waiting for transfers between devices, gather_col(): lax.all_to_all(copies, 'col', 0, 0, axis_index_groups=groups, tiled=True)  23.6 us
    ppermute x11, waiting for transfers between devices, slice_move(): return lax.ppermute(value, ('grp', 'col'), pairs)  19.8 us
    all_to_all x2, starting transfers between devices, gather_col(): lax.all_to_all(copies, 'col', 0, 0, axis_index_groups=groups, tiled=True)  18.1 us
    pallas_call x2, Pallas kernels, product(): pl.pallas_call(product_kernel, out_shape=jax.ShapeDtypeStruct((PEERS, row...  8.41 us
    unnamed x10, local copies, waits for them, and re-layouts  8.22 us
    ppermute x2, waiting for transfers between devices, per_device(): arrived = lax.ppermute(leaving, 'grp', [(i, i ^ 16) for i in range(32)])  5.8 us
  transfers between devices with their start and end apart: 16, of which 9 were waited for; matrix products, arithmetic and copies ran while one was open for 0% of the time, Pallas kernels for 8%

profile of v10, /device:TPU:6, one launch (start us, length us, event | category | flops | bytes accessed | tf_op | source)
XLA Modules:
  0.0 189.1 jit_solution(10490772394995082229)
XLA Ops:
  0.0 1.9 %collective-permute-start.1 = (bf16[3840,256]{1,0:T(8,128)(2,1)}, bf16[3840,256]{1,0:T(8,128)(2,1)S(1)}, u32[]{:S(2)}, u32[]{:S(2)}) collective-permute-start(bf16[3840,256]{1,0:T(8,128)(2,1)} %own_ref.1), channel_id=1, source_target_pairs={{0,1},{1,0},{2,3},{3,2},{4,5},{5,4},{6,7},{7,6},{8,9},{9,8},{10,11... | collective-permute-start | bytes 5898248 | tf_op jit(solution)/shard_map/ppermute | solution.py:163
  3.7 5.8 %shard_map.46 = (bf16[32,3840]{1,0:T(8,128)(2,1)S(1)}, bf16[32,3840]{1,0:T(8,128)(2,1)S(1)}, bf16[32,3840]{1,0:T(8,128)(2,1)S(1)}, bf16[32,3840]{1,0:T(8,128)(2,1)S(1)}, bf16[3840,128]{1,0:T(8,128)(2,1)S(1)}) custom-call(s32[3840]{0:T(1024)S(1)} %subtract_select_fusion.place_ref, bf16[64,3840]{1,0:T(8,128)(2,1)S(1)} %bitcast.15), custom_call_target="tpu_custom_call" | custom-call | tf_op jit(solution)/shard_map/pallas_call | solution.py:47
  9.4 15.7 %collective-permute-start = (bf16[32,3840]{1,0:T(8,128)(2,1)S(1)}, bf16[32,3840]{1,0:T(8,128)(2,1)S(1)}, u32[]{:S(2)}, u32[]{:S(2)}) collective-permute-start(bf16[32,3840]{1,0:T(8,128)(2,1)S(1)} %get-tuple-element.15), channel_id=1, source_target_pairs={{0,256},{16,272},{32,288},{48,304},{64,320},{80,336},{96,352},{112... | collective-permute-start | bytes 737288 | tf_op jit(solution)/shard_map/ppermute | solution.py:258
  25.8 1.5 copy-done.2
  27.4 3.5 %shard_map.47 = (bf16[3840,1024]{1,0:T(8,128)(2,1)S(1)}, f32[8,128]{1,0:T(8,128)S(1)}) custom-call(s32[1]{0:T(128)S(6)} %copy.9.kept_ref, bf16[3840,128]{1,0:T(8,128)(2,1)S(1)} %get-tuple-element.17.flag_ref, bf16[3840,256]{1,0:T(8,128)(2,1)S(1)} %copy-done.2, bf16[3840,256]{1,0:T(8,128)(2,1)S(1)} %collective-permute-done.1.other_ref), custom_call_target="tpu_custom_call" | custom-call | tf_op jit(solution)/shard_map/pallas_call | solution.py:83
  30.9 3.0 %copy-done = bf16[3840,1024]{1,0:T(8,128)(2,1)} copy-done((bf16[3840,1024]{1,0:T(8,128)(2,1)}, bf16[3840,1024]{1,0:T(8,128)(2,1)S(1)}, u32[]{:S(2)}) %copy-start) | copy-done | bytes 7864344
  33.9 2.7 %shard_map.48 = (bf16[256,3840]{1,0:T(8,128)(2,1)S(1)}, bf16[32,3840]{1,0:T(8,128)(2,1)S(1)}) custom-call(bf16[32,3840]{1,0:T(8,128)(2,1)S(1)} %get-tuple-element.14.refs_0_, bf16[32,3840]{1,0:T(8,128)(2,1)S(1)} %collective-permute-done.refs_1_, bf16[32,3840]{1,0:T(8,128)(2,1)S(1)} %get-tuple-element.16.refs_2_, f32[8,128]{1,0:T(8,128)S(1)} %get-tuple-element.18.refs_3_.refs_2_), custom_call_target="tpu_custom_call" | custom-call | tf_op jit(solution)/shard_map/pallas_call | solution.py:202
  36.6 1.3 copy-done.3
  37.9 10.3 %all-to-all-start = ((bf16[8,32,3840]{2,1,0:T(8,128)(2,1)}), bf16[8,32,3840]{2,1,0:T(8,128)(2,1)S(1)}, u32[]{:S(2)}, u32[]{:S(2)}) async-start(bf16[8,32,3840]{2,1,0:T(8,128)(2,1)} %bitcast.14), calls=%async_computation | async-start | bytes 3932160 | tf_op jit(solution)/shard_map/all_to_all | solution.py:236
  48.2 12.4 %collective-permute-start.2 = (bf16[32,3840]{1,0:T(8,128)(2,1)S(1)}, bf16[32,3840]{1,0:T(8,128)(2,1)S(1)}, u32[]{:S(2)}, u32[]{:S(2)}) collective-permute-start(bf16[32,3840]{1,0:T(8,128)(2,1)S(1)} %get-tuple-element.22), channel_id=1, source_target_pairs={{0,256},{16,272},{32,288},{48,304},{64,320},{80,336},{96,352},{112... | collective-permute-start | bytes 737288 | tf_op jit(solution)/shard_map/ppermute | solution.py:258
  60.7 5.8 %collective-permute-done.2.refs_1_ = bf16[32,3840]{1,0:T(8,128)(2,1)S(1)} collective-permute-done((bf16[32,3840]{1,0:T(8,128)(2,1)S(1)}, bf16[32,3840]{1,0:T(8,128)(2,1)S(1)}, u32[]{:S(2)}, u32[]{:S(2)}) %collective-permute-start.2) | collective-permute-done | bytes 245792 | tf_op jit(solution)/shard_map/ppermute | solution.py:258
  66.5 2.6 %shard_map.50 = bf16[256,3840]{1,0:T(8,128)(2,1)S(1)} custom-call(bf16[32,3840]{1,0:T(8,128)(2,1)S(1)} %get-tuple-element.21.refs_0_, bf16[32,3840]{1,0:T(8,128)(2,1)S(1)} %collective-permute-done.2.refs_1_, f32[8,128]{1,0:T(8,128)S(1)} %get-tuple-element.18.refs_3_.refs_2_), custom_call_target="tpu_custom_call" | custom-call | tf_op jit(solution)/shard_map/pallas_call | solution.py:202
  70.4 3.4 %all-to-all-done = bf16[8,32,3840]{2,1,0:T(8,128)(2,1)S(1)} async-done(((bf16[8,32,3840]{2,1,0:T(8,128)(2,1)}), bf16[8,32,3840]{2,1,0:T(8,128)(2,1)S(1)}, u32[]{:S(2)}, u32[]{:S(2)}) %all-to-all-start) | async-done | bytes 1966112 | tf_op jit(solution)/shard_map/all_to_all | solution.py:236
  73.8 7.8 %all-to-all-start.1 = ((bf16[8,32,3840]{2,1,0:T(8,128)(2,1)}), bf16[8,32,3840]{2,1,0:T(8,128)(2,1)}, u32[]{:S(2)}, u32[]{:S(2)}) async-start(bf16[8,32,3840]{2,1,0:T(8,128)(2,1)} %bitcast.13), calls=%async_computation.1 | async-start | bytes 3932160 | tf_op jit(solution)/shard_map/all_to_all | solution.py:236
  81.6 4.0 %shard_map.49.refs_0_ = f32[8,32,1024]{2,1,0:T(8,128)S(1)} custom-call(bf16[256,3840]{1,0:T(8,128)(2,1)S(1)} %bitcast.12, bf16[3840,1024]{1,0:T(8,128)(2,1)} %copy-done), custom_call_target="tpu_custom_call" | custom-call | tf_op jit(solution)/shard_map/pallas_call | solution.py:142
  85.6 20.2 %all-to-all-done.1 = bf16[8,32,3840]{2,1,0:T(8,128)(2,1)} async-done(((bf16[8,32,3840]{2,1,0:T(8,128)(2,1)}), bf16[8,32,3840]{2,1,0:T(8,128)(2,1)}, u32[]{:S(2)}, u32[]{:S(2)}) %all-to-all-start.1) | async-done | bytes 1966112 | tf_op jit(solution)/shard_map/all_to_all | solution.py:236
  105.8 4.4 %shard_map.51.refs_1_ = f32[8,32,1024]{2,1,0:T(8,128)S(1)} custom-call(bf16[256,3840]{1,0:T(8,128)(2,1)} %bitcast.4.piece_hbm, bf16[3840,1024]{1,0:T(8,128)(2,1)} %copy-done), custom_call_target="tpu_custom_call" | custom-call | tf_op jit(solution)/shard_map/pallas_call | solution.py:142
  110.3 17.2 %collective-permute-start.4 = (f32[64,1024]{1,0:T(8,128)S(1)}, f32[64,1024]{1,0:T(8,128)S(1)}, u32[]{:S(2)}, u32[]{:S(2)}) collective-permute-start(f32[64,1024]{1,0:T(8,128)S(1)} %shard_map.53), channel_id=1, source_target_pairs={{0,32},{1,481},{2,34},{3,483},{4,36},{5,485},{6,38},{7,487},{8,40}... | collective-permute-start | bytes 786440 | tf_op jit(solution)/shard_map/ppermute | solution.py:173
  127.5 1.9 %collective-permute-start.3 = (f32[64,1024]{1,0:T(8,128)S(1)}, f32[64,1024]{1,0:T(8,128)S(1)}, u32[]{:S(2)}, u32[]{:S(2)}) collective-permute-start(f32[64,1024]{1,0:T(8,128)S(1)} %shard_map.52), channel_id=1, source_target_pairs={{0,32},{1,481},{2,34},{3,483},{4,36},{5,485},{6,38},{7,487},{8,40}... | collective-permute-start | bytes 786440 | tf_op jit(solution)/shard_map/ppermute | solution.py:173
  129.5 2.4 %collective-permute-done.4.refs_2_ = f32[64,1024]{1,0:T(8,128)S(1)} collective-permute-done((f32[64,1024]{1,0:T(8,128)S(1)}, f32[64,1024]{1,0:T(8,128)S(1)}, u32[]{:S(2)}, u32[]{:S(2)}) %collective-permute-start.4) | collective-permute-done | bytes 262176 | tf_op jit(solution)/shard_map/ppermute | solution.py:173
  131.9 9.5 %collective-permute-start.6 = (f32[64,1024]{1,0:T(8,128)S(1)}, f32[64,1024]{1,0:T(8,128)S(1)}, u32[]{:S(2)}, u32[]{:S(2)}) collective-permute-start(f32[64,1024]{1,0:T(8,128)S(1)} %shard_map.54.refs_3_), channel_id=1, source_target_pairs={{0,480},{1,33},{2,482},{3,35},{4,484},{5,37},{6,486},{7,39},{8,488... | collective-permute-start | bytes 786440 | tf_op jit(solution)/shard_map/ppermute | solution.py:173
  141.5 5.0 %collective-permute-start.5 = (f32[64,1024]{1,0:T(8,128)S(1)}, f32[64,1024]{1,0:T(8,128)S(1)}, u32[]{:S(2)}, u32[]{:S(2)}) collective-permute-start(f32[64,1024]{1,0:T(8,128)S(1)} %shard_map.55), channel_id=1, source_target_pairs={{0,480},{1,33},{2,482},{3,35},{4,484},{5,37},{6,486},{7,39},{8,488... | collective-permute-start | bytes 786440 | tf_op jit(solution)/shard_map/ppermute | solution.py:173
  146.5 1.9 %collective-permute-start.8 = (f32[64,1024]{1,0:T(8,128)S(1)}, f32[64,1024]{1,0:T(8,128)S(1)}, u32[]{:S(2)}, u32[]{:S(2)}) collective-permute-start(f32[64,1024]{1,0:T(8,128)S(1)} %shard_map.56.refs_3_), channel_id=1, source_target_pairs={{0,32},{1,481},{2,34},{3,483},{4,36},{5,485},{6,38},{7,487},{8,40}... | collective-permute-start | bytes 786440 | tf_op jit(solution)/shard_map/ppermute | solution.py:173
  148.4 4.3 %collective-permute-done.5.refs_2_ = f32[64,1024]{1,0:T(8,128)S(1)} collective-permute-done((f32[64,1024]{1,0:T(8,128)S(1)}, f32[64,1024]{1,0:T(8,128)S(1)}, u32[]{:S(2)}, u32[]{:S(2)}) %collective-permute-start.5) | collective-permute-done | bytes 262176 | tf_op jit(solution)/shard_map/ppermute | solution.py:173
  152.8 1.9 %collective-permute-start.7 = (f32[64,1024]{1,0:T(8,128)S(1)}, f32[64,1024]{1,0:T(8,128)S(1)}, u32[]{:S(2)}, u32[]{:S(2)}) collective-permute-start(f32[64,1024]{1,0:T(8,128)S(1)} %shard_map.57), channel_id=1, source_target_pairs={{0,32},{1,481},{2,34},{3,483},{4,36},{5,485},{6,38},{7,487},{8,40}... | collective-permute-start | bytes 786440 | tf_op jit(solution)/shard_map/ppermute | solution.py:173
  154.8 4.9 %collective-permute-start.9 = (f32[64,1024]{1,0:T(8,128)S(1)}, f32[64,1024]{1,0:T(8,128)S(1)}, u32[]{:S(2)}, u32[]{:S(2)}) collective-permute-start(f32[64,1024]{1,0:T(8,128)S(1)} %shard_map.59), channel_id=1, source_target_pairs={{0,384},{1,129},{2,386},{3,131},{4,388},{5,133},{6,390},{7,135},{8... | collective-permute-start | bytes 786440 | tf_op jit(solution)/shard_map/ppermute | solution.py:173
  159.8 7.3 %collective-permute-done.7.refs_2_ = f32[64,1024]{1,0:T(8,128)S(1)} collective-permute-done((f32[64,1024]{1,0:T(8,128)S(1)}, f32[64,1024]{1,0:T(8,128)S(1)}, u32[]{:S(2)}, u32[]{:S(2)}) %collective-permute-start.7) | collective-permute-done | bytes 262176 | tf_op jit(solution)/shard_map/ppermute | solution.py:173
  167.1 3.1 %collective-permute-done.9 = f32[64,1024]{1,0:T(8,128)S(1)} collective-permute-done((f32[64,1024]{1,0:T(8,128)S(1)}, f32[64,1024]{1,0:T(8,128)S(1)}, u32[]{:S(2)}, u32[]{:S(2)}) %collective-permute-start.9) | collective-permute-done | bytes 262176 | tf_op jit(solution)/shard_map/ppermute | solution.py:173
  170.3 1.9 %collective-permute-start.12 = (f32[32,512]{1,0:T(8,128)S(1)}, f32[32,512]{1,0:T(8,128)S(1)}, u32[]{:S(2)}, u32[]{:S(2)}) collective-permute-start(f32[32,512]{1,0:T(8,128)S(1)} %get-tuple-element.23), channel_id=1, source_target_pairs={{0,17},{1,49},{2,19},{3,51},{4,21},{5,53},{6,23},{7,55},{8,25},{9,... | collective-permute-start | bytes 196616 | tf_op jit(solution)/shard_map/ppermute | solution.py:173
  172.9 7.9 %collective-permute-start.11 = (f32[32,512]{1,0:T(8,128)S(1)}, f32[32,512]{1,0:T(8,128)S(1)}, u32[]{:S(2)}, u32[]{:S(2)}) collective-permute-start(f32[32,512]{1,0:T(8,128)S(1)} %get-tuple-element.25), channel_id=1, source_target_pairs={{0,1},{1,33},{2,3},{3,35},{4,5},{5,37},{6,7},{7,39},{8,9},{9,41},{... | collective-permute-start | bytes 196616 | tf_op jit(solution)/shard_map/ppermute | solution.py:173
  180.8 5.0 %collective-permute-start.13 = (f32[32,512]{1,0:T(8,128)S(1)}, f32[32,512]{1,0:T(8,128)S(1)}, u32[]{:S(2)}, u32[]{:S(2)}) collective-permute-start(f32[32,512]{1,0:T(8,128)S(1)} %get-tuple-element.26), channel_id=1, source_target_pairs={{0,16},{1,32},{2,18},{3,34},{4,20},{5,36},{6,22},{7,38},{8,24},{9,... | collective-permute-start | bytes 196616 | tf_op jit(solution)/shard_map/ppermute | solution.py:173
  185.8 2.7 %collective-permute-done.13 = f32[32,512]{1,0:T(8,128)S(1)} collective-permute-done((f32[32,512]{1,0:T(8,128)S(1)}, f32[32,512]{1,0:T(8,128)S(1)}, u32[]{:S(2)}, u32[]{:S(2)}) %collective-permute-start.13) | collective-permute-done | bytes 65568 | tf_op jit(solution)/shard_map/ppermute | solution.py:173
  (29 shorter events, 4.7 us)
Async XLA Ops:
  0.0 25.8 %collective-permute-start.1 = (bf16[3840,256]{1,0:T(8,128)(2,1)}, bf16[3840,256]{1,0:T(8,128)(2,1)S(1)}, u32[]{:S(2)}, u32[]{:S(2)}) collective-permute-start(bf16[3840,256]{1,0:T(8,128)(2,1)} %own_ref.1), channel_id=1, source_target_pairs={{0,1},{1,0},{2,3},{3,2},{4,5},{5,4},{6,7},{7,6},{8,9},{9,8},{10,11... | collective-permute-start | bytes 5898248 | tf_op jit(solution)/shard_map/ppermute | solution.py:163
  2.7 1.0 copy-start.4
  9.4 24.5 %collective-permute-start = (bf16[32,3840]{1,0:T(8,128)(2,1)S(1)}, bf16[32,3840]{1,0:T(8,128)(2,1)S(1)}, u32[]{:S(2)}, u32[]{:S(2)}) collective-permute-start(bf16[32,3840]{1,0:T(8,128)(2,1)S(1)} %get-tuple-element.15), channel_id=1, source_target_pairs={{0,256},{16,272},{32,288},{48,304},{64,320},{80,336},{96,352},{112... | collective-permute-start | bytes 737288 | tf_op jit(solution)/shard_map/ppermute | solution.py:258
  25.8 1.5 copy-start.2
  30.8 3.1 %copy-start = (bf16[3840,1024]{1,0:T(8,128)(2,1)}, bf16[3840,1024]{1,0:T(8,128)(2,1)S(1)}, u32[]{:S(2)}) copy-start(bf16[3840,1024]{1,0:T(8,128)(2,1)S(1)} %get-tuple-element.20.s_hbm) | copy-start | bytes 23592964
  36.6 1.4 copy-start.3
  37.9 35.9 %all-to-all-start = ((bf16[8,32,3840]{2,1,0:T(8,128)(2,1)}), bf16[8,32,3840]{2,1,0:T(8,128)(2,1)S(1)}, u32[]{:S(2)}, u32[]{:S(2)}) async-start(bf16[8,32,3840]{2,1,0:T(8,128)(2,1)} %bitcast.14), calls=%async_computation | async-start | bytes 3932160 | tf_op jit(solution)/shard_map/all_to_all | solution.py:236
  48.2 18.2 %collective-permute-start.2 = (bf16[32,3840]{1,0:T(8,128)(2,1)S(1)}, bf16[32,3840]{1,0:T(8,128)(2,1)S(1)}, u32[]{:S(2)}, u32[]{:S(2)}) collective-permute-start(bf16[32,3840]{1,0:T(8,128)(2,1)S(1)} %get-tuple-element.22), channel_id=1, source_target_pairs={{0,256},{16,272},{32,288},{48,304},{64,320},{80,336},{96,352},{112... | collective-permute-start | bytes 737288 | tf_op jit(solution)/shard_map/ppermute | solution.py:258
  69.1 1.3 copy-start.1
  73.8 32.0 %all-to-all-start.1 = ((bf16[8,32,3840]{2,1,0:T(8,128)(2,1)}), bf16[8,32,3840]{2,1,0:T(8,128)(2,1)}, u32[]{:S(2)}, u32[]{:S(2)}) async-start(bf16[8,32,3840]{2,1,0:T(8,128)(2,1)} %bitcast.13), calls=%async_computation.1 | async-start | bytes 3932160 | tf_op jit(solution)/shard_map/all_to_all | solution.py:236
  110.3 21.6 %collective-permute-start.4 = (f32[64,1024]{1,0:T(8,128)S(1)}, f32[64,1024]{1,0:T(8,128)S(1)}, u32[]{:S(2)}, u32[]{:S(2)}) collective-permute-start(f32[64,1024]{1,0:T(8,128)S(1)} %shard_map.53), channel_id=1, source_target_pairs={{0,32},{1,481},{2,34},{3,483},{4,36},{5,485},{6,38},{7,487},{8,40}... | collective-permute-start | bytes 786440 | tf_op jit(solution)/shard_map/ppermute | solution.py:173
  127.5 13.9 %collective-permute-start.3 = (f32[64,1024]{1,0:T(8,128)S(1)}, f32[64,1024]{1,0:T(8,128)S(1)}, u32[]{:S(2)}, u32[]{:S(2)}) collective-permute-start(f32[64,1024]{1,0:T(8,128)S(1)} %shard_map.52), channel_id=1, source_target_pairs={{0,32},{1,481},{2,34},{3,483},{4,36},{5,485},{6,38},{7,487},{8,40}... | collective-permute-start | bytes 786440 | tf_op jit(solution)/shard_map/ppermute | solution.py:173
  131.9 14.6 %collective-permute-start.6 = (f32[64,1024]{1,0:T(8,128)S(1)}, f32[64,1024]{1,0:T(8,128)S(1)}, u32[]{:S(2)}, u32[]{:S(2)}) collective-permute-start(f32[64,1024]{1,0:T(8,128)S(1)} %shard_map.54.refs_3_), channel_id=1, source_target_pairs={{0,480},{1,33},{2,482},{3,35},{4,484},{5,37},{6,486},{7,39},{8,488... | collective-permute-start | bytes 786440 | tf_op jit(solution)/shard_map/ppermute | solution.py:173
  141.5 11.3 %collective-permute-start.5 = (f32[64,1024]{1,0:T(8,128)S(1)}, f32[64,1024]{1,0:T(8,128)S(1)}, u32[]{:S(2)}, u32[]{:S(2)}) collective-permute-start(f32[64,1024]{1,0:T(8,128)S(1)} %shard_map.55), channel_id=1, source_target_pairs={{0,480},{1,33},{2,482},{3,35},{4,484},{5,37},{6,486},{7,39},{8,488... | collective-permute-start | bytes 786440 | tf_op jit(solution)/shard_map/ppermute | solution.py:173
  146.5 8.3 %collective-permute-start.8 = (f32[64,1024]{1,0:T(8,128)S(1)}, f32[64,1024]{1,0:T(8,128)S(1)}, u32[]{:S(2)}, u32[]{:S(2)}) collective-permute-start(f32[64,1024]{1,0:T(8,128)S(1)} %shard_map.56.refs_3_), channel_id=1, source_target_pairs={{0,32},{1,481},{2,34},{3,483},{4,36},{5,485},{6,38},{7,487},{8,40}... | collective-permute-start | bytes 786440 | tf_op jit(solution)/shard_map/ppermute | solution.py:173
  152.8 14.3 %collective-permute-start.7 = (f32[64,1024]{1,0:T(8,128)S(1)}, f32[64,1024]{1,0:T(8,128)S(1)}, u32[]{:S(2)}, u32[]{:S(2)}) collective-permute-start(f32[64,1024]{1,0:T(8,128)S(1)} %shard_map.57), channel_id=1, source_target_pairs={{0,32},{1,481},{2,34},{3,483},{4,36},{5,485},{6,38},{7,487},{8,40}... | collective-permute-start | bytes 786440 | tf_op jit(solution)/shard_map/ppermute | solution.py:173
  154.8 15.4 %collective-permute-start.9 = (f32[64,1024]{1,0:T(8,128)S(1)}, f32[64,1024]{1,0:T(8,128)S(1)}, u32[]{:S(2)}, u32[]{:S(2)}) collective-permute-start(f32[64,1024]{1,0:T(8,128)S(1)} %shard_map.59), channel_id=1, source_target_pairs={{0,384},{1,129},{2,386},{3,131},{4,388},{5,133},{6,390},{7,135},{8... | collective-permute-start | bytes 786440 | tf_op jit(solution)/shard_map/ppermute | solution.py:173
  170.3 15.5 %collective-permute-start.12 = (f32[32,512]{1,0:T(8,128)S(1)}, f32[32,512]{1,0:T(8,128)S(1)}, u32[]{:S(2)}, u32[]{:S(2)}) collective-permute-start(f32[32,512]{1,0:T(8,128)S(1)} %get-tuple-element.23), channel_id=1, source_target_pairs={{0,17},{1,49},{2,19},{3,51},{4,21},{5,53},{6,23},{7,55},{8,25},{9,... | collective-permute-start | bytes 196616 | tf_op jit(solution)/shard_map/ppermute | solution.py:173
  172.2 13.6 %collective-permute-start.10 = (f32[32,512]{1,0:T(8,128)S(1)}, f32[32,512]{1,0:T(8,128)S(1)}, u32[]{:S(2)}, u32[]{:S(2)}) collective-permute-start(f32[32,512]{1,0:T(8,128)S(1)} %get-tuple-element.24), channel_id=1, source_target_pairs={{1,48},{3,50},{5,52},{7,54},{9,56},{11,58},{13,60},{15,62},{17,32}... | collective-permute-start | bytes 196616 | tf_op jit(solution)/shard_map/ppermute | solution.py:173
  172.9 12.9 %collective-permute-start.11 = (f32[32,512]{1,0:T(8,128)S(1)}, f32[32,512]{1,0:T(8,128)S(1)}, u32[]{:S(2)}, u32[]{:S(2)}) collective-permute-start(f32[32,512]{1,0:T(8,128)S(1)} %get-tuple-element.25), channel_id=1, source_target_pairs={{0,1},{1,33},{2,3},{3,35},{4,5},{5,37},{6,7},{7,39},{8,9},{9,41},{... | collective-permute-start | bytes 196616 | tf_op jit(solution)/shard_map/ppermute | solution.py:173
  180.8 7.7 %collective-permute-start.13 = (f32[32,512]{1,0:T(8,128)S(1)}, f32[32,512]{1,0:T(8,128)S(1)}, u32[]{:S(2)}, u32[]{:S(2)}) collective-permute-start(f32[32,512]{1,0:T(8,128)S(1)} %get-tuple-element.26), channel_id=1, source_target_pairs={{0,16},{1,32},{2,18},{3,34},{4,20},{5,36},{6,22},{7,38},{8,24},{9,... | collective-permute-start | bytes 196616 | tf_op jit(solution)/shard_map/ppermute | solution.py:173

commit v11 on v9

--- a/solution.py
+++ b/solution.py
@@ -10,7 +10,6 @@
 LANES = 128
 UNROLL = 32
 K_TILE = 768
-OUTER = 3
 CHUNKS = (32, 32)
 STARTS = tuple(sum(CHUNKS[:h]) for h in range(len(CHUNKS)))
 PEERS = 8
@@ -267,15 +266,12 @@
     s_both = pltpu.with_memory_space_constraint(s_both, pltpu.HBM)
     pieces = [pltpu.with_memory_space_constraint(piece, pltpu.HBM) for piece in pieces]
     terms = product(pieces, s_both)
-    outer, inner = terms[0], terms[OUTER]
-    for step in range(1, OUTER):
+    outer, inner = terms[0], terms[4]
+    for step in range(1, 4):
         outer = terms[step] + slice_move(outer, functools.partial(exchange, step))
-        inner = slice_move(inner, functools.partial(exchange, step + OUTER))
-        inner = add_term(terms, OUTER + step, inner, outer)
-    skipped = slice_move(outer, lambda z, y_hi, c: (z - 5 if (c - z) % 2 else z + 5, y_hi, c))
-    for step in range(OUTER, 8 - OUTER):
-        inner = terms[OUTER + step] + slice_move(inner, functools.partial(exchange, step + OUTER))
-    inner += skipped
+        inner = slice_move(inner, functools.partial(exchange, step))
+        inner = add_term(terms, 4 + step, inner, outer) if step < 3 else terms[7] + inner
+    inner += slice_move(outer, lambda z, y_hi, c: (z + 4 if (c - z) % 2 else z - 4, y_hi, c))
 
     half_cols = inner.shape[1] // 2
     mine, theirs = inner[:, :half_cols], inner[:, half_cols:]

time: 197 us -> 189 us (0.959)
  the two profiles are of different devices: /device:TPU:8 before, /device:TPU:6 now
where the time goes in v11:
time: 189 us; the launch traced here: 186 us
  starting transfers between devices  95.6 us (51%)
  waiting for transfers between devices  33.8 us (18%)
  blocking collectives  29.2 us (15%)
  Pallas kernels  19.5 us (10%)
  local copies, waits for them, and re-layouts  6.27 us (3%)
    ppermute x11, starting transfers between devices, slice_move(): return lax.ppermute(value, ('grp', 'col'), pairs)  54.4 us
    all_to_all x1, blocking collectives, gather_col(): lax.all_to_all(copies, 'col', 0, 0, axis_index_groups=groups, tiled=True)  29.2 us
    ppermute x2, starting transfers between devices, per_device(): arrived = lax.ppermute(leaving, 'grp', [(i, i ^ 16) for i in range(32)])  28.2 us
    ppermute x11, waiting for transfers between devices, slice_move(): return lax.ppermute(value, ('grp', 'col'), pairs)  23.2 us
    all_to_all x1, starting transfers between devices, gather_col(): lax.all_to_all(copies, 'col', 0, 0, axis_index_groups=groups, tiled=True)  11.1 us
    pallas_call x1, Pallas kernels, product(): pl.pallas_call(product_kernel, out_shape=jax.ShapeDtypeStruct((PEERS, blo...  6.17 us
    ppermute x2, waiting for transfers between devices, per_device(): arrived = lax.ppermute(leaving, 'grp', [(i, i ^ 16) for i in range(32)])  5.8 us
    pallas_call x1, Pallas kernels, scatter_rows(): pl.pallas_call(scatter_kernel, out_shape=[jax.ShapeDtypeStruct((rows, blk...  5.76 us
  transfers between devices with their start and end apart: 15, of which 8 were waited for; matrix products, arithmetic and copies ran while one was open for 0% of the time, Pallas kernels for 6%

profile of v11, /device:TPU:6, one launch (start us, length us, event | category | flops | bytes accessed | tf_op | source)
XLA Modules:
  0.0 186.2 jit_solution(2700086218094195273)
XLA Ops:
  0.0 1.9 %collective-permute-start.1 = (bf16[3840,256]{1,0:T(8,128)(2,1)}, bf16[3840,256]{1,0:T(8,128)(2,1)S(1)}, u32[]{:S(2)}, u32[]{:S(2)}) collective-permute-start(bf16[3840,256]{1,0:T(8,128)(2,1)} %own_ref.1), channel_id=1, source_target_pairs={{0,1},{1,0},{2,3},{3,2},{4,5},{5,4},{6,7},{7,6},{8,9},{9,8},{10,11... | collective-permute-start | bytes 5898248 | tf_op jit(solution)/shard_map/ppermute | solution.py:171
  1.9 0.7 subtract_select_fusion.place_ref
  2.7 1.0 copy-done.2
  3.7 5.8 %shard_map.46 = (bf16[32,3840]{1,0:T(8,128)(2,1)S(1)}, bf16[32,3840]{1,0:T(8,128)(2,1)S(1)}, bf16[32,3840]{1,0:T(8,128)(2,1)S(1)}, bf16[32,3840]{1,0:T(8,128)(2,1)S(1)}, bf16[3840,128]{1,0:T(8,128)(2,1)S(1)}) custom-call(s32[3840]{0:T(1024)S(1)} %subtract_select_fusion.place_ref, bf16[64,3840]{1,0:T(8,128)(2,1)S(1)} %bitcast.35), custom_call_target="tpu_custom_call" | custom-call | tf_op jit(solution)/shard_map/pallas_call | solution.py:47
  9.4 15.7 %collective-permute-start = (bf16[32,3840]{1,0:T(8,128)(2,1)S(1)}, bf16[32,3840]{1,0:T(8,128)(2,1)S(1)}, u32[]{:S(2)}, u32[]{:S(2)}) collective-permute-start(bf16[32,3840]{1,0:T(8,128)(2,1)S(1)} %get-tuple-element.15), channel_id=1, source_target_pairs={{0,256},{16,272},{32,288},{48,304},{64,320},{80,336},{96,352},{112... | collective-permute-start | bytes 737288 | tf_op jit(solution)/shard_map/ppermute | solution.py:260
  25.8 1.5 copy-done.1
  27.4 3.5 %shard_map.47 = (bf16[3840,1024]{1,0:T(8,128)(2,1)S(1)}, f32[8,128]{1,0:T(8,128)S(1)}) custom-call(s32[1]{0:T(128)S(6)} %copy.9.kept_ref, bf16[3840,128]{1,0:T(8,128)(2,1)S(1)} %get-tuple-element.17.flag_ref, bf16[3840,256]{1,0:T(8,128)(2,1)S(1)} %copy-done.1, bf16[3840,256]{1,0:T(8,128)(2,1)S(1)} %collective-permute-done.1.other_ref), custom_call_target="tpu_custom_call" | custom-call | tf_op jit(solution)/shard_map/pallas_call | solution.py:83
  30.9 3.0 %copy-done = bf16[3840,1024]{1,0:T(8,128)(2,1)} copy-done((bf16[3840,1024]{1,0:T(8,128)(2,1)}, bf16[3840,1024]{1,0:T(8,128)(2,1)S(1)}, u32[]{:S(2)}) %copy-start) | copy-done | bytes 7864344
  33.9 1.4 shard_map.48
  35.3 11.1 %all-to-all-start = ((bf16[8,32,3840]{2,1,0:T(8,128)(2,1)}), bf16[8,32,3840]{2,1,0:T(8,128)(2,1)}, u32[]{:S(2)}, u32[]{:S(2)}) async-start(bf16[8,32,3840]{2,1,0:T(8,128)(2,1)} %bitcast.1), calls=%async_computation | async-start | bytes 3932160 | tf_op jit(solution)/shard_map/all_to_all | solution.py:238
  46.3 12.4 %collective-permute-start.2 = (bf16[32,3840]{1,0:T(8,128)(2,1)S(1)}, bf16[32,3840]{1,0:T(8,128)(2,1)S(1)}, u32[]{:S(2)}, u32[]{:S(2)}) collective-permute-start(bf16[32,3840]{1,0:T(8,128)(2,1)S(1)} %get-tuple-element.21), channel_id=1, source_target_pairs={{0,256},{16,272},{32,288},{48,304},{64,320},{80,336},{96,352},{112... | collective-permute-start | bytes 737288 | tf_op jit(solution)/shard_map/ppermute | solution.py:260
  58.8 5.8 %collective-permute-done.2.refs_1_ = bf16[32,3840]{1,0:T(8,128)(2,1)S(1)} collective-permute-done((bf16[32,3840]{1,0:T(8,128)(2,1)S(1)}, bf16[32,3840]{1,0:T(8,128)(2,1)S(1)}, u32[]{:S(2)}, u32[]{:S(2)}) %collective-permute-start.2) | collective-permute-done | bytes 245792 | tf_op jit(solution)/shard_map/ppermute | solution.py:260
  64.6 2.6 %shard_map.49 = bf16[256,3840]{1,0:T(8,128)(2,1)S(1)} custom-call(bf16[32,3840]{1,0:T(8,128)(2,1)S(1)} %get-tuple-element.20.refs_0_, bf16[32,3840]{1,0:T(8,128)(2,1)S(1)} %collective-permute-done.2.refs_1_, f32[8,128]{1,0:T(8,128)S(1)} %get-tuple-element.18.refs_3_.refs_2_), custom_call_target="tpu_custom_call" | custom-call | tf_op jit(solution)/shard_map/pallas_call | solution.py:210
  67.2 4.8 %all-to-all-done = bf16[8,32,3840]{2,1,0:T(8,128)(2,1)} async-done(((bf16[8,32,3840]{2,1,0:T(8,128)(2,1)}), bf16[8,32,3840]{2,1,0:T(8,128)(2,1)}, u32[]{:S(2)}, u32[]{:S(2)}) %all-to-all-start) | async-done | bytes 1966112 | tf_op jit(solution)/shard_map/all_to_all | solution.py:238
  72.0 29.2 %all_to_all.22 = bf16[8,32,3840]{2,1,0:T(8,128)(2,1)} all-to-all(bf16[8,32,3840]{2,1,0:T(8,128)(2,1)S(1)} %bitcast.34), channel_id=1, replica_groups={{0,2,4,6,8,10,12,14},{1,3,5,7,9,11,13,15},{16,18,20,22,24,26,28,30},{17..., dimensions={0} | all-to-all | bytes 3932160 | tf_op jit(solution)/shard_map/all_to_all | solution.py:238
  101.2 6.2 %shard_map.50.terms_ref = f32[8,64,1024]{2,1,0:T(8,128)S(1)} custom-call(bf16[256,3840]{1,0:T(8,128)(2,1)} %bitcast.2.refs_0_, bf16[256,3840]{1,0:T(8,128)(2,1)} %bitcast.36, bf16[3840,1024]{1,0:T(8,128)(2,1)} %copy-done), custom_call_target="tpu_custom_call" | custom-call | tf_op jit(solution)/shard_map/pallas_call | solution.py:150
  107.5 15.3 %collective-permute-start.4 = (f32[64,1024]{1,0:T(8,128)S(1)}, f32[64,1024]{1,0:T(8,128)S(1)}, u32[]{:S(2)}, u32[]{:S(2)}) collective-permute-start(f32[64,1024]{1,0:T(8,128)S(1)} %get-tuple-element.26), channel_id=1, source_target_pairs={{0,32},{1,481},{2,34},{3,483},{4,36},{5,485},{6,38},{7,487},{8,40}... | collective-permute-start | bytes 786440 | tf_op jit(solution)/shard_map/ppermute | solution.py:181
  122.8 1.9 %collective-permute-start.3 = (f32[64,1024]{1,0:T(8,128)S(1)}, f32[64,1024]{1,0:T(8,128)S(1)}, u32[]{:S(2)}, u32[]{:S(2)}) collective-permute-start(f32[64,1024]{1,0:T(8,128)S(1)} %get-tuple-element.25), channel_id=1, source_target_pairs={{0,32},{1,481},{2,34},{3,483},{4,36},{5,485},{6,38},{7,487},{8,40}... | collective-permute-start | bytes 786440 | tf_op jit(solution)/shard_map/ppermute | solution.py:181
  124.7 2.4 %collective-permute-done.4 = f32[64,1024]{1,0:T(8,128)S(1)} collective-permute-done((f32[64,1024]{1,0:T(8,128)S(1)}, f32[64,1024]{1,0:T(8,128)S(1)}, u32[]{:S(2)}, u32[]{:S(2)}) %collective-permute-start.4) | collective-permute-done | bytes 262176 | tf_op jit(solution)/shard_map/ppermute | solution.py:181
  127.2 10.0 %collective-permute-start.6 = (f32[64,1024]{1,0:T(8,128)S(1)}, f32[64,1024]{1,0:T(8,128)S(1)}, u32[]{:S(2)}, u32[]{:S(2)}) collective-permute-start(f32[64,1024]{1,0:T(8,128)S(1)} %fusion.2.after_ref), channel_id=1, source_target_pairs={{0,480},{1,33},{2,482},{3,35},{4,484},{5,37},{6,486},{7,39},{8,488... | collective-permute-start | bytes 786440 | tf_op jit(solution)/shard_map/ppermute | solution.py:181
  137.2 5.4 %collective-permute-start.5 = (f32[64,1024]{1,0:T(8,128)S(1)}, f32[64,1024]{1,0:T(8,128)S(1)}, u32[]{:S(2)}, u32[]{:S(2)}) collective-permute-start(f32[64,1024]{1,0:T(8,128)S(1)} %shard_map.51), channel_id=1, source_target_pairs={{0,480},{1,33},{2,482},{3,35},{4,484},{5,37},{6,486},{7,39},{8,488... | collective-permute-start | bytes 786440 | tf_op jit(solution)/shard_map/ppermute | solution.py:181
  142.7 1.9 %collective-permute-start.8 = (f32[64,1024]{1,0:T(8,128)S(1)}, f32[64,1024]{1,0:T(8,128)S(1)}, u32[]{:S(2)}, u32[]{:S(2)}) collective-permute-start(f32[64,1024]{1,0:T(8,128)S(1)} %fusion.1.after_ref), channel_id=1, source_target_pairs={{0,32},{1,481},{2,34},{3,483},{4,36},{5,485},{6,38},{7,487},{8,40}... | collective-permute-start | bytes 786440 | tf_op jit(solution)/shard_map/ppermute | solution.py:181
  144.6 4.5 %collective-permute-done.5.arrived_ref = f32[64,1024]{1,0:T(8,128)S(1)} collective-permute-done((f32[64,1024]{1,0:T(8,128)S(1)}, f32[64,1024]{1,0:T(8,128)S(1)}, u32[]{:S(2)}, u32[]{:S(2)}) %collective-permute-start.5) | collective-permute-done | bytes 262176 | tf_op jit(solution)/shard_map/ppermute | solution.py:181
  149.1 1.9 %collective-permute-start.7 = (f32[64,1024]{1,0:T(8,128)S(1)}, f32[64,1024]{1,0:T(8,128)S(1)}, u32[]{:S(2)}, u32[]{:S(2)}) collective-permute-start(f32[64,1024]{1,0:T(8,128)S(1)} %shard_map.52), channel_id=1, source_target_pairs={{0,32},{1,481},{2,34},{3,483},{4,36},{5,485},{6,38},{7,487},{8,40}... | collective-permute-start | bytes 786440 | tf_op jit(solution)/shard_map/ppermute | solution.py:181
  151.1 4.4 %collective-permute-start.9 = (f32[64,1024]{1,0:T(8,128)S(1)}, f32[64,1024]{1,0:T(8,128)S(1)}, u32[]{:S(2)}, u32[]{:S(2)}) collective-permute-start(f32[64,1024]{1,0:T(8,128)S(1)} %fusion), channel_id=1, source_target_pairs={{0,384},{1,129},{2,386},{3,131},{4,388},{5,133},{6,390},{7,135},{8... | collective-permute-start | bytes 786440 | tf_op jit(solution)/shard_map/ppermute | solution.py:181
  155.6 9.7 %collective-permute-done.7 = f32[64,1024]{1,0:T(8,128)S(1)} collective-permute-done((f32[64,1024]{1,0:T(8,128)S(1)}, f32[64,1024]{1,0:T(8,128)S(1)}, u32[]{:S(2)}, u32[]{:S(2)}) %collective-permute-start.7) | collective-permute-done | bytes 262176 | tf_op jit(solution)/shard_map/ppermute | solution.py:181
  165.3 1.3 collective-permute-done.9
  167.4 5.0 %collective-permute-start.11 = (f32[32,512]{1,0:T(8,128)S(1)}, f32[32,512]{1,0:T(8,128)S(1)}, u32[]{:S(2)}, u32[]{:S(2)}) collective-permute-start(f32[32,512]{1,0:T(8,128)S(1)} %get-tuple-element.27), channel_id=1, source_target_pairs={{0,1},{1,33},{2,3},{3,35},{4,5},{5,37},{6,7},{7,39},{8,9},{9,41},{... | collective-permute-start | bytes 196616 | tf_op jit(solution)/shard_map/ppermute | solution.py:181
  172.4 5.5 %collective-permute-start.12 = (f32[32,512]{1,0:T(8,128)S(1)}, f32[32,512]{1,0:T(8,128)S(1)}, u32[]{:S(2)}, u32[]{:S(2)}) collective-permute-start(f32[32,512]{1,0:T(8,128)S(1)} %get-tuple-element.23), channel_id=1, source_target_pairs={{0,17},{1,49},{2,19},{3,51},{4,21},{5,53},{6,23},{7,55},{8,25},{9,... | collective-permute-start | bytes 196616 | tf_op jit(solution)/shard_map/ppermute | solution.py:181
  177.9 2.3 %collective-permute-start.13 = (f32[32,512]{1,0:T(8,128)S(1)}, f32[32,512]{1,0:T(8,128)S(1)}, u32[]{:S(2)}, u32[]{:S(2)}) collective-permute-start(f32[32,512]{1,0:T(8,128)S(1)} %get-tuple-element.28), channel_id=1, source_target_pairs={{0,16},{1,32},{2,18},{3,34},{4,20},{5,36},{6,22},{7,38},{8,24},{9,... | collective-permute-start | bytes 196616 | tf_op jit(solution)/shard_map/ppermute | solution.py:181
  180.3 1.9 %collective-permute-done.12 = f32[32,512]{1,0:T(8,128)S(1)} collective-permute-done((f32[32,512]{1,0:T(8,128)S(1)}, f32[32,512]{1,0:T(8,128)S(1)}, u32[]{:S(2)}, u32[]{:S(2)}) %collective-permute-start.12) | collective-permute-done | bytes 65568 | tf_op jit(solution)/shard_map/ppermute | solution.py:181
  182.2 3.4 %collective-permute-done.13 = f32[32,512]{1,0:T(8,128)S(1)} collective-permute-done((f32[32,512]{1,0:T(8,128)S(1)}, f32[32,512]{1,0:T(8,128)S(1)}, u32[]{:S(2)}, u32[]{:S(2)}) %collective-permute-start.13) | collective-permute-done | bytes 65568 | tf_op jit(solution)/shard_map/ppermute | solution.py:181
  (21 shorter events, 1.7 us)
Async XLA Ops:
  0.0 25.8 %collective-permute-start.1 = (bf16[3840,256]{1,0:T(8,128)(2,1)}, bf16[3840,256]{1,0:T(8,128)(2,1)S(1)}, u32[]{:S(2)}, u32[]{:S(2)}) collective-permute-start(bf16[3840,256]{1,0:T(8,128)(2,1)} %own_ref.1), channel_id=1, source_target_pairs={{0,1},{1,0},{2,3},{3,2},{4,5},{5,4},{6,7},{7,6},{8,9},{9,8},{10,11... | collective-permute-start | bytes 5898248 | tf_op jit(solution)/shard_map/ppermute | solution.py:171
  2.7 1.0 copy-start.2
  9.4 24.5 %collective-permute-start = (bf16[32,3840]{1,0:T(8,128)(2,1)S(1)}, bf16[32,3840]{1,0:T(8,128)(2,1)S(1)}, u32[]{:S(2)}, u32[]{:S(2)}) collective-permute-start(bf16[32,3840]{1,0:T(8,128)(2,1)S(1)} %get-tuple-element.15), channel_id=1, source_target_pairs={{0,256},{16,272},{32,288},{48,304},{64,320},{80,336},{96,352},{112... | collective-permute-start | bytes 737288 | tf_op jit(solution)/shard_map/ppermute | solution.py:260
  25.8 1.5 copy-start.1
  30.9 3.1 %copy-start = (bf16[3840,1024]{1,0:T(8,128)(2,1)}, bf16[3840,1024]{1,0:T(8,128)(2,1)S(1)}, u32[]{:S(2)}) copy-start(bf16[3840,1024]{1,0:T(8,128)(2,1)S(1)} %get-tuple-element.22.refs_2_) | copy-start | bytes 23592964
  35.3 36.7 %all-to-all-start = ((bf16[8,32,3840]{2,1,0:T(8,128)(2,1)}), bf16[8,32,3840]{2,1,0:T(8,128)(2,1)}, u32[]{:S(2)}, u32[]{:S(2)}) async-start(bf16[8,32,3840]{2,1,0:T(8,128)(2,1)} %bitcast.1), calls=%async_computation | async-start | bytes 3932160 | tf_op jit(solution)/shard_map/all_to_all | solution.py:238
  46.3 18.2 %collective-permute-start.2 = (bf16[32,3840]{1,0:T(8,128)(2,1)S(1)}, bf16[32,3840]{1,0:T(8,128)(2,1)S(1)}, u32[]{:S(2)}, u32[]{:S(2)}) collective-permute-start(bf16[32,3840]{1,0:T(8,128)(2,1)S(1)} %get-tuple-element.21), channel_id=1, source_target_pairs={{0,256},{16,272},{32,288},{48,304},{64,320},{80,336},{96,352},{112... | collective-permute-start | bytes 737288 | tf_op jit(solution)/shard_map/ppermute | solution.py:260
  107.5 19.7 %collective-permute-start.4 = (f32[64,1024]{1,0:T(8,128)S(1)}, f32[64,1024]{1,0:T(8,128)S(1)}, u32[]{:S(2)}, u32[]{:S(2)}) collective-permute-start(f32[64,1024]{1,0:T(8,128)S(1)} %get-tuple-element.26), channel_id=1, source_target_pairs={{0,32},{1,481},{2,34},{3,483},{4,36},{5,485},{6,38},{7,487},{8,40}... | collective-permute-start | bytes 786440 | tf_op jit(solution)/shard_map/ppermute | solution.py:181
  122.8 14.4 %collective-permute-start.3 = (f32[64,1024]{1,0:T(8,128)S(1)}, f32[64,1024]{1,0:T(8,128)S(1)}, u32[]{:S(2)}, u32[]{:S(2)}) collective-permute-start(f32[64,1024]{1,0:T(8,128)S(1)} %get-tuple-element.25), channel_id=1, source_target_pairs={{0,32},{1,481},{2,34},{3,483},{4,36},{5,485},{6,38},{7,487},{8,40}... | collective-permute-start | bytes 786440 | tf_op jit(solution)/shard_map/ppermute | solution.py:181
  127.2 15.5 %collective-permute-start.6 = (f32[64,1024]{1,0:T(8,128)S(1)}, f32[64,1024]{1,0:T(8,128)S(1)}, u32[]{:S(2)}, u32[]{:S(2)}) collective-permute-start(f32[64,1024]{1,0:T(8,128)S(1)} %fusion.2.after_ref), channel_id=1, source_target_pairs={{0,480},{1,33},{2,482},{3,35},{4,484},{5,37},{6,486},{7,39},{8,488... | collective-permute-start | bytes 786440 | tf_op jit(solution)/shard_map/ppermute | solution.py:181
  137.2 11.8 %collective-permute-start.5 = (f32[64,1024]{1,0:T(8,128)S(1)}, f32[64,1024]{1,0:T(8,128)S(1)}, u32[]{:S(2)}, u32[]{:S(2)}) collective-permute-start(f32[64,1024]{1,0:T(8,128)S(1)} %shard_map.51), channel_id=1, source_target_pairs={{0,480},{1,33},{2,482},{3,35},{4,484},{5,37},{6,486},{7,39},{8,488... | collective-permute-start | bytes 786440 | tf_op jit(solution)/shard_map/ppermute | solution.py:181
  142.7 8.4 %collective-permute-start.8 = (f32[64,1024]{1,0:T(8,128)S(1)}, f32[64,1024]{1,0:T(8,128)S(1)}, u32[]{:S(2)}, u32[]{:S(2)}) collective-permute-start(f32[64,1024]{1,0:T(8,128)S(1)} %fusion.1.after_ref), channel_id=1, source_target_pairs={{0,32},{1,481},{2,34},{3,483},{4,36},{5,485},{6,38},{7,487},{8,40}... | collective-permute-start | bytes 786440 | tf_op jit(solution)/shard_map/ppermute | solution.py:181
  149.1 16.2 %collective-permute-start.7 = (f32[64,1024]{1,0:T(8,128)S(1)}, f32[64,1024]{1,0:T(8,128)S(1)}, u32[]{:S(2)}, u32[]{:S(2)}) collective-permute-start(f32[64,1024]{1,0:T(8,128)S(1)} %shard_map.52), channel_id=1, source_target_pairs={{0,32},{1,481},{2,34},{3,483},{4,36},{5,485},{6,38},{7,487},{8,40}... | collective-permute-start | bytes 786440 | tf_op jit(solution)/shard_map/ppermute | solution.py:181
  151.1 15.5 %collective-permute-start.9 = (f32[64,1024]{1,0:T(8,128)S(1)}, f32[64,1024]{1,0:T(8,128)S(1)}, u32[]{:S(2)}, u32[]{:S(2)}) collective-permute-start(f32[64,1024]{1,0:T(8,128)S(1)} %fusion), channel_id=1, source_target_pairs={{0,384},{1,129},{2,386},{3,131},{4,388},{5,133},{6,390},{7,135},{8... | collective-permute-start | bytes 786440 | tf_op jit(solution)/shard_map/ppermute | solution.py:181
  166.7 13.6 %collective-permute-start.10 = (f32[32,512]{1,0:T(8,128)S(1)}, f32[32,512]{1,0:T(8,128)S(1)}, u32[]{:S(2)}, u32[]{:S(2)}) collective-permute-start(f32[32,512]{1,0:T(8,128)S(1)} %get-tuple-element.24), channel_id=1, source_target_pairs={{1,48},{3,50},{5,52},{7,54},{9,56},{11,58},{13,60},{15,62},{17,32}... | collective-permute-start | bytes 196616 | tf_op jit(solution)/shard_map/ppermute | solution.py:181
  167.4 12.9 %collective-permute-start.11 = (f32[32,512]{1,0:T(8,128)S(1)}, f32[32,512]{1,0:T(8,128)S(1)}, u32[]{:S(2)}, u32[]{:S(2)}) collective-permute-start(f32[32,512]{1,0:T(8,128)S(1)} %get-tuple-element.27), channel_id=1, source_target_pairs={{0,1},{1,33},{2,3},{3,35},{4,5},{5,37},{6,7},{7,39},{8,9},{9,41},{... | collective-permute-start | bytes 196616 | tf_op jit(solution)/shard_map/ppermute | solution.py:181
  172.4 9.8 %collective-permute-start.12 = (f32[32,512]{1,0:T(8,128)S(1)}, f32[32,512]{1,0:T(8,128)S(1)}, u32[]{:S(2)}, u32[]{:S(2)}) collective-permute-start(f32[32,512]{1,0:T(8,128)S(1)} %get-tuple-element.23), channel_id=1, source_target_pairs={{0,17},{1,49},{2,19},{3,51},{4,21},{5,53},{6,23},{7,55},{8,25},{9,... | collective-permute-start | bytes 196616 | tf_op jit(solution)/shard_map/ppermute | solution.py:181
  177.9 7.7 %collective-permute-start.13 = (f32[32,512]{1,0:T(8,128)S(1)}, f32[32,512]{1,0:T(8,128)S(1)}, u32[]{:S(2)}, u32[]{:S(2)}) collective-permute-start(f32[32,512]{1,0:T(8,128)S(1)} %get-tuple-element.28), channel_id=1, source_target_pairs={{0,16},{1,32},{2,18},{3,34},{4,20},{5,36},{6,22},{7,38},{8,24},{9,... | collective-permute-start | bytes 196616 | tf_op jit(solution)/shard_map/ppermute | solution.py:181

commit v12 on v10

--- a/solution.py
+++ b/solution.py
@@ -107,7 +107,8 @@
     return jnp.where(odd == 1, odd_slot, even_slot)
 
 
-def product_kernel(piece_hbm, s_hbm, out_ref, total, lhs_ref, s_ref, sems):
+def product_kernel(piece_hbm, s_hbm, *refs):
+    out_ref, total, lhs_ref, s_ref, sems = refs[-5:]
     z, c = lax.axis_index("grp") // 2, lax.axis_index("col")
     tiles = s_ref.shape[0] // K_TILE
     spans = [pl.ds(k * K_TILE, K_TILE) for k in range(tiles)]
@@ -136,13 +137,13 @@
         out_ref[slot_of(z, c % 2, peer)] = term[peer * rows : (peer + 1) * rows, :]
 
 
-def product(piece, s_both):
+def product(piece, s_both, after):
     blk, cols = s_both.shape
     rows = piece.shape[0]
     return pl.pallas_call(
         product_kernel,
         out_shape=jax.ShapeDtypeStruct((PEERS, rows // PEERS, cols), jnp.float32),
-        in_specs=[pl.BlockSpec(memory_space=pl.ANY)] * 2,
+        in_specs=[pl.BlockSpec(memory_space=pltpu.HBM)] * 2 + [pl.BlockSpec(memory_space=pl.ANY)] * len(after),
         out_specs=pl.BlockSpec(memory_space=pltpu.VMEM),
         scratch_shapes=[
             pltpu.VMEM((rows, cols), jnp.float32),
@@ -151,7 +152,7 @@
             pltpu.SemaphoreType.DMA((blk // K_TILE, 2)),
         ],
         compiler_params=pltpu.CompilerParams(vmem_limit_bytes=20 * 2**20),
-    )(piece, s_both)
+    )(pltpu.with_memory_space_constraint(piece, pltpu.HBM), s_both, *after)
 
 
 def col_move(value, target):
@@ -210,30 +211,37 @@
     )(*arrays, after)
 
 
-def add_term_kernel(slot, *refs):
-    terms, out_ref = refs[: len(CHUNKS)], refs[-1]
-    arrived_ref = refs[len(CHUNKS)] if len(refs) > len(CHUNKS) + 1 else None
-    for ref, rows, start in zip(terms, CHUNKS, STARTS):
-        value = ref[slot]
-        if arrived_ref is not None:
-            value += arrived_ref[start : start + rows, :]
-        out_ref[start : start + rows, :] = value
-
-
-def add_term(terms, slot, *arrived):
+def add_term_kernel(slot, terms_ref, arrived_ref, after_ref, out_ref):
+    out_ref[...] = terms_ref[slot] + arrived_ref[...]
+
+
+def add_term(terms, slot, arrived, after):
     whole = pl.BlockSpec(memory_space=pltpu.VMEM)
     return pl.pallas_call(
         functools.partial(add_term_kernel, slot),
-        out_shape=jax.ShapeDtypeStruct((sum(CHUNKS), terms[0].shape[2]), jnp.float32),
-        in_specs=[whole] * (len(terms) + len(arrived[:1])) + [pl.BlockSpec(memory_space=pl.ANY)] * len(arrived[1:]),
+        out_shape=jax.ShapeDtypeStruct(arrived.shape, arrived.dtype),
+        in_specs=[whole, whole, pl.BlockSpec(memory_space=pl.ANY)],
         out_specs=whole,
-        compiler_params=pltpu.CompilerParams(vmem_limit_bytes=8 * 2**20),
-    )(*terms, *arrived)
+        compiler_params=pltpu.CompilerParams(vmem_limit_bytes=4 * 2**20),
+    )(terms, arrived, after)
 
 
 def gather_col(copies):
     groups = [[peer * 2 + core for peer in range(PEERS)] for core in range(2)]
     return lax.all_to_all(copies, "col", 0, 0, axis_index_groups=groups, tiled=True)
+
+
+def sum_near(terms):
+    outer, inner = terms[0], terms[4]
+    for step in range(1, 4):
+        outer = terms[step] + slice_move(outer, functools.partial(exchange, step))
+        inner = slice_move(inner, functools.partial(exchange, step))
+        if step < 3:
+            inner = near = add_term(terms, 4 + step, inner, outer)
+        else:
+            inner = terms[7] + inner
+    inner += slice_move(outer, lambda z, y_hi, c: (z + 4 if (c - z) % 2 else z - 4, y_hi, c))
+    return inner, [outer, near]
 
 
 def per_device(window_rows, secular, source, kept_count):
@@ -262,14 +270,11 @@
         pieces.append(gather_col(here))
 
     s_both = pltpu.with_memory_space_constraint(s_both, pltpu.HBM)
-    terms = [product(piece, s_both) for piece in pieces]
-
-    outer, inner = add_term(terms, 0), add_term(terms, 4)
-    for step in range(1, 4):
-        outer = add_term(terms, step, slice_move(outer, functools.partial(exchange, step)))
-        inner = slice_move(inner, functools.partial(exchange, step))
-        inner = add_term(terms, 4 + step, inner, *([outer] if step < 3 else []))
-    inner += slice_move(outer, lambda z, y_hi, c: (z + 4 if (c - z) % 2 else z - 4, y_hi, c))
+    sums, after = [], [masked]
+    for piece in pieces:
+        total, after = sum_near(product(piece, s_both, after))
+        sums.append(total)
+    inner = jnp.concatenate(sums, axis=0)
 
     half_cols = inner.shape[1] // 2
     mine, theirs = inner[:, :half_cols], inner[:, half_cols:]

time: 193 us -> 187 us (0.969)
  the two profiles are of different devices: /device:TPU:6 before, /device:TPU:64 now
where the time goes in v12:
time: 187 us; the launch traced here: 186 us
  starting transfers between devices  123 us (66%)
  waiting for transfers between devices  33.6 us (18%)
  Pallas kernels  21 us (11%)
  local copies, waits for them, and re-layouts  6.28 us (3%)
    ppermute x18, starting transfers between devices, slice_move(): return lax.ppermute(value, ('grp', 'col'), pairs)  71.5 us
    ppermute x2, starting transfers between devices, per_device(): arrived = lax.ppermute(leaving, 'grp', [(i, i ^ 16) for i in range(32)])  32.6 us
    ppermute x18, waiting for transfers between devices, slice_move(): return lax.ppermute(value, ('grp', 'col'), pairs)  19.1 us
    all_to_all x2, starting transfers between devices, gather_col(): lax.all_to_all(copies, 'col', 0, 0, axis_index_groups=groups, tiled=True)  17.5 us
    ppermute x2, waiting for transfers between devices, per_device(): arrived = lax.ppermute(leaving, 'grp', [(i, i ^ 16) for i in range(32)])  10.3 us
    pallas_call x2, Pallas kernels, product(): pl.pallas_call(product_kernel, out_shape=jax.ShapeDtypeStruct((PEERS, row...  8.87 us
    pallas_call x1, Pallas kernels, scatter_rows(): pl.pallas_call(scatter_kernel, out_shape=[jax.ShapeDtypeStruct((rows, blk...  5.76 us
    unnamed x6, local copies, waits for them, and re-layouts  5.62 us
  transfers between devices with their start and end apart: 23, of which 11 were waited for; matrix products, arithmetic and copies ran while one was open for 0% of the time, Pallas kernels for 8%

profile of v12, /device:TPU:64, one launch (start us, length us, event | category | flops | bytes accessed | tf_op | source)
XLA Modules:
  0.0 186.4 jit_solution(13475939029043334726)
XLA Ops:
  3.7 5.8 %shard_map.46 = (bf16[32,3840]{1,0:T(8,128)(2,1)S(1)}, bf16[32,3840]{1,0:T(8,128)(2,1)S(1)}, bf16[32,3840]{1,0:T(8,128)(2,1)S(1)}, bf16[32,3840]{1,0:T(8,128)(2,1)S(1)}, bf16[3840,128]{1,0:T(8,128)(2,1)S(1)}) custom-call(s32[3840]{0:T(1024)S(1)} %subtract_select_fusion.place_ref, bf16[64,3840]{1,0:T(8,128)(2,1)S(1)} %bitcast.56), custom_call_target="tpu_custom_call" | custom-call | tf_op jit(solution)/shard_map/pallas_call | solution.py:47
  9.4 13.9 %collective-permute-start = (bf16[32,3840]{1,0:T(8,128)(2,1)S(1)}, bf16[32,3840]{1,0:T(8,128)(2,1)S(1)}, u32[]{:S(2)}, u32[]{:S(2)}) collective-permute-start(bf16[32,3840]{1,0:T(8,128)(2,1)S(1)} %get-tuple-element.16), channel_id=1, source_target_pairs={{0,256},{16,272},{32,288},{48,304},{64,320},{80,336},{96,352},{112... | collective-permute-start | bytes 737288 | tf_op jit(solution)/shard_map/ppermute | solution.py:266
  25.6 3.5 %shard_map.47 = (bf16[3840,1024]{1,0:T(8,128)(2,1)S(1)}, f32[8,128]{1,0:T(8,128)S(1)}) custom-call(s32[1]{0:T(128)S(6)} %copy.9.kept_ref, bf16[3840,128]{1,0:T(8,128)(2,1)S(1)} %get-tuple-element.18.flag_ref, bf16[3840,256]{1,0:T(8,128)(2,1)S(1)} %copy-done.1, bf16[3840,256]{1,0:T(8,128)(2,1)S(1)} %collective-permute-done.1.other_ref), custom_call_target="tpu_custom_call" | custom-call | tf_op jit(solution)/shard_map/pallas_call | solution.py:83
  29.1 3.0 %copy-done = bf16[3840,1024]{1,0:T(8,128)(2,1)} copy-done((bf16[3840,1024]{1,0:T(8,128)(2,1)}, bf16[3840,1024]{1,0:T(8,128)(2,1)S(1)}, u32[]{:S(2)}) %copy-start) | copy-done | bytes 7864344
  32.1 5.5 %collective-permute-done.refs_1_ = bf16[32,3840]{1,0:T(8,128)(2,1)S(1)} collective-permute-done((bf16[32,3840]{1,0:T(8,128)(2,1)S(1)}, bf16[32,3840]{1,0:T(8,128)(2,1)S(1)}, u32[]{:S(2)}, u32[]{:S(2)}) %collective-permute-start) | collective-permute-done | bytes 245792 | tf_op jit(solution)/shard_map/ppermute | solution.py:266
  39.1 6.4 %all-to-all-start.1 = ((bf16[8,32,3840]{2,1,0:T(8,128)(2,1)}), bf16[8,32,3840]{2,1,0:T(8,128)(2,1)}, u32[]{:S(2)}, u32[]{:S(2)}) async-start(bf16[8,32,3840]{2,1,0:T(8,128)(2,1)} %bitcast.3), calls=%async_computation.1 | async-start | bytes 3932160 | tf_op jit(solution)/shard_map/all_to_all | solution.py:231
  45.5 18.7 %collective-permute-start.2 = (bf16[32,3840]{1,0:T(8,128)(2,1)S(1)}, bf16[32,3840]{1,0:T(8,128)(2,1)S(1)}, u32[]{:S(2)}, u32[]{:S(2)}) collective-permute-start(bf16[32,3840]{1,0:T(8,128)(2,1)S(1)} %get-tuple-element.20), channel_id=1, source_target_pairs={{0,256},{16,272},{32,288},{48,304},{64,320},{80,336},{96,352},{112... | collective-permute-start | bytes 737288 | tf_op jit(solution)/shard_map/ppermute | solution.py:266
  64.2 4.7 %collective-permute-done.2.refs_1_ = bf16[32,3840]{1,0:T(8,128)(2,1)S(1)} collective-permute-done((bf16[32,3840]{1,0:T(8,128)(2,1)S(1)}, bf16[32,3840]{1,0:T(8,128)(2,1)S(1)}, u32[]{:S(2)}, u32[]{:S(2)}) %collective-permute-start.2) | collective-permute-done | bytes 245792 | tf_op jit(solution)/shard_map/ppermute | solution.py:266
  70.4 4.1 %all-to-all-done.1 = bf16[8,32,3840]{2,1,0:T(8,128)(2,1)} async-done(((bf16[8,32,3840]{2,1,0:T(8,128)(2,1)}), bf16[8,32,3840]{2,1,0:T(8,128)(2,1)}, u32[]{:S(2)}, u32[]{:S(2)}) %all-to-all-start.1) | async-done | bytes 1966112 | tf_op jit(solution)/shard_map/all_to_all | solution.py:231
  74.5 11.1 %all-to-all-start = ((bf16[8,32,3840]{2,1,0:T(8,128)(2,1)}), bf16[8,32,3840]{2,1,0:T(8,128)(2,1)}, u32[]{:S(2)}, u32[]{:S(2)}) async-start(bf16[8,32,3840]{2,1,0:T(8,128)(2,1)} %bitcast.1), calls=%async_computation | async-start | bytes 3932160 | tf_op jit(solution)/shard_map/all_to_all | solution.py:231
  85.6 4.4 %shard_map.50.terms_ref = f32[8,32,1024]{2,1,0:T(8,128)S(1)} custom-call(bf16[256,3840]{1,0:T(8,128)(2,1)} %bitcast.4.piece_hbm, bf16[3840,1024]{1,0:T(8,128)(2,1)} %copy-done, f32[8,128]{1,0:T(8,128)S(1)} %get-tuple-element.19.refs_3_.refs_2_.refs_0_), custom_call_target="tpu_custom_call" | custom-call | tf_op jit(solution)/shard_map/pallas_call | solution.py:143
  90.0 1.9 %collective-permute-start.3 = (f32[32,1024]{1,0:T(8,128)S(1)}, f32[32,1024]{1,0:T(8,128)S(1)}, u32[]{:S(2)}, u32[]{:S(2)}) collective-permute-start(f32[32,1024]{1,0:T(8,128)S(1)} %get-tuple-element.28), channel_id=1, source_target_pairs={{0,32},{1,481},{2,34},{3,483},{4,36},{5,485},{6,38},{7,487},{8,40}... | collective-permute-start | bytes 393224 | tf_op jit(solution)/shard_map/ppermute | solution.py:174
  92.0 3.9 %collective-permute-start.6 = (f32[32,1024]{1,0:T(8,128)S(1)}, f32[32,1024]{1,0:T(8,128)S(1)}, u32[]{:S(2)}, u32[]{:S(2)}) collective-permute-start(f32[32,1024]{1,0:T(8,128)S(1)} %get-tuple-element.27), channel_id=1, source_target_pairs={{0,32},{1,481},{2,34},{3,483},{4,36},{5,485},{6,38},{7,487},{8,40}... | collective-permute-start | bytes 393224 | tf_op jit(solution)/shard_map/ppermute | solution.py:174
  96.9 4.1 %collective-permute-start.4 = (f32[32,1024]{1,0:T(8,128)S(1)}, f32[32,1024]{1,0:T(8,128)S(1)}, u32[]{:S(2)}, u32[]{:S(2)}) collective-permute-start(f32[32,1024]{1,0:T(8,128)S(1)} %fusion.7.after_ref), channel_id=1, source_target_pairs={{0,480},{1,33},{2,482},{3,35},{4,484},{5,37},{6,486},{7,39},{8,488... | collective-permute-start | bytes 393224 | tf_op jit(solution)/shard_map/ppermute | solution.py:174
  101.1 1.9 %collective-permute-start.7 = (f32[32,1024]{1,0:T(8,128)S(1)}, f32[32,1024]{1,0:T(8,128)S(1)}, u32[]{:S(2)}, u32[]{:S(2)}) collective-permute-start(f32[32,1024]{1,0:T(8,128)S(1)} %shard_map.51), channel_id=1, source_target_pairs={{0,480},{1,33},{2,482},{3,35},{4,484},{5,37},{6,486},{7,39},{8,488... | collective-permute-start | bytes 393224 | tf_op jit(solution)/shard_map/ppermute | solution.py:174
  104.0 2.9 %collective-permute-start.5 = (f32[32,1024]{1,0:T(8,128)S(1)}, f32[32,1024]{1,0:T(8,128)S(1)}, u32[]{:S(2)}, u32[]{:S(2)}) collective-permute-start(f32[32,1024]{1,0:T(8,128)S(1)} %fusion.8.after_ref), channel_id=1, source_target_pairs={{0,32},{1,481},{2,34},{3,483},{4,36},{5,485},{6,38},{7,487},{8,40}... | collective-permute-start | bytes 393224 | tf_op jit(solution)/shard_map/ppermute | solution.py:174
  106.9 2.1 %collective-permute-done.7.arrived_ref = f32[32,1024]{1,0:T(8,128)S(1)} collective-permute-done((f32[32,1024]{1,0:T(8,128)S(1)}, f32[32,1024]{1,0:T(8,128)S(1)}, u32[]{:S(2)}, u32[]{:S(2)}) %collective-permute-start.7) | collective-permute-done | bytes 131104 | tf_op jit(solution)/shard_map/ppermute | solution.py:174
  110.9 4.4 %shard_map.53.terms_ref = f32[8,32,1024]{2,1,0:T(8,128)S(1)} custom-call(bf16[256,3840]{1,0:T(8,128)(2,1)} %bitcast.2.piece_hbm, bf16[3840,1024]{1,0:T(8,128)(2,1)} %copy-done, f32[32,1024]{1,0:T(8,128)S(1)} %fusion.9.refs_0_, f32[32,1024]{1,0:T(8,128)S(1)} %shard_map.52.refs_1_), custom_call_target="tpu_custom_call" | custom-call | tf_op jit(solution)/shard_map/pallas_call | solution.py:143
  115.3 2.9 %collective-permute-start.9 = (f32[32,1024]{1,0:T(8,128)S(1)}, f32[32,1024]{1,0:T(8,128)S(1)}, u32[]{:S(2)}, u32[]{:S(2)}) collective-permute-start(f32[32,1024]{1,0:T(8,128)S(1)} %get-tuple-element.26), channel_id=1, source_target_pairs={{0,32},{1,481},{2,34},{3,483},{4,36},{5,485},{6,38},{7,487},{8,40}... | collective-permute-start | bytes 393224 | tf_op jit(solution)/shard_map/ppermute | solution.py:174
  118.3 2.9 %collective-permute-start.8 = (f32[32,1024]{1,0:T(8,128)S(1)}, f32[32,1024]{1,0:T(8,128)S(1)}, u32[]{:S(2)}, u32[]{:S(2)}) collective-permute-start(f32[32,1024]{1,0:T(8,128)S(1)} %get-tuple-element.25), channel_id=1, source_target_pairs={{0,32},{1,481},{2,34},{3,483},{4,36},{5,485},{6,38},{7,487},{8,40}... | collective-permute-start | bytes 393224 | tf_op jit(solution)/shard_map/ppermute | solution.py:174
  122.2 9.0 %collective-permute-start.11 = (f32[32,1024]{1,0:T(8,128)S(1)}, f32[32,1024]{1,0:T(8,128)S(1)}, u32[]{:S(2)}, u32[]{:S(2)}) collective-permute-start(f32[32,1024]{1,0:T(8,128)S(1)} %fusion.4.after_ref), channel_id=1, source_target_pairs={{0,480},{1,33},{2,482},{3,35},{4,484},{5,37},{6,486},{7,39},{8,488... | collective-permute-start | bytes 393224 | tf_op jit(solution)/shard_map/ppermute | solution.py:174
  131.2 5.2 %collective-permute-start.10 = (f32[32,1024]{1,0:T(8,128)S(1)}, f32[32,1024]{1,0:T(8,128)S(1)}, u32[]{:S(2)}, u32[]{:S(2)}) collective-permute-start(f32[32,1024]{1,0:T(8,128)S(1)} %shard_map.54), channel_id=1, source_target_pairs={{0,480},{1,33},{2,482},{3,35},{4,484},{5,37},{6,486},{7,39},{8,488... | collective-permute-start | bytes 393224 | tf_op jit(solution)/shard_map/ppermute | solution.py:174
  136.5 1.9 %collective-permute-start.13 = (f32[32,1024]{1,0:T(8,128)S(1)}, f32[32,1024]{1,0:T(8,128)S(1)}, u32[]{:S(2)}, u32[]{:S(2)}) collective-permute-start(f32[32,1024]{1,0:T(8,128)S(1)} %fusion.3.after_ref), channel_id=1, source_target_pairs={{0,32},{1,481},{2,34},{3,483},{4,36},{5,485},{6,38},{7,487},{8,40}... | collective-permute-start | bytes 393224 | tf_op jit(solution)/shard_map/ppermute | solution.py:174
  138.4 3.9 %collective-permute-start.15 = (f32[32,1024]{1,0:T(8,128)S(1)}, f32[32,1024]{1,0:T(8,128)S(1)}, u32[]{:S(2)}, u32[]{:S(2)}) collective-permute-start(f32[32,1024]{1,0:T(8,128)S(1)} %shard_map.52.refs_1_), channel_id=1, source_target_pairs={{0,32},{1,481},{2,34},{3,483},{4,36},{5,485},{6,38},{7,487},{8,40}... | collective-permute-start | bytes 393224 | tf_op jit(solution)/shard_map/ppermute | solution.py:174
  142.4 9.4 %collective-permute-start.16 = (f32[32,1024]{1,0:T(8,128)S(1)}, f32[32,1024]{1,0:T(8,128)S(1)}, u32[]{:S(2)}, u32[]{:S(2)}) collective-permute-start(f32[32,1024]{1,0:T(8,128)S(1)} %fusion.9.refs_0_), channel_id=1, source_target_pairs={{0,384},{1,129},{2,386},{3,131},{4,388},{5,133},{6,390},{7,135},{8... | collective-permute-start | bytes 393224 | tf_op jit(solution)/shard_map/ppermute | solution.py:174
  151.8 2.3 %collective-permute-start.12 = (f32[32,1024]{1,0:T(8,128)S(1)}, f32[32,1024]{1,0:T(8,128)S(1)}, u32[]{:S(2)}, u32[]{:S(2)}) collective-permute-start(f32[32,1024]{1,0:T(8,128)S(1)} %shard_map.55), channel_id=1, source_target_pairs={{0,32},{1,481},{2,34},{3,483},{4,36},{5,485},{6,38},{7,487},{8,40}... | collective-permute-start | bytes 393224 | tf_op jit(solution)/shard_map/ppermute | solution.py:174
  154.1 2.8 %collective-permute-start.14 = (f32[32,1024]{1,0:T(8,128)S(1)}, f32[32,1024]{1,0:T(8,128)S(1)}, u32[]{:S(2)}, u32[]{:S(2)}) collective-permute-start(f32[32,1024]{1,0:T(8,128)S(1)} %fusion.2), channel_id=1, source_target_pairs={{0,384},{1,129},{2,386},{3,131},{4,388},{5,133},{6,390},{7,135},{8... | collective-permute-start | bytes 393224 | tf_op jit(solution)/shard_map/ppermute | solution.py:174
  157.0 4.8 %collective-permute-done.12 = f32[32,1024]{1,0:T(8,128)S(1)} collective-permute-done((f32[32,1024]{1,0:T(8,128)S(1)}, f32[32,1024]{1,0:T(8,128)S(1)}, u32[]{:S(2)}, u32[]{:S(2)}) %collective-permute-start.12) | collective-permute-done | bytes 131104 | tf_op jit(solution)/shard_map/ppermute | solution.py:174
  161.8 3.1 %collective-permute-done.14 = f32[32,1024]{1,0:T(8,128)S(1)} collective-permute-done((f32[32,1024]{1,0:T(8,128)S(1)}, f32[32,1024]{1,0:T(8,128)S(1)}, u32[]{:S(2)}, u32[]{:S(2)}) %collective-permute-start.14) | collective-permute-done | bytes 131104 | tf_op jit(solution)/shard_map/ppermute | solution.py:174
  167.6 10.5 %collective-permute-start.18 = (f32[32,512]{1,0:T(8,128)S(1)}, f32[32,512]{1,0:T(8,128)S(1)}, u32[]{:S(2)}, u32[]{:S(2)}) collective-permute-start(f32[32,512]{1,0:T(8,128)S(1)} %get-tuple-element.29), channel_id=1, source_target_pairs={{0,1},{1,33},{2,3},{3,35},{4,5},{5,37},{6,7},{7,39},{8,9},{9,41},{... | collective-permute-start | bytes 196616 | tf_op jit(solution)/shard_map/ppermute | solution.py:174
  178.1 3.3 %collective-permute-start.20 = (f32[32,512]{1,0:T(8,128)S(1)}, f32[32,512]{1,0:T(8,128)S(1)}, u32[]{:S(2)}, u32[]{:S(2)}) collective-permute-start(f32[32,512]{1,0:T(8,128)S(1)} %get-tuple-element.30), channel_id=1, source_target_pairs={{0,16},{1,32},{2,18},{3,34},{4,20},{5,36},{6,22},{7,38},{8,24},{9,... | collective-permute-start | bytes 196616 | tf_op jit(solution)/shard_map/ppermute | solution.py:174
  181.4 4.3 %collective-permute-done.20 = f32[32,512]{1,0:T(8,128)S(1)} collective-permute-done((f32[32,512]{1,0:T(8,128)S(1)}, f32[32,512]{1,0:T(8,128)S(1)}, u32[]{:S(2)}, u32[]{:S(2)}) %collective-permute-start.20) | collective-permute-done | bytes 65568 | tf_op jit(solution)/shard_map/ppermute | solution.py:174
  (44 shorter events, 16.4 us)
Async XLA Ops:
  0.0 24.0 %collective-permute-start.1 = (bf16[3840,256]{1,0:T(8,128)(2,1)}, bf16[3840,256]{1,0:T(8,128)(2,1)S(1)}, u32[]{:S(2)}, u32[]{:S(2)}) collective-permute-start(bf16[3840,256]{1,0:T(8,128)(2,1)} %own_ref.1), channel_id=1, source_target_pairs={{0,1},{1,0},{2,3},{3,2},{4,5},{5,4},{6,7},{7,6},{8,9},{9,8},{10,11... | collective-permute-start | bytes 5898248 | tf_op jit(solution)/shard_map/ppermute | solution.py:164
  2.7 1.0 copy-start.2
  9.4 28.2 %collective-permute-start = (bf16[32,3840]{1,0:T(8,128)(2,1)S(1)}, bf16[32,3840]{1,0:T(8,128)(2,1)S(1)}, u32[]{:S(2)}, u32[]{:S(2)}) collective-permute-start(bf16[32,3840]{1,0:T(8,128)(2,1)S(1)} %get-tuple-element.16), channel_id=1, source_target_pairs={{0,256},{16,272},{32,288},{48,304},{64,320},{80,336},{96,352},{112... | collective-permute-start | bytes 737288 | tf_op jit(solution)/shard_map/ppermute | solution.py:266
  24.0 1.5 copy-start.1
  29.1 3.1 %copy-start = (bf16[3840,1024]{1,0:T(8,128)(2,1)}, bf16[3840,1024]{1,0:T(8,128)(2,1)S(1)}, u32[]{:S(2)}) copy-start(bf16[3840,1024]{1,0:T(8,128)(2,1)S(1)} %get-tuple-element.21.s_hbm) | copy-start | bytes 23592964
  39.1 35.4 %all-to-all-start.1 = ((bf16[8,32,3840]{2,1,0:T(8,128)(2,1)}), bf16[8,32,3840]{2,1,0:T(8,128)(2,1)}, u32[]{:S(2)}, u32[]{:S(2)}) async-start(bf16[8,32,3840]{2,1,0:T(8,128)(2,1)} %bitcast.3), calls=%async_computation.1 | async-start | bytes 3932160 | tf_op jit(solution)/shard_map/all_to_all | solution.py:231
  45.5 23.4 %collective-permute-start.2 = (bf16[32,3840]{1,0:T(8,128)(2,1)S(1)}, bf16[32,3840]{1,0:T(8,128)(2,1)S(1)}, u32[]{:S(2)}, u32[]{:S(2)}) collective-permute-start(bf16[32,3840]{1,0:T(8,128)(2,1)S(1)} %get-tuple-element.20), channel_id=1, source_target_pairs={{0,256},{16,272},{32,288},{48,304},{64,320},{80,336},{96,352},{112... | collective-permute-start | bytes 737288 | tf_op jit(solution)/shard_map/ppermute | solution.py:266
  74.5 36.4 %all-to-all-start = ((bf16[8,32,3840]{2,1,0:T(8,128)(2,1)}), bf16[8,32,3840]{2,1,0:T(8,128)(2,1)}, u32[]{:S(2)}, u32[]{:S(2)}) async-start(bf16[8,32,3840]{2,1,0:T(8,128)(2,1)} %bitcast.1), calls=%async_computation | async-start | bytes 3932160 | tf_op jit(solution)/shard_map/all_to_all | solution.py:231
  90.0 6.9 %collective-permute-start.3 = (f32[32,1024]{1,0:T(8,128)S(1)}, f32[32,1024]{1,0:T(8,128)S(1)}, u32[]{:S(2)}, u32[]{:S(2)}) collective-permute-start(f32[32,1024]{1,0:T(8,128)S(1)} %get-tuple-element.28), channel_id=1, source_target_pairs={{0,32},{1,481},{2,34},{3,483},{4,36},{5,485},{6,38},{7,487},{8,40}... | collective-permute-start | bytes 393224 | tf_op jit(solution)/shard_map/ppermute | solution.py:174
  92.0 9.1 %collective-permute-start.6 = (f32[32,1024]{1,0:T(8,128)S(1)}, f32[32,1024]{1,0:T(8,128)S(1)}, u32[]{:S(2)}, u32[]{:S(2)}) collective-permute-start(f32[32,1024]{1,0:T(8,128)S(1)} %get-tuple-element.27), channel_id=1, source_target_pairs={{0,32},{1,481},{2,34},{3,483},{4,36},{5,485},{6,38},{7,487},{8,40}... | collective-permute-start | bytes 393224 | tf_op jit(solution)/shard_map/ppermute | solution.py:174
  96.9 7.0 %collective-permute-start.4 = (f32[32,1024]{1,0:T(8,128)S(1)}, f32[32,1024]{1,0:T(8,128)S(1)}, u32[]{:S(2)}, u32[]{:S(2)}) collective-permute-start(f32[32,1024]{1,0:T(8,128)S(1)} %fusion.7.after_ref), channel_id=1, source_target_pairs={{0,480},{1,33},{2,482},{3,35},{4,484},{5,37},{6,486},{7,39},{8,488... | collective-permute-start | bytes 393224 | tf_op jit(solution)/shard_map/ppermute | solution.py:174
  101.1 7.9 %collective-permute-start.7 = (f32[32,1024]{1,0:T(8,128)S(1)}, f32[32,1024]{1,0:T(8,128)S(1)}, u32[]{:S(2)}, u32[]{:S(2)}) collective-permute-start(f32[32,1024]{1,0:T(8,128)S(1)} %shard_map.51), channel_id=1, source_target_pairs={{0,480},{1,33},{2,482},{3,35},{4,484},{5,37},{6,486},{7,39},{8,488... | collective-permute-start | bytes 393224 | tf_op jit(solution)/shard_map/ppermute | solution.py:174
  104.0 6.9 %collective-permute-start.5 = (f32[32,1024]{1,0:T(8,128)S(1)}, f32[32,1024]{1,0:T(8,128)S(1)}, u32[]{:S(2)}, u32[]{:S(2)}) collective-permute-start(f32[32,1024]{1,0:T(8,128)S(1)} %fusion.8.after_ref), channel_id=1, source_target_pairs={{0,32},{1,481},{2,34},{3,483},{4,36},{5,485},{6,38},{7,487},{8,40}... | collective-permute-start | bytes 393224 | tf_op jit(solution)/shard_map/ppermute | solution.py:174
  115.3 6.9 %collective-permute-start.9 = (f32[32,1024]{1,0:T(8,128)S(1)}, f32[32,1024]{1,0:T(8,128)S(1)}, u32[]{:S(2)}, u32[]{:S(2)}) collective-permute-start(f32[32,1024]{1,0:T(8,128)S(1)} %get-tuple-element.26), channel_id=1, source_target_pairs={{0,32},{1,481},{2,34},{3,483},{4,36},{5,485},{6,38},{7,487},{8,40}... | collective-permute-start | bytes 393224 | tf_op jit(solution)/shard_map/ppermute | solution.py:174
  118.3 12.9 %collective-permute-start.8 = (f32[32,1024]{1,0:T(8,128)S(1)}, f32[32,1024]{1,0:T(8,128)S(1)}, u32[]{:S(2)}, u32[]{:S(2)}) collective-permute-start(f32[32,1024]{1,0:T(8,128)S(1)} %get-tuple-element.25), channel_id=1, source_target_pairs={{0,32},{1,481},{2,34},{3,483},{4,36},{5,485},{6,38},{7,487},{8,40}... | collective-permute-start | bytes 393224 | tf_op jit(solution)/shard_map/ppermute | solution.py:174
  122.2 14.2 %collective-permute-start.11 = (f32[32,1024]{1,0:T(8,128)S(1)}, f32[32,1024]{1,0:T(8,128)S(1)}, u32[]{:S(2)}, u32[]{:S(2)}) collective-permute-start(f32[32,1024]{1,0:T(8,128)S(1)} %fusion.4.after_ref), channel_id=1, source_target_pairs={{0,480},{1,33},{2,482},{3,35},{4,484},{5,37},{6,486},{7,39},{8,488... | collective-permute-start | bytes 393224 | tf_op jit(solution)/shard_map/ppermute | solution.py:174
  131.2 20.6 %collective-permute-start.10 = (f32[32,1024]{1,0:T(8,128)S(1)}, f32[32,1024]{1,0:T(8,128)S(1)}, u32[]{:S(2)}, u32[]{:S(2)}) collective-permute-start(f32[32,1024]{1,0:T(8,128)S(1)} %shard_map.54), channel_id=1, source_target_pairs={{0,480},{1,33},{2,482},{3,35},{4,484},{5,37},{6,486},{7,39},{8,488... | collective-permute-start | bytes 393224 | tf_op jit(solution)/shard_map/ppermute | solution.py:174
  136.5 17.6 %collective-permute-start.13 = (f32[32,1024]{1,0:T(8,128)S(1)}, f32[32,1024]{1,0:T(8,128)S(1)}, u32[]{:S(2)}, u32[]{:S(2)}) collective-permute-start(f32[32,1024]{1,0:T(8,128)S(1)} %fusion.3.after_ref), channel_id=1, source_target_pairs={{0,32},{1,481},{2,34},{3,483},{4,36},{5,485},{6,38},{7,487},{8,40}... | collective-permute-start | bytes 393224 | tf_op jit(solution)/shard_map/ppermute | solution.py:174
  138.4 18.5 %collective-permute-start.15 = (f32[32,1024]{1,0:T(8,128)S(1)}, f32[32,1024]{1,0:T(8,128)S(1)}, u32[]{:S(2)}, u32[]{:S(2)}) collective-permute-start(f32[32,1024]{1,0:T(8,128)S(1)} %shard_map.52.refs_1_), channel_id=1, source_target_pairs={{0,32},{1,481},{2,34},{3,483},{4,36},{5,485},{6,38},{7,487},{8,40}... | collective-permute-start | bytes 393224 | tf_op jit(solution)/shard_map/ppermute | solution.py:174
  142.4 14.6 %collective-permute-start.16 = (f32[32,1024]{1,0:T(8,128)S(1)}, f32[32,1024]{1,0:T(8,128)S(1)}, u32[]{:S(2)}, u32[]{:S(2)}) collective-permute-start(f32[32,1024]{1,0:T(8,128)S(1)} %fusion.9.refs_0_), channel_id=1, source_target_pairs={{0,384},{1,129},{2,386},{3,131},{4,388},{5,133},{6,390},{7,135},{8... | collective-permute-start | bytes 393224 | tf_op jit(solution)/shard_map/ppermute | solution.py:174
  151.8 10.0 %collective-permute-start.12 = (f32[32,1024]{1,0:T(8,128)S(1)}, f32[32,1024]{1,0:T(8,128)S(1)}, u32[]{:S(2)}, u32[]{:S(2)}) collective-permute-start(f32[32,1024]{1,0:T(8,128)S(1)} %shard_map.55), channel_id=1, source_target_pairs={{0,32},{1,481},{2,34},{3,483},{4,36},{5,485},{6,38},{7,487},{8,40}... | collective-permute-start | bytes 393224 | tf_op jit(solution)/shard_map/ppermute | solution.py:174
  154.1 10.8 %collective-permute-start.14 = (f32[32,1024]{1,0:T(8,128)S(1)}, f32[32,1024]{1,0:T(8,128)S(1)}, u32[]{:S(2)}, u32[]{:S(2)}) collective-permute-start(f32[32,1024]{1,0:T(8,128)S(1)} %fusion.2), channel_id=1, source_target_pairs={{0,384},{1,129},{2,386},{3,131},{4,388},{5,133},{6,390},{7,135},{8... | collective-permute-start | bytes 393224 | tf_op jit(solution)/shard_map/ppermute | solution.py:174
  165.0 16.4 %collective-permute-start.19 = (f32[32,512]{1,0:T(8,128)S(1)}, f32[32,512]{1,0:T(8,128)S(1)}, u32[]{:S(2)}, u32[]{:S(2)}) collective-permute-start(f32[32,512]{1,0:T(8,128)S(1)} %get-tuple-element.23), channel_id=1, source_target_pairs={{0,17},{1,49},{2,19},{3,51},{4,21},{5,53},{6,23},{7,55},{8,25},{9,... | collective-permute-start | bytes 196616 | tf_op jit(solution)/shard_map/ppermute | solution.py:174
  166.9 14.5 %collective-permute-start.17 = (f32[32,512]{1,0:T(8,128)S(1)}, f32[32,512]{1,0:T(8,128)S(1)}, u32[]{:S(2)}, u32[]{:S(2)}) collective-permute-start(f32[32,512]{1,0:T(8,128)S(1)} %get-tuple-element.24), channel_id=1, source_target_pairs={{1,48},{3,50},{5,52},{7,54},{9,56},{11,58},{13,60},{15,62},{17,32}... | collective-permute-start | bytes 196616 | tf_op jit(solution)/shard_map/ppermute | solution.py:174
  167.6 13.8 %collective-permute-start.18 = (f32[32,512]{1,0:T(8,128)S(1)}, f32[32,512]{1,0:T(8,128)S(1)}, u32[]{:S(2)}, u32[]{:S(2)}) collective-permute-start(f32[32,512]{1,0:T(8,128)S(1)} %get-tuple-element.29), channel_id=1, source_target_pairs={{0,1},{1,33},{2,3},{3,35},{4,5},{5,37},{6,7},{7,39},{8,9},{9,41},{... | collective-permute-start | bytes 196616 | tf_op jit(solution)/shard_map/ppermute | solution.py:174
  178.1 7.7 %collective-permute-start.20 = (f32[32,512]{1,0:T(8,128)S(1)}, f32[32,512]{1,0:T(8,128)S(1)}, u32[]{:S(2)}, u32[]{:S(2)}) collective-permute-start(f32[32,512]{1,0:T(8,128)S(1)} %get-tuple-element.30), channel_id=1, source_target_pairs={{0,16},{1,32},{2,18},{3,34},{4,20},{5,36},{6,22},{7,38},{8,24},{9,... | collective-permute-start | bytes 196616 | tf_op jit(solution)/shard_map/ppermute | solution.py:174

commit v13 on v12

--- a/solution.py
+++ b/solution.py
@@ -211,19 +211,19 @@
     )(*arrays, after)
 
 
-def add_term_kernel(slot, terms_ref, arrived_ref, after_ref, out_ref):
-    out_ref[...] = terms_ref[slot] + arrived_ref[...]
-
-
-def add_term(terms, slot, arrived, after):
+def add_term_kernel(slot, terms_ref, arrived_ref, *refs):
+    refs[-1][...] = terms_ref[slot] + arrived_ref[...]
+
+
+def add_term(terms, slot, arrived, *after):
     whole = pl.BlockSpec(memory_space=pltpu.VMEM)
     return pl.pallas_call(
         functools.partial(add_term_kernel, slot),
         out_shape=jax.ShapeDtypeStruct(arrived.shape, arrived.dtype),
-        in_specs=[whole, whole, pl.BlockSpec(memory_space=pl.ANY)],
+        in_specs=[whole, whole] + [pl.BlockSpec(memory_space=pl.ANY)] * len(after),
         out_specs=whole,
         compiler_params=pltpu.CompilerParams(vmem_limit_bytes=4 * 2**20),
-    )(terms, arrived, after)
+    )(terms, arrived, *after)
 
 
 def gather_col(copies):
@@ -231,17 +231,16 @@
     return lax.all_to_all(copies, "col", 0, 0, axis_index_groups=groups, tiled=True)
 
 
-def sum_near(terms):
+def sum_near(terms, before):
     outer, inner = terms[0], terms[4]
     for step in range(1, 4):
         outer = terms[step] + slice_move(outer, functools.partial(exchange, step))
         inner = slice_move(inner, functools.partial(exchange, step))
         if step < 3:
-            inner = near = add_term(terms, 4 + step, inner, outer)
-        else:
-            inner = terms[7] + inner
-    inner += slice_move(outer, lambda z, y_hi, c: (z + 4 if (c - z) % 2 else z - 4, y_hi, c))
-    return inner, [outer, near]
+            inner = add_term(terms, 4 + step, inner, outer, *(before if step == 1 else []))
+    inner = add_term(terms, 7, inner)
+    skipped = slice_move(outer, lambda z, y_hi, c: (z + 4 if (c - z) % 2 else z - 4, y_hi, c))
+    return inner, skipped, outer
 
 
 def per_device(window_rows, secular, source, kept_count):
@@ -270,10 +269,11 @@
         pieces.append(gather_col(here))
 
     s_both = pltpu.with_memory_space_constraint(s_both, pltpu.HBM)
-    sums, after = [], [masked]
+    sums, after, before = [], [masked], []
     for piece in pieces:
-        total, after = sum_near(product(piece, s_both, after))
-        sums.append(total)
+        inner, skipped, outer = sum_near(product(piece, s_both, after), before)
+        sums.append(inner + skipped)
+        after, before = [outer, inner], [skipped]
     inner = jnp.concatenate(sums, axis=0)
 
     half_cols = inner.shape[1] // 2

time: 187 us -> 190 us (1.016)
  the two profiles are of different devices: /device:TPU:64 before, /device:TPU:6 now
where the time goes in v13:
time: 190 us; the launch traced here: 189 us
  starting transfers between devices  123 us (65%)
  waiting for transfers between devices  36.5 us (19%)
  Pallas kernels  21 us (11%)
  local copies, waits for them, and re-layouts  6.28 us (3%)
    ppermute x18, starting transfers between devices, slice_move(): return lax.ppermute(value, ('grp', 'col'), pairs)  74.4 us
    ppermute x2, starting transfers between devices, per_device(): arrived = lax.ppermute(leaving, 'grp', [(i, i ^ 16) for i in range(32)])  28.2 us
    ppermute x18, waiting for transfers between devices, slice_move(): return lax.ppermute(value, ('grp', 'col'), pairs)  24.7 us
    all_to_all x2, starting transfers between devices, gather_col(): lax.all_to_all(copies, 'col', 0, 0, axis_index_groups=groups, tiled=True)  18.9 us
    pallas_call x2, Pallas kernels, product(): pl.pallas_call(product_kernel, out_shape=jax.ShapeDtypeStruct((PEERS, row...  8.87 us
    all_to_all x2, waiting for transfers between devices, gather_col(): lax.all_to_all(copies, 'col', 0, 0, axis_index_groups=groups, tiled=True)  5.99 us
    ppermute x2, waiting for transfers between devices, per_device(): arrived = lax.ppermute(leaving, 'grp', [(i, i ^ 16) for i in range(32)])  5.8 us
    pallas_call x1, Pallas kernels, scatter_rows(): pl.pallas_call(scatter_kernel, out_shape=[jax.ShapeDtypeStruct((rows, blk...  5.76 us
  transfers between devices with their start and end apart: 23, of which 12 were waited for; matrix products, arithmetic and copies ran while one was open for 0% of the time, Pallas kernels for 8%

profile of v13, /device:TPU:6, one launch (start us, length us, event | category | flops | bytes accessed | tf_op | source)
XLA Modules:
  0.0 189.2 jit_solution(11405351070041748164)
XLA Ops:
  3.7 5.8 %shard_map.46 = (bf16[32,3840]{1,0:T(8,128)(2,1)S(1)}, bf16[32,3840]{1,0:T(8,128)(2,1)S(1)}, bf16[32,3840]{1,0:T(8,128)(2,1)S(1)}, bf16[32,3840]{1,0:T(8,128)(2,1)S(1)}, bf16[3840,128]{1,0:T(8,128)(2,1)S(1)}) custom-call(s32[3840]{0:T(1024)S(1)} %subtract_select_fusion.place_ref, bf16[64,3840]{1,0:T(8,128)(2,1)S(1)} %bitcast.44), custom_call_target="tpu_custom_call" | custom-call | tf_op jit(solution)/shard_map/pallas_call | solution.py:47
  9.4 15.7 %collective-permute-start = (bf16[32,3840]{1,0:T(8,128)(2,1)S(1)}, bf16[32,3840]{1,0:T(8,128)(2,1)S(1)}, u32[]{:S(2)}, u32[]{:S(2)}) collective-permute-start(bf16[32,3840]{1,0:T(8,128)(2,1)S(1)} %get-tuple-element.16), channel_id=1, source_target_pairs={{0,256},{16,272},{32,288},{48,304},{64,320},{80,336},{96,352},{112... | collective-permute-start | bytes 737288 | tf_op jit(solution)/shard_map/ppermute | solution.py:265
  27.4 3.5 %shard_map.47 = (bf16[3840,1024]{1,0:T(8,128)(2,1)S(1)}, f32[8,128]{1,0:T(8,128)S(1)}) custom-call(s32[1]{0:T(128)S(6)} %copy.9.kept_ref, bf16[3840,128]{1,0:T(8,128)(2,1)S(1)} %get-tuple-element.18.flag_ref, bf16[3840,256]{1,0:T(8,128)(2,1)S(1)} %copy-done.1, bf16[3840,256]{1,0:T(8,128)(2,1)S(1)} %collective-permute-done.1.other_ref), custom_call_target="tpu_custom_call" | custom-call | tf_op jit(solution)/shard_map/pallas_call | solution.py:83
  30.9 3.0 %copy-done = bf16[3840,1024]{1,0:T(8,128)(2,1)} copy-done((bf16[3840,1024]{1,0:T(8,128)(2,1)}, bf16[3840,1024]{1,0:T(8,128)(2,1)S(1)}, u32[]{:S(2)}) %copy-start) | copy-done | bytes 7864344
  35.3 11.0 %all-to-all-start.1 = ((bf16[8,32,3840]{2,1,0:T(8,128)(2,1)}), bf16[8,32,3840]{2,1,0:T(8,128)(2,1)}, u32[]{:S(2)}, u32[]{:S(2)}) async-start(bf16[8,32,3840]{2,1,0:T(8,128)(2,1)} %bitcast.3), calls=%async_computation.1 | async-start | bytes 3932160 | tf_op jit(solution)/shard_map/all_to_all | solution.py:231
  46.4 12.4 %collective-permute-start.2 = (bf16[32,3840]{1,0:T(8,128)(2,1)S(1)}, bf16[32,3840]{1,0:T(8,128)(2,1)S(1)}, u32[]{:S(2)}, u32[]{:S(2)}) collective-permute-start(bf16[32,3840]{1,0:T(8,128)(2,1)S(1)} %get-tuple-element.20), channel_id=1, source_target_pairs={{0,256},{16,272},{32,288},{48,304},{64,320},{80,336},{96,352},{112... | collective-permute-start | bytes 737288 | tf_op jit(solution)/shard_map/ppermute | solution.py:265
  58.8 5.8 %collective-permute-done.2.refs_1_ = bf16[32,3840]{1,0:T(8,128)(2,1)S(1)} collective-permute-done((bf16[32,3840]{1,0:T(8,128)(2,1)S(1)}, bf16[32,3840]{1,0:T(8,128)(2,1)S(1)}, u32[]{:S(2)}, u32[]{:S(2)}) %collective-permute-start.2) | collective-permute-done | bytes 245792 | tf_op jit(solution)/shard_map/ppermute | solution.py:265
  66.0 6.0 %all-to-all-done.1 = bf16[8,32,3840]{2,1,0:T(8,128)(2,1)} async-done(((bf16[8,32,3840]{2,1,0:T(8,128)(2,1)}), bf16[8,32,3840]{2,1,0:T(8,128)(2,1)}, u32[]{:S(2)}, u32[]{:S(2)}) %all-to-all-start.1) | async-done | bytes 1966112 | tf_op jit(solution)/shard_map/all_to_all | solution.py:231
  72.0 7.8 %all-to-all-start = ((bf16[8,32,3840]{2,1,0:T(8,128)(2,1)}), bf16[8,32,3840]{2,1,0:T(8,128)(2,1)}, u32[]{:S(2)}, u32[]{:S(2)}) async-start(bf16[8,32,3840]{2,1,0:T(8,128)(2,1)} %bitcast.1), calls=%async_computation | async-start | bytes 3932160 | tf_op jit(solution)/shard_map/all_to_all | solution.py:231
  79.9 4.4 %shard_map.50.terms_ref = f32[8,32,1024]{2,1,0:T(8,128)S(1)} custom-call(bf16[256,3840]{1,0:T(8,128)(2,1)} %bitcast.4.piece_hbm, bf16[3840,1024]{1,0:T(8,128)(2,1)} %copy-done, f32[8,128]{1,0:T(8,128)S(1)} %get-tuple-element.19.refs_3_.refs_2_.refs_0_), custom_call_target="tpu_custom_call" | custom-call | tf_op jit(solution)/shard_map/pallas_call | solution.py:143
  84.3 12.1 %collective-permute-start.3 = (f32[32,1024]{1,0:T(8,128)S(1)}, f32[32,1024]{1,0:T(8,128)S(1)}, u32[]{:S(2)}, u32[]{:S(2)}) collective-permute-start(f32[32,1024]{1,0:T(8,128)S(1)} %get-tuple-element.27), channel_id=1, source_target_pairs={{0,32},{1,481},{2,34},{3,483},{4,36},{5,485},{6,38},{7,487},{8,40}... | collective-permute-start | bytes 393224 | tf_op jit(solution)/shard_map/ppermute | solution.py:174
  96.4 1.9 %collective-permute-start.6 = (f32[32,1024]{1,0:T(8,128)S(1)}, f32[32,1024]{1,0:T(8,128)S(1)}, u32[]{:S(2)}, u32[]{:S(2)}) collective-permute-start(f32[32,1024]{1,0:T(8,128)S(1)} %get-tuple-element.28), channel_id=1, source_target_pairs={{0,32},{1,481},{2,34},{3,483},{4,36},{5,485},{6,38},{7,487},{8,40}... | collective-permute-start | bytes 393224 | tf_op jit(solution)/shard_map/ppermute | solution.py:174
  99.4 9.8 %collective-permute-start.4 = (f32[32,1024]{1,0:T(8,128)S(1)}, f32[32,1024]{1,0:T(8,128)S(1)}, u32[]{:S(2)}, u32[]{:S(2)}) collective-permute-start(f32[32,1024]{1,0:T(8,128)S(1)} %fusion.3.refs_0_), channel_id=1, source_target_pairs={{0,480},{1,33},{2,482},{3,35},{4,484},{5,37},{6,486},{7,39},{8,488... | collective-permute-start | bytes 393224 | tf_op jit(solution)/shard_map/ppermute | solution.py:174
  109.3 4.3 %collective-permute-start.7 = (f32[32,1024]{1,0:T(8,128)S(1)}, f32[32,1024]{1,0:T(8,128)S(1)}, u32[]{:S(2)}, u32[]{:S(2)}) collective-permute-start(f32[32,1024]{1,0:T(8,128)S(1)} %shard_map.51), channel_id=1, source_target_pairs={{0,480},{1,33},{2,482},{3,35},{4,484},{5,37},{6,486},{7,39},{8,488... | collective-permute-start | bytes 393224 | tf_op jit(solution)/shard_map/ppermute | solution.py:174
  113.6 3.7 %collective-permute-done.7.arrived_ref = f32[32,1024]{1,0:T(8,128)S(1)} collective-permute-done((f32[32,1024]{1,0:T(8,128)S(1)}, f32[32,1024]{1,0:T(8,128)S(1)}, u32[]{:S(2)}, u32[]{:S(2)}) %collective-permute-start.7) | collective-permute-done | bytes 131104 | tf_op jit(solution)/shard_map/ppermute | solution.py:174
  117.4 1.9 %collective-permute-start.8 = (f32[32,1024]{1,0:T(8,128)S(1)}, f32[32,1024]{1,0:T(8,128)S(1)}, u32[]{:S(2)}, u32[]{:S(2)}) collective-permute-start(f32[32,1024]{1,0:T(8,128)S(1)} %shard_map.52), channel_id=1, source_target_pairs={{0,32},{1,481},{2,34},{3,483},{4,36},{5,485},{6,38},{7,487},{8,40}... | collective-permute-start | bytes 393224 | tf_op jit(solution)/shard_map/ppermute | solution.py:174
  119.3 3.9 %collective-permute-start.5 = (f32[32,1024]{1,0:T(8,128)S(1)}, f32[32,1024]{1,0:T(8,128)S(1)}, u32[]{:S(2)}, u32[]{:S(2)}) collective-permute-start(f32[32,1024]{1,0:T(8,128)S(1)} %fusion.4.refs_0_), channel_id=1, source_target_pairs={{0,32},{1,481},{2,34},{3,483},{4,36},{5,485},{6,38},{7,487},{8,40}... | collective-permute-start | bytes 393224 | tf_op jit(solution)/shard_map/ppermute | solution.py:174
  126.2 4.4 %shard_map.54.terms_ref = f32[8,32,1024]{2,1,0:T(8,128)S(1)} custom-call(bf16[256,3840]{1,0:T(8,128)(2,1)} %bitcast.2.piece_hbm, bf16[3840,1024]{1,0:T(8,128)(2,1)} %copy-done, f32[32,1024]{1,0:T(8,128)S(1)} %fusion.5.refs_0_, f32[32,1024]{1,0:T(8,128)S(1)} %shard_map.53.refs_1_), custom_call_target="tpu_custom_call" | custom-call | tf_op jit(solution)/shard_map/pallas_call | solution.py:143
  130.7 3.9 %collective-permute-start.10 = (f32[32,1024]{1,0:T(8,128)S(1)}, f32[32,1024]{1,0:T(8,128)S(1)}, u32[]{:S(2)}, u32[]{:S(2)}) collective-permute-start(f32[32,1024]{1,0:T(8,128)S(1)} %get-tuple-element.25), channel_id=1, source_target_pairs={{0,32},{1,481},{2,34},{3,483},{4,36},{5,485},{6,38},{7,487},{8,40}... | collective-permute-start | bytes 393224 | tf_op jit(solution)/shard_map/ppermute | solution.py:174
  134.6 3.2 %collective-permute-start.11 = (f32[32,1024]{1,0:T(8,128)S(1)}, f32[32,1024]{1,0:T(8,128)S(1)}, u32[]{:S(2)}, u32[]{:S(2)}) collective-permute-start(f32[32,1024]{1,0:T(8,128)S(1)} %fusion.5.refs_0_), channel_id=1, source_target_pairs={{0,384},{1,129},{2,386},{3,131},{4,388},{5,133},{6,390},{7,135},{8... | collective-permute-start | bytes 393224 | tf_op jit(solution)/shard_map/ppermute | solution.py:174
  137.8 1.9 %collective-permute-start.9 = (f32[32,1024]{1,0:T(8,128)S(1)}, f32[32,1024]{1,0:T(8,128)S(1)}, u32[]{:S(2)}, u32[]{:S(2)}) collective-permute-start(f32[32,1024]{1,0:T(8,128)S(1)} %get-tuple-element.26), channel_id=1, source_target_pairs={{0,32},{1,481},{2,34},{3,483},{4,36},{5,485},{6,38},{7,487},{8,40}... | collective-permute-start | bytes 393224 | tf_op jit(solution)/shard_map/ppermute | solution.py:174
  139.7 5.0 %collective-permute-start.13 = (f32[32,1024]{1,0:T(8,128)S(1)}, f32[32,1024]{1,0:T(8,128)S(1)}, u32[]{:S(2)}, u32[]{:S(2)}) collective-permute-start(f32[32,1024]{1,0:T(8,128)S(1)} %fusion.2.refs_0_), channel_id=1, source_target_pairs={{0,480},{1,33},{2,482},{3,35},{4,484},{5,37},{6,486},{7,39},{8,488... | collective-permute-start | bytes 393224 | tf_op jit(solution)/shard_map/ppermute | solution.py:174
  144.7 3.1 %collective-permute-done.9.arrived_ref = f32[32,1024]{1,0:T(8,128)S(1)} collective-permute-done((f32[32,1024]{1,0:T(8,128)S(1)}, f32[32,1024]{1,0:T(8,128)S(1)}, u32[]{:S(2)}, u32[]{:S(2)}) %collective-permute-start.9) | collective-permute-done | bytes 131104 | tf_op jit(solution)/shard_map/ppermute | solution.py:174
  147.9 3.1 %collective-permute-start.12 = (f32[32,1024]{1,0:T(8,128)S(1)}, f32[32,1024]{1,0:T(8,128)S(1)}, u32[]{:S(2)}, u32[]{:S(2)}) collective-permute-start(f32[32,1024]{1,0:T(8,128)S(1)} %shard_map.55), channel_id=1, source_target_pairs={{0,480},{1,33},{2,482},{3,35},{4,484},{5,37},{6,486},{7,39},{8,488... | collective-permute-start | bytes 393224 | tf_op jit(solution)/shard_map/ppermute | solution.py:174
  151.1 1.9 %collective-permute-start.15 = (f32[32,1024]{1,0:T(8,128)S(1)}, f32[32,1024]{1,0:T(8,128)S(1)}, u32[]{:S(2)}, u32[]{:S(2)}) collective-permute-start(f32[32,1024]{1,0:T(8,128)S(1)} %fusion.1.refs_0_), channel_id=1, source_target_pairs={{0,32},{1,481},{2,34},{3,483},{4,36},{5,485},{6,38},{7,487},{8,40}... | collective-permute-start | bytes 393224 | tf_op jit(solution)/shard_map/ppermute | solution.py:174
  153.0 3.4 %collective-permute-done.12.arrived_ref = f32[32,1024]{1,0:T(8,128)S(1)} collective-permute-done((f32[32,1024]{1,0:T(8,128)S(1)}, f32[32,1024]{1,0:T(8,128)S(1)}, u32[]{:S(2)}, u32[]{:S(2)}) %collective-permute-start.12) | collective-permute-done | bytes 131104 | tf_op jit(solution)/shard_map/ppermute | solution.py:174
  158.4 5.5 %collective-permute-start.16 = (f32[32,1024]{1,0:T(8,128)S(1)}, f32[32,1024]{1,0:T(8,128)S(1)}, u32[]{:S(2)}, u32[]{:S(2)}) collective-permute-start(f32[32,1024]{1,0:T(8,128)S(1)} %fusion), channel_id=1, source_target_pairs={{0,384},{1,129},{2,386},{3,131},{4,388},{5,133},{6,390},{7,135},{8... | collective-permute-start | bytes 393224 | tf_op jit(solution)/shard_map/ppermute | solution.py:174
  164.3 5.9 %collective-permute-done.16 = f32[32,1024]{1,0:T(8,128)S(1)} collective-permute-done((f32[32,1024]{1,0:T(8,128)S(1)}, f32[32,1024]{1,0:T(8,128)S(1)}, u32[]{:S(2)}, u32[]{:S(2)}) %collective-permute-start.16) | collective-permute-done | bytes 131104 | tf_op jit(solution)/shard_map/ppermute | solution.py:174
  171.0 6.2 %collective-permute-start.18 = (f32[32,512]{1,0:T(8,128)S(1)}, f32[32,512]{1,0:T(8,128)S(1)}, u32[]{:S(2)}, u32[]{:S(2)}) collective-permute-start(f32[32,512]{1,0:T(8,128)S(1)} %get-tuple-element.29), channel_id=1, source_target_pairs={{0,1},{1,33},{2,3},{3,35},{4,5},{5,37},{6,7},{7,39},{8,9},{9,41},{... | collective-permute-start | bytes 196616 | tf_op jit(solution)/shard_map/ppermute | solution.py:174
  177.2 3.7 %collective-permute-start.19 = (f32[32,512]{1,0:T(8,128)S(1)}, f32[32,512]{1,0:T(8,128)S(1)}, u32[]{:S(2)}, u32[]{:S(2)}) collective-permute-start(f32[32,512]{1,0:T(8,128)S(1)} %get-tuple-element.23), channel_id=1, source_target_pairs={{0,17},{1,49},{2,19},{3,51},{4,21},{5,53},{6,23},{7,55},{8,25},{9,... | collective-permute-start | bytes 196616 | tf_op jit(solution)/shard_map/ppermute | solution.py:174
  180.9 3.3 %collective-permute-start.20 = (f32[32,512]{1,0:T(8,128)S(1)}, f32[32,512]{1,0:T(8,128)S(1)}, u32[]{:S(2)}, u32[]{:S(2)}) collective-permute-start(f32[32,512]{1,0:T(8,128)S(1)} %get-tuple-element.30), channel_id=1, source_target_pairs={{0,16},{1,32},{2,18},{3,34},{4,20},{5,36},{6,22},{7,38},{8,24},{9,... | collective-permute-start | bytes 196616 | tf_op jit(solution)/shard_map/ppermute | solution.py:174
  184.2 2.8 %collective-permute-done.19 = f32[32,512]{1,0:T(8,128)S(1)} collective-permute-done((f32[32,512]{1,0:T(8,128)S(1)}, f32[32,512]{1,0:T(8,128)S(1)}, u32[]{:S(2)}, u32[]{:S(2)}) %collective-permute-start.19) | collective-permute-done | bytes 65568 | tf_op jit(solution)/shard_map/ppermute | solution.py:174
  (46 shorter events, 17.4 us)
Async XLA Ops:
  0.0 25.8 %collective-permute-start.1 = (bf16[3840,256]{1,0:T(8,128)(2,1)}, bf16[3840,256]{1,0:T(8,128)(2,1)S(1)}, u32[]{:S(2)}, u32[]{:S(2)}) collective-permute-start(bf16[3840,256]{1,0:T(8,128)(2,1)} %own_ref.1), channel_id=1, source_target_pairs={{0,1},{1,0},{2,3},{3,2},{4,5},{5,4},{6,7},{7,6},{8,9},{9,8},{10,11... | collective-permute-start | bytes 5898248 | tf_op jit(solution)/shard_map/ppermute | solution.py:164
  2.7 1.0 copy-start.2
  9.4 24.5 %collective-permute-start = (bf16[32,3840]{1,0:T(8,128)(2,1)S(1)}, bf16[32,3840]{1,0:T(8,128)(2,1)S(1)}, u32[]{:S(2)}, u32[]{:S(2)}) collective-permute-start(bf16[32,3840]{1,0:T(8,128)(2,1)S(1)} %get-tuple-element.16), channel_id=1, source_target_pairs={{0,256},{16,272},{32,288},{48,304},{64,320},{80,336},{96,352},{112... | collective-permute-start | bytes 737288 | tf_op jit(solution)/shard_map/ppermute | solution.py:265
  25.8 1.5 copy-start.1
  30.9 3.1 %copy-start = (bf16[3840,1024]{1,0:T(8,128)(2,1)}, bf16[3840,1024]{1,0:T(8,128)(2,1)S(1)}, u32[]{:S(2)}) copy-start(bf16[3840,1024]{1,0:T(8,128)(2,1)S(1)} %get-tuple-element.21.s_hbm) | copy-start | bytes 23592964
  35.3 36.7 %all-to-all-start.1 = ((bf16[8,32,3840]{2,1,0:T(8,128)(2,1)}), bf16[8,32,3840]{2,1,0:T(8,128)(2,1)}, u32[]{:S(2)}, u32[]{:S(2)}) async-start(bf16[8,32,3840]{2,1,0:T(8,128)(2,1)} %bitcast.3), calls=%async_computation.1 | async-start | bytes 3932160 | tf_op jit(solution)/shard_map/all_to_all | solution.py:231
  46.4 18.2 %collective-permute-start.2 = (bf16[32,3840]{1,0:T(8,128)(2,1)S(1)}, bf16[32,3840]{1,0:T(8,128)(2,1)S(1)}, u32[]{:S(2)}, u32[]{:S(2)}) collective-permute-start(bf16[32,3840]{1,0:T(8,128)(2,1)S(1)} %get-tuple-element.20), channel_id=1, source_target_pairs={{0,256},{16,272},{32,288},{48,304},{64,320},{80,336},{96,352},{112... | collective-permute-start | bytes 737288 | tf_op jit(solution)/shard_map/ppermute | solution.py:265
  72.0 54.1 %all-to-all-start = ((bf16[8,32,3840]{2,1,0:T(8,128)(2,1)}), bf16[8,32,3840]{2,1,0:T(8,128)(2,1)}, u32[]{:S(2)}, u32[]{:S(2)}) async-start(bf16[8,32,3840]{2,1,0:T(8,128)(2,1)} %bitcast.1), calls=%async_computation | async-start | bytes 3932160 | tf_op jit(solution)/shard_map/all_to_all | solution.py:231
  84.3 15.0 %collective-permute-start.3 = (f32[32,1024]{1,0:T(8,128)S(1)}, f32[32,1024]{1,0:T(8,128)S(1)}, u32[]{:S(2)}, u32[]{:S(2)}) collective-permute-start(f32[32,1024]{1,0:T(8,128)S(1)} %get-tuple-element.27), channel_id=1, source_target_pairs={{0,32},{1,481},{2,34},{3,483},{4,36},{5,485},{6,38},{7,487},{8,40}... | collective-permute-start | bytes 393224 | tf_op jit(solution)/shard_map/ppermute | solution.py:174
  96.4 12.8 %collective-permute-start.6 = (f32[32,1024]{1,0:T(8,128)S(1)}, f32[32,1024]{1,0:T(8,128)S(1)}, u32[]{:S(2)}, u32[]{:S(2)}) collective-permute-start(f32[32,1024]{1,0:T(8,128)S(1)} %get-tuple-element.28), channel_id=1, source_target_pairs={{0,32},{1,481},{2,34},{3,483},{4,36},{5,485},{6,38},{7,487},{8,40}... | collective-permute-start | bytes 393224 | tf_op jit(solution)/shard_map/ppermute | solution.py:174
  99.4 14.2 %collective-permute-start.4 = (f32[32,1024]{1,0:T(8,128)S(1)}, f32[32,1024]{1,0:T(8,128)S(1)}, u32[]{:S(2)}, u32[]{:S(2)}) collective-permute-start(f32[32,1024]{1,0:T(8,128)S(1)} %fusion.3.refs_0_), channel_id=1, source_target_pairs={{0,480},{1,33},{2,482},{3,35},{4,484},{5,37},{6,486},{7,39},{8,488... | collective-permute-start | bytes 393224 | tf_op jit(solution)/shard_map/ppermute | solution.py:174
  109.3 8.1 %collective-permute-start.7 = (f32[32,1024]{1,0:T(8,128)S(1)}, f32[32,1024]{1,0:T(8,128)S(1)}, u32[]{:S(2)}, u32[]{:S(2)}) collective-permute-start(f32[32,1024]{1,0:T(8,128)S(1)} %shard_map.51), channel_id=1, source_target_pairs={{0,480},{1,33},{2,482},{3,35},{4,484},{5,37},{6,486},{7,39},{8,488... | collective-permute-start | bytes 393224 | tf_op jit(solution)/shard_map/ppermute | solution.py:174
  117.4 6.9 %collective-permute-start.8 = (f32[32,1024]{1,0:T(8,128)S(1)}, f32[32,1024]{1,0:T(8,128)S(1)}, u32[]{:S(2)}, u32[]{:S(2)}) collective-permute-start(f32[32,1024]{1,0:T(8,128)S(1)} %shard_map.52), channel_id=1, source_target_pairs={{0,32},{1,481},{2,34},{3,483},{4,36},{5,485},{6,38},{7,487},{8,40}... | collective-permute-start | bytes 393224 | tf_op jit(solution)/shard_map/ppermute | solution.py:174
  119.3 6.9 %collective-permute-start.5 = (f32[32,1024]{1,0:T(8,128)S(1)}, f32[32,1024]{1,0:T(8,128)S(1)}, u32[]{:S(2)}, u32[]{:S(2)}) collective-permute-start(f32[32,1024]{1,0:T(8,128)S(1)} %fusion.4.refs_0_), channel_id=1, source_target_pairs={{0,32},{1,481},{2,34},{3,483},{4,36},{5,485},{6,38},{7,487},{8,40}... | collective-permute-start | bytes 393224 | tf_op jit(solution)/shard_map/ppermute | solution.py:174
  130.7 9.0 %collective-permute-start.10 = (f32[32,1024]{1,0:T(8,128)S(1)}, f32[32,1024]{1,0:T(8,128)S(1)}, u32[]{:S(2)}, u32[]{:S(2)}) collective-permute-start(f32[32,1024]{1,0:T(8,128)S(1)} %get-tuple-element.25), channel_id=1, source_target_pairs={{0,32},{1,481},{2,34},{3,483},{4,36},{5,485},{6,38},{7,487},{8,40}... | collective-permute-start | bytes 393224 | tf_op jit(solution)/shard_map/ppermute | solution.py:174
  134.6 13.3 %collective-permute-start.11 = (f32[32,1024]{1,0:T(8,128)S(1)}, f32[32,1024]{1,0:T(8,128)S(1)}, u32[]{:S(2)}, u32[]{:S(2)}) collective-permute-start(f32[32,1024]{1,0:T(8,128)S(1)} %fusion.5.refs_0_), channel_id=1, source_target_pairs={{0,384},{1,129},{2,386},{3,131},{4,388},{5,133},{6,390},{7,135},{8... | collective-permute-start | bytes 393224 | tf_op jit(solution)/shard_map/ppermute | solution.py:174
  137.8 10.1 %collective-permute-start.9 = (f32[32,1024]{1,0:T(8,128)S(1)}, f32[32,1024]{1,0:T(8,128)S(1)}, u32[]{:S(2)}, u32[]{:S(2)}) collective-permute-start(f32[32,1024]{1,0:T(8,128)S(1)} %get-tuple-element.26), channel_id=1, source_target_pairs={{0,32},{1,481},{2,34},{3,483},{4,36},{5,485},{6,38},{7,487},{8,40}... | collective-permute-start | bytes 393224 | tf_op jit(solution)/shard_map/ppermute | solution.py:174
  139.7 11.3 %collective-permute-start.13 = (f32[32,1024]{1,0:T(8,128)S(1)}, f32[32,1024]{1,0:T(8,128)S(1)}, u32[]{:S(2)}, u32[]{:S(2)}) collective-permute-start(f32[32,1024]{1,0:T(8,128)S(1)} %fusion.2.refs_0_), channel_id=1, source_target_pairs={{0,480},{1,33},{2,482},{3,35},{4,484},{5,37},{6,486},{7,39},{8,488... | collective-permute-start | bytes 393224 | tf_op jit(solution)/shard_map/ppermute | solution.py:174
  147.9 8.5 %collective-permute-start.12 = (f32[32,1024]{1,0:T(8,128)S(1)}, f32[32,1024]{1,0:T(8,128)S(1)}, u32[]{:S(2)}, u32[]{:S(2)}) collective-permute-start(f32[32,1024]{1,0:T(8,128)S(1)} %shard_map.55), channel_id=1, source_target_pairs={{0,480},{1,33},{2,482},{3,35},{4,484},{5,37},{6,486},{7,39},{8,488... | collective-permute-start | bytes 393224 | tf_op jit(solution)/shard_map/ppermute | solution.py:174
  151.1 7.3 %collective-permute-start.15 = (f32[32,1024]{1,0:T(8,128)S(1)}, f32[32,1024]{1,0:T(8,128)S(1)}, u32[]{:S(2)}, u32[]{:S(2)}) collective-permute-start(f32[32,1024]{1,0:T(8,128)S(1)} %fusion.1.refs_0_), channel_id=1, source_target_pairs={{0,32},{1,481},{2,34},{3,483},{4,36},{5,485},{6,38},{7,487},{8,40}... | collective-permute-start | bytes 393224 | tf_op jit(solution)/shard_map/ppermute | solution.py:174
  156.5 7.9 %collective-permute-start.14 = (f32[32,1024]{1,0:T(8,128)S(1)}, f32[32,1024]{1,0:T(8,128)S(1)}, u32[]{:S(2)}, u32[]{:S(2)}) collective-permute-start(f32[32,1024]{1,0:T(8,128)S(1)} %shard_map.56), channel_id=1, source_target_pairs={{0,32},{1,481},{2,34},{3,483},{4,36},{5,485},{6,38},{7,487},{8,40}... | collective-permute-start | bytes 393224 | tf_op jit(solution)/shard_map/ppermute | solution.py:174
  158.4 11.8 %collective-permute-start.16 = (f32[32,1024]{1,0:T(8,128)S(1)}, f32[32,1024]{1,0:T(8,128)S(1)}, u32[]{:S(2)}, u32[]{:S(2)}) collective-permute-start(f32[32,1024]{1,0:T(8,128)S(1)} %fusion), channel_id=1, source_target_pairs={{0,384},{1,129},{2,386},{3,131},{4,388},{5,133},{6,390},{7,135},{8... | collective-permute-start | bytes 393224 | tf_op jit(solution)/shard_map/ppermute | solution.py:174
  170.3 13.9 %collective-permute-start.17 = (f32[32,512]{1,0:T(8,128)S(1)}, f32[32,512]{1,0:T(8,128)S(1)}, u32[]{:S(2)}, u32[]{:S(2)}) collective-permute-start(f32[32,512]{1,0:T(8,128)S(1)} %get-tuple-element.24), channel_id=1, source_target_pairs={{1,48},{3,50},{5,52},{7,54},{9,56},{11,58},{13,60},{15,62},{17,32}... | collective-permute-start | bytes 196616 | tf_op jit(solution)/shard_map/ppermute | solution.py:174
  171.0 13.2 %collective-permute-start.18 = (f32[32,512]{1,0:T(8,128)S(1)}, f32[32,512]{1,0:T(8,128)S(1)}, u32[]{:S(2)}, u32[]{:S(2)}) collective-permute-start(f32[32,512]{1,0:T(8,128)S(1)} %get-tuple-element.29), channel_id=1, source_target_pairs={{0,1},{1,33},{2,3},{3,35},{4,5},{5,37},{6,7},{7,39},{8,9},{9,41},{... | collective-permute-start | bytes 196616 | tf_op jit(solution)/shard_map/ppermute | solution.py:174
  177.2 9.8 %collective-permute-start.19 = (f32[32,512]{1,0:T(8,128)S(1)}, f32[32,512]{1,0:T(8,128)S(1)}, u32[]{:S(2)}, u32[]{:S(2)}) collective-permute-start(f32[32,512]{1,0:T(8,128)S(1)} %get-tuple-element.23), channel_id=1, source_target_pairs={{0,17},{1,49},{2,19},{3,51},{4,21},{5,53},{6,23},{7,55},{8,25},{9,... | collective-permute-start | bytes 196616 | tf_op jit(solution)/shard_map/ppermute | solution.py:174
  180.9 7.7 %collective-permute-start.20 = (f32[32,512]{1,0:T(8,128)S(1)}, f32[32,512]{1,0:T(8,128)S(1)}, u32[]{:S(2)}, u32[]{:S(2)}) collective-permute-start(f32[32,512]{1,0:T(8,128)S(1)} %get-tuple-element.30), channel_id=1, source_target_pairs={{0,16},{1,32},{2,18},{3,34},{4,20},{5,36},{6,22},{7,38},{8,24},{9,... | collective-permute-start | bytes 196616 | tf_op jit(solution)/shard_map/ppermute | solution.py:174
